TPU v7x, 32 devices: a whole 2x2x4 slice. The times are simulated.
32 devices in a mesh: row: 4 (over y, x), col: 8 (over z, core).
Axes of the slice: x: 2, y: 2, z: 4, core: 2. Of those that a mesh axis runs over, the one named last changes fastest.
Arguments:
- features: bfloat16 [8192, 128], P('col'), may hold values from -6 to 6
- degrees: int32 [8192], replicated, may hold values from 1 to 400
- block_rows: int32 [4, 8, 384], P('row', 'col'), may hold values from 0 to 15
- block_cols: int32 [4, 8, 384], P('row', 'col'), may hold values from 0 to 7
- live_slots: int32 [4, 8], P('row', 'col'), may hold values from 96 to 384, as said below
- blocks: bfloat16 [4, 8, 384, 128, 128], P('row', 'col'), may hold values from 0 to 0.19921875
- weight: bfloat16 [128, 256], replicated, may hold values from -0.5 to 0.5
- cotangent: bfloat16 [8192, 256], P(('row', 'col')), may hold values from -6 to 6
Outputs:
- out_act: bfloat16 [8192, 256], P(('row', 'col'))
- feat_grad: float32 [8192, 128], P('col')
- weight_grad: float32 [128, 256], replicated
Inputs may be any that keep to these rules, and one draw needn't show every extreme that they name: `live_slots`: some tile uses all 384 slots.
All inputs are finite; a program needn't handle non-finite values.
Results may differ from a plain program's by a relative error of at most 0.0028.
Values sent between devices are 32-bit elements; how exact they have to be, the bound alone decides.
No kernel may reach another device: no remote copies, remote signals or barrier semaphores. Data moves between devices by JAX's collectives and lax.ppermute only.
A program may use at most 192 MiB of HBM per device.

v0:
```python
import jax
import jax.numpy as jnp
from jax import lax
from jax.sharding import PartitionSpec as P

HIGH = lax.Precision.HIGHEST


def smooth_act(values):
    return jax.nn.gelu(values, approximate=True)


def body(features, degrees, block_rows, block_cols, live_slots, blocks, weight, cotangent):
    col_count = lax.axis_size("col")
    row_index = lax.axis_index("row")
    col_index = lax.axis_index("col")
    node_dev = cotangent.shape[0]
    col_nodes = features.shape[0]
    row_nodes = node_dev * col_count
    nodes = col_nodes * col_count
    edge = blocks.shape[-1]
    inv_all = lax.rsqrt(degrees.astype(jnp.float32))
    inv_cols = lax.dynamic_slice_in_dim(inv_all, col_index * col_nodes, col_nodes)
    inv_rows = lax.dynamic_slice_in_dim(
        inv_all, (row_index * col_count + col_index) * node_dev, node_dev
    )
    scaled = (inv_cols[:, None] * features.astype(jnp.float32)).astype(jnp.bfloat16)
    tile_blocks = blocks[0, 0]
    row_slots = block_rows[0, 0]
    col_slots = block_cols[0, 0]
    in_use = (jnp.arange(tile_blocks.shape[0]) < live_slots[0, 0])[:, None, None]
    weight_wide = weight.astype(jnp.float32)
    width_now = scaled.shape[1]
    picked = scaled.reshape(col_nodes // edge, edge, width_now)[col_slots]
    products = jnp.einsum("sij,sjf->sif", tile_blocks, picked, preferred_element_type=jnp.float32)
    products = jnp.where(in_use, products, 0.0)
    summed_rows = jax.ops.segment_sum(products, row_slots, num_segments=row_nodes // edge)
    summed = lax.psum_scatter(
        summed_rows.reshape(row_nodes, width_now), "col", scatter_dimension=0, tiled=True
    )
    propagated = inv_rows[:, None] * summed
    preact = jnp.dot(propagated, weight_wide, precision=HIGH)
    out_act = smooth_act(preact).astype(jnp.bfloat16)
    unused, pullback = jax.vjp(smooth_act, preact)
    gprime = pullback(cotangent.astype(jnp.float32))[0]
    pulled = inv_rows[:, None] * jnp.dot(gprime, weight_wide.T, precision=HIGH)
    gathered = lax.all_gather(pulled, "col", axis=0, tiled=True)
    width_now = gathered.shape[1]
    picked = gathered.reshape(row_nodes // edge, edge, width_now)[row_slots]
    products = jnp.einsum("sij,sif->sjf", tile_blocks.astype(jnp.float32), picked, precision=HIGH)
    products = jnp.where(in_use, products, 0.0)
    summed_cols = jax.ops.segment_sum(products, col_slots, num_segments=col_nodes // edge)
    col_part = summed_cols.reshape(col_nodes, width_now)
    weight_part = lax.dot_general(propagated, gprime, (((0,), (0,)), ((), ())), precision=HIGH)
    col_total = lax.psum(col_part, "row")
    weight_total = lax.psum(weight_part, ("row", "col"))
    feat_grad = inv_cols[:, None] * col_total
    return (out_act, feat_grad, weight_total * float(nodes) ** (-0.5))


def solution(mesh):
    return jax.shard_map(
        body,
        mesh=mesh,
        in_specs=(
            P("col", None),
            P(),
            P("row", "col", None),
            P("row", "col", None),
            P("row", "col"),
            P("row", "col", None, None, None),
            P(),
            P(("row", "col"), None),
        ),
        out_specs=(P(("row", "col"), None), P("col", None), P()),
        check_vma=False,
    )
```

profile of v0, /device:TPU:0, one launch (start us, length us, event | category | flops | bytes accessed | tf_op | source)
XLA Modules:
  0.0 363.4 jit_solution(16968515573577608716)
XLA Ops:
  7.2 0.0 reduce-scatter.2.cloned.1.call-start
  7.2 0.8 convert_rsqrt_fusion
  8.0 0.7 fusion.23
  9.4 1.2 multiply_convert_fusion
  10.6 11.2 %gather_fusion = bf16[384,128,128]{2,1,0:T(8,128)(2,1)} fusion(bf16[8,128,128]{2,1,0:T(8,128)(2,1)S(1)} %bitcast.29, s32[1024]{0:T(1024)S(1)} %pad_clamp_fusion.1), kind=kCustom, calls=%fused_computation | custom fusion | bytes 25167360 | tf_op jit(solution)/shard_map/gather | solution.py:34
  21.8 22.7 %select_bitcast_fusion.1 = f32[384,128,128]{1,2,0:T(8,128)} fusion(pred[384]{0:T(512)(128)(4,1)S(1)} %iota_compare_fusion, bf16[384,128,128]{2,1,0:T(8,128)(2,1)} %gather_fusion, bf16[1,1,384,128,128]{4,3,2,1,0:T(8,128)(2,1)} %param.13), kind=kOutput, calls=%fused_computation.5 | convolution fusion | flops 1616904192 | bytes 50332032 | tf_op jit(solution)/shard_map/sij,sjf->sif/dot_general | solution.py:35
  44.4 24.7 %copy.14 = f32[384,128,128]{2,1,0:T(8,128)} copy(f32[384,128,128]{1,2,0:T(8,128)} %select_bitcast_fusion.1) | data formatting | bytes 50331648 | tf_op jit(solution)/shard_map/jit(_where)/select_n | solution.py:36
  69.1 0.1 broadcast_in_dim.29
  69.3 50.2 %scatter_fusion = f32[16,128,128]{2,1,0:T(8,128)S(1)} fusion(f32[16,128,128]{2,1,0:T(8,128)S(1)} %broadcast_in_dim.29, s32[384]{0:T(512)S(1)} %reduce, f32[384,128,128]{2,1,0:T(8,128)} %copy.14), kind=kCustom, calls=%fused_computation.2 | custom fusion | flops 6291456 | bytes 75499008 | tf_op jit(solution)/shard_map/scatter-add | solution.py:37
  119.5 1.0 copy-done.2
  120.5 0.0 reduce-scatter.2.cloned.1.call-update
  120.5 0.0 all-gather.2.cloned.1.call-start
  120.5 0.1 dynamic_slice.6
  120.6 35.0 %reduce-scatter.2.cloned.1.call-done = f32[256,128]{1,0:T(8,128)} async-done(((f32[2048,128]{1,0:T(8,128)}), f32[256,128]{1,0:T(8,128)}) %reduce-scatter.2.cloned.1.call-update) | async-done | bytes 131088 | tf_op jit(solution)/shard_map/reduce_scatter | solution.py:38
  155.7 1.9 multiply_convert_fusion.1
  157.6 1.1 convolution_multiply_fusion
  158.7 0.0 all-gather.2.cloned.1.call-update
  158.7 0.0 all-reduce.5.cloned.1.call-start
  158.8 2.1 fusion.17
  160.9 0.0 all-reduce.5.cloned.1.call-update
  160.9 0.0 all-reduce.3.cloned.1.call-start
  161.0 18.4 %all-gather.2.cloned.1.call-done = f32[2048,128]{1,0:T(8,128)} async-done(((f32[256,128]{1,0:T(8,128)}), f32[2048,128]{1,0:T(8,128)}) %all-gather.2.cloned.1.call-update) | async-done | bytes 1048592 | tf_op jit(solution)/shard_map/all_gather | solution.py:47
  179.3 16.4 %gather_fusion.1 = f32[384,128,128]{2,1,0:T(8,128)} fusion(f32[16,128,128]{2,1,0:T(8,128)} %bitcast.30, s32[1024]{0:T(1024)S(1)} %pad_clamp_fusion), kind=kCustom, calls=%fused_computation.1 | custom fusion | bytes 50333184 | tf_op jit(solution)/shard_map/gather | solution.py:49
  195.8 30.2 %select_bitcast_fusion = f32[384,128,128]{1,2,0:T(8,128)} fusion(pred[384]{0:T(512)(128)(4,1)S(1)} %iota_compare_fusion, f32[384,128,128]{2,1,0:T(8,128)} %gather_fusion.1, bf16[1,1,384,128,128]{4,3,2,1,0:T(8,128)(2,1)} %param.13), kind=kOutput, calls=%fused_computation.4 | convolution fusion | flops 9669967872 | bytes 62914944 | tf_op jit(solution)/shard_map/sij,sif->sjf/dot_general | solution.py:50
  225.9 24.7 %copy.16 = f32[384,128,128]{2,1,0:T(8,128)} copy(f32[384,128,128]{1,2,0:T(8,128)} %select_bitcast_fusion) | data formatting | bytes 50331648 | tf_op jit(solution)/shard_map/jit(_where)/select_n | solution.py:51
  250.6 50.2 %scatter_fusion.1 = f32[8,128,128]{2,1,0:T(8,128)S(1)} fusion(f32[8,128,128]{2,1,0:T(8,128)S(1)} %broadcast_in_dim.32, s32[384]{0:T(512)S(1)} %reduce.2, f32[384,128,128]{2,1,0:T(8,128)} %copy.16), kind=kCustom, calls=%fused_computation.3 | custom fusion | flops 6291456 | bytes 75499008 | tf_op jit(solution)/shard_map/scatter-add | solution.py:52
  300.8 0.8 copy-done.1
  301.6 0.0 all-reduce.3.cloned.1.call-update
  301.6 5.3 %all-reduce.5.cloned.1.call-done = f32[128,256]{1,0:T(8,128)} async-done(((f32[128,256]{1,0:T(8,128)}), f32[128,256]{1,0:T(8,128)}) %all-reduce.5.cloned.1.call-update) | async-done | bytes 131088 | tf_op jit(solution)/shard_map/psum | solution.py:56
  307.0 1.6 broadcast_multiply_fusion.1
  308.6 46.3 %all-reduce.3.cloned.1.call-done = f32[1024,128]{1,0:T(8,128)} async-done(((f32[1024,128]{1,0:T(8,128)}), f32[1024,128]{1,0:T(8,128)}) %all-reduce.3.cloned.1.call-update) | async-done | bytes 524304 | tf_op jit(solution)/shard_map/psum | solution.py:55
  354.8 2.0 broadcast_multiply_fusion
  (18 shorter events, 0.2 us)
Async XLA Ops:
  7.2 148.5 %copy-start = (bf16[128,256]{1,0:T(8,128)(2,1)S(1)}, bf16[128,256]{1,0:T(8,128)(2,1)}, u32[]{:S(2)}) copy-start(bf16[128,256]{1,0:T(8,128)(2,1)} %param.14) | copy-start | bytes 196612
  7.2 148.5 %reduce-scatter.2.cloned.1.call-start = ((), (), s32[]{:S(2)}) async-start(), calls=%async_computation.1 | async-start | bytes 1179648 | tf_op jit(solution)/shard_map/reduce_scatter | solution.py:38
  44.4 24.7 %copy-start.4 = (s32[1,1,384]{2,1,0:T(1,128)S(1)}, s32[1,1,384]{2,1,0:T(1,128)}, u32[]{:S(2)}) copy-start(s32[1,1,384]{2,1,0:T(1,128)} %param.10) | copy-start | bytes 4612
  69.2 88.4 %copy-start.5 = (bf16[256,256]{1,0:T(8,128)(2,1)S(1)}, bf16[256,256]{1,0:T(8,128)(2,1)}, u32[]{:S(2)}) copy-start(bf16[256,256]{1,0:T(8,128)(2,1)} %param.15) | copy-start | bytes 393220
  69.3 89.5 %copy-start.3 = (s32[1,1,384]{2,1,0:T(1,128)S(1)}, s32[1,1,384]{2,1,0:T(1,128)}, u32[]{:S(2)}) copy-start(s32[1,1,384]{2,1,0:T(1,128)} %param.11) | copy-start | bytes 4612
  119.5 1.0 copy-start.2
  120.5 58.9 %all-gather.2.cloned.1.call-start = ((), (), s32[]{:S(2)}) async-start(), calls=%async_computation.2 | async-start | bytes 1179648 | tf_op jit(solution)/shard_map/all_gather | solution.py:47
  158.7 148.3 %all-reduce.5.cloned.1.call-start = ((), (), s32[]{:S(2)}) async-start(), calls=%async_computation.4 | async-start | bytes 262144 | tf_op jit(solution)/shard_map/psum | solution.py:56
  160.9 193.9 %all-reduce.3.cloned.1.call-start = ((), (), s32[]{:S(2)}) async-start(), calls=%async_computation.3 | async-start | bytes 1048576 | tf_op jit(solution)/shard_map/psum | solution.py:55
  300.8 0.8 copy-start.1
Sparse Core Ops, SparseCore 0:
  120.6 35.0 reduce-scatter.1
  158.8 20.4 all-gather.1
  184.9 122.0 all-reduce.4
  310.4 44.3 all-reduce.2
where the time goes:
time: 366 us; the launch traced here: 363 us
  other arithmetic  107 us (29%)
  waiting for transfers between devices  105 us (29%)
  local copies, waits for them, and re-layouts  79 us (22%)
  matrix products  57.9 us (16%)
  between operations  14.5 us (4%)
    scatter-add x1, other arithmetic, body(): jax.ops.segment_sum(products, row_slots, num_segments=row_nodes // edge)  50.2 us
    scatter-add x1, other arithmetic, body(): jax.ops.segment_sum(products, col_slots, num_segments=col_nodes // edge)  50.2 us
    select_n x2, local copies, waits for them, and re-layouts, body(): products = jnp.where(in_use, products, 0.0)  49.4 us
    psum x1, waiting for transfers between devices, body(): col_total = lax.psum(col_part, 'row')  46.3 us
    reduce_scatter x1, waiting for transfers between devices, body(): lax.psum_scatter(summed_rows.reshape(row_nodes, width_now), 'col', scatte...  35 us
    dot_general x1, matrix products, body(): jnp.einsum('sij,sif->sjf', tile_blocks.astype(jnp.float32), picked, preci...  30.2 us
    dot_general x1, matrix products, body(): jnp.einsum('sij,sjf->sif', tile_blocks, picked, preferred_element_type=jn...  22.7 us
    all_gather x1, waiting for transfers between devices, body(): gathered = lax.all_gather(pulled, 'col', axis=0, tiled=True)  18.4 us
  transfers between devices with their start and end apart: 4, of which 4 were waited for; matrix products, arithmetic and copies ran while one was open for 34% of the time, Pallas kernels for 0%

commit v1 on v0

v1 whole, which is shorter than its diff:
```python
import functools

import jax
import jax.numpy as jnp
from jax import lax
from jax.experimental import pallas as pl
from jax.experimental.pallas import tpu as pltpu
from jax.sharding import PartitionSpec as P

HIGH = lax.Precision.HIGHEST
F32 = jnp.float32
BF16 = jnp.bfloat16
EDGE = 128
QUARTERS = 4
GROUP = 8
ACC_BYTES = 16 << 20
GELU_C = 0.7978845608028654
GELU_K = 0.044715


def inv_column(deg_ref, start):
    row = lax.rsqrt(deg_ref[pl.ds(start, 1), :].astype(F32))
    return jnp.transpose(jnp.broadcast_to(row, (EDGE, EDGE)))


def forward_kernel(
    n_col, chunk, panel_dev,
    rows_ref, cols_ref, live_ref, deg_ref, feat_ref, blocks_ref,
    keep_ref, send_ref, dense_ref,
    buf, acc0, acc1, acc2, acc3, hi_scr, lo_scr, scaled, in_sems, out_sems,
):
    accs = (acc0, acc1, acc2, acc3)
    n_chip = n_col // 2
    slots = buf.shape[0]
    part = EDGE // QUARTERS
    col_nodes, width = feat_ref.shape
    col_blocks = col_nodes // EDGE
    node_dev = keep_ref.shape[1]
    dev_blocks = node_dev // EDGE
    panel_blocks = panel_dev * dev_blocks
    positions = panel_blocks * col_blocks
    n_panels = n_col // panel_dev
    n_chunks = slots // chunk
    col = lax.axis_index("col")
    chip, core = col // 2, col % 2
    live = live_ref[0, 0]

    def block_copy(c):
        span = pl.ds(c * chunk, chunk)
        return pltpu.make_async_copy(blocks_ref.at[0, 0, span], buf.at[span], in_sems.at[c])

    def dense_copy(panel, j):
        span = pl.ds(j * node_dev, node_dev)
        there = pl.ds((panel * panel_dev + j) * node_dev, node_dev)
        return pltpu.make_async_copy(hi_scr.at[span], dense_ref.at[there], out_sems.at[j])

    for c in range(n_chunks):
        block_copy(c).start()

    for k in range(col_blocks):
        inv = inv_column(deg_ref, col * col_blocks + k)
        span = pl.ds(k * EDGE, EDGE)
        scaled[span, :] = (inv * feat_ref[span, :].astype(F32)).astype(BF16)

    def do_panel(panel, first):
        base = panel * panel_blocks

        @pl.loop(0, positions)
        def _(p):
            for acc in accs:
                acc[p] = jnp.zeros((part, EDGE), F32)

        @pl.loop(0, n_chunks)
        def _(c):
            if first is True:
                block_copy(c).wait()
            else:
                @pl.when(first)
                def _():
                    block_copy(c).wait()

            @pl.loop(0, chunk // GROUP)
            def _(g):
                for u in range(GROUP):
                    s = c * chunk + g * GROUP + u
                    r = rows_ref[0, 0, s] - base
                    ok = s < live
                    if n_panels > 1:
                        ok = ok & (r >= 0) & (r < panel_blocks)
                    p = jnp.where(ok, r * col_blocks + cols_ref[0, 0, s], positions)
                    for q in range(QUARTERS):
                        accs[q][p] += buf[s, q * part:(q + 1) * part, :].astype(F32)

        @pl.loop(0, panel_dev)
        def _(j):
            if first is not True:
                @pl.when(jnp.logical_not(first))
                def _():
                    dense_copy(panel, j).wait()
            for b in range(dev_blocks):
                for cb in range(col_blocks):
                    for q in range(QUARTERS):
                        value = accs[q][(j * dev_blocks + b) * col_blocks + cb]
                        hi = value.astype(BF16)
                        lo = (value - hi.astype(F32)).astype(BF16)
                        at = b * EDGE + q * part
                        lanes = slice(cb * EDGE, (cb + 1) * EDGE)
                        hi_scr[pl.ds(j * node_dev + at, part), lanes] = hi
                        lo_scr[pl.ds(at, part), lanes] = lo
            dense_copy(panel, j).start()
            total = jnp.dot(
                hi_scr[pl.ds(j * node_dev, node_dev), :], scaled[...], preferred_element_type=F32
            ) + jnp.dot(lo_scr[...], scaled[...], preferred_element_type=F32)
            dev = panel * panel_dev + j
            place = lax.rem(dev // 2 - chip + n_chip, n_chip)
            mine = dev % 2 == core

            @pl.when(mine)
            def _():
                keep_ref[place] = total

            @pl.when(jnp.logical_not(mine))
            def _():
                send_ref[place] = total

    if n_panels == 1:
        do_panel(0, True)
    else:
        @pl.loop(0, n_panels)
        def _(panel):
            do_panel(panel, panel == 0)

    for j in range(panel_dev):
        dense_copy(n_panels - 1, j).wait()


def middle_kernel(
    n_col, n_row, n_in, scale, deg_ref, cot_ref, weight_ref, *refs
):
    parts, (act_ref, pulled_ref, wkeep_ref, wsend_ref) = refs[:n_in], refs[n_in:]
    row, col = lax.axis_index("row"), lax.axis_index("col")
    core = col % 2
    node_dev = cot_ref.shape[0]
    dev_blocks = node_dev // EDGE
    summed = parts[0][...]
    for ref in parts[1:]:
        summed = summed + ref[...]
    base = (row * n_col + col) * dev_blocks
    inv = jnp.concatenate([inv_column(deg_ref, base + k) for k in range(dev_blocks)], axis=0)
    weight = weight_ref[...].astype(F32)
    propagated = inv * summed
    v = jnp.dot(propagated, weight, precision=HIGH, preferred_element_type=F32)
    t = jnp.tanh(GELU_C * (v + GELU_K * v * v * v))
    act_ref[...] = (0.5 * v * (1.0 + t)).astype(BF16)
    slope = 0.5 * (1.0 + t) + 0.5 * v * (1.0 - t * t) * (GELU_C * (1.0 + 3.0 * GELU_K * v * v))
    gprime = cot_ref[...].astype(F32) * slope
    pulled = inv * lax.dot_general(
        gprime, weight, (((1,), (1,)), ((), ())), precision=HIGH, preferred_element_type=F32
    )
    pulled_ref[...] = jnp.transpose(pulled)
    wpart = scale * lax.dot_general(
        propagated, gprime, (((0,), (0,)), ((), ())), precision=HIGH, preferred_element_type=F32
    )
    pieces, piece = wkeep_ref.shape[0], wkeep_ref.shape[1]
    for half in range(2):
        for j in range(pieces):
            at = (half * pieces + j) * piece
            place = lax.rem(j - row + n_row, n_row)

            @pl.when(core == half)
            def _():
                wkeep_ref[place] = wpart[at:at + piece]

            @pl.when(core != half)
            def _():
                wsend_ref[place] = wpart[at:at + piece]


def backward_kernel(n_col, deg_ref, dense_ref, *refs):
    parts, (out_ref, dense, lhs, sems) = refs[:n_col], refs[n_col:]
    n_chip = n_col // 2
    col = lax.axis_index("col")
    chip, core = col // 2, col % 2
    width, node_dev = parts[0].shape
    col_nodes = dense.shape[1]

    def dense_copy(j):
        span = pl.ds(j * node_dev, node_dev)
        return pltpu.make_async_copy(dense_ref.at[span], dense.at[span], sems.at[j])

    for j in range(n_col):
        dense_copy(j).start()
    for i in range(n_col):
        k, other = i % n_chip, i // n_chip
        source = lax.rem(chip - k + n_chip, n_chip) * 2 + (core if other == 0 else 1 - core)
        lanes = pl.ds(pl.multiple_of(source * node_dev, EDGE), node_dev)
        value = parts[i][...]
        hi = value.astype(BF16)
        lhs[:width, lanes] = hi
        lhs[width:, lanes] = (value - hi.astype(F32)).astype(BF16)
    for j in range(n_col):
        dense_copy(j).wait()
    step = 2 * EDGE if col_nodes % (2 * EDGE) == 0 else EDGE
    for n in range(col_nodes // step):
        both = jnp.dot(lhs[...], dense[:, n * step:(n + 1) * step], preferred_element_type=F32)
        total = both[:width] + both[width:]
        for b in range(step // EDGE):
            at = n * step + b * EDGE
            inv = inv_column(deg_ref, col * (col_nodes // EDGE) + at // EDGE)
            out_ref[at:at + EDGE, :] = inv * jnp.transpose(total[:, b * EDGE:(b + 1) * EDGE])


def whole_vmem():
    return pl.BlockSpec(memory_space=pltpu.VMEM)


def body(n_row, n_col, features, degrees, block_rows, block_cols, live_slots, blocks, weight, cotangent):
    n_chip = n_col // 2
    node_dev, hidden = cotangent.shape
    col_nodes, width = features.shape
    row_nodes = node_dev * n_col
    nodes = col_nodes * n_col
    slots = blocks.shape[2]
    deg = degrees.reshape(nodes // EDGE, EDGE)
    col_blocks = col_nodes // EDGE
    chunk = 32

    panel_dev = n_col
    while panel_dev % 2 == 0 and panel_dev * node_dev * col_nodes * 4 > ACC_BYTES:
        panel_dev //= 2
    positions = panel_dev * (node_dev // EDGE) * col_blocks
    smem = pl.BlockSpec(memory_space=pltpu.SMEM)
    hbm = pl.BlockSpec(memory_space=pl.ANY)
    vmem = whole_vmem()
    limit = 60 << 20

    keep, send, dense = pl.pallas_call(
        functools.partial(forward_kernel, n_col, chunk, panel_dev),
        out_shape=(
            jax.ShapeDtypeStruct((n_chip, node_dev, width), F32),
            jax.ShapeDtypeStruct((n_chip, node_dev, width), F32),
            jax.ShapeDtypeStruct((row_nodes, col_nodes), BF16),
        ),
        in_specs=[smem, smem, smem, vmem, vmem, hbm],
        out_specs=(vmem, vmem, hbm),
        scratch_shapes=[pltpu.VMEM((slots, EDGE, EDGE), BF16)]
        + [pltpu.VMEM((positions + 1, EDGE // QUARTERS, EDGE), F32) for _ in range(QUARTERS)]
        + [
            pltpu.VMEM((panel_dev * node_dev, col_nodes), BF16),
            pltpu.VMEM((node_dev, col_nodes), BF16),
            pltpu.VMEM((col_nodes, width), BF16),
            pltpu.SemaphoreType.DMA((slots // chunk,)),
            pltpu.SemaphoreType.DMA((panel_dev,)),
        ],
        compiler_params=pltpu.CompilerParams(vmem_limit_bytes=limit),
        name="densify_forward",
    )(block_rows, block_cols, live_slots, deg, features, blocks)

    swap = [(i, i ^ 1) for i in range(n_col)]

    def to_sibling(x):
        return lax.ppermute(x, "col", swap)

    def to_chip(x, k):
        pairs = [(i, ((i // 2 + k) % n_chip) * 2 + i % 2) for i in range(n_col)]
        return lax.ppermute(x, "col", pairs)

    def to_row(x, k):
        return lax.ppermute(x, "row", [(i, (i + k) % n_row) for i in range(n_row)])

    def row_flip(x, bit):
        return lax.ppermute(x, "row", [(i, i ^ (1 << bit)) for i in range(n_row)])

    got = to_sibling(send)
    arrived = [to_chip(keep[k] + got[k], k) for k in range(1, n_chip)]
    parts = [keep[0], got[0]] + arrived

    half = width // 2
    out_act, pulled, wkeep, wsend = pl.pallas_call(
        functools.partial(middle_kernel, n_col, n_row, len(parts), float(nodes) ** (-0.5)),
        out_shape=(
            jax.ShapeDtypeStruct((node_dev, hidden), BF16),
            jax.ShapeDtypeStruct((width, node_dev), F32),
            jax.ShapeDtypeStruct((n_row, half // n_row, hidden), F32),
            jax.ShapeDtypeStruct((n_row, half // n_row, hidden), F32),
        ),
        in_specs=[vmem] * (3 + len(parts)),
        out_specs=(vmem,) * 4,
        compiler_params=pltpu.CompilerParams(vmem_limit_bytes=limit),
        name="middle",
    )(deg, cotangent, weight, *parts)

    own = [pulled] + [to_chip(pulled, k) for k in range(1, n_chip)]
    sibling = [to_sibling(x) for x in own]
    col_part = pl.pallas_call(
        functools.partial(backward_kernel, n_col),
        out_shape=jax.ShapeDtypeStruct((col_nodes, width), F32),
        in_specs=[vmem, hbm] + [vmem] * n_col,
        out_specs=vmem,
        scratch_shapes=[
            pltpu.VMEM((row_nodes, col_nodes), BF16),
            pltpu.VMEM((2 * width, row_nodes), BF16),
            pltpu.SemaphoreType.DMA((n_col,)),
        ],
        compiler_params=pltpu.CompilerParams(vmem_limit_bytes=limit),
        name="backward",
    )(deg, dense, *own, *sibling)

    bits = n_row.bit_length() - 1
    if n_row == 1 << bits and bits > 0:
        pieces = bits
        while col_nodes % (8 * pieces):
            pieces -= 1
        size = col_nodes // pieces
        done = []
        for i in range(pieces):
            value = col_part[i * size:(i + 1) * size]
            for t in range(bits):
                value = value + row_flip(value, (i + t) % bits)
            done.append(value)
        feat_grad = jnp.concatenate(done, axis=0) if pieces > 1 else done[0]
    else:
        feat_grad = lax.psum(col_part, "row")

    wgot = to_sibling(wsend)
    wpiece = wkeep[0] + wgot[0]
    for k in range(1, n_row):
        wpiece = wpiece + to_row(wkeep[k] + wgot[k], k)
    others = jnp.stack([wpiece] + [to_chip(wpiece, k) for k in range(1, n_chip)])
    chip = lax.axis_index("col") // 2
    ordered = jnp.roll(others[::-1], chip + 1, axis=0)
    wsum = ordered[0]
    for k in range(1, n_chip):
        wsum = wsum + ordered[k]
    ring = jnp.stack([wsum] + [to_row(wsum, k) for k in range(1, n_row)])
    whole_half = jnp.roll(ring[::-1], lax.axis_index("row") + 1, axis=0).reshape(half, hidden)
    other_half = to_sibling(whole_half)
    low = lax.axis_index("col") % 2 == 0
    weight_grad = jnp.concatenate(
        [jnp.where(low, whole_half, other_half), jnp.where(low, other_half, whole_half)], axis=0
    )
    return out_act, feat_grad, weight_grad


def solution(mesh):
    n_row, n_col = mesh.shape["row"], mesh.shape["col"]
    return jax.shard_map(
        functools.partial(body, n_row, n_col),
        mesh=mesh,
        in_specs=(
            P("col", None),
            P(),
            P("row", "col", None),
            P("row", "col", None),
            P("row", "col"),
            P("row", "col", None, None, None),
            P(),
            P(("row", "col"), None),
        ),
        out_specs=(P(("row", "col"), None), P("col", None), P()),
        check_vma=False,
    )
```

time: 366 us -> 97.1 us (0.27)
  other arithmetic: 107 us -> 6.06 us
  local copies, waits for them, and re-layouts: 79 us -> 2.46 us
  waiting for transfers between devices: 105 us -> 39 us
  matrix products: 57.9 us -> 0 us
  starting transfers between devices: 0.16 us -> 26.4 us
  Pallas kernels: 0 us -> 21.3 us
  between operations: 14.5 us -> 1.47 us
    scatter-add x2 -> x0, other arithmetic: 100 us -> none  [the longest x1 50.2 us: body(): jax.ops.segment_sum(products, row_slots, num_segments=row_nodes // edge)]
    dot_general x5 -> x0, matrix products: 57.9 us -> none  [the longest x1 30.2 us: body(): jnp.einsum('sij,sif->sjf', tile_blocks.astype(jnp.float32), picked, preci...]
    psum x2 -> x0, waiting for transfers between devices: 51.6 us -> none  [the longest x1 46.3 us: body(): col_total = lax.psum(col_part, 'row')]
    select_n x2 -> x0, local copies, waits for them, and re-layouts: 49.4 us -> none  [body(): products = jnp.where(in_use, products, 0.0)]
    ppermute x0 -> x26, waiting for transfers between devices: none -> 39 us  [the longest x9 22.2 us: to_chip(): return lax.ppermute(x, 'col', pairs)]
    reduce_scatter x1 -> x0, waiting for transfers between devices: 35 us -> none  [body(): lax.psum_scatter(summed_rows.reshape(row_nodes, width_now), 'col', scatte...]
    gather x2 -> x0, local copies, waits for them, and re-layouts: 27.7 us -> none  [the longest x1 16.4 us: body(): picked = gathered.reshape(row_nodes // edge, edge, width_now)[row_slots]]
    ppermute x0 -> x26, starting transfers between devices: none -> 26.4 us  [the longest x9 13.5 us: to_chip(): return lax.ppermute(x, 'col', pairs)]
  transfers between devices with their start and end apart: 4 -> 26, of which waited for: 4 -> 14; matrix products, arithmetic and copies ran while one was open for 34% -> 3% of each run, Pallas kernels for 0% -> 6%
where the time goes in v1:
time: 97.1 us; the launch traced here: 96.7 us
  waiting for transfers between devices  39 us (40%)
  starting transfers between devices  26.4 us (27%)
  Pallas kernels  21.3 us (22%)
  other arithmetic  6.06 us (6%)
  local copies, waits for them, and re-layouts  2.46 us (3%)
  between operations  1.47 us (2%)
    ppermute x9, waiting for transfers between devices, to_chip(): return lax.ppermute(x, 'col', pairs)  22.2 us
    ppermute x9, starting transfers between devices, to_chip(): return lax.ppermute(x, 'col', pairs)  13.5 us
    pallas_call x1, Pallas kernels, body(): pl.pallas_call(functools.partial(forward_kernel, n_col, chunk, panel_dev)...  12.3 us
    ppermute x4, waiting for transfers between devices, row_flip(): return lax.ppermute(x, 'row', [(i, i ^ 1 << bit) for i in range(n_row)])  11.4 us
    ppermute x6, starting transfers between devices, to_row(): return lax.ppermute(x, 'row', [(i, (i + k) % n_row) for i in range(n_row)])  8.04 us
    pallas_call x1, Pallas kernels, body(): pl.pallas_call(functools.partial(backward_kernel, n_col), out_shape=jax.S...  5.74 us
    ppermute x4, starting transfers between devices, row_flip(): return lax.ppermute(x, 'row', [(i, i ^ 1 << bit) for i in range(n_row)])  3.73 us
    pallas_call x1, Pallas kernels, body(): pl.pallas_call(functools.partial(middle_kernel, n_col, n_row, len(parts),...  3.29 us
  transfers between devices with their start and end apart: 26, of which 14 were waited for; matrix products, arithmetic and copies ran while one was open for 3% of the time, Pallas kernels for 6%

profile of v1, /device:TPU:0, one launch (start us, length us, event | category | flops | bytes accessed | tf_op | source)
XLA Modules:
  0.0 96.7 jit_solution(13378793174357913047)
XLA Ops:
  1.3 12.3 %densify_forward.1 = (f32[4,256,128]{2,1,0:T(8,128)}, f32[4,256,128]{2,1,0:T(8,128)}, bf16[2048,1024]{1,0:T(8,128)(2,1)}) custom-call(s32[1,1,384]{2,1,0:T(1,128)} %rows_ref.1, s32[1,1,384]{2,1,0:T(1,128)} %cols_ref.1, s32[1,1]{1,0:T(1,128)S(6)} %copy.11.live_ref, s32[64,128]{1,0:T(8,128)} %bitcast.37, bf16[1024,128]{1,0:T(8,128)(2,1)} %feat_ref.1, ...), custom_call_target="tpu_custom_call" | custom-call | tf_op jit(solution)/shard_map/densify_forward/pallas_call | solution.py:237
  14.1 1.7 %collective-permute-done = f32[4,256,128]{2,1,0:T(8,128)S(1)} collective-permute-done((f32[4,256,128]{2,1,0:T(8,128)}, f32[4,256,128]{2,1,0:T(8,128)S(1)}, u32[]{:S(2)}, u32[]{:S(2)}) %collective-permute-start) | collective-permute-done | bytes 524320 | tf_op jit(solution)/shard_map/ppermute | solution.py:262
  15.8 1.8 %fusion = (f32[256,128]{1,0:T(8,128)S(1)}, f32[256,128]{1,0:T(8,128)S(1)}, f32[256,128]{1,0:T(8,128)S(1)}, f32[256,128]{1,0:T(8,128)}, f32[256,128]{1,0:T(8,128)}) fusion(f32[4,256,128]{2,1,0:T(8,128)S(1)} %collective-permute-done, f32[4,256,128]{2,1,0:T(8,128)} %get-tuple-element.11), kind=kLoop, calls=%fused_computation.2 | loop fusion | flops 98304 | bytes 1703936 | tf_op jit(solution)/shard_map/add | solution.py:275
  17.7 5.0 %collective-permute-start.3 = (f32[256,128]{1,0:T(8,128)S(1)}, f32[256,128]{1,0:T(8,128)S(1)}, u32[]{:S(2)}, u32[]{:S(2)}) collective-permute-start(f32[256,128]{1,0:T(8,128)S(1)} %get-tuple-element.18), channel_id=1, source_target_pairs={{0,6},{1,7},{2,0},{3,1},{4,2},{5,3},{6,4},{7,5},{8,14},{9,15},{10,... | collective-permute-start | bytes 393224 | tf_op jit(solution)/shard_map/ppermute | solution.py:266
  22.7 1.0 %collective-permute-start.1 = (f32[256,128]{1,0:T(8,128)S(1)}, f32[256,128]{1,0:T(8,128)S(1)}, u32[]{:S(2)}, u32[]{:S(2)}) collective-permute-start(f32[256,128]{1,0:T(8,128)S(1)} %get-tuple-element.20), channel_id=1, source_target_pairs={{0,2},{1,3},{2,4},{3,5},{4,6},{5,7},{6,0},{7,1},{8,10},{9,11},{10,... | collective-permute-start | bytes 393224 | tf_op jit(solution)/shard_map/ppermute | solution.py:266
  23.7 2.9 %collective-permute-done.3.refs_4_ = f32[256,128]{1,0:T(8,128)S(1)} collective-permute-done((f32[256,128]{1,0:T(8,128)S(1)}, f32[256,128]{1,0:T(8,128)S(1)}, u32[]{:S(2)}, u32[]{:S(2)}) %collective-permute-start.3) | collective-permute-done | bytes 131104 | tf_op jit(solution)/shard_map/ppermute | solution.py:266
  26.6 7.7 %collective-permute-done.2.refs_3_ = f32[256,128]{1,0:T(8,128)S(1)} collective-permute-done((f32[256,128]{1,0:T(8,128)S(1)}, f32[256,128]{1,0:T(8,128)S(1)}, u32[]{:S(2)}, u32[]{:S(2)}) %collective-permute-start.2) | collective-permute-done | bytes 131104 | tf_op jit(solution)/shard_map/ppermute | solution.py:266
  35.0 3.3 %middle.1 = (bf16[256,256]{1,0:T(8,128)(2,1)}, f32[128,256]{1,0:T(8,128)}, f32[4,16,256]{2,1,0:T(8,128)}, f32[4,16,256]{2,1,0:T(8,128)}) custom-call(s32[64,128]{1,0:T(8,128)} %bitcast.38, bf16[256,256]{1,0:T(8,128)(2,1)} %cot_ref.1, bf16[128,256]{1,0:T(8,128)(2,1)} %weight_ref.1, f32[256,128]{1,0:T(8,128)} %get-tuple-element.25.refs_0_, ...), custom_call_target="tpu_custom_call" | custom-call | tf_op jit(solution)/shard_map/middle/pallas_call | solution.py:279
  38.3 1.5 %collective-permute-done.15 = f32[4,16,256]{2,1,0:T(8,128)S(1)} collective-permute-done((f32[4,16,256]{2,1,0:T(8,128)}, f32[4,16,256]{2,1,0:T(8,128)S(1)}, u32[]{:S(2)}, u32[]{:S(2)}) %collective-permute-start.15) | collective-permute-done | bytes 65568 | tf_op jit(solution)/shard_map/ppermute | solution.py:262
  40.6 1.5 %collective-permute-start.16 = (f32[16,256]{1,0:T(8,128)S(1)}, f32[16,256]{1,0:T(8,128)S(1)}, u32[]{:S(2)}, u32[]{:S(2)}) collective-permute-start(f32[16,256]{1,0:T(8,128)S(1)} %get-tuple-element.29), channel_id=1, source_target_pairs={{0,8},{8,16},{16,24},{24,0},{1,9},{9,17},{17,25},{25,1},{2,10},{10... | collective-permute-start | bytes 49160 | tf_op jit(solution)/shard_map/ppermute | solution.py:269
  42.1 1.4 %collective-permute-start.18 = (f32[16,256]{1,0:T(8,128)S(1)}, f32[16,256]{1,0:T(8,128)S(1)}, u32[]{:S(2)}, u32[]{:S(2)}) collective-permute-start(f32[16,256]{1,0:T(8,128)S(1)} %get-tuple-element.30), channel_id=1, source_target_pairs={{0,24},{8,0},{16,8},{24,16},{1,25},{9,1},{17,9},{25,17},{2,26},{10... | collective-permute-start | bytes 49160 | tf_op jit(solution)/shard_map/ppermute | solution.py:269
  43.5 1.5 %collective-permute-start.17 = (f32[16,256]{1,0:T(8,128)S(1)}, f32[16,256]{1,0:T(8,128)S(1)}, u32[]{:S(2)}, u32[]{:S(2)}) collective-permute-start(f32[16,256]{1,0:T(8,128)S(1)} %get-tuple-element.31), channel_id=1, source_target_pairs={{0,16},{8,24},{16,0},{24,8},{1,17},{9,25},{17,1},{25,9},{2,18},{10... | collective-permute-start | bytes 49160 | tf_op jit(solution)/shard_map/ppermute | solution.py:269
  45.8 1.4 %collective-permute-done.17 = f32[16,256]{1,0:T(8,128)S(1)} collective-permute-done((f32[16,256]{1,0:T(8,128)S(1)}, f32[16,256]{1,0:T(8,128)S(1)}, u32[]{:S(2)}, u32[]{:S(2)}) %collective-permute-start.17) | collective-permute-done | bytes 16416 | tf_op jit(solution)/shard_map/ppermute | solution.py:269
  48.0 1.4 %collective-permute-start.21 = (f32[16,256]{1,0:T(8,128)S(1)}, f32[16,256]{1,0:T(8,128)S(1)}, u32[]{:S(2)}, u32[]{:S(2)}) collective-permute-start(f32[16,256]{1,0:T(8,128)S(1)} %fusion.11), channel_id=1, source_target_pairs={{0,6},{1,7},{2,0},{3,1},{4,2},{5,3},{6,4},{7,5},{8,14},{9,15},{10,... | collective-permute-start | bytes 49160 | tf_op jit(solution)/shard_map/ppermute | solution.py:266
  49.4 1.1 %collective-permute-start.20 = (f32[16,256]{1,0:T(8,128)S(1)}, f32[16,256]{1,0:T(8,128)S(1)}, u32[]{:S(2)}, u32[]{:S(2)}) collective-permute-start(f32[16,256]{1,0:T(8,128)S(1)} %fusion.11), channel_id=1, source_target_pairs={{0,4},{1,5},{2,6},{3,7},{4,0},{5,1},{6,2},{7,3},{8,12},{9,13},{10,... | collective-permute-start | bytes 49160 | tf_op jit(solution)/shard_map/ppermute | solution.py:266
  50.5 2.0 %collective-permute-start.19 = (f32[16,256]{1,0:T(8,128)S(1)}, f32[16,256]{1,0:T(8,128)S(1)}, u32[]{:S(2)}, u32[]{:S(2)}) collective-permute-start(f32[16,256]{1,0:T(8,128)S(1)} %fusion.11), channel_id=1, source_target_pairs={{0,2},{1,3},{2,4},{3,5},{4,6},{5,7},{6,0},{7,1},{8,10},{9,11},{10,... | collective-permute-start | bytes 49160 | tf_op jit(solution)/shard_map/ppermute | solution.py:266
  52.5 1.9 %collective-permute-start.6 = (f32[128,256]{1,0:T(8,128)}, f32[128,256]{1,0:T(8,128)S(1)}, u32[]{:S(2)}, u32[]{:S(2)}) collective-permute-start(f32[128,256]{1,0:T(8,128)} %get-tuple-element.15.refs_0_), channel_id=1, source_target_pairs={{0,6},{1,7},{2,0},{3,1},{4,2},{5,3},{6,4},{7,5},{8,14},{9,15},{10,... | collective-permute-start | bytes 393224 | tf_op jit(solution)/shard_map/ppermute | solution.py:266
  54.4 1.1 %collective-permute-start.4 = (f32[128,256]{1,0:T(8,128)}, f32[128,256]{1,0:T(8,128)S(1)}, u32[]{:S(2)}, u32[]{:S(2)}) collective-permute-start(f32[128,256]{1,0:T(8,128)} %get-tuple-element.15.refs_0_), channel_id=1, source_target_pairs={{0,2},{1,3},{2,4},{3,5},{4,6},{5,7},{6,0},{7,1},{8,10},{9,11},{10,... | collective-permute-start | bytes 393224 | tf_op jit(solution)/shard_map/ppermute | solution.py:266
  56.2 2.8 %collective-permute-done.6.refs_3_ = f32[128,256]{1,0:T(8,128)S(1)} collective-permute-done((f32[128,256]{1,0:T(8,128)}, f32[128,256]{1,0:T(8,128)S(1)}, u32[]{:S(2)}, u32[]{:S(2)}) %collective-permute-start.6) | collective-permute-done | bytes 131104 | tf_op jit(solution)/shard_map/ppermute | solution.py:266
  59.1 8.0 %collective-permute-done.5.refs_2_ = f32[128,256]{1,0:T(8,128)S(1)} collective-permute-done((f32[128,256]{1,0:T(8,128)}, f32[128,256]{1,0:T(8,128)S(1)}, u32[]{:S(2)}, u32[]{:S(2)}) %collective-permute-start.5) | collective-permute-done | bytes 131104 | tf_op jit(solution)/shard_map/ppermute | solution.py:266
  67.6 1.5 %collective-permute-start.24 = (f32[16,256]{1,0:T(8,128)S(1)}, f32[16,256]{1,0:T(8,128)S(1)}, u32[]{:S(2)}, u32[]{:S(2)}) collective-permute-start(f32[16,256]{1,0:T(8,128)S(1)} %fusion.13), channel_id=1, source_target_pairs={{0,24},{8,0},{16,8},{24,16},{1,25},{9,1},{17,9},{25,17},{2,26},{10... | collective-permute-start | bytes 49160 | tf_op jit(solution)/shard_map/ppermute | solution.py:269
  69.1 0.9 collective-permute-start.23
  70.0 1.1 %collective-permute-start.22 = (f32[16,256]{1,0:T(8,128)S(1)}, f32[16,256]{1,0:T(8,128)S(1)}, u32[]{:S(2)}, u32[]{:S(2)}) collective-permute-start(f32[16,256]{1,0:T(8,128)S(1)} %fusion.13), channel_id=1, source_target_pairs={{0,8},{8,16},{16,24},{24,0},{1,9},{9,17},{17,25},{25,1},{2,10},{10... | collective-permute-start | bytes 49160 | tf_op jit(solution)/shard_map/ppermute | solution.py:269
  71.9 5.7 %backward.1 = f32[1024,128]{1,0:T(8,128)} custom-call(s32[64,128]{1,0:T(8,128)} %bitcast.39, bf16[2048,1024]{1,0:T(8,128)(2,1)} %get-tuple-element.14.dense_ref, f32[128,256]{1,0:T(8,128)} %get-tuple-element.15.refs_0_, f32[128,256]{1,0:T(8,128)} %copy-done.3, f32[128,256]{1,0:T(8,128)} %copy-done.2, f32[128,256]{1,0:T(8,128)} %copy-done.1, ...), custom_call_target="tpu_custom_call" | custom-call | tf_op jit(solution)/shard_map/backward/pallas_call | solution.py:295
  77.6 1.1 %fusion.12 = (f32[512,128]{1,0:T(8,128)S(1)}, f32[512,128]{1,0:T(8,128)S(1)}) fusion(f32[1024,128]{1,0:T(8,128)} %backward.1), kind=kLoop, calls=%fused_computation.36 | loop fusion | bytes 1048576 | tf_op jit(solution)/shard_map/slice | solution.py:317
  78.7 1.5 %collective-permute-start.11 = (f32[512,128]{1,0:T(8,128)S(1)}, f32[512,128]{1,0:T(8,128)S(1)}, u32[]{:S(2)}, u32[]{:S(2)}) collective-permute-start(f32[512,128]{1,0:T(8,128)S(1)} %get-tuple-element.23), channel_id=1, source_target_pairs={{0,8},{8,0},{16,24},{24,16},{1,9},{9,1},{17,25},{25,17},{2,10},{10... | collective-permute-start | bytes 786440 | tf_op jit(solution)/shard_map/ppermute | solution.py:272
  80.2 0.9 collective-permute-start.13
  81.3 4.9 %collective-permute-done.11 = f32[512,128]{1,0:T(8,128)S(1)} collective-permute-done((f32[512,128]{1,0:T(8,128)S(1)}, f32[512,128]{1,0:T(8,128)S(1)}, u32[]{:S(2)}, u32[]{:S(2)}) %collective-permute-start.11) | collective-permute-done | bytes 262176 | tf_op jit(solution)/shard_map/ppermute | solution.py:272
  86.2 1.2 %collective-permute-done.13 = f32[512,128]{1,0:T(8,128)S(1)} collective-permute-done((f32[512,128]{1,0:T(8,128)S(1)}, f32[512,128]{1,0:T(8,128)S(1)}, u32[]{:S(2)}, u32[]{:S(2)}) %collective-permute-start.13) | collective-permute-done | bytes 262176 | tf_op jit(solution)/shard_map/ppermute | solution.py:272
  87.4 1.1 %slice_add_fusion.11 = (f32[512,128]{1,0:T(8,128)S(1)}, f32[512,128]{1,0:T(8,128)S(1)}) fusion(f32[512,128]{1,0:T(8,128)S(1)} %collective-permute-done.11, f32[1024,128]{1,0:T(8,128)} %backward.1, f32[512,128]{1,0:T(8,128)S(1)} %collective-permute-done.13), kind=kLoop, calls=%fused_computation.35 | loop fusion | flops 131072 | bytes 1572864 | tf_op jit(solution)/shard_map/add | solution.py:319
  88.5 0.9 collective-permute-start.12
  90.5 4.4 %collective-permute-done.12 = f32[512,128]{1,0:T(8,128)S(1)} collective-permute-done((f32[512,128]{1,0:T(8,128)S(1)}, f32[512,128]{1,0:T(8,128)S(1)}, u32[]{:S(2)}, u32[]{:S(2)}) %collective-permute-start.12) | collective-permute-done | bytes 262176 | tf_op jit(solution)/shard_map/ppermute | solution.py:272
  (61 shorter events, 8.4 us)
Async XLA Ops:
  13.5 2.3 %collective-permute-start = (f32[4,256,128]{2,1,0:T(8,128)}, f32[4,256,128]{2,1,0:T(8,128)S(1)}, u32[]{:S(2)}, u32[]{:S(2)}) collective-permute-start(f32[4,256,128]{2,1,0:T(8,128)} %get-tuple-element.12), channel_id=1, source_target_pairs={{0,1},{1,0},{2,3},{3,2},{4,5},{5,4},{6,7},{7,6},{8,9},{9,8},{10,11... | collective-permute-start | bytes 1572872 | tf_op jit(solution)/shard_map/ppermute | solution.py:262
  17.7 8.9 %collective-permute-start.3 = (f32[256,128]{1,0:T(8,128)S(1)}, f32[256,128]{1,0:T(8,128)S(1)}, u32[]{:S(2)}, u32[]{:S(2)}) collective-permute-start(f32[256,128]{1,0:T(8,128)S(1)} %get-tuple-element.18), channel_id=1, source_target_pairs={{0,6},{1,7},{2,0},{3,1},{4,2},{5,3},{6,4},{7,5},{8,14},{9,15},{10,... | collective-permute-start | bytes 393224 | tf_op jit(solution)/shard_map/ppermute | solution.py:266
  22.7 11.7 %collective-permute-start.2 = (f32[256,128]{1,0:T(8,128)S(1)}, f32[256,128]{1,0:T(8,128)S(1)}, u32[]{:S(2)}, u32[]{:S(2)}) collective-permute-start(f32[256,128]{1,0:T(8,128)S(1)} %get-tuple-element.19), channel_id=1, source_target_pairs={{0,4},{1,5},{2,6},{3,7},{4,0},{5,1},{6,2},{7,3},{8,12},{9,13},{10,... | collective-permute-start | bytes 393224 | tf_op jit(solution)/shard_map/ppermute | solution.py:266
  22.7 11.7 %collective-permute-start.1 = (f32[256,128]{1,0:T(8,128)S(1)}, f32[256,128]{1,0:T(8,128)S(1)}, u32[]{:S(2)}, u32[]{:S(2)}) collective-permute-start(f32[256,128]{1,0:T(8,128)S(1)} %get-tuple-element.20), channel_id=1, source_target_pairs={{0,2},{1,3},{2,4},{3,5},{4,6},{5,7},{6,0},{7,1},{8,10},{9,11},{10,... | collective-permute-start | bytes 393224 | tf_op jit(solution)/shard_map/ppermute | solution.py:266
  26.6 7.8 %copy-start.7 = (f32[256,128]{1,0:T(8,128)}, f32[256,128]{1,0:T(8,128)S(1)}, u32[]{:S(2)}) copy-start(f32[256,128]{1,0:T(8,128)S(1)} %collective-permute-done.3.refs_4_) | copy-start | bytes 393220
  38.3 1.5 %collective-permute-start.15 = (f32[4,16,256]{2,1,0:T(8,128)}, f32[4,16,256]{2,1,0:T(8,128)S(1)}, u32[]{:S(2)}, u32[]{:S(2)}) collective-permute-start(f32[4,16,256]{2,1,0:T(8,128)} %get-tuple-element.17), channel_id=1, source_target_pairs={{0,1},{1,0},{2,3},{3,2},{4,5},{5,4},{6,7},{7,6},{8,9},{9,8},{10,11... | collective-permute-start | bytes 196616 | tf_op jit(solution)/shard_map/ppermute | solution.py:262
  40.6 4.7 %collective-permute-start.16 = (f32[16,256]{1,0:T(8,128)S(1)}, f32[16,256]{1,0:T(8,128)S(1)}, u32[]{:S(2)}, u32[]{:S(2)}) collective-permute-start(f32[16,256]{1,0:T(8,128)S(1)} %get-tuple-element.29), channel_id=1, source_target_pairs={{0,8},{8,16},{16,24},{24,0},{1,9},{9,17},{17,25},{25,1},{2,10},{10... | collective-permute-start | bytes 49160 | tf_op jit(solution)/shard_map/ppermute | solution.py:269
  42.1 3.7 %collective-permute-start.18 = (f32[16,256]{1,0:T(8,128)S(1)}, f32[16,256]{1,0:T(8,128)S(1)}, u32[]{:S(2)}, u32[]{:S(2)}) collective-permute-start(f32[16,256]{1,0:T(8,128)S(1)} %get-tuple-element.30), channel_id=1, source_target_pairs={{0,24},{8,0},{16,8},{24,16},{1,25},{9,1},{17,9},{25,17},{2,26},{10... | collective-permute-start | bytes 49160 | tf_op jit(solution)/shard_map/ppermute | solution.py:269
  43.5 3.7 %collective-permute-start.17 = (f32[16,256]{1,0:T(8,128)S(1)}, f32[16,256]{1,0:T(8,128)S(1)}, u32[]{:S(2)}, u32[]{:S(2)}) collective-permute-start(f32[16,256]{1,0:T(8,128)S(1)} %get-tuple-element.31), channel_id=1, source_target_pairs={{0,16},{8,24},{16,0},{24,8},{1,17},{9,25},{17,1},{25,9},{2,18},{10... | collective-permute-start | bytes 49160 | tf_op jit(solution)/shard_map/ppermute | solution.py:269
  48.0 6.4 %collective-permute-start.21 = (f32[16,256]{1,0:T(8,128)S(1)}, f32[16,256]{1,0:T(8,128)S(1)}, u32[]{:S(2)}, u32[]{:S(2)}) collective-permute-start(f32[16,256]{1,0:T(8,128)S(1)} %fusion.11), channel_id=1, source_target_pairs={{0,6},{1,7},{2,0},{3,1},{4,2},{5,3},{6,4},{7,5},{8,14},{9,15},{10,... | collective-permute-start | bytes 49160 | tf_op jit(solution)/shard_map/ppermute | solution.py:266
  49.4 5.0 %collective-permute-start.20 = (f32[16,256]{1,0:T(8,128)S(1)}, f32[16,256]{1,0:T(8,128)S(1)}, u32[]{:S(2)}, u32[]{:S(2)}) collective-permute-start(f32[16,256]{1,0:T(8,128)S(1)} %fusion.11), channel_id=1, source_target_pairs={{0,4},{1,5},{2,6},{3,7},{4,0},{5,1},{6,2},{7,3},{8,12},{9,13},{10,... | collective-permute-start | bytes 49160 | tf_op jit(solution)/shard_map/ppermute | solution.py:266
  50.5 5.7 %collective-permute-start.19 = (f32[16,256]{1,0:T(8,128)S(1)}, f32[16,256]{1,0:T(8,128)S(1)}, u32[]{:S(2)}, u32[]{:S(2)}) collective-permute-start(f32[16,256]{1,0:T(8,128)S(1)} %fusion.11), channel_id=1, source_target_pairs={{0,2},{1,3},{2,4},{3,5},{4,6},{5,7},{6,0},{7,1},{8,10},{9,11},{10,... | collective-permute-start | bytes 49160 | tf_op jit(solution)/shard_map/ppermute | solution.py:266
  52.5 16.7 %collective-permute-start.7 = (f32[128,256]{1,0:T(8,128)}, f32[128,256]{1,0:T(8,128)S(1)}, u32[]{:S(2)}, u32[]{:S(2)}) collective-permute-start(f32[128,256]{1,0:T(8,128)} %get-tuple-element.15.refs_0_), channel_id=1, source_target_pairs={{0,1},{1,0},{2,3},{3,2},{4,5},{5,4},{6,7},{7,6},{8,9},{9,8},{10,11... | collective-permute-start | bytes 393224 | tf_op jit(solution)/shard_map/ppermute | solution.py:262
  52.5 6.6 %collective-permute-start.6 = (f32[128,256]{1,0:T(8,128)}, f32[128,256]{1,0:T(8,128)S(1)}, u32[]{:S(2)}, u32[]{:S(2)}) collective-permute-start(f32[128,256]{1,0:T(8,128)} %get-tuple-element.15.refs_0_), channel_id=1, source_target_pairs={{0,6},{1,7},{2,0},{3,1},{4,2},{5,3},{6,4},{7,5},{8,14},{9,15},{10,... | collective-permute-start | bytes 393224 | tf_op jit(solution)/shard_map/ppermute | solution.py:266
  54.3 12.7 %collective-permute-start.5 = (f32[128,256]{1,0:T(8,128)}, f32[128,256]{1,0:T(8,128)S(1)}, u32[]{:S(2)}, u32[]{:S(2)}) collective-permute-start(f32[128,256]{1,0:T(8,128)} %get-tuple-element.15.refs_0_), channel_id=1, source_target_pairs={{0,4},{1,5},{2,6},{3,7},{4,0},{5,1},{6,2},{7,3},{8,12},{9,13},{10,... | collective-permute-start | bytes 393224 | tf_op jit(solution)/shard_map/ppermute | solution.py:266
  54.4 12.7 %collective-permute-start.4 = (f32[128,256]{1,0:T(8,128)}, f32[128,256]{1,0:T(8,128)S(1)}, u32[]{:S(2)}, u32[]{:S(2)}) collective-permute-start(f32[128,256]{1,0:T(8,128)} %get-tuple-element.15.refs_0_), channel_id=1, source_target_pairs={{0,2},{1,3},{2,4},{3,5},{4,6},{5,7},{6,0},{7,1},{8,10},{9,11},{10,... | collective-permute-start | bytes 393224 | tf_op jit(solution)/shard_map/ppermute | solution.py:266
  59.1 12.1 %copy-start.1 = (f32[128,256]{1,0:T(8,128)}, f32[128,256]{1,0:T(8,128)S(1)}, u32[]{:S(2)}) copy-start(f32[128,256]{1,0:T(8,128)S(1)} %collective-permute-done.6.refs_3_) | copy-start | bytes 393220
  59.1 10.9 %collective-permute-start.10 = (f32[128,256]{1,0:T(8,128)S(1)}, f32[128,256]{1,0:T(8,128)S(1)}, u32[]{:S(2)}, u32[]{:S(2)}) collective-permute-start(f32[128,256]{1,0:T(8,128)S(1)} %collective-permute-done.6.refs_3_), channel_id=1, source_target_pairs={{0,1},{1,0},{2,3},{3,2},{4,5},{5,4},{6,7},{7,6},{8,9},{9,8},{10,11... | collective-permute-start | bytes 393224 | tf_op jit(solution)/shard_map/ppermute | solution.py:262
  67.1 4.1 %copy-start.2 = (f32[128,256]{1,0:T(8,128)}, f32[128,256]{1,0:T(8,128)S(1)}, u32[]{:S(2)}) copy-start(f32[128,256]{1,0:T(8,128)S(1)} %collective-permute-done.5.refs_2_) | copy-start | bytes 393220
  67.1 4.1 %collective-permute-start.9 = (f32[128,256]{1,0:T(8,128)S(1)}, f32[128,256]{1,0:T(8,128)S(1)}, u32[]{:S(2)}, u32[]{:S(2)}) collective-permute-start(f32[128,256]{1,0:T(8,128)S(1)} %collective-permute-done.5.refs_2_), channel_id=1, source_target_pairs={{0,1},{1,0},{2,3},{3,2},{4,5},{5,4},{6,7},{7,6},{8,9},{9,8},{10,11... | collective-permute-start | bytes 393224 | tf_op jit(solution)/shard_map/ppermute | solution.py:262
  67.1 4.1 %copy-start.3 = (f32[128,256]{1,0:T(8,128)}, f32[128,256]{1,0:T(8,128)S(1)}, u32[]{:S(2)}) copy-start(f32[128,256]{1,0:T(8,128)S(1)} %collective-permute-done.4.refs_1_) | copy-start | bytes 393220
  67.1 4.1 %collective-permute-start.8 = (f32[128,256]{1,0:T(8,128)S(1)}, f32[128,256]{1,0:T(8,128)S(1)}, u32[]{:S(2)}, u32[]{:S(2)}) collective-permute-start(f32[128,256]{1,0:T(8,128)S(1)} %collective-permute-done.4.refs_1_), channel_id=1, source_target_pairs={{0,1},{1,0},{2,3},{3,2},{4,5},{5,4},{6,7},{7,6},{8,9},{9,8},{10,11... | collective-permute-start | bytes 393224 | tf_op jit(solution)/shard_map/ppermute | solution.py:262
  67.6 13.5 %collective-permute-start.24 = (f32[16,256]{1,0:T(8,128)S(1)}, f32[16,256]{1,0:T(8,128)S(1)}, u32[]{:S(2)}, u32[]{:S(2)}) collective-permute-start(f32[16,256]{1,0:T(8,128)S(1)} %fusion.13), channel_id=1, source_target_pairs={{0,24},{8,0},{16,8},{24,16},{1,25},{9,1},{17,9},{25,17},{2,26},{10... | collective-permute-start | bytes 49160 | tf_op jit(solution)/shard_map/ppermute | solution.py:269
  69.1 2.1 %copy-start = (f32[128,256]{1,0:T(8,128)}, f32[128,256]{1,0:T(8,128)S(1)}, u32[]{:S(2)}) copy-start(f32[128,256]{1,0:T(8,128)S(1)} %collective-permute-done.7.refs_4_) | copy-start | bytes 393220
  69.1 12.0 %collective-permute-start.23 = (f32[16,256]{1,0:T(8,128)S(1)}, f32[16,256]{1,0:T(8,128)S(1)}, u32[]{:S(2)}, u32[]{:S(2)}) collective-permute-start(f32[16,256]{1,0:T(8,128)S(1)} %fusion.13), channel_id=1, source_target_pairs={{0,16},{8,24},{16,0},{24,8},{1,17},{9,25},{17,1},{25,9},{2,18},{10... | collective-permute-start | bytes 49160 | tf_op jit(solution)/shard_map/ppermute | solution.py:269
  70.0 1.2 %copy-start.4 = (f32[128,256]{1,0:T(8,128)}, f32[128,256]{1,0:T(8,128)S(1)}, u32[]{:S(2)}) copy-start(f32[128,256]{1,0:T(8,128)S(1)} %collective-permute-done.10.refs_7_) | copy-start | bytes 393220
  70.0 11.1 %collective-permute-start.22 = (f32[16,256]{1,0:T(8,128)S(1)}, f32[16,256]{1,0:T(8,128)S(1)}, u32[]{:S(2)}, u32[]{:S(2)}) collective-permute-start(f32[16,256]{1,0:T(8,128)S(1)} %fusion.13), channel_id=1, source_target_pairs={{0,8},{8,16},{16,24},{24,0},{1,9},{9,17},{17,25},{25,1},{2,10},{10... | collective-permute-start | bytes 49160 | tf_op jit(solution)/shard_map/ppermute | solution.py:269
  78.7 7.5 %collective-permute-start.11 = (f32[512,128]{1,0:T(8,128)S(1)}, f32[512,128]{1,0:T(8,128)S(1)}, u32[]{:S(2)}, u32[]{:S(2)}) collective-permute-start(f32[512,128]{1,0:T(8,128)S(1)} %get-tuple-element.23), channel_id=1, source_target_pairs={{0,8},{8,0},{16,24},{24,16},{1,9},{9,1},{17,25},{25,17},{2,10},{10... | collective-permute-start | bytes 786440 | tf_op jit(solution)/shard_map/ppermute | solution.py:272
  80.2 7.2 %collective-permute-start.13 = (f32[512,128]{1,0:T(8,128)S(1)}, f32[512,128]{1,0:T(8,128)S(1)}, u32[]{:S(2)}, u32[]{:S(2)}) collective-permute-start(f32[512,128]{1,0:T(8,128)S(1)} %get-tuple-element.24), channel_id=1, source_target_pairs={{0,16},{8,24},{16,0},{24,8},{1,17},{9,25},{17,1},{25,9},{2,18},{10... | collective-permute-start | bytes 786440 | tf_op jit(solution)/shard_map/ppermute | solution.py:272
  81.2 8.6 %collective-permute-start.25 = (f32[64,256]{1,0:T(8,128)S(1)}, f32[64,256]{1,0:T(8,128)S(1)}, u32[]{:S(2)}, u32[]{:S(2)}) collective-permute-start(f32[64,256]{1,0:T(8,128)S(1)} %bitcast.40), channel_id=1, source_target_pairs={{0,1},{1,0},{2,3},{3,2},{4,5},{5,4},{6,7},{7,6},{8,9},{9,8},{10,11... | collective-permute-start | bytes 196616 | tf_op jit(solution)/shard_map/ppermute | solution.py:262
  88.5 6.4 %collective-permute-start.12 = (f32[512,128]{1,0:T(8,128)S(1)}, f32[512,128]{1,0:T(8,128)S(1)}, u32[]{:S(2)}, u32[]{:S(2)}) collective-permute-start(f32[512,128]{1,0:T(8,128)S(1)} %get-tuple-element.21), channel_id=1, source_target_pairs={{0,16},{8,24},{16,0},{24,8},{1,17},{9,25},{17,1},{25,9},{2,18},{10... | collective-permute-start | bytes 786440 | tf_op jit(solution)/shard_map/ppermute | solution.py:272
  89.5 6.4 %collective-permute-start.14 = (f32[512,128]{1,0:T(8,128)S(1)}, f32[512,128]{1,0:T(8,128)S(1)}, u32[]{:S(2)}, u32[]{:S(2)}) collective-permute-start(f32[512,128]{1,0:T(8,128)S(1)} %get-tuple-element.22), channel_id=1, source_target_pairs={{0,8},{8,0},{16,24},{24,16},{1,9},{9,1},{17,25},{25,17},{2,10},{10... | collective-permute-start | bytes 786440 | tf_op jit(solution)/shard_map/ppermute | solution.py:272
  (4 other events, 2.7 us)

commit v2 on v1

--- a/solution.py
+++ b/solution.py
@@ -30,7 +30,6 @@
     buf, acc0, acc1, acc2, acc3, hi_scr, lo_scr, scaled, in_sems, out_sems,
 ):
     accs = (acc0, acc1, acc2, acc3)
-    n_chip = n_col // 2
     slots = buf.shape[0]
     part = EDGE // QUARTERS
     col_nodes, width = feat_ref.shape
@@ -42,7 +41,7 @@
     n_panels = n_col // panel_dev
     n_chunks = slots // chunk
     col = lax.axis_index("col")
-    chip, core = col // 2, col % 2
+    core = col % 2
     live = live_ref[0, 0]
 
     def block_copy(c):
@@ -112,7 +111,7 @@
                 hi_scr[pl.ds(j * node_dev, node_dev), :], scaled[...], preferred_element_type=F32
             ) + jnp.dot(lo_scr[...], scaled[...], preferred_element_type=F32)
             dev = panel * panel_dev + j
-            place = lax.rem(dev // 2 - chip + n_chip, n_chip)
+            place = dev // 2
             mine = dev % 2 == core
 
             @pl.when(mine)
@@ -135,16 +134,16 @@
 
 
 def middle_kernel(
-    n_col, n_row, n_in, scale, deg_ref, cot_ref, weight_ref, *refs
+    n_col, scale, deg_ref, cot_ref, weight_ref, parts_ref,
+    act_ref, pulled_ref, wkeep_ref, wsend_ref,
 ):
-    parts, (act_ref, pulled_ref, wkeep_ref, wsend_ref) = refs[:n_in], refs[n_in:]
     row, col = lax.axis_index("row"), lax.axis_index("col")
     core = col % 2
     node_dev = cot_ref.shape[0]
     dev_blocks = node_dev // EDGE
-    summed = parts[0][...]
-    for ref in parts[1:]:
-        summed = summed + ref[...]
+    summed = parts_ref[0]
+    for k in range(1, parts_ref.shape[0]):
+        summed = summed + parts_ref[k]
     base = (row * n_col + col) * dev_blocks
     inv = jnp.concatenate([inv_column(deg_ref, base + k) for k in range(dev_blocks)], axis=0)
     weight = weight_ref[...].astype(F32)
@@ -154,34 +153,24 @@
     act_ref[...] = (0.5 * v * (1.0 + t)).astype(BF16)
     slope = 0.5 * (1.0 + t) + 0.5 * v * (1.0 - t * t) * (GELU_C * (1.0 + 3.0 * GELU_K * v * v))
     gprime = cot_ref[...].astype(F32) * slope
-    pulled = inv * lax.dot_general(
+    pulled = jnp.transpose(inv * lax.dot_general(
         gprime, weight, (((1,), (1,)), ((), ())), precision=HIGH, preferred_element_type=F32
-    )
-    pulled_ref[...] = jnp.transpose(pulled)
+    ))
+    for k in range(pulled_ref.shape[0]):
+        pulled_ref[k] = pulled
     wpart = scale * lax.dot_general(
         propagated, gprime, (((0,), (0,)), ((), ())), precision=HIGH, preferred_element_type=F32
     )
-    pieces, piece = wkeep_ref.shape[0], wkeep_ref.shape[1]
-    for half in range(2):
-        for j in range(pieces):
-            at = (half * pieces + j) * piece
-            place = lax.rem(j - row + n_row, n_row)
-
-            @pl.when(core == half)
-            def _():
-                wkeep_ref[place] = wpart[at:at + piece]
-
-            @pl.when(core != half)
-            def _():
-                wsend_ref[place] = wpart[at:at + piece]
-
-
-def backward_kernel(n_col, deg_ref, dense_ref, *refs):
-    parts, (out_ref, dense, lhs, sems) = refs[:n_col], refs[n_col:]
-    n_chip = n_col // 2
+    half = wkeep_ref.shape[0]
+    low = core == 0
+    wkeep_ref[...] = jnp.where(low, wpart[:half], wpart[half:])
+    wsend_ref[...] = jnp.where(low, wpart[half:], wpart[:half])
+
+
+def backward_kernel(n_col, deg_ref, dense_ref, own_ref, sibling_ref, out_ref, dense, lhs, sems):
+    n_chip, width, node_dev = own_ref.shape
+    core = lax.axis_index("col") % 2
     col = lax.axis_index("col")
-    chip, core = col // 2, col % 2
-    width, node_dev = parts[0].shape
     col_nodes = dense.shape[1]
 
     def dense_copy(j):
@@ -190,14 +179,13 @@
 
     for j in range(n_col):
         dense_copy(j).start()
-    for i in range(n_col):
-        k, other = i % n_chip, i // n_chip
-        source = lax.rem(chip - k + n_chip, n_chip) * 2 + (core if other == 0 else 1 - core)
-        lanes = pl.ds(pl.multiple_of(source * node_dev, EDGE), node_dev)
-        value = parts[i][...]
-        hi = value.astype(BF16)
-        lhs[:width, lanes] = hi
-        lhs[width:, lanes] = (value - hi.astype(F32)).astype(BF16)
+    for k in range(n_chip):
+        for ref, place in ((own_ref, core), (sibling_ref, 1 - core)):
+            lanes = pl.ds(pl.multiple_of((2 * k + place) * node_dev, EDGE), node_dev)
+            value = ref[k]
+            hi = value.astype(BF16)
+            lhs[:width, lanes] = hi
+            lhs[width:, lanes] = (value - hi.astype(F32)).astype(BF16)
     for j in range(n_col):
         dense_copy(j).wait()
     step = 2 * EDGE if col_nodes % (2 * EDGE) == 0 else EDGE
@@ -257,45 +245,44 @@
     )(block_rows, block_cols, live_slots, deg, features, blocks)
 
     swap = [(i, i ^ 1) for i in range(n_col)]
+    same_core = [list(range(c, n_col, 2)) for c in range(2)]
 
     def to_sibling(x):
         return lax.ppermute(x, "col", swap)
 
-    def to_chip(x, k):
-        pairs = [(i, ((i // 2 + k) % n_chip) * 2 + i % 2) for i in range(n_col)]
-        return lax.ppermute(x, "col", pairs)
-
-    def to_row(x, k):
-        return lax.ppermute(x, "row", [(i, (i + k) % n_row) for i in range(n_row)])
-
-    def row_flip(x, bit):
-        return lax.ppermute(x, "row", [(i, i ^ (1 << bit)) for i in range(n_row)])
-
-    got = to_sibling(send)
-    arrived = [to_chip(keep[k] + got[k], k) for k in range(1, n_chip)]
-    parts = [keep[0], got[0]] + arrived
+    def chips(x):
+        return lax.all_to_all(x, "col", 0, 0, axis_index_groups=same_core)
+
+    def rows(x):
+        return lax.all_to_all(x, "row", 0, 0)
+
+    def copies(x, n):
+        return jnp.broadcast_to(x[None], (n,) + x.shape)
+
+    parts = chips(keep + to_sibling(send))
 
     half = width // 2
     out_act, pulled, wkeep, wsend = pl.pallas_call(
-        functools.partial(middle_kernel, n_col, n_row, len(parts), float(nodes) ** (-0.5)),
+        functools.partial(middle_kernel, n_col, float(nodes) ** (-0.5)),
         out_shape=(
             jax.ShapeDtypeStruct((node_dev, hidden), BF16),
-            jax.ShapeDtypeStruct((width, node_dev), F32),
-            jax.ShapeDtypeStruct((n_row, half // n_row, hidden), F32),
-            jax.ShapeDtypeStruct((n_row, half // n_row, hidden), F32),
+            jax.ShapeDtypeStruct((n_chip, width, node_dev), F32),
+            jax.ShapeDtypeStruct((half, hidden), F32),
+            jax.ShapeDtypeStruct((half, hidden), F32),
         ),
-        in_specs=[vmem] * (3 + len(parts)),
+        in_specs=[vmem] * 4,
         out_specs=(vmem,) * 4,
         compiler_params=pltpu.CompilerParams(vmem_limit_bytes=limit),
         name="middle",
-    )(deg, cotangent, weight, *parts)
-
-    own = [pulled] + [to_chip(pulled, k) for k in range(1, n_chip)]
-    sibling = [to_sibling(x) for x in own]
+    )(deg, cotangent, weight, parts)
+
+    own = chips(pulled)
+    own, wkeep, wsend = lax.optimization_barrier((own, wkeep, wsend))
+    sibling = to_sibling(own)
     col_part = pl.pallas_call(
         functools.partial(backward_kernel, n_col),
         out_shape=jax.ShapeDtypeStruct((col_nodes, width), F32),
-        in_specs=[vmem, hbm] + [vmem] * n_col,
+        in_specs=[vmem, hbm, vmem, vmem],
         out_specs=vmem,
         scratch_shapes=[
             pltpu.VMEM((row_nodes, col_nodes), BF16),
@@ -304,36 +291,14 @@
         ],
         compiler_params=pltpu.CompilerParams(vmem_limit_bytes=limit),
         name="backward",
-    )(deg, dense, *own, *sibling)
-
-    bits = n_row.bit_length() - 1
-    if n_row == 1 << bits and bits > 0:
-        pieces = bits
-        while col_nodes % (8 * pieces):
-            pieces -= 1
-        size = col_nodes // pieces
-        done = []
-        for i in range(pieces):
-            value = col_part[i * size:(i + 1) * size]
-            for t in range(bits):
-                value = value + row_flip(value, (i + t) % bits)
-            done.append(value)
-        feat_grad = jnp.concatenate(done, axis=0) if pieces > 1 else done[0]
-    else:
-        feat_grad = lax.psum(col_part, "row")
-
-    wgot = to_sibling(wsend)
-    wpiece = wkeep[0] + wgot[0]
-    for k in range(1, n_row):
-        wpiece = wpiece + to_row(wkeep[k] + wgot[k], k)
-    others = jnp.stack([wpiece] + [to_chip(wpiece, k) for k in range(1, n_chip)])
-    chip = lax.axis_index("col") // 2
-    ordered = jnp.roll(others[::-1], chip + 1, axis=0)
-    wsum = ordered[0]
-    for k in range(1, n_chip):
-        wsum = wsum + ordered[k]
-    ring = jnp.stack([wsum] + [to_row(wsum, k) for k in range(1, n_row)])
-    whole_half = jnp.roll(ring[::-1], lax.axis_index("row") + 1, axis=0).reshape(half, hidden)
+    )(deg, dense, own, sibling)
+
+    feat = rows(col_part.reshape(n_row, col_nodes // n_row, width))
+    feat_grad = rows(copies(feat.sum(axis=0), n_row)).reshape(col_nodes, width)
+
+    wparts = rows((wkeep + to_sibling(wsend)).reshape(n_row, half // n_row, hidden))
+    wsum = chips(copies(wparts.sum(axis=0), n_chip)).sum(axis=0)
+    whole_half = rows(copies(wsum, n_row)).reshape(half, hidden)
     other_half = to_sibling(whole_half)
     low = lax.axis_index("col") % 2 == 0
     weight_grad = jnp.concatenate(

time: 97.1 us -> 111 us (1.14)
  blocking collectives: 0 us -> 55.1 us
  waiting for transfers between devices: 39 us -> 15.5 us
  starting transfers between devices: 26.4 us -> 12 us
  other arithmetic: 6.06 us -> 2.7 us
    all_to_all x0 -> x4, blocking collectives: none -> 55.1 us  [the longest x3 46.7 us: chips(): return lax.all_to_all(x, 'col', 0, 0, axis_index_groups=same_core)]
    ppermute x19 -> x0, waiting for transfers between devices: 35.8 us -> none  [the longest x9 22.2 us: to_chip(): return lax.ppermute(x, 'col', pairs)]
    ppermute x19 -> x0, starting transfers between devices: 25.3 us -> none  [the longest x9 13.5 us: to_chip(): return lax.ppermute(x, 'col', pairs)]
    all_to_all x0 -> x3, waiting for transfers between devices: none -> 12.4 us  [rows(): return lax.all_to_all(x, 'row', 0, 0)]
    all_to_all x0 -> x3, starting transfers between devices: none -> 10.9 us  [rows(): return lax.all_to_all(x, 'row', 0, 0)]
    add x8 -> x2, other arithmetic: 4.49 us -> 1.97 us  [the longest x1 1.12 us: body(): parts = chips(keep + to_sibling(send))]
    broadcast_in_dim x0 -> x3, local copies, waits for them, and re-layouts: none -> 1.47 us  [copies(): return jnp.broadcast_to(x[None], (n,) + x.shape)]
    ppermute x7 -> x4, waiting for transfers between devices: 3.22 us -> 3.09 us  [to_sibling(): return lax.ppermute(x, 'col', swap)]
  transfers between devices with their start and end apart: 26 -> 7, of which waited for: 14 -> 4; matrix products, arithmetic and copies ran while one was open for 3% -> 3% of each run, Pallas kernels for 6% -> 5%
where the time goes in v2:
time: 111 us
  blocking collectives  55.1 us (50%)
  Pallas kernels  21.1 us (19%)
  waiting for transfers between devices  15.5 us (14%)
  starting transfers between devices  12 us (11%)
  local copies, waits for them, and re-layouts  3.05 us (3%)
  other arithmetic  2.7 us (2%)
  between operations  1.4 us (1%)
    all_to_all x3, blocking collectives, chips(): return lax.all_to_all(x, 'col', 0, 0, axis_index_groups=same_core)  46.7 us
    all_to_all x3, waiting for transfers between devices, rows(): return lax.all_to_all(x, 'row', 0, 0)  12.4 us
    pallas_call x1, Pallas kernels, body(): pl.pallas_call(functools.partial(forward_kernel, n_col, chunk, panel_dev)...  12.2 us
    all_to_all x3, starting transfers between devices, rows(): return lax.all_to_all(x, 'row', 0, 0)  10.9 us
    all_to_all x1, blocking collectives, rows(): return lax.all_to_all(x, 'row', 0, 0)  8.38 us
    pallas_call x1, Pallas kernels, body(): pl.pallas_call(functools.partial(backward_kernel, n_col), out_shape=jax.S...  5.65 us
    pallas_call x1, Pallas kernels, body(): pl.pallas_call(functools.partial(middle_kernel, n_col, float(nodes) ** (-...  3.23 us
    ppermute x4, waiting for transfers between devices, to_sibling(): return lax.ppermute(x, 'col', swap)  3.09 us
  transfers between devices with their start and end apart: 7, of which 4 were waited for; matrix products, arithmetic and copies ran while one was open for 3% of the time, Pallas kernels for 5%

profile of v2, /device:TPU:0, one launch (start us, length us, event | category | flops | bytes accessed | tf_op | source)
XLA Modules:
  0.0 110.8 jit_solution(7556802532092934915)
XLA Ops:
  1.3 12.2 %densify_forward.1 = (f32[4,256,128]{2,1,0:T(8,128)}, f32[4,256,128]{2,1,0:T(8,128)}, bf16[2048,1024]{1,0:T(8,128)(2,1)}) custom-call(s32[1,1,384]{2,1,0:T(1,128)} %rows_ref.1, s32[1,1,384]{2,1,0:T(1,128)} %cols_ref.1, s32[1,1]{1,0:T(1,128)S(6)} %copy.12.live_ref, s32[64,128]{1,0:T(8,128)} %bitcast.9, bf16[1024,128]{1,0:T(8,128)(2,1)} %feat_ref.1, ...), custom_call_target="tpu_custom_call" | custom-call | tf_op jit(solution)/shard_map/densify_forward/pallas_call | solution.py:225
  13.5 0.6 collective-permute-start
  14.1 1.7 %collective-permute-done = f32[4,256,128]{2,1,0:T(8,128)S(1)} collective-permute-done((f32[4,256,128]{2,1,0:T(8,128)}, f32[4,256,128]{2,1,0:T(8,128)S(1)}, u32[]{:S(2)}, u32[]{:S(2)}) %collective-permute-start) | collective-permute-done | bytes 524320 | tf_op jit(solution)/shard_map/ppermute | solution.py:251
  15.8 1.1 %add.10 = f32[4,256,128]{2,1,0:T(8,128)S(1)} add(f32[4,256,128]{2,1,0:T(8,128)} %get-tuple-element.13, f32[4,256,128]{2,1,0:T(8,128)S(1)} %collective-permute-done) | non-fusion elementwise | flops 131072 | bytes 1572864 | tf_op jit(solution)/shard_map/add | solution.py:262
  17.0 20.9 %all_to_all.35.parts_ref = f32[4,256,128]{2,1,0:T(8,128)} all-to-all(f32[4,256,128]{2,1,0:T(8,128)S(1)} %add.10), channel_id=1, replica_groups={{0,2,4,6},{1,3,5,7},{8,10,12,14},{9,11,13,15},{16,18,20,22},{17,19,21,2..., dimensions={0} | all-to-all | bytes 1048576 | tf_op jit(solution)/shard_map/all_to_all | solution.py:254
  37.9 3.2 %middle.1 = (bf16[256,256]{1,0:T(8,128)(2,1)}, f32[4,128,256]{2,1,0:T(8,128)}, f32[64,256]{1,0:T(8,128)}, f32[64,256]{1,0:T(8,128)}) custom-call(s32[64,128]{1,0:T(8,128)} %bitcast.10, bf16[256,256]{1,0:T(8,128)(2,1)} %cot_ref.1, bf16[128,256]{1,0:T(8,128)(2,1)} %weight_ref.1, f32[4,256,128]{2,1,0:T(8,128)} %all_to_all.35.parts_ref), custom_call_target="tpu_custom_call" | custom-call | tf_op jit(solution)/shard_map/middle/pallas_call | solution.py:265
  41.1 17.5 %all_to_all.36.own_ref = f32[4,128,256]{2,1,0:T(8,128)S(1)} all-to-all(f32[4,128,256]{2,1,0:T(8,128)} %get-tuple-element.17), channel_id=1, replica_groups={{0,2,4,6},{1,3,5,7},{8,10,12,14},{9,11,13,15},{16,18,20,22},{17,19,21,2..., dimensions={0} | all-to-all | bytes 1048576 | tf_op jit(solution)/shard_map/all_to_all | solution.py:254
  58.6 0.0 copy-start
  58.6 0.0 collective-permute-start.1
  58.6 0.5 collective-permute-start.2
  59.1 1.3 %collective-permute-done.2 = f32[64,256]{1,0:T(8,128)S(1)} collective-permute-done((f32[64,256]{1,0:T(8,128)}, f32[64,256]{1,0:T(8,128)S(1)}, u32[]{:S(2)}, u32[]{:S(2)}) %collective-permute-start.2) | collective-permute-done | bytes 65568 | tf_op jit(solution)/shard_map/ppermute | solution.py:251
  60.4 0.8 add.12
  61.3 8.4 %all_to_all.37 = f32[4,16,256]{2,1,0:T(8,128)S(1)} all-to-all(f32[4,16,256]{2,1,0:T(8,128)S(1)} %bitcast.12), channel_id=1, replica_groups=mesh['row'=4,'col'=8] {'row'}, dimensions={0} | all-to-all | bytes 131072 | tf_op jit(solution)/shard_map/all_to_all | solution.py:257
  69.7 8.3 %all_to_all.38 = f32[4,16,256]{2,1,0:T(8,128)S(1)} all-to-all(f32[4,16,256]{2,1,0:T(8,128)S(1)} %broadcast_in_dim.7), channel_id=1, replica_groups={{0,2,4,6},{1,3,5,7},{8,10,12,14},{9,11,13,15},{16,18,20,22},{17,19,21,2..., dimensions={0} | all-to-all | bytes 131072 | tf_op jit(solution)/shard_map/all_to_all | solution.py:254
  78.0 0.6 broadcast_in_dim.8
  78.6 3.3 %all-to-all-start.6 = ((f32[4,16,256]{2,1,0:T(8,128)}), f32[4,16,256]{2,1,0:T(8,128)S(1)}, u32[]{:S(2)}, u32[]{:S(2)}) async-start(f32[4,16,256]{2,1,0:T(8,128)} %broadcast_in_dim.8), calls=%async_computation.6 | async-start | bytes 131072 | tf_op jit(solution)/shard_map/all_to_all | solution.py:257
  81.9 0.0 collective-permute-done.1.sibling_ref
  81.9 0.0 copy-start.1
  81.9 0.0 copy-done
  81.9 0.8 copy-done.1
  82.7 5.7 %backward.1 = f32[1024,128]{1,0:T(8,128)} custom-call(s32[64,128]{1,0:T(8,128)} %bitcast.11, bf16[2048,1024]{1,0:T(8,128)(2,1)} %get-tuple-element.16.dense_ref, f32[4,128,256]{2,1,0:T(8,128)} %copy-done, f32[4,128,256]{2,1,0:T(8,128)} %copy-done.1), custom_call_target="tpu_custom_call" | custom-call | tf_op jit(solution)/shard_map/backward/pallas_call | solution.py:282
  88.4 0.0 all-to-all-done.6
  88.4 4.2 %all-to-all-start.2 = ((f32[4,256,128]{2,1,0:T(8,128)}), f32[4,256,128]{2,1,0:T(8,128)S(1)}, u32[]{:S(2)}, u32[]{:S(2)}) async-start(f32[4,256,128]{2,1,0:T(8,128)} %bitcast.8), calls=%async_computation.2 | async-start | bytes 1048576 | tf_op jit(solution)/shard_map/all_to_all | solution.py:257
  92.6 0.0 collective-permute-start.3
  92.6 6.6 %all-to-all-done.2 = f32[4,256,128]{2,1,0:T(8,128)S(1)} async-done(((f32[4,256,128]{2,1,0:T(8,128)}), f32[4,256,128]{2,1,0:T(8,128)S(1)}, u32[]{:S(2)}, u32[]{:S(2)}) %all-to-all-start.2) | async-done | bytes 524320 | tf_op jit(solution)/shard_map/all_to_all | solution.py:257
  99.2 0.8 broadcast_in_dim.6
  100.0 3.5 %all-to-all-start.3 = ((f32[4,256,128]{2,1,0:T(8,128)}), f32[4,256,128]{2,1,0:T(8,128)S(1)}, u32[]{:S(2)}, u32[]{:S(2)}) async-start(f32[4,256,128]{2,1,0:T(8,128)} %broadcast_in_dim.6), calls=%async_computation.3 | async-start | bytes 1048576 | tf_op jit(solution)/shard_map/all_to_all | solution.py:257
  103.5 0.0 collective-permute-done.3
  103.5 0.7 pad_maximum_fusion
  104.2 5.8 %all-to-all-done.3 = f32[4,256,128]{2,1,0:T(8,128)S(1)} async-done(((f32[4,256,128]{2,1,0:T(8,128)}), f32[4,256,128]{2,1,0:T(8,128)S(1)}, u32[]{:S(2)}, u32[]{:S(2)}) %all-to-all-start.3) | async-done | bytes 524320 | tf_op jit(solution)/shard_map/all_to_all | solution.py:257
  110.0 0.8 copy.13
  (5 shorter events, 0.1 us)
Async XLA Ops:
  13.5 2.3 %collective-permute-start = (f32[4,256,128]{2,1,0:T(8,128)}, f32[4,256,128]{2,1,0:T(8,128)S(1)}, u32[]{:S(2)}, u32[]{:S(2)}) collective-permute-start(f32[4,256,128]{2,1,0:T(8,128)} %get-tuple-element.14), channel_id=1, source_target_pairs={{0,1},{1,0},{2,3},{3,2},{4,5},{5,4},{6,7},{7,6},{8,9},{9,8},{10,11... | collective-permute-start | bytes 1572872 | tf_op jit(solution)/shard_map/ppermute | solution.py:251
  58.6 23.3 %copy-start = (f32[4,128,256]{2,1,0:T(8,128)}, f32[4,128,256]{2,1,0:T(8,128)S(1)}, u32[]{:S(2)}) copy-start(f32[4,128,256]{2,1,0:T(8,128)S(1)} %all_to_all.36.own_ref) | copy-start | bytes 1572868
  58.6 23.3 %collective-permute-start.1 = (f32[4,128,256]{2,1,0:T(8,128)S(1)}, f32[4,128,256]{2,1,0:T(8,128)S(1)}, u32[]{:S(2)}, u32[]{:S(2)}) collective-permute-start(f32[4,128,256]{2,1,0:T(8,128)S(1)} %all_to_all.36.own_ref), channel_id=1, source_target_pairs={{0,1},{1,0},{2,3},{3,2},{4,5},{5,4},{6,7},{7,6},{8,9},{9,8},{10,11... | collective-permute-start | bytes 1572872 | tf_op jit(solution)/shard_map/ppermute | solution.py:251
  58.6 1.8 %collective-permute-start.2 = (f32[64,256]{1,0:T(8,128)}, f32[64,256]{1,0:T(8,128)S(1)}, u32[]{:S(2)}, u32[]{:S(2)}) collective-permute-start(f32[64,256]{1,0:T(8,128)} %get-tuple-element.22), channel_id=1, source_target_pairs={{0,1},{1,0},{2,3},{3,2},{4,5},{5,4},{6,7},{7,6},{8,9},{9,8},{10,11... | collective-permute-start | bytes 196616 | tf_op jit(solution)/shard_map/ppermute | solution.py:251
  78.6 9.8 %all-to-all-start.6 = ((f32[4,16,256]{2,1,0:T(8,128)}), f32[4,16,256]{2,1,0:T(8,128)S(1)}, u32[]{:S(2)}, u32[]{:S(2)}) async-start(f32[4,16,256]{2,1,0:T(8,128)} %broadcast_in_dim.8), calls=%async_computation.6 | async-start | bytes 131072 | tf_op jit(solution)/shard_map/all_to_all | solution.py:257
  81.9 0.8 copy-start.1
  88.4 10.7 %all-to-all-start.2 = ((f32[4,256,128]{2,1,0:T(8,128)}), f32[4,256,128]{2,1,0:T(8,128)S(1)}, u32[]{:S(2)}, u32[]{:S(2)}) async-start(f32[4,256,128]{2,1,0:T(8,128)} %bitcast.8), calls=%async_computation.2 | async-start | bytes 1048576 | tf_op jit(solution)/shard_map/all_to_all | solution.py:257
  92.6 10.9 %collective-permute-start.3 = (f32[64,256]{1,0:T(8,128)S(1)}, f32[64,256]{1,0:T(8,128)S(1)}, u32[]{:S(2)}, u32[]{:S(2)}) collective-permute-start(f32[64,256]{1,0:T(8,128)S(1)} %bitcast.13), channel_id=1, source_target_pairs={{0,1},{1,0},{2,3},{3,2},{4,5},{5,4},{6,7},{7,6},{8,9},{9,8},{10,11... | collective-permute-start | bytes 196616 | tf_op jit(solution)/shard_map/ppermute | solution.py:251
  100.0 10.0 %all-to-all-start.3 = ((f32[4,256,128]{2,1,0:T(8,128)}), f32[4,256,128]{2,1,0:T(8,128)S(1)}, u32[]{:S(2)}, u32[]{:S(2)}) async-start(f32[4,256,128]{2,1,0:T(8,128)} %broadcast_in_dim.6), calls=%async_computation.3 | async-start | bytes 1048576 | tf_op jit(solution)/shard_map/all_to_all | solution.py:257

commit v3 on v0

v3 whole, which is shorter than its diff:
```python
import functools

import jax
import jax.numpy as jnp
from jax import lax
from jax.experimental import pallas as pl
from jax.experimental.pallas import tpu as pltpu
from jax.sharding import PartitionSpec as P

HIGH = lax.Precision.HIGHEST
F32 = jnp.float32
BF16 = jnp.bfloat16
EDGE = 128
GROUP = 8
ACC_BYTES = 16 << 20
GELU_C = 0.7978845608028654
GELU_K = 0.044715


def inv_column(deg_ref, start):
    row = lax.rsqrt(deg_ref[pl.ds(start, 1), :].astype(F32))
    return jnp.transpose(jnp.broadcast_to(row, (EDGE, EDGE)))


def split(value):
    hi = value.astype(BF16)
    return hi, (value - hi.astype(F32)).astype(BF16)


def fetch(pairs, sems):
    copies = [pltpu.make_async_copy(src, dst, sems.at[i]) for i, (src, dst) in enumerate(pairs)]
    for copy in copies:
        copy.start()
    return copies


def forward_kernel(
    n_col, chunk, panel_dev, node_dev, groups,
    rows_ref, cols_ref, live_ref, deg_ref, feat_ref, blocks_ref, *refs,
):
    n_out = 2 * len(groups) + 1
    outs, dense_ref = refs[:n_out - 1], refs[n_out - 1]
    acc, both, buf, scaled, in_sems, out_sems = refs[n_out:]
    slots = buf.shape[0]
    col_nodes, width = feat_ref.shape
    col_blocks = col_nodes // EDGE
    dev_blocks = node_dev // EDGE
    panel_blocks = panel_dev * dev_blocks
    positions = panel_blocks * col_blocks
    n_panels = n_col // panel_dev
    n_chunks = slots // chunk
    me = lax.axis_index("col")
    live = live_ref[0, 0]

    def block_copy(c):
        span = pl.ds(c * chunk, chunk)
        return pltpu.make_async_copy(blocks_ref.at[0, 0, span], buf.at[span], in_sems.at[c])

    def dense_copy(panel, j):
        there = pl.ds((panel * panel_dev + j) * node_dev, node_dev)
        return pltpu.make_async_copy(
            both.at[j, pl.ds(0, node_dev)], dense_ref.at[there], out_sems.at[j]
        )

    for c in range(n_chunks):
        block_copy(c).start()

    for k in range(col_blocks):
        inv = inv_column(deg_ref, me * col_blocks + k)
        span = pl.ds(k * EDGE, EDGE)
        scaled[span, :] = (inv * feat_ref[span, :].astype(F32)).astype(BF16)

    def emit(rel, total):
        for g, members in enumerate(groups):
            for q in range(2):
                ref = outs[2 * g + q]
                if isinstance(rel, int):
                    if rel % 2 == q and rel // 2 in members:
                        ref[members.index(rel // 2)] = total
                else:
                    first = members[0]
                    inside = (rel % 2 == q) & (rel // 2 <= first) & (rel // 2 > first - len(members))

                    @pl.when(inside)
                    def _():
                        ref[first - rel // 2] = total

    def do_panel(panel, first):
        base = panel * panel_blocks

        @pl.loop(0, positions, unroll=4)
        def _(p):
            acc[p] = jnp.zeros((EDGE, EDGE), F32)

        def place(s):
            r = rows_ref[0, 0, s]
            r = ((r // dev_blocks) ^ me) * dev_blocks + r % dev_blocks - base
            ok = s < live
            if n_panels > 1:
                ok = ok & (r >= 0) & (r < panel_blocks)
            return jnp.where(ok, r * col_blocks + cols_ref[0, 0, s], positions)

        @pl.loop(0, n_chunks)
        def _(c):
            if first is True:
                block_copy(c).wait()
            else:
                @pl.when(first)
                def _():
                    block_copy(c).wait()

            @pl.loop(0, chunk // GROUP)
            def _(g):
                for u in range(0, GROUP, 2):
                    s = c * chunk + g * GROUP + u
                    p0, p1 = place(s), place(s + 1)
                    same = jnp.where(p0 == p1, 1.0, 0.0).astype(F32)
                    b0, b1 = buf[s].astype(F32), buf[s + 1].astype(F32)
                    a0, a1 = acc[p0], acc[p1]
                    acc[p0] = a0 + b0
                    acc[p1] = a1 + (b1 + same * b0)

        def one(j):
            for b in range(dev_blocks):
                for cb in range(col_blocks):
                    hi, lo = split(acc[(j * dev_blocks + b) * col_blocks + cb])
                    lanes = slice(cb * EDGE, (cb + 1) * EDGE)
                    both[j, b * EDGE:(b + 1) * EDGE, lanes] = hi
                    both[j, node_dev + b * EDGE:node_dev + (b + 1) * EDGE, lanes] = lo
            dense_copy(panel, j).start()
            pair = jnp.dot(both[j], scaled[...], preferred_element_type=F32)
            total = pair[:node_dev] + pair[node_dev:]
            emit(panel * panel_dev + j, total)

        if n_panels == 1:
            for j in reversed(range(panel_dev)):
                one(j)
        else:
            @pl.loop(0, panel_dev)
            def _(j):
                @pl.when(panel > 0)
                def _():
                    dense_copy(panel, j).wait()
                one(j)

    if n_panels == 1:
        do_panel(0, True)
    else:
        @pl.loop(0, n_panels)
        def _(panel):
            do_panel(panel, panel == 0)

    for j in range(panel_dev):
        dense_copy(n_panels - 1, j).wait()


def middle_kernel(n_col, n_in, deg_ref, cot_ref, weight_ref, *refs):
    parts = refs[:n_in]
    act_ref, pulled_ref, prop_ref, gprime_ref = refs[n_in:n_in + 4]
    node_dev = cot_ref.shape[0]
    dev_blocks = node_dev // EDGE
    base = (lax.axis_index("row") * n_col + lax.axis_index("col")) * dev_blocks
    inv = jnp.concatenate([inv_column(deg_ref, base + k) for k in range(dev_blocks)], axis=0)
    summed = parts[0][...].reshape(node_dev, EDGE)
    for ref in parts[1:]:
        summed = summed + ref[...].reshape(node_dev, EDGE)
    propagated = inv * summed
    prop_ref[...] = propagated
    weight = weight_ref[...]
    pair = jnp.dot(jnp.concatenate(split(propagated), axis=0), weight, preferred_element_type=F32)
    v = pair[:node_dev] + pair[node_dev:]
    t = jnp.tanh(GELU_C * (v + GELU_K * v * v * v))
    act_ref[...] = (0.5 * v * (1.0 + t)).astype(BF16)
    slope = 0.5 * (1.0 + t) + 0.5 * v * (1.0 - t * t) * (GELU_C * (1.0 + 3.0 * GELU_K * v * v))
    gprime = cot_ref[...].astype(F32) * slope
    gprime_ref[...] = gprime
    pair = lax.dot_general(
        jnp.concatenate(split(gprime), axis=0), weight, (((1,), (1,)), ((), ())),
        preferred_element_type=F32,
    )
    pulled_ref[...] = jnp.transpose(inv * (pair[:node_dev] + pair[node_dev:]))


def weight_kernel(scale, prop_ref, gprime_ref, keep_ref, send_ref):
    part = scale * lax.dot_general(
        prop_ref[...], gprime_ref[...], (((0,), (0,)), ((), ())),
        precision=HIGH, preferred_element_type=F32,
    )
    half = keep_ref.shape[0]
    low = lax.axis_index("col") % 2 == 0
    keep_ref[...] = jnp.where(low, part[:half], part[half:])
    send_ref[...] = jnp.where(low, part[half:], part[:half])


def load_lhs(parts, stage, lhs, copies):
    width = parts[0].shape[0]
    node_dev = parts[0].shape[1]
    for i in range(len(parts)):
        copies[i].wait()
        hi, lo = split(stage[i])
        lhs[:width, i * node_dev:(i + 1) * node_dev] = hi
        lhs[width:, i * node_dev:(i + 1) * node_dev] = lo


def partial_kernel(n_in, dense_ref, *refs):
    parts, (out_ref, dense, stage, lhs, sems, dense_sems) = refs[:n_in], refs[n_in:]
    width, node_dev = parts[0].shape
    col_nodes = dense.shape[1]
    blocks = fetch(
        [(dense_ref.at[pl.ds(i * node_dev, node_dev)], dense.at[pl.ds(i * node_dev, node_dev)])
         for i in range(n_in)], dense_sems)
    load_lhs(parts, stage, lhs, fetch([(r, stage.at[i]) for i, r in enumerate(parts)], sems))
    for copy in blocks:
        copy.wait()
    step = 2 * EDGE if col_nodes % (2 * EDGE) == 0 else EDGE
    for n in range(0, col_nodes, step):
        pair = jnp.dot(lhs[...], dense[:, n:n + step], preferred_element_type=F32)
        out_ref[:, n:n + step] = pair[:width] + pair[width:]


def last_kernel(n_in, n_out, start, deg_ref, dense_ref, sofar_ref, *refs):
    parts, outs = refs[:n_in], refs[n_in:n_in + n_out]
    dense, stage, lhs, sofar, sems, dense_sem, sofar_sem = refs[n_in + n_out:]
    width, node_dev = parts[0].shape
    col_nodes = dense.shape[1]
    block = pltpu.make_async_copy(
        dense_ref.at[pl.ds(start, n_in * node_dev)], dense, dense_sem)
    before = pltpu.make_async_copy(sofar_ref, sofar, sofar_sem)
    block.start()
    copies = fetch([(r, stage.at[i]) for i, r in enumerate(parts)], sems)
    before.start()
    load_lhs(parts, stage, lhs, copies)
    block.wait()
    before.wait()
    step = 2 * EDGE if col_nodes % (2 * EDGE) == 0 else EDGE
    size = col_nodes // n_out
    first = lax.axis_index("col") * (col_nodes // EDGE)
    for n in range(0, col_nodes, step):
        pair = jnp.dot(lhs[...], dense[:, n:n + step], preferred_element_type=F32)
        total = sofar[:, n:n + step] + (pair[:width] + pair[width:])
        for at in range(n, n + step, EDGE):
            inv = inv_column(deg_ref, first + at // EDGE)
            out = outs[at // size]
            out[at % size:at % size + EDGE, :] = inv * jnp.transpose(total[:, at - n:at - n + EDGE])


def body(n_row, n_col, features, degrees, block_rows, block_cols, live_slots, blocks, weight, cotangent):
    n_chip = n_col // 2
    chip_bits, row_bits = n_chip.bit_length() - 1, n_row.bit_length() - 1
    assert n_col == 2 << chip_bits and n_row == 1 << row_bits
    node_dev, hidden = cotangent.shape
    col_nodes, width = features.shape
    row_nodes = node_dev * n_col
    nodes = col_nodes * n_col
    slots = blocks.shape[2]
    deg = degrees.reshape(nodes // EDGE, EDGE)
    col_blocks = col_nodes // EDGE
    chunk = 32

    panel_dev = n_col
    while panel_dev % 2 == 0 and panel_dev * node_dev * col_nodes * 4 > ACC_BYTES:
        panel_dev //= 2
    positions = panel_dev * (node_dev // EDGE) * col_blocks
    groups = [g for g in ([n_chip - 1], list(range(n_chip - 2, 0, -1)), [0]) if g]
    if n_chip == 1:
        groups = [[0]]
    smem = pl.BlockSpec(memory_space=pltpu.SMEM)
    hbm = pl.BlockSpec(memory_space=pl.ANY)
    vmem = pl.BlockSpec(memory_space=pltpu.VMEM)

    def params(mib):
        return pltpu.CompilerParams(vmem_limit_bytes=mib << 20)

    pieces = [
        jax.ShapeDtypeStruct((len(g), node_dev, width), F32) for g in groups for _ in range(2)
    ]
    *pieces, dense = pl.pallas_call(
        functools.partial(forward_kernel, n_col, chunk, panel_dev, node_dev, groups),
        out_shape=(*pieces, jax.ShapeDtypeStruct((row_nodes, col_nodes), BF16)),
        in_specs=[smem, smem, smem, vmem, vmem, hbm],
        out_specs=(vmem,) * len(pieces) + (hbm,),
        scratch_shapes=[
            pltpu.VMEM((positions + 1, EDGE, EDGE), F32),
            pltpu.VMEM((panel_dev, 2 * node_dev, col_nodes), BF16),
            pltpu.VMEM((slots, EDGE, EDGE), BF16),
            pltpu.VMEM((col_nodes, width), BF16),
            pltpu.SemaphoreType.DMA((slots // chunk,)),
            pltpu.SemaphoreType.DMA((panel_dev,)),
        ],
        compiler_params=params(60),
        name="densify_forward",
    )(block_rows, block_cols, live_slots, deg, features, blocks)

    swap_pairs = [(i, i ^ 1) for i in range(n_col)]

    def swap(x):
        return lax.ppermute(x, "col", swap_pairs)

    def chip_flip(x, bit):
        return lax.ppermute(x, "col", [(i, i ^ (2 << bit)) for i in range(n_col)])

    def row_flip(x, bit):
        return lax.ppermute(x, "row", [(i, i ^ (1 << bit)) for i in range(n_row)])

    def low_bit(m):
        return (m & -m).bit_length() - 1

    terms = {}
    for g, members in enumerate(groups):
        keep, got = pieces[2 * g], swap(pieces[2 * g + 1])
        for i, m in enumerate(members):
            terms[m] = [keep[i], got[i]]
    for m in range(n_chip - 1, 0, -1):
        terms[m & (m - 1)].append(chip_flip(functools.reduce(jnp.add, terms[m]), low_bit(m)))
    parts = terms[0]

    out_act, pulled, prop, gprime = pl.pallas_call(
        functools.partial(middle_kernel, n_col, len(parts)),
        out_shape=(
            jax.ShapeDtypeStruct((node_dev, hidden), BF16),
            jax.ShapeDtypeStruct((width, node_dev), F32),
            jax.ShapeDtypeStruct((node_dev, width), F32),
            jax.ShapeDtypeStruct((node_dev, hidden), F32),
        ),
        in_specs=[vmem] * (3 + len(parts)),
        out_specs=(vmem,) * 4,
        compiler_params=params(16),
        name="middle",
    )(deg, cotangent, weight, *parts)

    own = {0: pulled}
    for m in range(1, n_chip):
        own[m] = chip_flip(own[m & (m - 1)], low_bit(m))
    other = {m: swap(own[m]) for m in range(n_chip)}

    other[0], prop, gprime = lax.optimization_barrier((other[0], prop, gprime))
    half = width // 2
    wkeep, wsend = pl.pallas_call(
        functools.partial(weight_kernel, float(nodes) ** (-0.5)),
        out_shape=(jax.ShapeDtypeStruct((half, hidden), F32),) * 2,
        in_specs=[vmem] * 2,
        out_specs=(vmem,) * 2,
        compiler_params=params(16),
        name="weight_part",
    )(prop, gprime)

    early = [x for m in range(n_chip - 1) for x in (own[m], other[m])]
    late = [own[n_chip - 1], other[n_chip - 1]]
    tile_mib = row_nodes * col_nodes * 2 >> 20
    sofar = pl.pallas_call(
        functools.partial(partial_kernel, len(early)),
        out_shape=jax.ShapeDtypeStruct((width, col_nodes), F32),
        in_specs=[hbm] * (1 + len(early)),
        out_specs=vmem,
        scratch_shapes=[
            pltpu.VMEM((len(early) * node_dev, col_nodes), BF16),
            pltpu.VMEM((len(early), width, node_dev), F32),
            pltpu.VMEM((2 * width, len(early) * node_dev), BF16),
            pltpu.SemaphoreType.DMA((len(early),)),
            pltpu.SemaphoreType.DMA((len(early),)),
        ],
        compiler_params=params(tile_mib + 20),
        name="backward_early",
    )(dense, *early)

    n_piece = max(1, row_bits)
    while col_nodes % (EDGE * n_piece):
        n_piece -= 1
    size = col_nodes // n_piece
    parts = pl.pallas_call(
        functools.partial(last_kernel, len(late), n_piece, len(early) * node_dev),
        out_shape=(jax.ShapeDtypeStruct((size, width), F32),) * n_piece,
        in_specs=[vmem, hbm, hbm] + [hbm] * len(late),
        out_specs=(vmem,) * n_piece,
        scratch_shapes=[
            pltpu.VMEM((len(late) * node_dev, col_nodes), BF16),
            pltpu.VMEM((len(late), width, node_dev), F32),
            pltpu.VMEM((2 * width, len(late) * node_dev), BF16),
            pltpu.VMEM((width, col_nodes), F32),
            pltpu.SemaphoreType.DMA((len(late),)),
            pltpu.SemaphoreType.DMA,
            pltpu.SemaphoreType.DMA,
        ],
        compiler_params=params(16),
        name="backward_late",
    )(deg, dense, sofar, *late)

    done = list(parts)
    for t in range(row_bits):
        done = [x + row_flip(x, (i + t) % row_bits) for i, x in enumerate(done)]
    feat_grad = jnp.concatenate(done, axis=0) if n_piece > 1 else done[0]

    wsum = wkeep + swap(wsend)
    for t in range(row_bits):
        wsum = wsum + row_flip(wsum, t)
    for t in range(chip_bits):
        wsum = wsum + chip_flip(wsum, t)
    wother = swap(wsum)
    low = lax.axis_index("col") % 2 == 0
    weight_grad = jnp.concatenate(
        [jnp.where(low, wsum, wother), jnp.where(low, wother, wsum)], axis=0
    )
    return out_act, feat_grad, weight_grad


def solution(mesh):
    n_row, n_col = mesh.shape["row"], mesh.shape["col"]
    return jax.shard_map(
        functools.partial(body, n_row, n_col),
        mesh=mesh,
        in_specs=(
            P("col", None),
            P(),
            P("row", "col", None),
            P("row", "col", None),
            P("row", "col"),
            P("row", "col", None, None, None),
            P(),
            P(("row", "col"), None),
        ),
        out_specs=(P(("row", "col"), None), P("col", None), P()),
        check_vma=False,
    )
```

time: 366 us -> 87.3 us (0.24)
  other arithmetic: 107 us -> 4.45 us
  local copies, waits for them, and re-layouts: 79 us -> 3.09 us
  waiting for transfers between devices: 105 us -> 41.9 us
  matrix products: 57.9 us -> 0 us
  starting transfers between devices: 0.16 us -> 19.4 us
  Pallas kernels: 0 us -> 16.7 us
  between operations: 14.5 us -> 1.52 us
    scatter-add x2 -> x0, other arithmetic: 100 us -> none  [the longest x1 50.2 us: body(): jax.ops.segment_sum(products, row_slots, num_segments=row_nodes // edge)]
    dot_general x5 -> x0, matrix products: 57.9 us -> none  [the longest x1 30.2 us: body(): jnp.einsum('sij,sif->sjf', tile_blocks.astype(jnp.float32), picked, preci...]
    psum x2 -> x0, waiting for transfers between devices: 51.6 us -> none  [the longest x1 46.3 us: body(): col_total = lax.psum(col_part, 'row')]
    select_n x2 -> x0, local copies, waits for them, and re-layouts: 49.4 us -> none  [body(): products = jnp.where(in_use, products, 0.0)]
    ppermute x0 -> x23, waiting for transfers between devices: none -> 41.9 us  [the longest x8 27.4 us: chip_flip(): return lax.ppermute(x, 'col', [(i, i ^ 2 << bit) for i in range(n_col)])]
    reduce_scatter x1 -> x0, waiting for transfers between devices: 35 us -> none  [body(): lax.psum_scatter(summed_rows.reshape(row_nodes, width_now), 'col', scatte...]
    gather x2 -> x0, local copies, waits for them, and re-layouts: 27.7 us -> none  [the longest x1 16.4 us: body(): picked = gathered.reshape(row_nodes // edge, edge, width_now)[row_slots]]
    ppermute x0 -> x23, starting transfers between devices: none -> 19.4 us  [the longest x8 11.1 us: chip_flip(): return lax.ppermute(x, 'col', [(i, i ^ 2 << bit) for i in range(n_col)])]
  transfers between devices with their start and end apart: 4 -> 23, of which waited for: 4 -> 13; matrix products, arithmetic and copies ran while one was open for 34% -> 4% of each run, Pallas kernels for 0% -> 3%
where the time goes in v3:
time: 87.3 us; the launch traced here: 87 us
  waiting for transfers between devices  41.9 us (48%)
  starting transfers between devices  19.4 us (22%)
  Pallas kernels  16.7 us (19%)
  other arithmetic  4.45 us (5%)
  local copies, waits for them, and re-layouts  3.09 us (4%)
  between operations  1.52 us (2%)
    ppermute x8, waiting for transfers between devices, chip_flip(): return lax.ppermute(x, 'col', [(i, i ^ 2 << bit) for i in range(n_col)])  27.4 us
    ppermute x6, waiting for transfers between devices, row_flip(): return lax.ppermute(x, 'row', [(i, i ^ 1 << bit) for i in range(n_row)])  13.3 us
    pallas_call x1, Pallas kernels, body(): pl.pallas_call(functools.partial(forward_kernel, n_col, chunk, panel_dev,...  11.7 us
    ppermute x8, starting transfers between devices, chip_flip(): return lax.ppermute(x, 'col', [(i, i ^ 2 << bit) for i in range(n_col)])  11.1 us
    ppermute x6, starting transfers between devices, row_flip(): return lax.ppermute(x, 'row', [(i, i ^ 1 << bit) for i in range(n_row)])  6.99 us
    unnamed x10, local copies, waits for them, and re-layouts  3.09 us
    add x3, other arithmetic, body(): functools.reduce(jnp.add, terms[m])  2.78 us
    pallas_call x1, Pallas kernels, body(): pl.pallas_call(functools.partial(partial_kernel, len(early)), out_shape=j...  2.42 us
  transfers between devices with their start and end apart: 23, of which 13 were waited for; matrix products, arithmetic and copies ran while one was open for 4% of the time, Pallas kernels for 3%

profile of v3, /device:TPU:0, one launch (start us, length us, event | category | flops | bytes accessed | tf_op | source)
XLA Modules:
  0.0 87.0 jit_solution(12676760952850672237)
XLA Ops:
  1.3 11.7 %densify_forward.1 = (f32[1,256,128]{2,1,0:T(8,128)}, f32[1,256,128]{2,1,0:T(8,128)}, f32[2,256,128]{2,1,0:T(8,128)}, f32[2,256,128]{2,1,0:T(8,128)}, f32[1,256,...) custom-call(s32[1,1,384]{2,1,0:T(1,128)} %rows_ref.1, s32[1,1,384]{2,1,0:T(1,128)} %cols_ref.1, ...), custom_call_target="tpu_custom_call" | custom-call | tf_op jit(solution)/shard_map/densify_forward/pallas_call | solution.py:277
  13.6 1.1 %collective-permute-done.2 = f32[1,256,128]{2,1,0:T(8,128)S(1)} collective-permute-done((f32[1,256,128]{2,1,0:T(8,128)}, f32[1,256,128]{2,1,0:T(8,128)S(1)}, u32[]{:S(2)}, u32[]{:S(2)}) %collective-permute-start.2) | collective-permute-done | bytes 131104 | tf_op jit(solution)/shard_map/ppermute | solution.py:297
  14.7 0.9 %add_bitcast_fusion = f32[256,128]{1,0:T(8,128)S(1)} fusion(f32[1,256,128]{2,1,0:T(8,128)} %get-tuple-element.25, f32[1,256,128]{2,1,0:T(8,128)S(1)} %collective-permute-done.2), kind=kLoop, calls=%fused_computation.7 | loop fusion | flops 32768 | bytes 393216 | tf_op jit(solution)/shard_map/add | solution.py:314
  15.6 3.0 %collective-permute-start.3 = (f32[256,128]{1,0:T(8,128)S(1)}, f32[256,128]{1,0:T(8,128)S(1)}, u32[]{:S(2)}, u32[]{:S(2)}) collective-permute-start(f32[256,128]{1,0:T(8,128)S(1)} %add_bitcast_fusion), channel_id=1, source_target_pairs={{0,2},{1,3},{2,0},{3,1},{4,6},{5,7},{6,4},{7,5},{8,10},{9,11},{10,... | collective-permute-start | bytes 393224 | tf_op jit(solution)/shard_map/ppermute | solution.py:300
  18.6 3.8 %collective-permute-done.3 = f32[256,128]{1,0:T(8,128)S(1)} collective-permute-done((f32[256,128]{1,0:T(8,128)S(1)}, f32[256,128]{1,0:T(8,128)S(1)}, u32[]{:S(2)}, u32[]{:S(2)}) %collective-permute-start.3) | collective-permute-done | bytes 131104 | tf_op jit(solution)/shard_map/ppermute | solution.py:300
  22.5 0.9 %fusion.2 = f32[256,128]{1,0:T(8,128)S(1)} fusion(f32[256,128]{1,0:T(8,128)S(1)} %collective-permute-done.3, f32[2,256,128]{2,1,0:T(8,128)S(1)} %collective-permute-done.1, f32[2,256,128]{2,1,0:T(8,128)} %get-tuple-element.23), kind=kLoop, calls=%fused_computation.5 | loop fusion | flops 65536 | bytes 524288 | tf_op jit(solution)/shard_map/add | solution.py:314
  23.4 2.8 %collective-permute-start.4 = (f32[256,128]{1,0:T(8,128)S(1)}, f32[256,128]{1,0:T(8,128)S(1)}, u32[]{:S(2)}, u32[]{:S(2)}) collective-permute-start(f32[256,128]{1,0:T(8,128)S(1)} %fusion.2), channel_id=1, source_target_pairs={{0,4},{1,5},{2,6},{3,7},{4,0},{5,1},{6,2},{7,3},{8,12},{9,13},{10,... | collective-permute-start | bytes 393224 | tf_op jit(solution)/shard_map/ppermute | solution.py:300
  26.2 0.9 %fusion = f32[256,128]{1,0:T(8,128)S(1)} fusion(f32[2,256,128]{2,1,0:T(8,128)S(1)} %collective-permute-done.1, f32[2,256,128]{2,1,0:T(8,128)} %get-tuple-element.23), kind=kLoop, calls=%fused_computation.2 | loop fusion | flops 32768 | bytes 393216 | tf_op jit(solution)/shard_map/add | solution.py:314
  27.1 1.6 %collective-permute-start.5 = (f32[256,128]{1,0:T(8,128)S(1)}, f32[256,128]{1,0:T(8,128)S(1)}, u32[]{:S(2)}, u32[]{:S(2)}) collective-permute-start(f32[256,128]{1,0:T(8,128)S(1)} %fusion), channel_id=1, source_target_pairs={{0,2},{1,3},{2,0},{3,1},{4,6},{5,7},{6,4},{7,5},{8,10},{9,11},{10,... | collective-permute-start | bytes 393224 | tf_op jit(solution)/shard_map/ppermute | solution.py:300
  28.8 3.5 %collective-permute-done.4.refs_2_ = f32[256,128]{1,0:T(8,128)S(1)} collective-permute-done((f32[256,128]{1,0:T(8,128)S(1)}, f32[256,128]{1,0:T(8,128)S(1)}, u32[]{:S(2)}, u32[]{:S(2)}) %collective-permute-start.4) | collective-permute-done | bytes 131104 | tf_op jit(solution)/shard_map/ppermute | solution.py:300
  32.3 1.2 %collective-permute-done.5.refs_3_ = f32[256,128]{1,0:T(8,128)S(1)} collective-permute-done((f32[256,128]{1,0:T(8,128)S(1)}, f32[256,128]{1,0:T(8,128)S(1)}, u32[]{:S(2)}, u32[]{:S(2)}) %collective-permute-start.5) | collective-permute-done | bytes 131104 | tf_op jit(solution)/shard_map/ppermute | solution.py:300
  33.5 0.9 %copy-done.3 = f32[1,256,128]{2,1,0:T(8,128)S(1)} copy-done((f32[1,256,128]{2,1,0:T(8,128)S(1)}, f32[1,256,128]{2,1,0:T(8,128)}, u32[]{:S(2)}) %copy-start.3) | copy-done | bytes 131096
  34.4 1.2 %middle.1 = (bf16[256,256]{1,0:T(8,128)(2,1)}, f32[128,256]{1,0:T(8,128)S(1)}, f32[256,128]{1,0:T(8,128)S(1)}, f32[256,256]{1,0:T(8,128)S(1)}) custom-call(s32[64,128]{1,0:T(8,128)S(1)} %bitcast.12, bf16[256,256]{1,0:T(8,128)(2,1)S(1)} %copy-done.2, bf16[128,256]{1,0:T(8,128)(2,1)S(1)} %copy-done.4, f32[256,128]{1,0:T(8,128)S(1)} %bitcast.14, ...), custom_call_target="tpu_custom_call" | custom-call | tf_op jit(solution)/shard_map/middle/pallas_call | solution.py:317
  35.6 0.7 collective-permute-start.9
  36.3 2.5 %collective-permute-start.7 = (f32[128,256]{1,0:T(8,128)S(1)}, f32[128,256]{1,0:T(8,128)S(1)}, u32[]{:S(2)}, u32[]{:S(2)}) collective-permute-start(f32[128,256]{1,0:T(8,128)S(1)} %get-tuple-element.29.refs_0_), channel_id=1, source_target_pairs={{0,2},{1,3},{2,0},{3,1},{4,6},{5,7},{6,4},{7,5},{8,10},{9,11},{10,... | collective-permute-start | bytes 393224 | tf_op jit(solution)/shard_map/ppermute | solution.py:300
  38.7 5.2 %collective-permute-done.9.refs_4_ = f32[128,256]{1,0:T(8,128)S(1)} collective-permute-done((f32[128,256]{1,0:T(8,128)S(1)}, f32[128,256]{1,0:T(8,128)S(1)}, u32[]{:S(2)}, u32[]{:S(2)}) %collective-permute-start.9) | collective-permute-done | bytes 131104 | tf_op jit(solution)/shard_map/ppermute | solution.py:300
  45.3 3.6 %collective-permute-done.11.refs_0_ = f32[128,256]{1,0:T(8,128)S(1)} collective-permute-done((f32[128,256]{1,0:T(8,128)S(1)}, f32[128,256]{1,0:T(8,128)S(1)}, u32[]{:S(2)}, u32[]{:S(2)}) %collective-permute-start.11) | collective-permute-done | bytes 131104 | tf_op jit(solution)/shard_map/ppermute | solution.py:300
  49.0 1.3 %collective-permute-start.18 = (f32[64,256]{1,0:T(8,128)S(1)}, f32[64,256]{1,0:T(8,128)S(1)}, u32[]{:S(2)}, u32[]{:S(2)}) collective-permute-start(f32[64,256]{1,0:T(8,128)S(1)} %add.64), channel_id=1, source_target_pairs={{0,8},{8,0},{16,24},{24,16},{1,9},{9,1},{17,25},{25,17},{2,10},{10... | collective-permute-start | bytes 196616 | tf_op jit(solution)/shard_map/ppermute | solution.py:303
  50.3 3.3 %collective-permute-done.18 = f32[64,256]{1,0:T(8,128)S(1)} collective-permute-done((f32[64,256]{1,0:T(8,128)S(1)}, f32[64,256]{1,0:T(8,128)S(1)}, u32[]{:S(2)}, u32[]{:S(2)}) %collective-permute-start.18) | collective-permute-done | bytes 65568 | tf_op jit(solution)/shard_map/ppermute | solution.py:303
  53.6 2.2 %copy-done = bf16[2048,1024]{1,0:T(8,128)(2,1)S(1)} copy-done((bf16[2048,1024]{1,0:T(8,128)(2,1)S(1)}, bf16[2048,1024]{1,0:T(8,128)(2,1)}, u32[]{:S(2)}) %copy-start) | copy-done | bytes 4194328
  55.7 2.4 %backward_early.1.sofar_ref = f32[128,1024]{1,0:T(8,128)S(1)} custom-call(bf16[2048,1024]{1,0:T(8,128)(2,1)S(1)} %copy-done, f32[128,256]{1,0:T(8,128)S(1)} %get-tuple-element.29.refs_0_, f32[128,256]{1,0:T(8,128)S(1)} %collective-permute-done.6.refs_1_, f32[128,256]{1,0:T(8,128)S(1)} %collective-permute-done.7.refs_2_, ...), custom_call_target="tpu_custom_call" | custom-call | tf_op jit(solution)/shard_map/backward_early/pallas_call | solution.py:350
  58.2 1.1 %backward_late.1 = (f32[512,128]{1,0:T(8,128)S(1)}, f32[512,128]{1,0:T(8,128)S(1)}) custom-call(s32[64,128]{1,0:T(8,128)S(1)} %bitcast.13, bf16[2048,1024]{1,0:T(8,128)(2,1)S(1)} %copy-done, f32[128,1024]{1,0:T(8,128)S(1)} %backward_early.1.sofar_ref, f32[128,256]{1,0:T(8,128)S(1)} %collective-permute-done.11.refs_0_, ...), custom_call_target="tpu_custom_call" | custom-call | tf_op jit(solution)/shard_map/backward_late/pallas_call | solution.py:370
  59.3 1.3 %collective-permute-start.13 = (f32[512,128]{1,0:T(8,128)S(1)}, f32[512,128]{1,0:T(8,128)S(1)}, u32[]{:S(2)}, u32[]{:S(2)}) collective-permute-start(f32[512,128]{1,0:T(8,128)S(1)} %get-tuple-element.33), channel_id=1, source_target_pairs={{0,8},{8,0},{16,24},{24,16},{1,9},{9,1},{17,25},{25,17},{2,10},{10... | collective-permute-start | bytes 786440 | tf_op jit(solution)/shard_map/ppermute | solution.py:303
  60.6 1.5 %collective-permute-start.19 = (f32[64,256]{1,0:T(8,128)S(1)}, f32[64,256]{1,0:T(8,128)S(1)}, u32[]{:S(2)}, u32[]{:S(2)}) collective-permute-start(f32[64,256]{1,0:T(8,128)S(1)} %add.65), channel_id=1, source_target_pairs={{0,16},{8,24},{16,0},{24,8},{1,17},{9,25},{17,1},{25,9},{2,18},{10... | collective-permute-start | bytes 196616 | tf_op jit(solution)/shard_map/ppermute | solution.py:303
  62.7 2.9 %collective-permute-done.19 = f32[64,256]{1,0:T(8,128)S(1)} collective-permute-done((f32[64,256]{1,0:T(8,128)S(1)}, f32[64,256]{1,0:T(8,128)S(1)}, u32[]{:S(2)}, u32[]{:S(2)}) %collective-permute-start.19) | collective-permute-done | bytes 65568 | tf_op jit(solution)/shard_map/ppermute | solution.py:303
  65.9 4.0 %collective-permute-done.20 = f32[64,256]{1,0:T(8,128)S(1)} collective-permute-done((f32[64,256]{1,0:T(8,128)S(1)}, f32[64,256]{1,0:T(8,128)S(1)}, u32[]{:S(2)}, u32[]{:S(2)}) %collective-permute-start.20) | collective-permute-done | bytes 65568 | tf_op jit(solution)/shard_map/ppermute | solution.py:300
  70.2 5.6 %collective-permute-done.21 = f32[64,256]{1,0:T(8,128)S(1)} collective-permute-done((f32[64,256]{1,0:T(8,128)S(1)}, f32[64,256]{1,0:T(8,128)S(1)}, u32[]{:S(2)}, u32[]{:S(2)}) %collective-permute-start.21) | collective-permute-done | bytes 65568 | tf_op jit(solution)/shard_map/ppermute | solution.py:300
  76.0 1.7 %collective-permute-start.14 = (f32[512,128]{1,0:T(8,128)S(1)}, f32[512,128]{1,0:T(8,128)S(1)}, u32[]{:S(2)}, u32[]{:S(2)}) collective-permute-start(f32[512,128]{1,0:T(8,128)S(1)} %add.59), channel_id=1, source_target_pairs={{0,16},{8,24},{16,0},{24,8},{1,17},{9,25},{17,1},{25,9},{2,18},{10... | collective-permute-start | bytes 786440 | tf_op jit(solution)/shard_map/ppermute | solution.py:303
  78.3 0.7 pad_maximum_fusion.1
  79.0 5.7 %collective-permute-done.14 = f32[512,128]{1,0:T(8,128)S(1)} collective-permute-done((f32[512,128]{1,0:T(8,128)S(1)}, f32[512,128]{1,0:T(8,128)S(1)}, u32[]{:S(2)}, u32[]{:S(2)}) %collective-permute-start.14) | collective-permute-done | bytes 262176 | tf_op jit(solution)/shard_map/ppermute | solution.py:303
  84.7 1.4 %collective-permute-done.16 = f32[512,128]{1,0:T(8,128)S(1)} collective-permute-done((f32[512,128]{1,0:T(8,128)S(1)}, f32[512,128]{1,0:T(8,128)S(1)}, u32[]{:S(2)}, u32[]{:S(2)}) %collective-permute-start.16) | collective-permute-done | bytes 262176 | tf_op jit(solution)/shard_map/ppermute | solution.py:303
  86.2 0.8 pad_maximum_fusion
  (44 shorter events, 4.0 us)
Async XLA Ops:
  0.6 32.9 %copy-start.1 = (s32[8192]{0:T(1024)S(1)}, s32[8192]{0:T(1024)}, u32[]{:S(2)}) copy-start(s32[8192]{0:T(1024)} %param.9) | copy-start | bytes 98308
  0.6 32.8 %copy-start.4 = (bf16[128,256]{1,0:T(8,128)(2,1)S(1)}, bf16[128,256]{1,0:T(8,128)(2,1)}, u32[]{:S(2)}) copy-start(bf16[128,256]{1,0:T(8,128)(2,1)} %weight_ref.1) | copy-start | bytes 196612
  0.7 32.8 %copy-start.2 = (bf16[256,256]{1,0:T(8,128)(2,1)S(1)}, bf16[256,256]{1,0:T(8,128)(2,1)}, u32[]{:S(2)}) copy-start(bf16[256,256]{1,0:T(8,128)(2,1)} %cot_ref.1) | copy-start | bytes 393220
  13.0 1.7 %collective-permute-start.2 = (f32[1,256,128]{2,1,0:T(8,128)}, f32[1,256,128]{2,1,0:T(8,128)S(1)}, u32[]{:S(2)}, u32[]{:S(2)}) collective-permute-start(f32[1,256,128]{2,1,0:T(8,128)} %get-tuple-element.26), channel_id=1, source_target_pairs={{0,1},{1,0},{2,3},{3,2},{4,5},{5,4},{6,7},{7,6},{8,9},{9,8},{10,11... | collective-permute-start | bytes 393224 | tf_op jit(solution)/shard_map/ppermute | solution.py:297
  13.5 8.9 %collective-permute-start.1 = (f32[2,256,128]{2,1,0:T(8,128)}, f32[2,256,128]{2,1,0:T(8,128)S(1)}, u32[]{:S(2)}, u32[]{:S(2)}) collective-permute-start(f32[2,256,128]{2,1,0:T(8,128)} %get-tuple-element.24), channel_id=1, source_target_pairs={{0,1},{1,0},{2,3},{3,2},{4,5},{5,4},{6,7},{7,6},{8,9},{9,8},{10,11... | collective-permute-start | bytes 786440 | tf_op jit(solution)/shard_map/ppermute | solution.py:297
  15.6 6.8 %collective-permute-start.3 = (f32[256,128]{1,0:T(8,128)S(1)}, f32[256,128]{1,0:T(8,128)S(1)}, u32[]{:S(2)}, u32[]{:S(2)}) collective-permute-start(f32[256,128]{1,0:T(8,128)S(1)} %add_bitcast_fusion), channel_id=1, source_target_pairs={{0,2},{1,3},{2,0},{3,1},{4,6},{5,7},{6,4},{7,5},{8,10},{9,11},{10,... | collective-permute-start | bytes 393224 | tf_op jit(solution)/shard_map/ppermute | solution.py:300
  18.6 10.1 %collective-permute-start = (f32[1,256,128]{2,1,0:T(8,128)}, f32[1,256,128]{2,1,0:T(8,128)S(1)}, u32[]{:S(2)}, u32[]{:S(2)}) collective-permute-start(f32[1,256,128]{2,1,0:T(8,128)} %get-tuple-element.22), channel_id=1, source_target_pairs={{0,1},{1,0},{2,3},{3,2},{4,5},{5,4},{6,7},{7,6},{8,9},{9,8},{10,11... | collective-permute-start | bytes 393224 | tf_op jit(solution)/shard_map/ppermute | solution.py:297
  23.4 8.9 %collective-permute-start.4 = (f32[256,128]{1,0:T(8,128)S(1)}, f32[256,128]{1,0:T(8,128)S(1)}, u32[]{:S(2)}, u32[]{:S(2)}) collective-permute-start(f32[256,128]{1,0:T(8,128)S(1)} %fusion.2), channel_id=1, source_target_pairs={{0,4},{1,5},{2,6},{3,7},{4,0},{5,1},{6,2},{7,3},{8,12},{9,13},{10,... | collective-permute-start | bytes 393224 | tf_op jit(solution)/shard_map/ppermute | solution.py:300
  27.1 6.4 %collective-permute-start.5 = (f32[256,128]{1,0:T(8,128)S(1)}, f32[256,128]{1,0:T(8,128)S(1)}, u32[]{:S(2)}, u32[]{:S(2)}) collective-permute-start(f32[256,128]{1,0:T(8,128)S(1)} %fusion), channel_id=1, source_target_pairs={{0,2},{1,3},{2,0},{3,1},{4,6},{5,7},{6,4},{7,5},{8,10},{9,11},{10,... | collective-permute-start | bytes 393224 | tf_op jit(solution)/shard_map/ppermute | solution.py:300
  33.5 0.9 %copy-start.3 = (f32[1,256,128]{2,1,0:T(8,128)S(1)}, f32[1,256,128]{2,1,0:T(8,128)}, u32[]{:S(2)}) copy-start(f32[1,256,128]{2,1,0:T(8,128)} %get-tuple-element.21) | copy-start | bytes 393220
  35.6 8.3 %collective-permute-start.9 = (f32[128,256]{1,0:T(8,128)S(1)}, f32[128,256]{1,0:T(8,128)S(1)}, u32[]{:S(2)}, u32[]{:S(2)}) collective-permute-start(f32[128,256]{1,0:T(8,128)S(1)} %get-tuple-element.29.refs_0_), channel_id=1, source_target_pairs={{0,4},{1,5},{2,6},{3,7},{4,0},{5,1},{6,2},{7,3},{8,12},{9,13},{10,... | collective-permute-start | bytes 393224 | tf_op jit(solution)/shard_map/ppermute | solution.py:300
  36.3 7.6 %collective-permute-start.6 = (f32[128,256]{1,0:T(8,128)S(1)}, f32[128,256]{1,0:T(8,128)S(1)}, u32[]{:S(2)}, u32[]{:S(2)}) collective-permute-start(f32[128,256]{1,0:T(8,128)S(1)} %get-tuple-element.29.refs_0_), channel_id=1, source_target_pairs={{0,1},{1,0},{2,3},{3,2},{4,5},{5,4},{6,7},{7,6},{8,9},{9,8},{10,11... | collective-permute-start | bytes 393224 | tf_op jit(solution)/shard_map/ppermute | solution.py:297
  36.3 9.1 %collective-permute-start.7 = (f32[128,256]{1,0:T(8,128)S(1)}, f32[128,256]{1,0:T(8,128)S(1)}, u32[]{:S(2)}, u32[]{:S(2)}) collective-permute-start(f32[128,256]{1,0:T(8,128)S(1)} %get-tuple-element.29.refs_0_), channel_id=1, source_target_pairs={{0,2},{1,3},{2,0},{3,1},{4,6},{5,7},{6,4},{7,5},{8,10},{9,11},{10,... | collective-permute-start | bytes 393224 | tf_op jit(solution)/shard_map/ppermute | solution.py:300
  43.9 5.0 %collective-permute-start.11 = (f32[128,256]{1,0:T(8,128)S(1)}, f32[128,256]{1,0:T(8,128)S(1)}, u32[]{:S(2)}, u32[]{:S(2)}) collective-permute-start(f32[128,256]{1,0:T(8,128)S(1)} %collective-permute-done.9.refs_4_), channel_id=1, source_target_pairs={{0,2},{1,3},{2,0},{3,1},{4,6},{5,7},{6,4},{7,5},{8,10},{9,11},{10,... | collective-permute-start | bytes 393224 | tf_op jit(solution)/shard_map/ppermute | solution.py:300
  44.3 4.7 %collective-permute-start.17 = (f32[64,256]{1,0:T(8,128)S(1)}, f32[64,256]{1,0:T(8,128)S(1)}, u32[]{:S(2)}, u32[]{:S(2)}) collective-permute-start(f32[64,256]{1,0:T(8,128)S(1)} %get-tuple-element.38), channel_id=1, source_target_pairs={{0,1},{1,0},{2,3},{3,2},{4,5},{5,4},{6,7},{7,6},{8,9},{9,8},{10,11... | collective-permute-start | bytes 196616 | tf_op jit(solution)/shard_map/ppermute | solution.py:297
  44.3 9.2 %collective-permute-start.10 = (f32[128,256]{1,0:T(8,128)S(1)}, f32[128,256]{1,0:T(8,128)S(1)}, u32[]{:S(2)}, u32[]{:S(2)}) collective-permute-start(f32[128,256]{1,0:T(8,128)S(1)} %collective-permute-done.9.refs_4_), channel_id=1, source_target_pairs={{0,1},{1,0},{2,3},{3,2},{4,5},{5,4},{6,7},{7,6},{8,9},{9,8},{10,11... | collective-permute-start | bytes 393224 | tf_op jit(solution)/shard_map/ppermute | solution.py:297
  45.3 8.2 %collective-permute-start.8 = (f32[128,256]{1,0:T(8,128)S(1)}, f32[128,256]{1,0:T(8,128)S(1)}, u32[]{:S(2)}, u32[]{:S(2)}) collective-permute-start(f32[128,256]{1,0:T(8,128)S(1)} %collective-permute-done.7.refs_2_), channel_id=1, source_target_pairs={{0,1},{1,0},{2,3},{3,2},{4,5},{5,4},{6,7},{7,6},{8,9},{9,8},{10,11... | collective-permute-start | bytes 393224 | tf_op jit(solution)/shard_map/ppermute | solution.py:297
  48.9 9.2 %collective-permute-start.12 = (f32[128,256]{1,0:T(8,128)S(1)}, f32[128,256]{1,0:T(8,128)S(1)}, u32[]{:S(2)}, u32[]{:S(2)}) collective-permute-start(f32[128,256]{1,0:T(8,128)S(1)} %collective-permute-done.11.refs_0_), channel_id=1, source_target_pairs={{0,1},{1,0},{2,3},{3,2},{4,5},{5,4},{6,7},{7,6},{8,9},{9,8},{10,11... | collective-permute-start | bytes 393224 | tf_op jit(solution)/shard_map/ppermute | solution.py:297
  49.0 4.6 %collective-permute-start.18 = (f32[64,256]{1,0:T(8,128)S(1)}, f32[64,256]{1,0:T(8,128)S(1)}, u32[]{:S(2)}, u32[]{:S(2)}) collective-permute-start(f32[64,256]{1,0:T(8,128)S(1)} %add.64), channel_id=1, source_target_pairs={{0,8},{8,0},{16,24},{24,16},{1,9},{9,1},{17,25},{25,17},{2,10},{10... | collective-permute-start | bytes 196616 | tf_op jit(solution)/shard_map/ppermute | solution.py:303
  53.6 2.2 %copy-start = (bf16[2048,1024]{1,0:T(8,128)(2,1)S(1)}, bf16[2048,1024]{1,0:T(8,128)(2,1)}, u32[]{:S(2)}) copy-start(bf16[2048,1024]{1,0:T(8,128)(2,1)} %get-tuple-element.28.dense_ref) | copy-start | bytes 12582916
  59.3 16.6 %collective-permute-start.13 = (f32[512,128]{1,0:T(8,128)S(1)}, f32[512,128]{1,0:T(8,128)S(1)}, u32[]{:S(2)}, u32[]{:S(2)}) collective-permute-start(f32[512,128]{1,0:T(8,128)S(1)} %get-tuple-element.33), channel_id=1, source_target_pairs={{0,8},{8,0},{16,24},{24,16},{1,9},{9,1},{17,25},{25,17},{2,10},{10... | collective-permute-start | bytes 786440 | tf_op jit(solution)/shard_map/ppermute | solution.py:303
  60.6 5.0 %collective-permute-start.19 = (f32[64,256]{1,0:T(8,128)S(1)}, f32[64,256]{1,0:T(8,128)S(1)}, u32[]{:S(2)}, u32[]{:S(2)}) collective-permute-start(f32[64,256]{1,0:T(8,128)S(1)} %add.65), channel_id=1, source_target_pairs={{0,16},{8,24},{16,0},{24,8},{1,17},{9,25},{17,1},{25,9},{2,18},{10... | collective-permute-start | bytes 196616 | tf_op jit(solution)/shard_map/ppermute | solution.py:303
  62.2 15.5 %collective-permute-start.15 = (f32[512,128]{1,0:T(8,128)S(1)}, f32[512,128]{1,0:T(8,128)S(1)}, u32[]{:S(2)}, u32[]{:S(2)}) collective-permute-start(f32[512,128]{1,0:T(8,128)S(1)} %get-tuple-element.34), channel_id=1, source_target_pairs={{0,16},{8,24},{16,0},{24,8},{1,17},{9,25},{17,1},{25,9},{2,18},{10... | collective-permute-start | bytes 786440 | tf_op jit(solution)/shard_map/ppermute | solution.py:303
  65.6 4.3 %collective-permute-start.20 = (f32[64,256]{1,0:T(8,128)S(1)}, f32[64,256]{1,0:T(8,128)S(1)}, u32[]{:S(2)}, u32[]{:S(2)}) collective-permute-start(f32[64,256]{1,0:T(8,128)S(1)} %add.66), channel_id=1, source_target_pairs={{0,2},{1,3},{2,0},{3,1},{4,6},{5,7},{6,4},{7,5},{8,10},{9,11},{10,... | collective-permute-start | bytes 196616 | tf_op jit(solution)/shard_map/ppermute | solution.py:300
  70.0 5.8 %collective-permute-start.21 = (f32[64,256]{1,0:T(8,128)S(1)}, f32[64,256]{1,0:T(8,128)S(1)}, u32[]{:S(2)}, u32[]{:S(2)}) collective-permute-start(f32[64,256]{1,0:T(8,128)S(1)} %add.67), channel_id=1, source_target_pairs={{0,4},{1,5},{2,6},{3,7},{4,0},{5,1},{6,2},{7,3},{8,12},{9,13},{10,... | collective-permute-start | bytes 196616 | tf_op jit(solution)/shard_map/ppermute | solution.py:300
  75.8 2.5 %collective-permute-start.22 = (f32[64,256]{1,0:T(8,128)S(1)}, f32[64,256]{1,0:T(8,128)S(1)}, u32[]{:S(2)}, u32[]{:S(2)}) collective-permute-start(f32[64,256]{1,0:T(8,128)S(1)} %add.68), channel_id=1, source_target_pairs={{0,1},{1,0},{2,3},{3,2},{4,5},{5,4},{6,7},{7,6},{8,9},{9,8},{10,11... | collective-permute-start | bytes 196616 | tf_op jit(solution)/shard_map/ppermute | solution.py:297
  76.0 8.7 %collective-permute-start.14 = (f32[512,128]{1,0:T(8,128)S(1)}, f32[512,128]{1,0:T(8,128)S(1)}, u32[]{:S(2)}, u32[]{:S(2)}) collective-permute-start(f32[512,128]{1,0:T(8,128)S(1)} %add.59), channel_id=1, source_target_pairs={{0,16},{8,24},{16,0},{24,8},{1,17},{9,25},{17,1},{25,9},{2,18},{10... | collective-permute-start | bytes 786440 | tf_op jit(solution)/shard_map/ppermute | solution.py:303
  77.7 8.5 %collective-permute-start.16 = (f32[512,128]{1,0:T(8,128)S(1)}, f32[512,128]{1,0:T(8,128)S(1)}, u32[]{:S(2)}, u32[]{:S(2)}) collective-permute-start(f32[512,128]{1,0:T(8,128)S(1)} %add.61), channel_id=1, source_target_pairs={{0,8},{8,0},{16,24},{24,16},{1,9},{9,1},{17,25},{25,17},{2,10},{10... | collective-permute-start | bytes 786440 | tf_op jit(solution)/shard_map/ppermute | solution.py:303

commit v4 on v3

v4 whole, which is shorter than its diff:
```python
import functools

import jax
import jax.numpy as jnp
from jax import lax
from jax.experimental import pallas as pl
from jax.experimental.pallas import tpu as pltpu
from jax.sharding import PartitionSpec as P

HIGH = lax.Precision.HIGHEST
F32 = jnp.float32
BF16 = jnp.bfloat16
EDGE = 128
GROUP = 8
QUAD = 4
RING = 128
ACC_BYTES = 12 << 20
GELU_C = 0.7978845608028654
GELU_K = 0.044715


def inv_column(deg_ref, start):
    row = lax.rsqrt(deg_ref[pl.ds(start, 1), :].astype(F32))
    return jnp.transpose(jnp.broadcast_to(row, (EDGE, EDGE)))


def split(value):
    hi = value.astype(BF16)
    return hi, (value - hi.astype(F32)).astype(BF16)


def fetch(pairs, sems):
    copies = [pltpu.make_async_copy(src, dst, sems.at[i]) for i, (src, dst) in enumerate(pairs)]
    for copy in copies:
        copy.start()
    return copies


def halve(value, size):
    if size & (size - 1) == 0:
        shift = size.bit_length() - 1
        return lax.shift_right_logical(value, shift), value & (size - 1)
    return lax.div(value, size), lax.rem(value, size)


def forward_kernel(
    first_unit, n_panels, node_dev,
    rows_ref, cols_ref, live_ref, deg_ref, feat_ref, blocks_ref, *refs,
):
    keep_ref, send_ref, dense_ref = refs[-13:-10]
    acc, both, ring, scaled, result, slot_list, place_list, in_sems, dense_sems, out_sems = refs[-10:]
    slots = rows_ref.shape[2]
    col_nodes, width = feat_ref.shape
    col_blocks = col_nodes // EDGE
    dev_blocks = node_dev // EDGE
    panel_dev = both.shape[0]
    panel_units = panel_dev // 2
    positions = panel_dev * dev_blocks * col_blocks
    quads = ring.shape[0] // QUAD
    me = lax.axis_index("col")
    live = live_ref[0, 0]

    def block_copy(i, u):
        at = lax.rem(i, quads)
        return pltpu.make_async_copy(
            blocks_ref.at[0, 0, slot_list[i * QUAD + u]], ring.at[at * QUAD + u], in_sems.at[at])

    def start_quad(i):
        for u in range(QUAD):
            block_copy(i, u).start()

    def dense_copy(panel, j):
        there = pl.ds((panel * panel_dev + j) * node_dev, node_dev)
        return pltpu.make_async_copy(
            both.at[j, pl.ds(0, node_dev)], dense_ref.at[there], dense_sems.at[j])

    def result_copy(panel, j):
        ref = send_ref if j % 2 else keep_ref
        return pltpu.make_async_copy(
            result.at[j], ref.at[panel * panel_units + j // 2], out_sems.at[j])

    def do_panel(panel):
        base = first_unit + panel * panel_units

        def scan(g, count):
            for u in range(GROUP):
                s = g * GROUP + u
                dev, inner = halve(rows_ref[0, 0, s], dev_blocks)
                rel = (dev ^ me) - 2 * base
                hit = (rel >= 0) & (rel < panel_dev) & (s < live)
                slot_list[count] = s
                place_list[count] = (rel * dev_blocks + inner) * col_blocks + cols_ref[0, 0, s]
                count = count + jnp.where(hit, 1, 0)
            return count

        count = lax.fori_loop(0, slots // GROUP, scan, 0)
        for u in range(QUAD - 1):
            slot_list[count + u] = 0
            place_list[count + u] = positions
        n_quads = lax.shift_right_logical(count + (QUAD - 1), QUAD.bit_length() - 1)

        @pl.loop(0, jnp.minimum(n_quads, quads))
        def _(i):
            start_quad(i)

        @pl.when(panel == 0)
        def _():
            for k in range(col_blocks):
                inv = inv_column(deg_ref, me * col_blocks + k)
                span = pl.ds(k * EDGE, EDGE)
                scaled[span, :] = (inv * feat_ref[span, :].astype(F32)).astype(BF16)

        @pl.loop(0, positions // 4)
        def _(p):
            for u in range(4):
                acc[p * 4 + u] = jnp.zeros((EDGE, EDGE), F32)

        @pl.loop(0, n_quads)
        def _(i):
            at = lax.rem(i, quads) * QUAD
            for u in range(QUAD):
                block_copy(i, u).wait()
            for u in range(0, QUAD, 2):
                p0, p1 = place_list[i * QUAD + u], place_list[i * QUAD + u + 1]
                same = jnp.where(p0 == p1, 1.0, 0.0).astype(F32)
                b0, b1 = ring[at + u].astype(F32), ring[at + u + 1].astype(F32)
                a0, a1 = acc[p0], acc[p1]
                acc[p0] = a0 + b0
                acc[p1] = a1 + (b1 + same * b0)

            @pl.when(i + quads < n_quads)
            def _():
                start_quad(i + quads)

        for j in range(panel_dev):
            if n_panels > 1:
                @pl.when(panel > 0)
                def _():
                    dense_copy(panel, j).wait()
                    result_copy(panel, j).wait()
            for b in range(dev_blocks):
                for cb in range(col_blocks):
                    hi, lo = split(acc[(j * dev_blocks + b) * col_blocks + cb])
                    lanes = slice(cb * EDGE, (cb + 1) * EDGE)
                    both[j, b * EDGE:(b + 1) * EDGE, lanes] = hi
                    both[j, node_dev + b * EDGE:node_dev + (b + 1) * EDGE, lanes] = lo
            dense_copy(panel, j).start()
            pair = jnp.dot(both[j], scaled[...], preferred_element_type=F32)
            result[j] = pair[:node_dev] + pair[node_dev:]
            result_copy(panel, j).start()

    if n_panels == 1:
        do_panel(0)
    else:
        @pl.loop(0, n_panels)
        def _(panel):
            do_panel(panel)

    for j in range(panel_dev):
        dense_copy(n_panels - 1, j).wait()
        result_copy(n_panels - 1, j).wait()


def middle_kernel(n_col, n_in, deg_ref, cot_ref, weight_ref, *refs):
    parts = refs[:n_in]
    act_ref, pulled_ref, prop_ref, gprime_ref, stage, sems = refs[n_in:]
    copies = fetch([(ref, stage.at[i]) for i, ref in enumerate(parts)], sems)
    node_dev = cot_ref.shape[0]
    dev_blocks = node_dev // EDGE
    base = (lax.axis_index("row") * n_col + lax.axis_index("col")) * dev_blocks
    inv = jnp.concatenate([inv_column(deg_ref, base + k) for k in range(dev_blocks)], axis=0)
    for copy in copies:
        copy.wait()
    summed = stage[0]
    for i in range(1, n_in):
        summed = summed + stage[i]
    propagated = inv * summed
    prop_ref[...] = propagated
    weight = weight_ref[...]
    pair = jnp.dot(jnp.concatenate(split(propagated), axis=0), weight, preferred_element_type=F32)
    v = pair[:node_dev] + pair[node_dev:]
    t = jnp.tanh(GELU_C * (v + GELU_K * v * v * v))
    act_ref[...] = (0.5 * v * (1.0 + t)).astype(BF16)
    slope = 0.5 * (1.0 + t) + 0.5 * v * (1.0 - t * t) * (GELU_C * (1.0 + 3.0 * GELU_K * v * v))
    gprime = cot_ref[...].astype(F32) * slope
    gprime_ref[...] = gprime
    pair = lax.dot_general(
        jnp.concatenate(split(gprime), axis=0), weight, (((1,), (1,)), ((), ())),
        preferred_element_type=F32,
    )
    pulled_ref[...] = jnp.transpose(inv * (pair[:node_dev] + pair[node_dev:]))


def add_kernel(*refs):
    total = refs[0][...]
    for ref in refs[1:-1]:
        total = total + ref[...]
    refs[-1][...] = total


def weight_kernel(scale, prop_ref, gprime_ref, keep_ref, send_ref):
    part = scale * lax.dot_general(
        prop_ref[...], gprime_ref[...], (((0,), (0,)), ((), ())),
        precision=HIGH, preferred_element_type=F32,
    )
    half = keep_ref.shape[0]
    low = lax.axis_index("col") % 2 == 0
    keep_ref[...] = jnp.where(low, part[:half], part[half:])
    send_ref[...] = jnp.where(low, part[half:], part[:half])


def load_lhs(parts, stage, lhs, copies):
    width = parts[0].shape[0]
    node_dev = parts[0].shape[1]
    for i in range(len(parts)):
        copies[i].wait()
        hi, lo = split(stage[i])
        lhs[:width, i * node_dev:(i + 1) * node_dev] = hi
        lhs[width:, i * node_dev:(i + 1) * node_dev] = lo


def partial_kernel(n_in, spans, *refs):
    n_dense = len(spans)
    tiles, parts = refs[:n_dense], refs[n_dense:n_dense + n_in]
    out_ref, dense, stage, lhs, sems, dense_sems = refs[n_dense + n_in:]
    width, node_dev = parts[0].shape
    col_nodes = dense.shape[1]
    blocks = fetch(
        [(tile, dense.at[pl.ds(at, size)]) for tile, (at, size) in zip(tiles, spans)], dense_sems)
    load_lhs(parts, stage, lhs, fetch([(r, stage.at[i]) for i, r in enumerate(parts)], sems))
    for copy in blocks:
        copy.wait()
    step = 2 * EDGE if col_nodes % (2 * EDGE) == 0 else EDGE
    for n in range(0, col_nodes, step):
        pair = jnp.dot(lhs[...], dense[:, n:n + step], preferred_element_type=F32)
        out_ref[:, n:n + step] = pair[:width] + pair[width:]


def last_kernel(n_in, n_out, deg_ref, dense_ref, sofar_ref, *refs):
    parts, outs = refs[:n_in], refs[n_in:n_in + n_out]
    dense, stage, lhs, sofar, sems, dense_sem, sofar_sem = refs[n_in + n_out:]
    width, node_dev = parts[0].shape
    col_nodes = dense.shape[1]
    block = pltpu.make_async_copy(dense_ref, dense, dense_sem)
    before = pltpu.make_async_copy(sofar_ref, sofar, sofar_sem)
    block.start()
    copies = fetch([(r, stage.at[i]) for i, r in enumerate(parts)], sems)
    before.start()
    load_lhs(parts, stage, lhs, copies)
    block.wait()
    before.wait()
    step = 2 * EDGE if col_nodes % (2 * EDGE) == 0 else EDGE
    size = col_nodes // n_out
    first = lax.axis_index("col") * (col_nodes // EDGE)
    for n in range(0, col_nodes, step):
        pair = jnp.dot(lhs[...], dense[:, n:n + step], preferred_element_type=F32)
        total = sofar[:, n:n + step] + (pair[:width] + pair[width:])
        for at in range(n, n + step, EDGE):
            inv = inv_column(deg_ref, first + at // EDGE)
            out = outs[at // size]
            out[at % size:at % size + EDGE, :] = inv * jnp.transpose(total[:, at - n:at - n + EDGE])


def body(n_row, n_col, features, degrees, block_rows, block_cols, live_slots, blocks, weight, cotangent):
    n_chip = n_col // 2
    chip_bits, row_bits = n_chip.bit_length() - 1, n_row.bit_length() - 1
    assert n_col == 2 << chip_bits and n_row == 1 << row_bits
    node_dev, hidden = cotangent.shape
    col_nodes, width = features.shape
    row_nodes = node_dev * n_col
    nodes = col_nodes * n_col
    slots = blocks.shape[2]
    deg = degrees.reshape(nodes // EDGE, EDGE)
    col_blocks = col_nodes // EDGE
    dev_blocks = node_dev // EDGE
    assert n_chip >= 4
    groups = [(n_chip - 1, 1), (1, n_chip - 2), (0, 1)]
    smem = pl.BlockSpec(memory_space=pltpu.SMEM)
    any_space = pl.BlockSpec(memory_space=pl.ANY)
    hbm = pl.BlockSpec(memory_space=pltpu.HBM)
    vmem = pl.BlockSpec(memory_space=pltpu.VMEM)

    def params(mib):
        return pltpu.CompilerParams(vmem_limit_bytes=mib << 20)

    def cost(flops, read):
        return pl.CostEstimate(flops=flops, bytes_accessed=read, transcendentals=0)

    def forward(first, units, after):
        panel = units
        while units % panel or 2 * panel * node_dev * col_nodes * 4 > ACC_BYTES:
            panel -= 1
        devs = 2 * panel
        return pl.pallas_call(
            functools.partial(forward_kernel, first, units // panel, node_dev),
            out_shape=(
                jax.ShapeDtypeStruct((units, node_dev, width), F32),
                jax.ShapeDtypeStruct((units, node_dev, width), F32),
                jax.ShapeDtypeStruct((units * 2 * node_dev, col_nodes), BF16),
            ),
            in_specs=[smem, smem, smem, vmem, vmem, hbm] + [any_space] * len(after),
            out_specs=(any_space, any_space, hbm),
            scratch_shapes=[
                pltpu.VMEM((devs * dev_blocks * col_blocks + 1, EDGE, EDGE), F32),
                pltpu.VMEM((devs, 2 * node_dev, col_nodes), BF16),
                pltpu.VMEM((RING, EDGE, EDGE), BF16),
                pltpu.VMEM((col_nodes, width), BF16),
                pltpu.VMEM((devs, node_dev, width), F32),
                pltpu.SMEM((slots + QUAD,), jnp.int32),
                pltpu.SMEM((slots + QUAD,), jnp.int32),
                pltpu.SemaphoreType.DMA((RING // QUAD,)),
                pltpu.SemaphoreType.DMA((devs,)),
                pltpu.SemaphoreType.DMA((devs,)),
            ],
            compiler_params=params(46 if after else 54),
            cost_estimate=cost(units * node_dev * col_nodes * width * 16, units * 5 << 20),
            name=f"forward_{first}",
        )(block_rows, block_cols, live_slots, deg, features, blocks, *after)

    swap_pairs = [(i, i ^ 1) for i in range(n_col)]

    def swap(x):
        return lax.ppermute(x, "col", swap_pairs)

    def chip_flip(x, bit):
        return lax.ppermute(x, "col", [(i, i ^ (2 << bit)) for i in range(n_col)])

    def row_flip(x, bit):
        return lax.ppermute(x, "row", [(i, i ^ (1 << bit)) for i in range(n_row)])

    def low_bit(m):
        return (m & -m).bit_length() - 1

    def add_up(*terms):
        return pl.pallas_call(
            add_kernel,
            out_shape=jax.ShapeDtypeStruct(terms[0].shape, F32),
            in_specs=[vmem] * len(terms),
            out_specs=vmem,
            compiler_params=params(16),
            cost_estimate=cost(0, 32 << 20),
            name="add_up",
        )(*terms)

    kept, got, arrived, tiles = {}, {}, {}, []

    def unit_sum(m):
        return (add_up(kept[m], *arrived[m]) if m in arrived else kept[m]) + got[m]

    def forward_group(i, after, sends):
        first, units = groups[i]
        loads = [unit_sum(m) for m in sends]
        keep, send, tile = forward(first, units, after)
        moved = [chip_flip(x, low_bit(m)) for x, m in zip(loads, sends)]
        for x, m in zip(moved, sends):
            arrived.setdefault(m & (m - 1), []).append(x)
        tiles.append(tile)
        for j in range(units):
            kept[first + j], got[first + j] = keep[j], swap(send[j])

    forward_group(0, [], [])
    last = n_chip - 1
    forward_group(1, [unit_sum(last)], [last])
    for m in range(last - 1, 2, -1):
        arrived.setdefault(m & (m - 1), []).append(chip_flip(unit_sum(m), low_bit(m)))
    forward_group(2, [unit_sum(1)], [2, 1])
    parts = [kept[0], got[0], add_up(*arrived[0])]

    out_act, pulled, prop, gprime = pl.pallas_call(
        functools.partial(middle_kernel, n_col, len(parts)),
        out_shape=(
            jax.ShapeDtypeStruct((node_dev, hidden), BF16),
            jax.ShapeDtypeStruct((width, node_dev), F32),
            jax.ShapeDtypeStruct((node_dev, width), F32),
            jax.ShapeDtypeStruct((node_dev, hidden), F32),
        ),
        in_specs=[vmem] * 3 + [any_space] * len(parts),
        out_specs=(vmem,) * 4,
        scratch_shapes=[
            pltpu.VMEM((len(parts), node_dev, width), F32),
            pltpu.SemaphoreType.DMA((len(parts),)),
        ],
        compiler_params=params(16),
        name="middle",
    )(deg, cotangent, weight, *parts)

    own = {0: pulled}
    for m in (1, 2):
        own[m] = chip_flip(pulled, low_bit(m))
    other = {0: swap(pulled)}
    half = width // 2
    wkeep, wsend = pl.pallas_call(
        functools.partial(weight_kernel, float(nodes) ** (-0.5)),
        out_shape=(jax.ShapeDtypeStruct((half, hidden), F32),) * 2,
        in_specs=[vmem] * 2,
        out_specs=(vmem,) * 2,
        compiler_params=params(16),
        name="weight_part",
    )(prop, gprime)

    wsum = wkeep + swap(wsend)
    for m in range(3, n_chip):
        own[m] = chip_flip(own[m & (m - 1)], low_bit(m))
    for m in range(1, n_chip):
        other[m] = swap(own[m])
    wsum = wsum + row_flip(wsum, 0)
    for t in range(1, row_bits):
        wsum = wsum + row_flip(wsum, t)

    early = [x for m in range(n_chip - 1) for x in (own[m], other[m])]
    late = [own[n_chip - 1], other[n_chip - 1]]
    spans = [(0, 2 * node_dev), (2 * node_dev, (n_chip - 2) * 2 * node_dev)]
    tile_mib = row_nodes * col_nodes * 2 >> 20
    sofar = pl.pallas_call(
        functools.partial(partial_kernel, len(early), spans),
        out_shape=jax.ShapeDtypeStruct((width, col_nodes), F32),
        in_specs=[hbm] * 2 + [any_space] * len(early),
        out_specs=vmem,
        scratch_shapes=[
            pltpu.VMEM((len(early) * node_dev, col_nodes), BF16),
            pltpu.VMEM((len(early), width, node_dev), F32),
            pltpu.VMEM((2 * width, len(early) * node_dev), BF16),
            pltpu.SemaphoreType.DMA((len(early),)),
            pltpu.SemaphoreType.DMA((2,)),
        ],
        compiler_params=params(tile_mib + 20),
        name="backward_early",
    )(tiles[2], tiles[1], *early)

    n_piece = max(1, row_bits)
    while col_nodes % (EDGE * n_piece):
        n_piece -= 1
    size = col_nodes // n_piece
    done = pl.pallas_call(
        functools.partial(last_kernel, len(late), n_piece),
        out_shape=(jax.ShapeDtypeStruct((size, width), F32),) * n_piece,
        in_specs=[vmem, hbm, any_space] + [any_space] * len(late),
        out_specs=(vmem,) * n_piece,
        scratch_shapes=[
            pltpu.VMEM((len(late) * node_dev, col_nodes), BF16),
            pltpu.VMEM((len(late), width, node_dev), F32),
            pltpu.VMEM((2 * width, len(late) * node_dev), BF16),
            pltpu.VMEM((width, col_nodes), F32),
            pltpu.SemaphoreType.DMA((len(late),)),
            pltpu.SemaphoreType.DMA,
            pltpu.SemaphoreType.DMA,
        ],
        compiler_params=params(16),
        name="backward_late",
    )(deg, tiles[0], sofar, *late)

    for t in range(row_bits):
        done = [x + row_flip(x, (i + t) % row_bits) for i, x in enumerate(done)]
        if t == 0:
            for bit in range(chip_bits):
                wsum = wsum + chip_flip(wsum, bit)
    feat_grad = jnp.concatenate(done, axis=0) if n_piece > 1 else done[0]

    wother = swap(wsum)
    low = lax.axis_index("col") % 2 == 0
    weight_grad = jnp.concatenate(
        [jnp.where(low, wsum, wother), jnp.where(low, wother, wsum)], axis=0
    )
    return out_act, feat_grad, weight_grad


def solution(mesh):
    n_row, n_col = mesh.shape["row"], mesh.shape["col"]
    return jax.shard_map(
        functools.partial(body, n_row, n_col),
        mesh=mesh,
        in_specs=(
            P("col", None),
            P(),
            P("row", "col", None),
            P("row", "col", None),
            P("row", "col"),
            P("row", "col", None, None, None),
            P(),
            P(("row", "col"), None),
        ),
        out_specs=(P(("row", "col"), None), P("col", None), P()),
        check_vma=False,
    )
```

time: 87.3 us -> 96.7 us (1.11)
  Pallas kernels: 16.7 us -> 31.9 us
  local copies, waits for them, and re-layouts: 3.09 us -> 0.06 us
  waiting for transfers between devices: 41.9 us -> 39.6 us
  other arithmetic: 4.45 us -> 2.62 us
  starting transfers between devices: 19.4 us -> 20.4 us
    pallas_call x3 -> x7, Pallas kernels: 15.2 us -> 29.8 us  [the longest x3 26.2 us: forward(): pl.pallas_call(functools.partial(forward_kernel, first, units // panel, n...]
    ppermute x8, waiting for transfers between devices: 27.4 us -> 22.9 us  [chip_flip(): return lax.ppermute(x, 'col', [(i, i ^ 2 << bit) for i in range(n_col)])]
    unnamed x10 -> x14, local copies, waits for them, and re-layouts: 3.09 us -> 0.03 us
    add x5 -> x6, other arithmetic: 2.8 us -> 0.98 us  [the longest x3 0.96 us: unit_sum(): return (add_up(kept[m], *arrived[m]) if m in arrived else kept[m]) + got[m]]
    ppermute x9 -> x10, waiting for transfers between devices: 1.14 us -> 2.58 us  [swap(): return lax.ppermute(x, 'col', swap_pairs)]
  transfers between devices with their start and end apart: 23 -> 24, of which waited for: 13 -> 12; matrix products, arithmetic and copies ran while one was open for 4% -> 1% of each run, Pallas kernels for 3% -> 11%
where the time goes in v4:
time: 96.7 us; the launch traced here: 96.2 us
  waiting for transfers between devices  39.6 us (41%)
  Pallas kernels  31.9 us (33%)
  starting transfers between devices  20.4 us (21%)
  other arithmetic  2.62 us (3%)
  between operations  1.67 us (2%)
    pallas_call x3, Pallas kernels, forward(): pl.pallas_call(functools.partial(forward_kernel, first, units // panel, n...  26.2 us
    ppermute x8, waiting for transfers between devices, chip_flip(): return lax.ppermute(x, 'col', [(i, i ^ 2 << bit) for i in range(n_col)])  22.9 us
    ppermute x6, waiting for transfers between devices, row_flip(): return lax.ppermute(x, 'row', [(i, i ^ 1 << bit) for i in range(n_row)])  14.2 us
    ppermute x8, starting transfers between devices, chip_flip(): return lax.ppermute(x, 'col', [(i, i ^ 2 << bit) for i in range(n_col)])  10.7 us
    ppermute x6, starting transfers between devices, row_flip(): return lax.ppermute(x, 'row', [(i, i ^ 1 << bit) for i in range(n_row)])  7.88 us
    ppermute x10, waiting for transfers between devices, swap(): return lax.ppermute(x, 'col', swap_pairs)  2.58 us
    pallas_call x1, Pallas kernels, body(): pl.pallas_call(functools.partial(partial_kernel, len(early), spans), out_...  2.39 us
  transfers between devices with their start and end apart: 24, of which 12 were waited for; matrix products, arithmetic and copies ran while one was open for 1% of the time, Pallas kernels for 11%

profile of v4, /device:TPU:0, one launch (start us, length us, event | category | flops | bytes accessed | tf_op | source)
XLA Modules:
  0.0 96.2 jit_solution(10894117111282402995)
XLA Ops:
  1.4 7.5 %forward_3.1 = (f32[1,256,128]{2,1,0:T(8,128)}, f32[1,256,128]{2,1,0:T(8,128)}, bf16[512,1024]{1,0:T(8,128)(2,1)}) custom-call(s32[1,1,384]{2,1,0:T(1,128)} %rows_ref.5, s32[1,1,384]{2,1,0:T(1,128)} %cols_ref.5, s32[1,1]{1,0:T(1,128)S(6)} %copy.11.live_ref, s32[64,128]{1,0:T(8,128)} %bitcast.14, bf16[1024,128]{1,0:T(8,128)(2,1)} %feat_ref.5, ...), custom_call_target="tpu_custom_call" | custom-call | flops 536870912 | bytes 5242880 | tf_op jit(solution)/shard_map/forward_3/pallas_call | solution.py:294
  9.0 1.5 %collective-permute-done = f32[256,128]{1,0:T(8,128)S(1)} collective-permute-done((f32[256,128]{1,0:T(8,128)}, f32[256,128]{1,0:T(8,128)S(1)}, u32[]{:S(2)}, u32[]{:S(2)}) %collective-permute-start) | collective-permute-done | bytes 131104 | tf_op jit(solution)/shard_map/ppermute | solution.py:323
  10.5 0.9 bitcast_add_fusion.1.refs_0_
  11.5 11.2 %forward_1.1 = (f32[2,256,128]{2,1,0:T(8,128)S(1)}, f32[2,256,128]{2,1,0:T(8,128)S(1)}, bf16[1024,1024]{1,0:T(8,128)(2,1)S(1)}) custom-call(s32[1,1,384]{2,1,0:T(1,128)S(1)} %copy-done.5, s32[1,1,384]{2,1,0:T(1,128)S(1)} %copy-done.6, s32[1,1]{1,0:T(1,128)S(6)} %copy.11.live_ref, s32[64,128]{1,0:T(8,128)S(1)} %bitcast.15, bf16[1024,128]{1,0:T(8,128)(2,1)S(1)} %copy-done, ...), custom_call_target="tpu_custom_call" | custom-call | flops 1073741824 | bytes 10485760 | tf_op jit(solution)/shard_map/forward_1/pallas_call | solution.py:294
  22.7 1.4 %collective-permute-start.3 = (f32[256,128]{1,0:T(8,128)S(1)}, f32[256,128]{1,0:T(8,128)S(1)}, u32[]{:S(2)}, u32[]{:S(2)}) collective-permute-start(f32[256,128]{1,0:T(8,128)S(1)} %bitcast_add_fusion.1.refs_0_), channel_id=1, source_target_pairs={{0,2},{1,3},{2,0},{3,1},{4,6},{5,7},{6,4},{7,5},{8,10},{9,11},{10,... | collective-permute-start | bytes 393224 | tf_op jit(solution)/shard_map/ppermute | solution.py:326
  24.3 0.5 collective-permute-start.1
  24.8 1.0 %collective-permute-done.1 = f32[256,128]{1,0:T(8,128)S(1)} collective-permute-done((f32[256,128]{1,0:T(8,128)S(1)}, f32[256,128]{1,0:T(8,128)S(1)}, u32[]{:S(2)}, u32[]{:S(2)}) %collective-permute-start.1) | collective-permute-done | bytes 131104 | tf_op jit(solution)/shard_map/ppermute | solution.py:323
  25.8 0.7 collective-permute-start.6
  26.5 1.2 %collective-permute-done.3.refs_1_ = f32[256,128]{1,0:T(8,128)S(1)} collective-permute-done((f32[256,128]{1,0:T(8,128)S(1)}, f32[256,128]{1,0:T(8,128)S(1)}, u32[]{:S(2)}, u32[]{:S(2)}) %collective-permute-start.3) | collective-permute-done | bytes 131104 | tf_op jit(solution)/shard_map/ppermute | solution.py:326
  27.8 7.5 %forward_0.1 = (f32[1,256,128]{2,1,0:T(8,128)S(1)}, f32[1,256,128]{2,1,0:T(8,128)S(1)}, bf16[512,1024]{1,0:T(8,128)(2,1)S(1)}) custom-call(s32[1,1,384]{2,1,0:T(1,128)S(1)} %copy-done.5, s32[1,1,384]{2,1,0:T(1,128)S(1)} %copy-done.6, s32[1,1]{1,0:T(1,128)S(6)} %copy.11.live_ref, s32[64,128]{1,0:T(8,128)S(1)} %bitcast.16, bf16[1024,128]{1,0:T(8,128)(2,1)S(1)} %copy-done, ...), custom_call_target="tpu_custom_call" | custom-call | flops 536870912 | bytes 5242880 | tf_op jit(solution)/shard_map/forward_0/pallas_call | solution.py:294
  35.3 4.0 %collective-permute-start.5 = (f32[256,128]{1,0:T(8,128)S(1)}, f32[256,128]{1,0:T(8,128)S(1)}, u32[]{:S(2)}, u32[]{:S(2)}) collective-permute-start(f32[256,128]{1,0:T(8,128)S(1)} %add.44), channel_id=1, source_target_pairs={{0,4},{1,5},{2,6},{3,7},{4,0},{5,1},{6,2},{7,3},{8,12},{9,13},{10,... | collective-permute-start | bytes 393224 | tf_op jit(solution)/shard_map/ppermute | solution.py:326
  39.3 5.3 %collective-permute-done.5.refs_0_ = f32[256,128]{1,0:T(8,128)S(1)} collective-permute-done((f32[256,128]{1,0:T(8,128)S(1)}, f32[256,128]{1,0:T(8,128)S(1)}, u32[]{:S(2)}, u32[]{:S(2)}) %collective-permute-start.5) | collective-permute-done | bytes 131104 | tf_op jit(solution)/shard_map/ppermute | solution.py:326
  44.7 1.8 %middle.1 = (bf16[256,256]{1,0:T(8,128)(2,1)}, f32[128,256]{1,0:T(8,128)S(1)}, f32[256,128]{1,0:T(8,128)S(1)}, f32[256,256]{1,0:T(8,128)S(1)}) custom-call(s32[64,128]{1,0:T(8,128)S(1)} %bitcast.17, bf16[256,256]{1,0:T(8,128)(2,1)S(1)} %copy-done.3, bf16[128,256]{1,0:T(8,128)(2,1)S(1)} %copy-done.4, f32[256,128]{1,0:T(8,128)S(1)} %bitcast.19, ...), custom_call_target="tpu_custom_call" | custom-call | tf_op jit(solution)/shard_map/middle/pallas_call | solution.py:369
  46.4 0.7 collective-permute-start.10
  47.2 2.7 %collective-permute-start.8 = (f32[128,256]{1,0:T(8,128)S(1)}, f32[128,256]{1,0:T(8,128)S(1)}, u32[]{:S(2)}, u32[]{:S(2)}) collective-permute-start(f32[128,256]{1,0:T(8,128)S(1)} %get-tuple-element.30.refs_2_), channel_id=1, source_target_pairs={{0,2},{1,3},{2,0},{3,1},{4,6},{5,7},{6,4},{7,5},{8,10},{9,11},{10,... | collective-permute-start | bytes 393224 | tf_op jit(solution)/shard_map/ppermute | solution.py:326
  49.8 4.1 %collective-permute-done.10.refs_6_ = f32[128,256]{1,0:T(8,128)S(1)} collective-permute-done((f32[128,256]{1,0:T(8,128)S(1)}, f32[128,256]{1,0:T(8,128)S(1)}, u32[]{:S(2)}, u32[]{:S(2)}) %collective-permute-start.10) | collective-permute-done | bytes 131104 | tf_op jit(solution)/shard_map/ppermute | solution.py:326
  54.6 0.5 collective-permute-start.7
  55.6 3.3 %collective-permute-done.12.refs_0_ = f32[128,256]{1,0:T(8,128)S(1)} collective-permute-done((f32[128,256]{1,0:T(8,128)S(1)}, f32[128,256]{1,0:T(8,128)S(1)}, u32[]{:S(2)}, u32[]{:S(2)}) %collective-permute-start.12) | collective-permute-done | bytes 131104 | tf_op jit(solution)/shard_map/ppermute | solution.py:326
  58.9 0.4 collective-permute-start.19
  59.4 4.1 %collective-permute-done.19 = f32[64,256]{1,0:T(8,128)S(1)} collective-permute-done((f32[64,256]{1,0:T(8,128)S(1)}, f32[64,256]{1,0:T(8,128)S(1)}, u32[]{:S(2)}, u32[]{:S(2)}) %collective-permute-start.19) | collective-permute-done | bytes 65568 | tf_op jit(solution)/shard_map/ppermute | solution.py:329
  63.5 2.4 %backward_early.1.sofar_ref = f32[128,1024]{1,0:T(8,128)S(1)} custom-call(bf16[512,1024]{1,0:T(8,128)(2,1)S(1)} %get-tuple-element.28.refs_0_, bf16[1024,1024]{1,0:T(8,128)(2,1)S(1)} %get-tuple-element.29.refs_1_, f32[128,256]{1,0:T(8,128)S(1)} %get-tuple-element.30.refs_2_, f32[128,256]{1,0:T(8,128)S(1)} %collective-permute-done.7.refs_3_, ...), custom_call_target="tpu_custom_call" | custom-call | tf_op jit(solution)/shard_map/backward_early/pallas_call | solution.py:414
  65.9 1.1 %backward_late.1 = (f32[512,128]{1,0:T(8,128)S(1)}, f32[512,128]{1,0:T(8,128)S(1)}) custom-call(s32[64,128]{1,0:T(8,128)S(1)} %bitcast.18, bf16[512,1024]{1,0:T(8,128)(2,1)S(1)} %copy-done.1, f32[128,1024]{1,0:T(8,128)S(1)} %backward_early.1.sofar_ref, f32[128,256]{1,0:T(8,128)S(1)} %collective-permute-done.12.refs_0_, ...), custom_call_target="tpu_custom_call" | custom-call | tf_op jit(solution)/shard_map/backward_late/pallas_call | solution.py:434
  67.5 4.1 %collective-permute-start.20 = (f32[64,256]{1,0:T(8,128)S(1)}, f32[64,256]{1,0:T(8,128)S(1)}, u32[]{:S(2)}, u32[]{:S(2)}) collective-permute-start(f32[64,256]{1,0:T(8,128)S(1)} %add.51), channel_id=1, source_target_pairs={{0,16},{8,24},{16,0},{24,8},{1,17},{9,25},{17,1},{25,9},{2,18},{10... | collective-permute-start | bytes 196616 | tf_op jit(solution)/shard_map/ppermute | solution.py:329
  71.7 2.7 %collective-permute-done.20 = f32[64,256]{1,0:T(8,128)S(1)} collective-permute-done((f32[64,256]{1,0:T(8,128)S(1)}, f32[64,256]{1,0:T(8,128)S(1)}, u32[]{:S(2)}, u32[]{:S(2)}) %collective-permute-start.20) | collective-permute-done | bytes 65568 | tf_op jit(solution)/shard_map/ppermute | solution.py:329
  74.6 4.1 %collective-permute-done.21 = f32[64,256]{1,0:T(8,128)S(1)} collective-permute-done((f32[64,256]{1,0:T(8,128)S(1)}, f32[64,256]{1,0:T(8,128)S(1)}, u32[]{:S(2)}, u32[]{:S(2)}) %collective-permute-start.21) | collective-permute-done | bytes 65568 | tf_op jit(solution)/shard_map/ppermute | solution.py:326
  78.7 0.6 collective-permute-start.22
  79.3 5.0 %collective-permute-done.22 = f32[64,256]{1,0:T(8,128)S(1)} collective-permute-done((f32[64,256]{1,0:T(8,128)S(1)}, f32[64,256]{1,0:T(8,128)S(1)}, u32[]{:S(2)}, u32[]{:S(2)}) %collective-permute-start.22) | collective-permute-done | bytes 65568 | tf_op jit(solution)/shard_map/ppermute | solution.py:326
  84.4 2.4 %collective-permute-start.15 = (f32[512,128]{1,0:T(8,128)S(1)}, f32[512,128]{1,0:T(8,128)S(1)}, u32[]{:S(2)}, u32[]{:S(2)}) collective-permute-start(f32[512,128]{1,0:T(8,128)S(1)} %add.45), channel_id=1, source_target_pairs={{0,16},{8,24},{16,0},{24,8},{1,17},{9,25},{17,1},{25,9},{2,18},{10... | collective-permute-start | bytes 786440 | tf_op jit(solution)/shard_map/ppermute | solution.py:329
  87.3 0.7 pad_maximum_fusion.1
  88.0 5.8 %collective-permute-done.15 = f32[512,128]{1,0:T(8,128)S(1)} collective-permute-done((f32[512,128]{1,0:T(8,128)S(1)}, f32[512,128]{1,0:T(8,128)S(1)}, u32[]{:S(2)}, u32[]{:S(2)}) %collective-permute-start.15) | collective-permute-done | bytes 262176 | tf_op jit(solution)/shard_map/ppermute | solution.py:329
  93.8 1.5 %collective-permute-done.17 = f32[512,128]{1,0:T(8,128)S(1)} collective-permute-done((f32[512,128]{1,0:T(8,128)S(1)}, f32[512,128]{1,0:T(8,128)S(1)}, u32[]{:S(2)}, u32[]{:S(2)}) %collective-permute-start.17) | collective-permute-done | bytes 262176 | tf_op jit(solution)/shard_map/ppermute | solution.py:329
  95.4 0.8 pad_maximum_fusion
  (56 shorter events, 2.9 us)
Async XLA Ops:
  0.6 10.8 %copy-start.2 = (s32[8192]{0:T(1024)S(1)}, s32[8192]{0:T(1024)}, u32[]{:S(2)}) copy-start(s32[8192]{0:T(1024)} %param.9) | copy-start | bytes 98308
  0.6 10.8 %copy-start.5 = (s32[1,1,384]{2,1,0:T(1,128)S(1)}, s32[1,1,384]{2,1,0:T(1,128)}, u32[]{:S(2)}) copy-start(s32[1,1,384]{2,1,0:T(1,128)} %rows_ref.5) | copy-start | bytes 4612
  0.7 10.8 %copy-start.6 = (s32[1,1,384]{2,1,0:T(1,128)S(1)}, s32[1,1,384]{2,1,0:T(1,128)}, u32[]{:S(2)}) copy-start(s32[1,1,384]{2,1,0:T(1,128)} %cols_ref.5) | copy-start | bytes 4612
  0.7 10.8 %copy-start = (bf16[1024,128]{1,0:T(8,128)(2,1)S(1)}, bf16[1024,128]{1,0:T(8,128)(2,1)}, u32[]{:S(2)}) copy-start(bf16[1024,128]{1,0:T(8,128)(2,1)} %feat_ref.5) | copy-start | bytes 786436
  8.9 1.6 %collective-permute-start = (f32[256,128]{1,0:T(8,128)}, f32[256,128]{1,0:T(8,128)S(1)}, u32[]{:S(2)}, u32[]{:S(2)}) collective-permute-start(f32[256,128]{1,0:T(8,128)} %bitcast.21), channel_id=1, source_target_pairs={{0,1},{1,0},{2,3},{3,2},{4,5},{5,4},{6,7},{7,6},{8,9},{9,8},{10,11... | collective-permute-start | bytes 393224 | tf_op jit(solution)/shard_map/ppermute | solution.py:323
  11.5 33.2 %copy-start.3 = (bf16[256,256]{1,0:T(8,128)(2,1)S(1)}, bf16[256,256]{1,0:T(8,128)(2,1)}, u32[]{:S(2)}) copy-start(bf16[256,256]{1,0:T(8,128)(2,1)} %cot_ref.1) | copy-start | bytes 393220
  11.5 33.2 %copy-start.4 = (bf16[128,256]{1,0:T(8,128)(2,1)S(1)}, bf16[128,256]{1,0:T(8,128)(2,1)}, u32[]{:S(2)}) copy-start(bf16[128,256]{1,0:T(8,128)(2,1)} %weight_ref.1) | copy-start | bytes 196612
  22.7 43.2 %copy-start.1 = (bf16[512,1024]{1,0:T(8,128)(2,1)S(1)}, bf16[512,1024]{1,0:T(8,128)(2,1)}, u32[]{:S(2)}) copy-start(bf16[512,1024]{1,0:T(8,128)(2,1)} %get-tuple-element.27.dense_ref) | copy-start | bytes 3145732
  22.7 5.0 %collective-permute-start.3 = (f32[256,128]{1,0:T(8,128)S(1)}, f32[256,128]{1,0:T(8,128)S(1)}, u32[]{:S(2)}, u32[]{:S(2)}) collective-permute-start(f32[256,128]{1,0:T(8,128)S(1)} %bitcast_add_fusion.1.refs_0_), channel_id=1, source_target_pairs={{0,2},{1,3},{2,0},{3,1},{4,6},{5,7},{6,4},{7,5},{8,10},{9,11},{10,... | collective-permute-start | bytes 393224 | tf_op jit(solution)/shard_map/ppermute | solution.py:326
  24.2 11.1 %collective-permute-start.4 = (f32[256,128]{1,0:T(8,128)S(1)}, f32[256,128]{1,0:T(8,128)S(1)}, u32[]{:S(2)}, u32[]{:S(2)}) collective-permute-start(f32[256,128]{1,0:T(8,128)S(1)} %get-tuple-element.37), channel_id=1, source_target_pairs={{0,1},{1,0},{2,3},{3,2},{4,5},{5,4},{6,7},{7,6},{8,9},{9,8},{10,11... | collective-permute-start | bytes 393224 | tf_op jit(solution)/shard_map/ppermute | solution.py:323
  24.3 1.5 %collective-permute-start.1 = (f32[256,128]{1,0:T(8,128)S(1)}, f32[256,128]{1,0:T(8,128)S(1)}, u32[]{:S(2)}, u32[]{:S(2)}) collective-permute-start(f32[256,128]{1,0:T(8,128)S(1)} %get-tuple-element.38), channel_id=1, source_target_pairs={{0,1},{1,0},{2,3},{3,2},{4,5},{5,4},{6,7},{7,6},{8,9},{9,8},{10,11... | collective-permute-start | bytes 393224 | tf_op jit(solution)/shard_map/ppermute | solution.py:323
  25.8 18.8 %collective-permute-start.6 = (f32[256,128]{1,0:T(8,128)S(1)}, f32[256,128]{1,0:T(8,128)S(1)}, u32[]{:S(2)}, u32[]{:S(2)}) collective-permute-start(f32[256,128]{1,0:T(8,128)S(1)} %bitcast_add_fusion.refs_0_), channel_id=1, source_target_pairs={{0,2},{1,3},{2,0},{3,1},{4,6},{5,7},{6,4},{7,5},{8,10},{9,11},{10,... | collective-permute-start | bytes 393224 | tf_op jit(solution)/shard_map/ppermute | solution.py:326
  35.3 9.3 %collective-permute-start.5 = (f32[256,128]{1,0:T(8,128)S(1)}, f32[256,128]{1,0:T(8,128)S(1)}, u32[]{:S(2)}, u32[]{:S(2)}) collective-permute-start(f32[256,128]{1,0:T(8,128)S(1)} %add.44), channel_id=1, source_target_pairs={{0,4},{1,5},{2,6},{3,7},{4,0},{5,1},{6,2},{7,3},{8,12},{9,13},{10,... | collective-permute-start | bytes 393224 | tf_op jit(solution)/shard_map/ppermute | solution.py:326
  39.3 5.3 %collective-permute-start.2 = (f32[256,128]{1,0:T(8,128)S(1)}, f32[256,128]{1,0:T(8,128)S(1)}, u32[]{:S(2)}, u32[]{:S(2)}) collective-permute-start(f32[256,128]{1,0:T(8,128)S(1)} %bitcast.20), channel_id=1, source_target_pairs={{0,1},{1,0},{2,3},{3,2},{4,5},{5,4},{6,7},{7,6},{8,9},{9,8},{10,11... | collective-permute-start | bytes 393224 | tf_op jit(solution)/shard_map/ppermute | solution.py:323
  46.4 7.5 %collective-permute-start.10 = (f32[128,256]{1,0:T(8,128)S(1)}, f32[128,256]{1,0:T(8,128)S(1)}, u32[]{:S(2)}, u32[]{:S(2)}) collective-permute-start(f32[128,256]{1,0:T(8,128)S(1)} %get-tuple-element.30.refs_2_), channel_id=1, source_target_pairs={{0,4},{1,5},{2,6},{3,7},{4,0},{5,1},{6,2},{7,3},{8,12},{9,13},{10,... | collective-permute-start | bytes 393224 | tf_op jit(solution)/shard_map/ppermute | solution.py:326
  47.2 8.0 %collective-permute-start.8 = (f32[128,256]{1,0:T(8,128)S(1)}, f32[128,256]{1,0:T(8,128)S(1)}, u32[]{:S(2)}, u32[]{:S(2)}) collective-permute-start(f32[128,256]{1,0:T(8,128)S(1)} %get-tuple-element.30.refs_2_), channel_id=1, source_target_pairs={{0,2},{1,3},{2,0},{3,1},{4,6},{5,7},{6,4},{7,5},{8,10},{9,11},{10,... | collective-permute-start | bytes 393224 | tf_op jit(solution)/shard_map/ppermute | solution.py:326
  53.9 5.0 %collective-permute-start.12 = (f32[128,256]{1,0:T(8,128)S(1)}, f32[128,256]{1,0:T(8,128)S(1)}, u32[]{:S(2)}, u32[]{:S(2)}) collective-permute-start(f32[128,256]{1,0:T(8,128)S(1)} %collective-permute-done.10.refs_6_), channel_id=1, source_target_pairs={{0,2},{1,3},{2,0},{3,1},{4,6},{5,7},{6,4},{7,5},{8,10},{9,11},{10,... | collective-permute-start | bytes 393224 | tf_op jit(solution)/shard_map/ppermute | solution.py:326
  54.5 4.3 %collective-permute-start.18 = (f32[64,256]{1,0:T(8,128)S(1)}, f32[64,256]{1,0:T(8,128)S(1)}, u32[]{:S(2)}, u32[]{:S(2)}) collective-permute-start(f32[64,256]{1,0:T(8,128)S(1)} %get-tuple-element.36), channel_id=1, source_target_pairs={{0,1},{1,0},{2,3},{3,2},{4,5},{5,4},{6,7},{7,6},{8,9},{9,8},{10,11... | collective-permute-start | bytes 196616 | tf_op jit(solution)/shard_map/ppermute | solution.py:323
  54.6 8.9 %collective-permute-start.7 = (f32[128,256]{1,0:T(8,128)S(1)}, f32[128,256]{1,0:T(8,128)S(1)}, u32[]{:S(2)}, u32[]{:S(2)}) collective-permute-start(f32[128,256]{1,0:T(8,128)S(1)} %get-tuple-element.30.refs_2_), channel_id=1, source_target_pairs={{0,1},{1,0},{2,3},{3,2},{4,5},{5,4},{6,7},{7,6},{8,9},{9,8},{10,11... | collective-permute-start | bytes 393224 | tf_op jit(solution)/shard_map/ppermute | solution.py:323
  55.1 8.4 %collective-permute-start.11 = (f32[128,256]{1,0:T(8,128)S(1)}, f32[128,256]{1,0:T(8,128)S(1)}, u32[]{:S(2)}, u32[]{:S(2)}) collective-permute-start(f32[128,256]{1,0:T(8,128)S(1)} %collective-permute-done.10.refs_6_), channel_id=1, source_target_pairs={{0,1},{1,0},{2,3},{3,2},{4,5},{5,4},{6,7},{7,6},{8,9},{9,8},{10,11... | collective-permute-start | bytes 393224 | tf_op jit(solution)/shard_map/ppermute | solution.py:323
  55.2 8.3 %collective-permute-start.9 = (f32[128,256]{1,0:T(8,128)S(1)}, f32[128,256]{1,0:T(8,128)S(1)}, u32[]{:S(2)}, u32[]{:S(2)}) collective-permute-start(f32[128,256]{1,0:T(8,128)S(1)} %collective-permute-done.8.refs_4_), channel_id=1, source_target_pairs={{0,1},{1,0},{2,3},{3,2},{4,5},{5,4},{6,7},{7,6},{8,9},{9,8},{10,11... | collective-permute-start | bytes 393224 | tf_op jit(solution)/shard_map/ppermute | solution.py:323
  58.9 7.0 %collective-permute-start.13 = (f32[128,256]{1,0:T(8,128)S(1)}, f32[128,256]{1,0:T(8,128)S(1)}, u32[]{:S(2)}, u32[]{:S(2)}) collective-permute-start(f32[128,256]{1,0:T(8,128)S(1)} %collective-permute-done.12.refs_0_), channel_id=1, source_target_pairs={{0,1},{1,0},{2,3},{3,2},{4,5},{5,4},{6,7},{7,6},{8,9},{9,8},{10,11... | collective-permute-start | bytes 393224 | tf_op jit(solution)/shard_map/ppermute | solution.py:323
  58.9 4.6 %collective-permute-start.19 = (f32[64,256]{1,0:T(8,128)S(1)}, f32[64,256]{1,0:T(8,128)S(1)}, u32[]{:S(2)}, u32[]{:S(2)}) collective-permute-start(f32[64,256]{1,0:T(8,128)S(1)} %add.50), channel_id=1, source_target_pairs={{0,8},{8,0},{16,24},{24,16},{1,9},{9,1},{17,25},{25,17},{2,10},{10... | collective-permute-start | bytes 196616 | tf_op jit(solution)/shard_map/ppermute | solution.py:329
  67.1 17.3 %collective-permute-start.14 = (f32[512,128]{1,0:T(8,128)S(1)}, f32[512,128]{1,0:T(8,128)S(1)}, u32[]{:S(2)}, u32[]{:S(2)}) collective-permute-start(f32[512,128]{1,0:T(8,128)S(1)} %get-tuple-element.31), channel_id=1, source_target_pairs={{0,8},{8,0},{16,24},{24,16},{1,9},{9,1},{17,25},{25,17},{2,10},{10... | collective-permute-start | bytes 786440 | tf_op jit(solution)/shard_map/ppermute | solution.py:329
  67.5 6.8 %collective-permute-start.20 = (f32[64,256]{1,0:T(8,128)S(1)}, f32[64,256]{1,0:T(8,128)S(1)}, u32[]{:S(2)}, u32[]{:S(2)}) collective-permute-start(f32[64,256]{1,0:T(8,128)S(1)} %add.51), channel_id=1, source_target_pairs={{0,16},{8,24},{16,0},{24,8},{1,17},{9,25},{17,1},{25,9},{2,18},{10... | collective-permute-start | bytes 196616 | tf_op jit(solution)/shard_map/ppermute | solution.py:329
  71.6 15.2 %collective-permute-start.16 = (f32[512,128]{1,0:T(8,128)S(1)}, f32[512,128]{1,0:T(8,128)S(1)}, u32[]{:S(2)}, u32[]{:S(2)}) collective-permute-start(f32[512,128]{1,0:T(8,128)S(1)} %get-tuple-element.32), channel_id=1, source_target_pairs={{0,16},{8,24},{16,0},{24,8},{1,17},{9,25},{17,1},{25,9},{2,18},{10... | collective-permute-start | bytes 786440 | tf_op jit(solution)/shard_map/ppermute | solution.py:329
  74.4 4.3 %collective-permute-start.21 = (f32[64,256]{1,0:T(8,128)S(1)}, f32[64,256]{1,0:T(8,128)S(1)}, u32[]{:S(2)}, u32[]{:S(2)}) collective-permute-start(f32[64,256]{1,0:T(8,128)S(1)} %add.52), channel_id=1, source_target_pairs={{0,2},{1,3},{2,0},{3,1},{4,6},{5,7},{6,4},{7,5},{8,10},{9,11},{10,... | collective-permute-start | bytes 196616 | tf_op jit(solution)/shard_map/ppermute | solution.py:326
  78.7 5.6 %collective-permute-start.22 = (f32[64,256]{1,0:T(8,128)S(1)}, f32[64,256]{1,0:T(8,128)S(1)}, u32[]{:S(2)}, u32[]{:S(2)}) collective-permute-start(f32[64,256]{1,0:T(8,128)S(1)} %add.53), channel_id=1, source_target_pairs={{0,4},{1,5},{2,6},{3,7},{4,0},{5,1},{6,2},{7,3},{8,12},{9,13},{10,... | collective-permute-start | bytes 196616 | tf_op jit(solution)/shard_map/ppermute | solution.py:326
  84.3 3.0 %collective-permute-start.23 = (f32[64,256]{1,0:T(8,128)S(1)}, f32[64,256]{1,0:T(8,128)S(1)}, u32[]{:S(2)}, u32[]{:S(2)}) collective-permute-start(f32[64,256]{1,0:T(8,128)S(1)} %add.54), channel_id=1, source_target_pairs={{0,1},{1,0},{2,3},{3,2},{4,5},{5,4},{6,7},{7,6},{8,9},{9,8},{10,11... | collective-permute-start | bytes 196616 | tf_op jit(solution)/shard_map/ppermute | solution.py:323
  84.4 9.4 %collective-permute-start.15 = (f32[512,128]{1,0:T(8,128)S(1)}, f32[512,128]{1,0:T(8,128)S(1)}, u32[]{:S(2)}, u32[]{:S(2)}) collective-permute-start(f32[512,128]{1,0:T(8,128)S(1)} %add.45), channel_id=1, source_target_pairs={{0,16},{8,24},{16,0},{24,8},{1,17},{9,25},{17,1},{25,9},{2,18},{10... | collective-permute-start | bytes 786440 | tf_op jit(solution)/shard_map/ppermute | solution.py:329
  86.9 8.5 %collective-permute-start.17 = (f32[512,128]{1,0:T(8,128)S(1)}, f32[512,128]{1,0:T(8,128)S(1)}, u32[]{:S(2)}, u32[]{:S(2)}) collective-permute-start(f32[512,128]{1,0:T(8,128)S(1)} %add.47), channel_id=1, source_target_pairs={{0,8},{8,0},{16,24},{24,16},{1,9},{9,1},{17,25},{25,17},{2,10},{10... | collective-permute-start | bytes 786440 | tf_op jit(solution)/shard_map/ppermute | solution.py:329

commit v5 on v3

v5 whole, which is shorter than its diff:
```python
import functools

import jax
import jax.numpy as jnp
from jax import lax
from jax.experimental import pallas as pl
from jax.experimental.pallas import tpu as pltpu
from jax.sharding import PartitionSpec as P

HIGH = lax.Precision.HIGHEST
F32 = jnp.float32
BF16 = jnp.bfloat16
EDGE = 128
GROUP = 16
QUARTERS = 4
AHEAD = 2
ACC_BYTES = 8 << 20
GELU_C = 0.7978845608028654
GELU_K = 0.044715


def inv_column(deg_ref, start):
    row = lax.rsqrt(deg_ref[pl.ds(start, 1), :].astype(F32))
    return jnp.transpose(jnp.broadcast_to(row, (EDGE, EDGE)))


def split(value):
    hi = value.astype(BF16)
    return hi, (value - hi.astype(F32)).astype(BF16)


def fetch(pairs, sems):
    copies = [pltpu.make_async_copy(src, dst, sems.at[i]) for i, (src, dst) in enumerate(pairs)]
    for copy in copies:
        copy.start()
    return copies


def halve(value, size):
    if size & (size - 1) == 0:
        shift = size.bit_length() - 1
        return lax.shift_right_logical(value, shift), value & (size - 1)
    return lax.div(value, size), lax.rem(value, size)


def forward_kernel(
    n_col, chunk, panel_dev, node_dev,
    rows_ref, cols_ref, live_ref, deg_ref, feat_ref, blocks_ref, *refs,
):
    outs, dense_ref = refs[:n_col], refs[n_col]
    accs, (both, buf, scaled, result, in_sems, dense_sems, out_sems) = refs[n_col + 1:-7], refs[-7:]
    part = EDGE // len(accs)
    slots = buf.shape[0]
    col_nodes, width = feat_ref.shape
    col_blocks = col_nodes // EDGE
    dev_blocks = node_dev // EDGE
    panel_blocks = panel_dev * dev_blocks
    positions = panel_blocks * col_blocks
    n_panels = n_col // panel_dev
    n_chunks = slots // chunk
    me = lax.axis_index("col")
    live = live_ref[0, 0]

    def block_copy(c):
        span = pl.ds(c * chunk, chunk)
        return pltpu.make_async_copy(blocks_ref.at[0, 0, span], buf.at[span], in_sems.at[c])

    def dense_copy(panel, j):
        there = pl.ds((panel * panel_dev + j) * node_dev, node_dev)
        return pltpu.make_async_copy(
            both.at[j, pl.ds(0, node_dev)], dense_ref.at[there], dense_sems.at[j])

    def result_copy(rel, j):
        return pltpu.make_async_copy(result.at[j], outs[rel], out_sems.at[j])

    for c in range(n_chunks):
        block_copy(c).start()

    for k in range(col_blocks):
        inv = inv_column(deg_ref, me * col_blocks + k)
        span = pl.ds(k * EDGE, EDGE)
        scaled[span, :] = (inv * feat_ref[span, :].astype(F32)).astype(BF16)

    def add_slots(first, place):
        pending = []

        def finish():
            acc, p0, p1, same, a0, a1, b0, b1 = pending.pop(0)
            b0, b1 = b0.astype(F32), b1.astype(F32)
            acc[p0] = a0 + b0
            acc[p1] = a1 + (b1 + same * b0)

        for u in range(0, GROUP, 2):
            s = first + u
            p0, p1 = place(s), place(s + 1)
            same = jnp.where(p0 == p1, 1.0, 0.0).astype(F32)
            for q, acc in enumerate(accs):
                at = slice(q * part, (q + 1) * part)
                pending.append((acc, p0, p1, same, acc[p0], acc[p1], buf[s, at, :], buf[s + 1, at, :]))
                if len(pending) > AHEAD:
                    finish()
        while pending:
            finish()

    for panel in range(n_panels):
        base = panel * panel_blocks

        @pl.loop(0, positions)
        def _(p):
            for acc in accs:
                acc[p] = jnp.zeros((part, EDGE), F32)

        def place(s):
            dev, inner = halve(rows_ref[0, 0, s], dev_blocks)
            r = (dev ^ me) * dev_blocks + inner - base
            ok = s < live
            if n_panels > 1:
                ok = ok & (r >= 0) & (r < panel_blocks)
            return jnp.where(ok, r * col_blocks + cols_ref[0, 0, s], positions)

        @pl.loop(0, n_chunks)
        def _(c):
            if panel == 0:
                block_copy(c).wait()

            @pl.loop(0, chunk // GROUP)
            def _(g):
                add_slots(c * chunk + g * GROUP, place)

        for j in reversed(range(panel_dev)):
            rel = panel * panel_dev + j
            if panel:
                dense_copy(panel - 1, j).wait()
                result_copy(rel - panel_dev, j).wait()
            for b in range(dev_blocks):
                for cb in range(col_blocks):
                    lanes = slice(cb * EDGE, (cb + 1) * EDGE)
                    for q, acc in enumerate(accs):
                        hi, lo = split(acc[(j * dev_blocks + b) * col_blocks + cb])
                        at = b * EDGE + q * part
                        both[j, at:at + part, lanes] = hi
                        both[j, node_dev + at:node_dev + at + part, lanes] = lo
            dense_copy(panel, j).start()
            pair = jnp.dot(both[j], scaled[...], preferred_element_type=F32)
            result[j] = pair[:node_dev] + pair[node_dev:]
            result_copy(rel, j).start()

    for j in range(panel_dev):
        dense_copy(n_panels - 1, j).wait()
        result_copy((n_panels - 1) * panel_dev + j, j).wait()


def middle_kernel(n_col, n_in, deg_ref, cot_ref, weight_ref, *refs):
    parts = refs[:n_in]
    act_ref, pulled_ref, prop_ref, gprime_ref, stage, sems = refs[n_in:]
    copies = fetch([(ref, stage.at[i]) for i, ref in enumerate(parts)], sems)
    node_dev = cot_ref.shape[0]
    dev_blocks = node_dev // EDGE
    base = (lax.axis_index("row") * n_col + lax.axis_index("col")) * dev_blocks
    inv = jnp.concatenate([inv_column(deg_ref, base + k) for k in range(dev_blocks)], axis=0)
    for copy in copies:
        copy.wait()
    summed = stage[0]
    for i in range(1, n_in):
        summed = summed + stage[i]
    propagated = inv * summed
    prop_ref[...] = propagated
    weight = weight_ref[...]
    pair = jnp.dot(jnp.concatenate(split(propagated), axis=0), weight, preferred_element_type=F32)
    v = pair[:node_dev] + pair[node_dev:]
    t = jnp.tanh(GELU_C * (v + GELU_K * v * v * v))
    act_ref[...] = (0.5 * v * (1.0 + t)).astype(BF16)
    slope = 0.5 * (1.0 + t) + 0.5 * v * (1.0 - t * t) * (GELU_C * (1.0 + 3.0 * GELU_K * v * v))
    gprime = cot_ref[...].astype(F32) * slope
    gprime_ref[...] = gprime
    pair = lax.dot_general(
        jnp.concatenate(split(gprime), axis=0), weight, (((1,), (1,)), ((), ())),
        preferred_element_type=F32,
    )
    pulled_ref[...] = jnp.transpose(inv * (pair[:node_dev] + pair[node_dev:]))


def add_kernel(*refs):
    total = refs[0][...]
    for ref in refs[1:-1]:
        total = total + ref[...]
    refs[-1][...] = total


def weight_kernel(scale, prop_ref, gprime_ref, after_ref, keep_ref, send_ref):
    part = scale * lax.dot_general(
        prop_ref[...], gprime_ref[...], (((0,), (0,)), ((), ())),
        precision=HIGH, preferred_element_type=F32,
    )
    half = keep_ref.shape[0]
    low = lax.axis_index("col") % 2 == 0
    keep_ref[...] = jnp.where(low, part[:half], part[half:])
    send_ref[...] = jnp.where(low, part[half:], part[:half])


def load_lhs(parts, stage, lhs, copies):
    width = parts[0].shape[0]
    node_dev = parts[0].shape[1]
    for i in range(len(parts)):
        copies[i].wait()
        hi, lo = split(stage[i])
        lhs[:width, i * node_dev:(i + 1) * node_dev] = hi
        lhs[width:, i * node_dev:(i + 1) * node_dev] = lo


def partial_kernel(n_in, dense_ref, *refs):
    parts, (out_ref, dense, stage, lhs, sems, dense_sems) = refs[:n_in], refs[n_in:]
    width, node_dev = parts[0].shape
    col_nodes = dense.shape[1]
    blocks = fetch(
        [(dense_ref.at[pl.ds(i * node_dev, node_dev)], dense.at[pl.ds(i * node_dev, node_dev)])
         for i in range(n_in)], dense_sems)
    load_lhs(parts, stage, lhs, fetch([(r, stage.at[i]) for i, r in enumerate(parts)], sems))
    for copy in blocks:
        copy.wait()
    step = 2 * EDGE if col_nodes % (2 * EDGE) == 0 else EDGE
    for n in range(0, col_nodes, step):
        pair = jnp.dot(lhs[...], dense[:, n:n + step], preferred_element_type=F32)
        out_ref[:, n:n + step] = pair[:width] + pair[width:]


def last_kernel(n_in, n_out, deg_ref, dense_ref, sofar_ref, wsum_ref, *refs):
    parts, outs = refs[:n_in], refs[n_in:n_in + n_out]
    dense, stage, lhs, sofar, sems, dense_sem, sofar_sem = refs[n_in + n_out:]
    width, node_dev = parts[0].shape
    col_nodes = dense.shape[1]
    rows = n_in * node_dev
    block = pltpu.make_async_copy(
        dense_ref.at[pl.ds(dense_ref.shape[0] - rows, rows)], dense, dense_sem)
    before = pltpu.make_async_copy(sofar_ref, sofar, sofar_sem)
    block.start()
    size = col_nodes // n_out
    lanes = wsum_ref.shape[1] // n_out
    for i, out in enumerate(outs):
        for n in range(0, lanes, EDGE):
            at = size + wsum_ref.shape[0] * (n // EDGE)
            out[at:at + wsum_ref.shape[0], :] = wsum_ref[:, i * lanes + n:i * lanes + n + EDGE]
    copies = fetch([(r, stage.at[i]) for i, r in enumerate(parts)], sems)
    before.start()
    load_lhs(parts, stage, lhs, copies)
    block.wait()
    before.wait()
    step = 2 * EDGE if col_nodes % (2 * EDGE) == 0 else EDGE
    first = lax.axis_index("col") * (col_nodes // EDGE)
    for n in range(0, col_nodes, step):
        pair = jnp.dot(lhs[...], dense[:, n:n + step], preferred_element_type=F32)
        total = sofar[:, n:n + step] + (pair[:width] + pair[width:])
        for at in range(n, n + step, EDGE):
            inv = inv_column(deg_ref, first + at // EDGE)
            out = outs[at // size]
            out[at % size:at % size + EDGE, :] = inv * jnp.transpose(total[:, at - n:at - n + EDGE])


def body(n_row, n_col, features, degrees, block_rows, block_cols, live_slots, blocks, weight, cotangent):
    n_chip = n_col // 2
    chip_bits, row_bits = n_chip.bit_length() - 1, n_row.bit_length() - 1
    assert n_col == 2 << chip_bits and n_row == 1 << row_bits
    node_dev, hidden = cotangent.shape
    col_nodes, width = features.shape
    row_nodes = node_dev * n_col
    nodes = col_nodes * n_col
    slots = blocks.shape[2]
    deg = degrees.reshape(nodes // EDGE, EDGE)
    col_blocks = col_nodes // EDGE
    dev_blocks = node_dev // EDGE
    assert n_chip >= 4
    chunk = 32
    panel_dev = n_col
    while panel_dev % 2 == 0 and panel_dev * node_dev * col_nodes * 4 > ACC_BYTES:
        panel_dev //= 2
    positions = panel_dev * dev_blocks * col_blocks
    smem = pl.BlockSpec(memory_space=pltpu.SMEM)
    any_space = pl.BlockSpec(memory_space=pl.ANY)
    vmem = pl.BlockSpec(memory_space=pltpu.VMEM)

    def params(mib):
        return pltpu.CompilerParams(vmem_limit_bytes=mib << 20)

    def cost(flops, read):
        return pl.CostEstimate(flops=flops, bytes_accessed=read, transcendentals=0)

    *pieces, tile = pl.pallas_call(
        functools.partial(forward_kernel, n_col, chunk, panel_dev, node_dev),
        out_shape=[jax.ShapeDtypeStruct((node_dev, width), F32)] * n_col
        + [jax.ShapeDtypeStruct((row_nodes, col_nodes), BF16)],
        in_specs=[smem, smem, smem, vmem, vmem, any_space],
        out_specs=[any_space] * (n_col + 1),
        scratch_shapes=[
            pltpu.VMEM((positions + 1, EDGE // QUARTERS, EDGE), F32) for _ in range(QUARTERS)
        ] + [
            pltpu.VMEM((panel_dev, 2 * node_dev, col_nodes), BF16),
            pltpu.VMEM((slots, EDGE, EDGE), BF16),
            pltpu.VMEM((col_nodes, width), BF16),
            pltpu.VMEM((panel_dev, node_dev, width), F32),
            pltpu.SemaphoreType.DMA((slots // chunk,)),
            pltpu.SemaphoreType.DMA((panel_dev,)),
            pltpu.SemaphoreType.DMA((panel_dev,)),
        ],
        compiler_params=params(54),
        name="densify_forward",
    )(block_rows, block_cols, live_slots, deg, features, blocks)
    keep, send = pieces[0::2], pieces[1::2]

    swap_pairs = [(i, i ^ 1) for i in range(n_col)]

    def swap(x):
        return lax.ppermute(x, "col", swap_pairs)

    def chip_flip(x, bit):
        return lax.ppermute(x, "col", [(i, i ^ (2 << bit)) for i in range(n_col)])

    def row_flip(x, bit):
        return lax.ppermute(x, "row", [(i, i ^ (1 << bit)) for i in range(n_row)])

    def low_bit(m):
        return (m & -m).bit_length() - 1

    terms = {m: [keep[m], swap(send[m])] for m in range(n_chip - 1, -1, -1)}
    for m in range(n_chip - 1, 0, -1):
        terms[m & (m - 1)].append(chip_flip(functools.reduce(jnp.add, terms[m]), low_bit(m)))
    parts = terms[0]

    out_act, pulled, prop, gprime = pl.pallas_call(
        functools.partial(middle_kernel, n_col, len(parts)),
        out_shape=(
            jax.ShapeDtypeStruct((node_dev, hidden), BF16),
            jax.ShapeDtypeStruct((width, node_dev), F32),
            jax.ShapeDtypeStruct((node_dev, width), F32),
            jax.ShapeDtypeStruct((node_dev, hidden), F32),
        ),
        in_specs=[vmem] * 3 + [any_space] * len(parts),
        out_specs=(vmem,) * 4,
        scratch_shapes=[
            pltpu.VMEM((len(parts), node_dev, width), F32),
            pltpu.SemaphoreType.DMA((len(parts),)),
        ],
        compiler_params=params(16),
        name="middle",
    )(deg, cotangent, weight, *parts)

    own = {0: pulled}
    for m in (1, 2):
        own[m] = chip_flip(pulled, low_bit(m))
    other = {0: swap(pulled)}
    half = width // 2
    wkeep, wsend = pl.pallas_call(
        functools.partial(weight_kernel, float(nodes) ** (-0.5)),
        out_shape=(jax.ShapeDtypeStruct((half, hidden), F32),) * 2,
        in_specs=[vmem] * 2 + [any_space],
        out_specs=(vmem,) * 2,
        compiler_params=params(16),
        name="weight_part",
    )(prop, gprime, other[0])

    wsum = wkeep + swap(wsend)
    for m in range(3, n_chip):
        own[m] = chip_flip(own[m & (m - 1)], low_bit(m))
    for m in range(1, n_chip):
        other[m] = swap(own[m])
    for t in range(chip_bits):
        wsum = wsum + chip_flip(wsum, t)

    early = [x for m in range(n_chip - 1) for x in (own[m], other[m])]
    late = [own[n_chip - 1], other[n_chip - 1]]
    sofar = pl.pallas_call(
        functools.partial(partial_kernel, len(early)),
        out_shape=jax.ShapeDtypeStruct((width, col_nodes), F32),
        in_specs=[any_space] * (1 + len(early)),
        out_specs=vmem,
        scratch_shapes=[
            pltpu.VMEM((len(early) * node_dev, col_nodes), BF16),
            pltpu.VMEM((len(early), width, node_dev), F32),
            pltpu.VMEM((2 * width, len(early) * node_dev), BF16),
            pltpu.SemaphoreType.DMA((len(early),)),
            pltpu.SemaphoreType.DMA((len(early),)),
        ],
        compiler_params=params(52),
        name="backward_early",
    )(tile, *early)

    n_piece = max(1, row_bits)
    while col_nodes % (EDGE * n_piece):
        n_piece -= 1
    size = col_nodes // n_piece
    extra = half * hidden // n_piece // EDGE
    done = pl.pallas_call(
        functools.partial(last_kernel, len(late), n_piece),
        out_shape=(jax.ShapeDtypeStruct((size + extra, width), F32),) * n_piece,
        in_specs=[vmem, any_space, any_space, vmem] + [any_space] * len(late),
        out_specs=(vmem,) * n_piece,
        scratch_shapes=[
            pltpu.VMEM((len(late) * node_dev, col_nodes), BF16),
            pltpu.VMEM((len(late), width, node_dev), F32),
            pltpu.VMEM((2 * width, len(late) * node_dev), BF16),
            pltpu.VMEM((width, col_nodes), F32),
            pltpu.SemaphoreType.DMA((len(late),)),
            pltpu.SemaphoreType.DMA,
            pltpu.SemaphoreType.DMA,
        ],
        compiler_params=params(52),
        name="backward_late",
    )(deg, tile, sofar, wsum, *late)

    for t in range(row_bits):
        done = [x + row_flip(x, (i + t) % row_bits) for i, x in enumerate(done)]
    feat_grad = jnp.concatenate([x[:size] for x in done], axis=0)
    wsum = jnp.concatenate(
        [x[size + i:size + i + half] for x in done for i in range(0, extra, half)], axis=1)

    wother = swap(wsum)
    low = lax.axis_index("col") % 2 == 0
    weight_grad = jnp.concatenate(
        [jnp.where(low, wsum, wother), jnp.where(low, wother, wsum)], axis=0
    )
    return out_act, feat_grad, weight_grad


def solution(mesh):
    n_row, n_col = mesh.shape["row"], mesh.shape["col"]
    return jax.shard_map(
        functools.partial(body, n_row, n_col),
        mesh=mesh,
        in_specs=(
            P("col", None),
            P(),
            P("row", "col", None),
            P("row", "col", None),
            P("row", "col"),
            P("row", "col", None, None, None),
            P(),
            P(("row", "col"), None),
        ),
        out_specs=(P(("row", "col"), None), P("col", None), P()),
        check_vma=False,
    )
```

time: 87.3 us -> 75.7 us (0.87)
  waiting for transfers between devices: 41.9 us -> 29.8 us
  starting transfers between devices: 19.4 us -> 21.6 us
  local copies, waits for them, and re-layouts: 3.09 us -> 0.96 us
    ppermute x8, waiting for transfers between devices: 27.4 us -> 16.9 us  [chip_flip(): return lax.ppermute(x, 'col', [(i, i ^ 2 << bit) for i in range(n_col)])]
    ppermute x8, starting transfers between devices: 11.1 us -> 13.6 us  [chip_flip(): return lax.ppermute(x, 'col', [(i, i ^ 2 << bit) for i in range(n_col)])]
    unnamed x10 -> x8, local copies, waits for them, and re-layouts: 3.09 us -> 0.91 us
    ppermute x6 -> x4, waiting for transfers between devices: 13.3 us -> 11.3 us  [row_flip(): return lax.ppermute(x, 'row', [(i, i ^ 1 << bit) for i in range(n_row)])]
    pallas_call x1, Pallas kernels: 11.7 us -> 10.1 us  [body(): pl.pallas_call(functools.partial(forward_kernel, n_col, chunk, panel_dev,...]
    ppermute x6 -> x4, starting transfers between devices: 6.99 us -> 6.22 us  [row_flip(): return lax.ppermute(x, 'row', [(i, i ^ 1 << bit) for i in range(n_row)])]
    ppermute x9 -> x10, starting transfers between devices: 1.24 us -> 1.77 us  [swap(): return lax.ppermute(x, 'col', swap_pairs)]
  transfers between devices with their start and end apart: 23 -> 22, of which waited for: 13 -> 13; matrix products, arithmetic and copies ran while one was open for 4% -> 5% of each run, Pallas kernels for 3% -> 4%
where the time goes in v5:
time: 75.7 us; the launch traced here: 75.4 us
  waiting for transfers between devices  29.8 us (39%)
  starting transfers between devices  21.6 us (29%)
  Pallas kernels  17.1 us (23%)
  other arithmetic  4.44 us (6%)
  between operations  1.52 us (2%)
  local copies, waits for them, and re-layouts  0.96 us (1%)
    ppermute x8, waiting for transfers between devices, chip_flip(): return lax.ppermute(x, 'col', [(i, i ^ 2 << bit) for i in range(n_col)])  16.9 us
    ppermute x8, starting transfers between devices, chip_flip(): return lax.ppermute(x, 'col', [(i, i ^ 2 << bit) for i in range(n_col)])  13.6 us
    ppermute x4, waiting for transfers between devices, row_flip(): return lax.ppermute(x, 'row', [(i, i ^ 1 << bit) for i in range(n_row)])  11.3 us
    pallas_call x1, Pallas kernels, body(): pl.pallas_call(functools.partial(forward_kernel, n_col, chunk, panel_dev,...  10.1 us
    ppermute x4, starting transfers between devices, row_flip(): return lax.ppermute(x, 'row', [(i, i ^ 1 << bit) for i in range(n_row)])  6.22 us
    pallas_call x1, Pallas kernels, body(): pl.pallas_call(functools.partial(partial_kernel, len(early)), out_shape=j...  2.92 us
    add x3, other arithmetic, body(): functools.reduce(jnp.add, terms[m])  2.77 us
    pallas_call x1, Pallas kernels, body(): pl.pallas_call(functools.partial(middle_kernel, n_col, len(parts)), out_s...  1.91 us
  transfers between devices with their start and end apart: 22, of which 13 were waited for; matrix products, arithmetic and copies ran while one was open for 5% of the time, Pallas kernels for 4%

profile of v5, /device:TPU:0, one launch (start us, length us, event | category | flops | bytes accessed | tf_op | source)
XLA Modules:
  0.0 75.4 jit_solution(10353923070269256939)
XLA Ops:
  1.3 10.1 %densify_forward.1 = (f32[256,128]{1,0:T(8,128)}, f32[256,128]{1,0:T(8,128)}, f32[256,128]{1,0:T(8,128)}, f32[256,128]{1,0:T(8,128)}, f32[256,128]{1,0:T(8,128)}...) custom-call(s32[1,1,384]{2,1,0:T(1,128)} %rows_ref.1, ...), custom_call_target="tpu_custom_call" | custom-call | tf_op jit(solution)/shard_map/densify_forward/pallas_call | solution.py:287
  11.4 0.5 collective-permute-start.2
  12.5 0.7 collective-permute-done.2
  13.2 0.9 %add.38 = f32[256,128]{1,0:T(8,128)S(1)} add(f32[256,128]{1,0:T(8,128)} %get-tuple-element.24, f32[256,128]{1,0:T(8,128)S(1)} %collective-permute-done.2) | non-fusion elementwise | flops 32768 | bytes 393216 | tf_op jit(solution)/shard_map/add | solution.py:325
  14.1 3.0 %collective-permute-start.3 = (f32[256,128]{1,0:T(8,128)S(1)}, f32[256,128]{1,0:T(8,128)S(1)}, u32[]{:S(2)}, u32[]{:S(2)}) collective-permute-start(f32[256,128]{1,0:T(8,128)S(1)} %add.38), channel_id=1, source_target_pairs={{0,2},{1,3},{2,0},{3,1},{4,6},{5,7},{6,4},{7,5},{8,10},{9,11},{10,... | collective-permute-start | bytes 393224 | tf_op jit(solution)/shard_map/ppermute | solution.py:315
  17.1 0.9 %add.40 = f32[256,128]{1,0:T(8,128)S(1)} add(f32[256,128]{1,0:T(8,128)} %get-tuple-element.26, f32[256,128]{1,0:T(8,128)S(1)} %collective-permute-done.5) | non-fusion elementwise | flops 32768 | bytes 393216 | tf_op jit(solution)/shard_map/add | solution.py:325
  18.3 2.6 %collective-permute-done.3 = f32[256,128]{1,0:T(8,128)S(1)} collective-permute-done((f32[256,128]{1,0:T(8,128)S(1)}, f32[256,128]{1,0:T(8,128)S(1)}, u32[]{:S(2)}, u32[]{:S(2)}) %collective-permute-start.3) | collective-permute-done | bytes 131104 | tf_op jit(solution)/shard_map/ppermute | solution.py:315
  20.9 0.9 %add_add_fusion = f32[256,128]{1,0:T(8,128)S(1)} fusion(f32[256,128]{1,0:T(8,128)S(1)} %collective-permute-done.3, f32[256,128]{1,0:T(8,128)} %get-tuple-element.22, f32[256,128]{1,0:T(8,128)S(1)} %collective-permute-done.1), kind=kLoop, calls=%fused_computation.2 | loop fusion | flops 65536 | bytes 524288 | tf_op jit(solution)/shard_map/add | solution.py:325
  21.9 2.8 %collective-permute-start.4 = (f32[256,128]{1,0:T(8,128)S(1)}, f32[256,128]{1,0:T(8,128)S(1)}, u32[]{:S(2)}, u32[]{:S(2)}) collective-permute-start(f32[256,128]{1,0:T(8,128)S(1)} %add_add_fusion), channel_id=1, source_target_pairs={{0,4},{1,5},{2,6},{3,7},{4,0},{5,1},{6,2},{7,3},{8,12},{9,13},{10,... | collective-permute-start | bytes 393224 | tf_op jit(solution)/shard_map/ppermute | solution.py:315
  24.6 6.0 %collective-permute-done.4.refs_2_ = f32[256,128]{1,0:T(8,128)S(1)} collective-permute-done((f32[256,128]{1,0:T(8,128)S(1)}, f32[256,128]{1,0:T(8,128)S(1)}, u32[]{:S(2)}, u32[]{:S(2)}) %collective-permute-start.4) | collective-permute-done | bytes 131104 | tf_op jit(solution)/shard_map/ppermute | solution.py:315
  30.6 0.9 %copy-done.2 = f32[256,128]{1,0:T(8,128)S(1)} copy-done((f32[256,128]{1,0:T(8,128)S(1)}, f32[256,128]{1,0:T(8,128)}, u32[]{:S(2)}) %copy-start.2) | copy-done | bytes 131096
  31.5 1.9 %middle.1 = (bf16[256,256]{1,0:T(8,128)(2,1)}, f32[128,256]{1,0:T(8,128)S(1)}, f32[256,128]{1,0:T(8,128)S(1)}, f32[256,256]{1,0:T(8,128)S(1)}) custom-call(s32[64,128]{1,0:T(8,128)S(1)} %bitcast.2, bf16[256,256]{1,0:T(8,128)(2,1)S(1)} %copy-done.1, bf16[128,256]{1,0:T(8,128)(2,1)S(1)} %copy-done.3, f32[256,128]{1,0:T(8,128)S(1)} %copy-done.2, ...), custom_call_target="tpu_custom_call" | custom-call | tf_op jit(solution)/shard_map/middle/pallas_call | solution.py:328
  33.6 3.8 %collective-permute-start.8 = (f32[128,256]{1,0:T(8,128)S(1)}, f32[128,256]{1,0:T(8,128)S(1)}, u32[]{:S(2)}, u32[]{:S(2)}) collective-permute-start(f32[128,256]{1,0:T(8,128)S(1)} %get-tuple-element.30.refs_0_), channel_id=1, source_target_pairs={{0,2},{1,3},{2,0},{3,1},{4,6},{5,7},{6,4},{7,5},{8,10},{9,11},{10,... | collective-permute-start | bytes 393224 | tf_op jit(solution)/shard_map/ppermute | solution.py:315
  37.4 4.5 %collective-permute-done.10.refs_4_ = f32[128,256]{1,0:T(8,128)S(1)} collective-permute-done((f32[128,256]{1,0:T(8,128)S(1)}, f32[128,256]{1,0:T(8,128)S(1)}, u32[]{:S(2)}, u32[]{:S(2)}) %collective-permute-start.10) | collective-permute-done | bytes 131104 | tf_op jit(solution)/shard_map/ppermute | solution.py:315
  42.3 0.5 collective-permute-start.11
  43.1 0.5 collective-permute-done.12
  43.6 2.1 %collective-permute-start.13 = (f32[64,256]{1,0:T(8,128)S(1)}, f32[64,256]{1,0:T(8,128)S(1)}, u32[]{:S(2)}, u32[]{:S(2)}) collective-permute-start(f32[64,256]{1,0:T(8,128)S(1)} %add.41), channel_id=1, source_target_pairs={{0,2},{1,3},{2,0},{3,1},{4,6},{5,7},{6,4},{7,5},{8,10},{9,11},{10,... | collective-permute-start | bytes 196616 | tf_op jit(solution)/shard_map/ppermute | solution.py:315
  45.7 1.4 %collective-permute-done.15.refs_0_ = f32[128,256]{1,0:T(8,128)S(1)} collective-permute-done((f32[128,256]{1,0:T(8,128)S(1)}, f32[128,256]{1,0:T(8,128)S(1)}, u32[]{:S(2)}, u32[]{:S(2)}) %collective-permute-start.15) | collective-permute-done | bytes 131104 | tf_op jit(solution)/shard_map/ppermute | solution.py:315
  47.1 1.2 %collective-permute-done.13 = f32[64,256]{1,0:T(8,128)S(1)} collective-permute-done((f32[64,256]{1,0:T(8,128)S(1)}, f32[64,256]{1,0:T(8,128)S(1)}, u32[]{:S(2)}, u32[]{:S(2)}) %collective-permute-start.13) | collective-permute-done | bytes 65568 | tf_op jit(solution)/shard_map/ppermute | solution.py:315
  48.3 1.6 %collective-permute-start.14 = (f32[64,256]{1,0:T(8,128)S(1)}, f32[64,256]{1,0:T(8,128)S(1)}, u32[]{:S(2)}, u32[]{:S(2)}) collective-permute-start(f32[64,256]{1,0:T(8,128)S(1)} %add.42), channel_id=1, source_target_pairs={{0,4},{1,5},{2,6},{3,7},{4,0},{5,1},{6,2},{7,3},{8,12},{9,13},{10,... | collective-permute-start | bytes 196616 | tf_op jit(solution)/shard_map/ppermute | solution.py:315
  49.9 2.9 %backward_early.1.sofar_ref = f32[128,1024]{1,0:T(8,128)S(1)} custom-call(bf16[2048,1024]{1,0:T(8,128)(2,1)} %get-tuple-element.29.dense_ref, f32[128,256]{1,0:T(8,128)S(1)} %get-tuple-element.30.refs_0_, f32[128,256]{1,0:T(8,128)S(1)} %collective-permute-done.7.refs_1_.after_ref, f32[128,256]{1,0:T(8,128)S(1)} %collective-permute-done.8.refs_2_, ...), custom_call_target="tpu_custom_call" | custom-call | tf_op jit(solution)/shard_map/backward_early/pallas_call | solution.py:370
  52.8 1.0 %collective-permute-done.14 = f32[64,256]{1,0:T(8,128)S(1)} collective-permute-done((f32[64,256]{1,0:T(8,128)S(1)}, f32[64,256]{1,0:T(8,128)S(1)}, u32[]{:S(2)}, u32[]{:S(2)}) %collective-permute-start.14) | collective-permute-done | bytes 65568 | tf_op jit(solution)/shard_map/ppermute | solution.py:315
  53.8 1.9 %backward_late.1 = (f32[576,128]{1,0:T(8,128)S(1)}, f32[576,128]{1,0:T(8,128)S(1)}) custom-call(s32[64,128]{1,0:T(8,128)S(1)} %bitcast.3, bf16[2048,1024]{1,0:T(8,128)(2,1)} %get-tuple-element.29.dense_ref, f32[128,1024]{1,0:T(8,128)S(1)} %backward_early.1.sofar_ref, f32[64,256]{1,0:T(8,128)S(1)} %add.43.wsum_ref, ...), custom_call_target="tpu_custom_call" | custom-call | tf_op jit(solution)/shard_map/backward_late/pallas_call | solution.py:391
  55.6 1.6 %collective-permute-start.17 = (f32[576,128]{1,0:T(8,128)S(1)}, f32[576,128]{1,0:T(8,128)S(1)}, u32[]{:S(2)}, u32[]{:S(2)}) collective-permute-start(f32[576,128]{1,0:T(8,128)S(1)} %get-tuple-element.35), channel_id=1, source_target_pairs={{0,8},{8,0},{16,24},{24,16},{1,9},{9,1},{17,25},{25,17},{2,10},{10... | collective-permute-start | bytes 884744 | tf_op jit(solution)/shard_map/ppermute | solution.py:318
  57.2 1.5 %collective-permute-start.19 = (f32[576,128]{1,0:T(8,128)S(1)}, f32[576,128]{1,0:T(8,128)S(1)}, u32[]{:S(2)}, u32[]{:S(2)}) collective-permute-start(f32[576,128]{1,0:T(8,128)S(1)} %get-tuple-element.36), channel_id=1, source_target_pairs={{0,16},{8,24},{16,0},{24,8},{1,17},{9,25},{17,1},{25,9},{2,18},{10... | collective-permute-start | bytes 884744 | tf_op jit(solution)/shard_map/ppermute | solution.py:318
  58.7 5.5 %collective-permute-done.17 = f32[576,128]{1,0:T(8,128)S(1)} collective-permute-done((f32[576,128]{1,0:T(8,128)S(1)}, f32[576,128]{1,0:T(8,128)S(1)}, u32[]{:S(2)}, u32[]{:S(2)}) %collective-permute-start.17) | collective-permute-done | bytes 294944 | tf_op jit(solution)/shard_map/ppermute | solution.py:318
  64.3 1.6 %collective-permute-start.18 = (f32[576,128]{1,0:T(8,128)S(1)}, f32[576,128]{1,0:T(8,128)S(1)}, u32[]{:S(2)}, u32[]{:S(2)}) collective-permute-start(f32[576,128]{1,0:T(8,128)S(1)} %add.44), channel_id=1, source_target_pairs={{0,16},{8,24},{16,0},{24,8},{1,17},{9,25},{17,1},{25,9},{2,18},{10... | collective-permute-start | bytes 884744 | tf_op jit(solution)/shard_map/ppermute | solution.py:318
  65.9 1.6 %collective-permute-start.20 = (f32[576,128]{1,0:T(8,128)S(1)}, f32[576,128]{1,0:T(8,128)S(1)}, u32[]{:S(2)}, u32[]{:S(2)}) collective-permute-start(f32[576,128]{1,0:T(8,128)S(1)} %add.46), channel_id=1, source_target_pairs={{0,8},{8,0},{16,24},{24,16},{1,9},{9,1},{17,25},{25,17},{2,10},{10... | collective-permute-start | bytes 884744 | tf_op jit(solution)/shard_map/ppermute | solution.py:318
  67.4 4.5 %collective-permute-done.18 = f32[576,128]{1,0:T(8,128)S(1)} collective-permute-done((f32[576,128]{1,0:T(8,128)S(1)}, f32[576,128]{1,0:T(8,128)S(1)}, u32[]{:S(2)}, u32[]{:S(2)}) %collective-permute-start.18) | collective-permute-done | bytes 294944 | tf_op jit(solution)/shard_map/ppermute | solution.py:318
  72.0 1.3 %collective-permute-done.20 = f32[576,128]{1,0:T(8,128)S(1)} collective-permute-done((f32[576,128]{1,0:T(8,128)S(1)}, f32[576,128]{1,0:T(8,128)S(1)}, u32[]{:S(2)}, u32[]{:S(2)}) %collective-permute-start.20) | collective-permute-done | bytes 294944 | tf_op jit(solution)/shard_map/ppermute | solution.py:318
  73.5 0.8 %pad_maximum_fusion = f32[1024,128]{1,0:T(8,128)} fusion(f32[512,128]{1,0:T(8,128)S(1)} %slice.17, f32[512,128]{1,0:T(8,128)S(1)} %slice.16), kind=kLoop, calls=%fused_computation | loop fusion | flops 131072 | bytes 1048576 | tf_op jit(solution)/shard_map/concatenate | solution.py:411
  74.7 0.7 pad_maximum_fusion.1
  (43 shorter events, 2.4 us)
Async XLA Ops:
  0.6 30.0 %copy-start = (s32[8192]{0:T(1024)S(1)}, s32[8192]{0:T(1024)}, u32[]{:S(2)}) copy-start(s32[8192]{0:T(1024)} %param.9) | copy-start | bytes 98308
  0.6 30.0 %copy-start.3 = (bf16[128,256]{1,0:T(8,128)(2,1)S(1)}, bf16[128,256]{1,0:T(8,128)(2,1)}, u32[]{:S(2)}) copy-start(bf16[128,256]{1,0:T(8,128)(2,1)} %weight_ref.1) | copy-start | bytes 196612
  0.7 30.0 %copy-start.1 = (bf16[256,256]{1,0:T(8,128)(2,1)S(1)}, bf16[256,256]{1,0:T(8,128)(2,1)}, u32[]{:S(2)}) copy-start(bf16[256,256]{1,0:T(8,128)(2,1)} %cot_ref.1) | copy-start | bytes 393220
  11.4 1.7 %collective-permute-start.2 = (f32[256,128]{1,0:T(8,128)}, f32[256,128]{1,0:T(8,128)S(1)}, u32[]{:S(2)}, u32[]{:S(2)}) collective-permute-start(f32[256,128]{1,0:T(8,128)} %get-tuple-element.25), channel_id=1, source_target_pairs={{0,1},{1,0},{2,3},{3,2},{4,5},{5,4},{6,7},{7,6},{8,9},{9,8},{10,11... | collective-permute-start | bytes 393224 | tf_op jit(solution)/shard_map/ppermute | solution.py:312
  12.0 5.1 %collective-permute-start.5 = (f32[256,128]{1,0:T(8,128)}, f32[256,128]{1,0:T(8,128)S(1)}, u32[]{:S(2)}, u32[]{:S(2)}) collective-permute-start(f32[256,128]{1,0:T(8,128)} %get-tuple-element.27), channel_id=1, source_target_pairs={{0,1},{1,0},{2,3},{3,2},{4,5},{5,4},{6,7},{7,6},{8,9},{9,8},{10,11... | collective-permute-start | bytes 393224 | tf_op jit(solution)/shard_map/ppermute | solution.py:312
  12.0 6.3 %collective-permute-start.1 = (f32[256,128]{1,0:T(8,128)}, f32[256,128]{1,0:T(8,128)S(1)}, u32[]{:S(2)}, u32[]{:S(2)}) collective-permute-start(f32[256,128]{1,0:T(8,128)} %get-tuple-element.23), channel_id=1, source_target_pairs={{0,1},{1,0},{2,3},{3,2},{4,5},{5,4},{6,7},{7,6},{8,9},{9,8},{10,11... | collective-permute-start | bytes 393224 | tf_op jit(solution)/shard_map/ppermute | solution.py:312
  14.1 6.8 %collective-permute-start.3 = (f32[256,128]{1,0:T(8,128)S(1)}, f32[256,128]{1,0:T(8,128)S(1)}, u32[]{:S(2)}, u32[]{:S(2)}) collective-permute-start(f32[256,128]{1,0:T(8,128)S(1)} %add.38), channel_id=1, source_target_pairs={{0,2},{1,3},{2,0},{3,1},{4,6},{5,7},{6,4},{7,5},{8,10},{9,11},{10,... | collective-permute-start | bytes 393224 | tf_op jit(solution)/shard_map/ppermute | solution.py:315
  17.1 7.6 %collective-permute-start = (f32[256,128]{1,0:T(8,128)}, f32[256,128]{1,0:T(8,128)S(1)}, u32[]{:S(2)}, u32[]{:S(2)}) collective-permute-start(f32[256,128]{1,0:T(8,128)} %get-tuple-element.21), channel_id=1, source_target_pairs={{0,1},{1,0},{2,3},{3,2},{4,5},{5,4},{6,7},{7,6},{8,9},{9,8},{10,11... | collective-permute-start | bytes 393224 | tf_op jit(solution)/shard_map/ppermute | solution.py:312
  18.0 6.6 %collective-permute-start.6 = (f32[256,128]{1,0:T(8,128)S(1)}, f32[256,128]{1,0:T(8,128)S(1)}, u32[]{:S(2)}, u32[]{:S(2)}) collective-permute-start(f32[256,128]{1,0:T(8,128)S(1)} %add.40), channel_id=1, source_target_pairs={{0,2},{1,3},{2,0},{3,1},{4,6},{5,7},{6,4},{7,5},{8,10},{9,11},{10,... | collective-permute-start | bytes 393224 | tf_op jit(solution)/shard_map/ppermute | solution.py:315
  21.9 8.8 %collective-permute-start.4 = (f32[256,128]{1,0:T(8,128)S(1)}, f32[256,128]{1,0:T(8,128)S(1)}, u32[]{:S(2)}, u32[]{:S(2)}) collective-permute-start(f32[256,128]{1,0:T(8,128)S(1)} %add_add_fusion), channel_id=1, source_target_pairs={{0,4},{1,5},{2,6},{3,7},{4,0},{5,1},{6,2},{7,3},{8,12},{9,13},{10,... | collective-permute-start | bytes 393224 | tf_op jit(solution)/shard_map/ppermute | solution.py:315
  30.6 0.9 %copy-start.2 = (f32[256,128]{1,0:T(8,128)S(1)}, f32[256,128]{1,0:T(8,128)}, u32[]{:S(2)}) copy-start(f32[256,128]{1,0:T(8,128)} %get-tuple-element.20.refs_0_) | copy-start | bytes 393220
  33.5 8.4 %collective-permute-start.10 = (f32[128,256]{1,0:T(8,128)S(1)}, f32[128,256]{1,0:T(8,128)S(1)}, u32[]{:S(2)}, u32[]{:S(2)}) collective-permute-start(f32[128,256]{1,0:T(8,128)S(1)} %get-tuple-element.30.refs_0_), channel_id=1, source_target_pairs={{0,4},{1,5},{2,6},{3,7},{4,0},{5,1},{6,2},{7,3},{8,12},{9,13},{10,... | collective-permute-start | bytes 393224 | tf_op jit(solution)/shard_map/ppermute | solution.py:315
  33.5 8.4 %collective-permute-start.7 = (f32[128,256]{1,0:T(8,128)S(1)}, f32[128,256]{1,0:T(8,128)S(1)}, u32[]{:S(2)}, u32[]{:S(2)}) collective-permute-start(f32[128,256]{1,0:T(8,128)S(1)} %get-tuple-element.30.refs_0_), channel_id=1, source_target_pairs={{0,1},{1,0},{2,3},{3,2},{4,5},{5,4},{6,7},{7,6},{8,9},{9,8},{10,11... | collective-permute-start | bytes 393224 | tf_op jit(solution)/shard_map/ppermute | solution.py:312
  33.6 9.5 %collective-permute-start.8 = (f32[128,256]{1,0:T(8,128)S(1)}, f32[128,256]{1,0:T(8,128)S(1)}, u32[]{:S(2)}, u32[]{:S(2)}) collective-permute-start(f32[128,256]{1,0:T(8,128)S(1)} %get-tuple-element.30.refs_0_), channel_id=1, source_target_pairs={{0,2},{1,3},{2,0},{3,1},{4,6},{5,7},{6,4},{7,5},{8,10},{9,11},{10,... | collective-permute-start | bytes 393224 | tf_op jit(solution)/shard_map/ppermute | solution.py:315
  41.9 5.1 %collective-permute-start.15 = (f32[128,256]{1,0:T(8,128)S(1)}, f32[128,256]{1,0:T(8,128)S(1)}, u32[]{:S(2)}, u32[]{:S(2)}) collective-permute-start(f32[128,256]{1,0:T(8,128)S(1)} %collective-permute-done.10.refs_4_), channel_id=1, source_target_pairs={{0,2},{1,3},{2,0},{3,1},{4,6},{5,7},{6,4},{7,5},{8,10},{9,11},{10,... | collective-permute-start | bytes 393224 | tf_op jit(solution)/shard_map/ppermute | solution.py:315
  42.2 1.3 %collective-permute-start.12 = (f32[64,256]{1,0:T(8,128)S(1)}, f32[64,256]{1,0:T(8,128)S(1)}, u32[]{:S(2)}, u32[]{:S(2)}) collective-permute-start(f32[64,256]{1,0:T(8,128)S(1)} %get-tuple-element.34), channel_id=1, source_target_pairs={{0,1},{1,0},{2,3},{3,2},{4,5},{5,4},{6,7},{7,6},{8,9},{9,8},{10,11... | collective-permute-start | bytes 196616 | tf_op jit(solution)/shard_map/ppermute | solution.py:312
  42.3 7.5 %collective-permute-start.11 = (f32[128,256]{1,0:T(8,128)S(1)}, f32[128,256]{1,0:T(8,128)S(1)}, u32[]{:S(2)}, u32[]{:S(2)}) collective-permute-start(f32[128,256]{1,0:T(8,128)S(1)} %collective-permute-done.10.refs_4_), channel_id=1, source_target_pairs={{0,1},{1,0},{2,3},{3,2},{4,5},{5,4},{6,7},{7,6},{8,9},{9,8},{10,11... | collective-permute-start | bytes 393224 | tf_op jit(solution)/shard_map/ppermute | solution.py:312
  43.1 6.8 %collective-permute-start.9 = (f32[128,256]{1,0:T(8,128)S(1)}, f32[128,256]{1,0:T(8,128)S(1)}, u32[]{:S(2)}, u32[]{:S(2)}) collective-permute-start(f32[128,256]{1,0:T(8,128)S(1)} %collective-permute-done.8.refs_2_), channel_id=1, source_target_pairs={{0,1},{1,0},{2,3},{3,2},{4,5},{5,4},{6,7},{7,6},{8,9},{9,8},{10,11... | collective-permute-start | bytes 393224 | tf_op jit(solution)/shard_map/ppermute | solution.py:312
  43.6 4.7 %collective-permute-start.13 = (f32[64,256]{1,0:T(8,128)S(1)}, f32[64,256]{1,0:T(8,128)S(1)}, u32[]{:S(2)}, u32[]{:S(2)}) collective-permute-start(f32[64,256]{1,0:T(8,128)S(1)} %add.41), channel_id=1, source_target_pairs={{0,2},{1,3},{2,0},{3,1},{4,6},{5,7},{6,4},{7,5},{8,10},{9,11},{10,... | collective-permute-start | bytes 196616 | tf_op jit(solution)/shard_map/ppermute | solution.py:315
  47.0 6.7 %collective-permute-start.16 = (f32[128,256]{1,0:T(8,128)S(1)}, f32[128,256]{1,0:T(8,128)S(1)}, u32[]{:S(2)}, u32[]{:S(2)}) collective-permute-start(f32[128,256]{1,0:T(8,128)S(1)} %collective-permute-done.15.refs_0_), channel_id=1, source_target_pairs={{0,1},{1,0},{2,3},{3,2},{4,5},{5,4},{6,7},{7,6},{8,9},{9,8},{10,11... | collective-permute-start | bytes 393224 | tf_op jit(solution)/shard_map/ppermute | solution.py:312
  48.3 5.4 %collective-permute-start.14 = (f32[64,256]{1,0:T(8,128)S(1)}, f32[64,256]{1,0:T(8,128)S(1)}, u32[]{:S(2)}, u32[]{:S(2)}) collective-permute-start(f32[64,256]{1,0:T(8,128)S(1)} %add.42), channel_id=1, source_target_pairs={{0,4},{1,5},{2,6},{3,7},{4,0},{5,1},{6,2},{7,3},{8,12},{9,13},{10,... | collective-permute-start | bytes 196616 | tf_op jit(solution)/shard_map/ppermute | solution.py:315
  55.6 8.6 %collective-permute-start.17 = (f32[576,128]{1,0:T(8,128)S(1)}, f32[576,128]{1,0:T(8,128)S(1)}, u32[]{:S(2)}, u32[]{:S(2)}) collective-permute-start(f32[576,128]{1,0:T(8,128)S(1)} %get-tuple-element.35), channel_id=1, source_target_pairs={{0,8},{8,0},{16,24},{24,16},{1,9},{9,1},{17,25},{25,17},{2,10},{10... | collective-permute-start | bytes 884744 | tf_op jit(solution)/shard_map/ppermute | solution.py:318
  57.2 8.7 %collective-permute-start.19 = (f32[576,128]{1,0:T(8,128)S(1)}, f32[576,128]{1,0:T(8,128)S(1)}, u32[]{:S(2)}, u32[]{:S(2)}) collective-permute-start(f32[576,128]{1,0:T(8,128)S(1)} %get-tuple-element.36), channel_id=1, source_target_pairs={{0,16},{8,24},{16,0},{24,8},{1,17},{9,25},{17,1},{25,9},{2,18},{10... | collective-permute-start | bytes 884744 | tf_op jit(solution)/shard_map/ppermute | solution.py:318
  64.3 7.7 %collective-permute-start.18 = (f32[576,128]{1,0:T(8,128)S(1)}, f32[576,128]{1,0:T(8,128)S(1)}, u32[]{:S(2)}, u32[]{:S(2)}) collective-permute-start(f32[576,128]{1,0:T(8,128)S(1)} %add.44), channel_id=1, source_target_pairs={{0,16},{8,24},{16,0},{24,8},{1,17},{9,25},{17,1},{25,9},{2,18},{10... | collective-permute-start | bytes 884744 | tf_op jit(solution)/shard_map/ppermute | solution.py:318
  65.9 7.4 %collective-permute-start.20 = (f32[576,128]{1,0:T(8,128)S(1)}, f32[576,128]{1,0:T(8,128)S(1)}, u32[]{:S(2)}, u32[]{:S(2)}) collective-permute-start(f32[576,128]{1,0:T(8,128)S(1)} %add.46), channel_id=1, source_target_pairs={{0,8},{8,0},{16,24},{24,16},{1,9},{9,1},{17,25},{25,17},{2,10},{10... | collective-permute-start | bytes 884744 | tf_op jit(solution)/shard_map/ppermute | solution.py:318
  73.4 1.3 %collective-permute-start.21 = (f32[64,256]{1,0:T(8,128)S(1)}, f32[64,256]{1,0:T(8,128)S(1)}, u32[]{:S(2)}, u32[]{:S(2)}) collective-permute-start(f32[64,256]{1,0:T(8,128)S(1)} %pad_maximum_fusion.2), channel_id=1, source_target_pairs={{0,1},{1,0},{2,3},{3,2},{4,5},{5,4},{6,7},{7,6},{8,9},{9,8},{10,11... | collective-permute-start | bytes 196616 | tf_op jit(solution)/shard_map/ppermute | solution.py:312

commit v6 on v5

--- a/solution.py
+++ b/solution.py
@@ -7,13 +7,13 @@
 from jax.experimental.pallas import tpu as pltpu
 from jax.sharding import PartitionSpec as P
 
-HIGH = lax.Precision.HIGHEST
 F32 = jnp.float32
 BF16 = jnp.bfloat16
 EDGE = 128
 GROUP = 16
 QUARTERS = 4
 AHEAD = 2
+FWD = 46
 ACC_BYTES = 8 << 20
 GELU_C = 0.7978845608028654
 GELU_K = 0.044715
@@ -27,6 +27,10 @@
 def split(value):
     hi = value.astype(BF16)
     return hi, (value - hi.astype(F32)).astype(BF16)
+
+
+def across(a, b):
+    return lax.dot_general(a, b, (((0,), (0,)), ((), ())), preferred_element_type=F32)
 
 
 def fetch(pairs, sems):
@@ -150,48 +154,34 @@
         result_copy((n_panels - 1) * panel_dev + j, j).wait()
 
 
-def middle_kernel(n_col, n_in, deg_ref, cot_ref, weight_ref, *refs):
+def middle_kernel(n_col, n_in, scale, deg_ref, cot_ref, weight_ref, *refs):
     parts = refs[:n_in]
-    act_ref, pulled_ref, prop_ref, gprime_ref, stage, sems = refs[n_in:]
-    copies = fetch([(ref, stage.at[i]) for i, ref in enumerate(parts)], sems)
+    act_ref, pulled_ref, keep_ref, send_ref = refs[n_in:]
     node_dev = cot_ref.shape[0]
     dev_blocks = node_dev // EDGE
     base = (lax.axis_index("row") * n_col + lax.axis_index("col")) * dev_blocks
     inv = jnp.concatenate([inv_column(deg_ref, base + k) for k in range(dev_blocks)], axis=0)
-    for copy in copies:
-        copy.wait()
-    summed = stage[0]
-    for i in range(1, n_in):
-        summed = summed + stage[i]
+    summed = parts[0][...]
+    for ref in parts[1:]:
+        summed = summed + ref[...]
     propagated = inv * summed
-    prop_ref[...] = propagated
+    prop_hi, prop_lo = split(propagated)
     weight = weight_ref[...]
-    pair = jnp.dot(jnp.concatenate(split(propagated), axis=0), weight, preferred_element_type=F32)
+    pair = jnp.dot(
+        jnp.concatenate([prop_hi, prop_lo], axis=0), weight, preferred_element_type=F32)
     v = pair[:node_dev] + pair[node_dev:]
     t = jnp.tanh(GELU_C * (v + GELU_K * v * v * v))
     act_ref[...] = (0.5 * v * (1.0 + t)).astype(BF16)
     slope = 0.5 * (1.0 + t) + 0.5 * v * (1.0 - t * t) * (GELU_C * (1.0 + 3.0 * GELU_K * v * v))
     gprime = cot_ref[...].astype(F32) * slope
-    gprime_ref[...] = gprime
+    hi, lo = split(gprime)
     pair = lax.dot_general(
-        jnp.concatenate(split(gprime), axis=0), weight, (((1,), (1,)), ((), ())),
+        jnp.concatenate([hi, lo], axis=0), weight, (((1,), (1,)), ((), ())),
         preferred_element_type=F32,
     )
     pulled_ref[...] = jnp.transpose(inv * (pair[:node_dev] + pair[node_dev:]))
-
-
-def add_kernel(*refs):
-    total = refs[0][...]
-    for ref in refs[1:-1]:
-        total = total + ref[...]
-    refs[-1][...] = total
-
-
-def weight_kernel(scale, prop_ref, gprime_ref, after_ref, keep_ref, send_ref):
-    part = scale * lax.dot_general(
-        prop_ref[...], gprime_ref[...], (((0,), (0,)), ((), ())),
-        precision=HIGH, preferred_element_type=F32,
-    )
+    pair = across(jnp.concatenate([prop_hi, prop_lo], axis=1), hi)
+    part = scale * (pair[:EDGE] + (pair[EDGE:] + across(prop_hi, lo)))
     half = keep_ref.shape[0]
     low = lax.axis_index("col") % 2 == 0
     keep_ref[...] = jnp.where(low, part[:half], part[half:])
@@ -281,6 +271,9 @@
     def params(mib):
         return pltpu.CompilerParams(vmem_limit_bytes=mib << 20)
 
+    def after(x, other):
+        return x + 0.0 * other[0, 0]
+
     def cost(flops, read):
         return pl.CostEstimate(flops=flops, bytes_accessed=read, transcendentals=0)
 
@@ -301,7 +294,8 @@
             pltpu.SemaphoreType.DMA((panel_dev,)),
             pltpu.SemaphoreType.DMA((panel_dev,)),
         ],
-        compiler_params=params(54),
+        compiler_params=params(FWD),
+        cost_estimate=cost(100 * row_nodes * col_nodes * width, 1 << 20),
         name="densify_forward",
     )(block_rows, block_cols, live_slots, deg, features, blocks)
     keep, send = pieces[0::2], pieces[1::2]
@@ -325,20 +319,17 @@
         terms[m & (m - 1)].append(chip_flip(functools.reduce(jnp.add, terms[m]), low_bit(m)))
     parts = terms[0]
 
-    out_act, pulled, prop, gprime = pl.pallas_call(
-        functools.partial(middle_kernel, n_col, len(parts)),
+    half = width // 2
+    out_act, pulled, wkeep, wsend = pl.pallas_call(
+        functools.partial(middle_kernel, n_col, len(parts), float(nodes) ** (-0.5)),
         out_shape=(
             jax.ShapeDtypeStruct((node_dev, hidden), BF16),
             jax.ShapeDtypeStruct((width, node_dev), F32),
-            jax.ShapeDtypeStruct((node_dev, width), F32),
-            jax.ShapeDtypeStruct((node_dev, hidden), F32),
+            jax.ShapeDtypeStruct((half, hidden), F32),
+            jax.ShapeDtypeStruct((half, hidden), F32),
         ),
-        in_specs=[vmem] * 3 + [any_space] * len(parts),
+        in_specs=[vmem] * (3 + len(parts)),
         out_specs=(vmem,) * 4,
-        scratch_shapes=[
-            pltpu.VMEM((len(parts), node_dev, width), F32),
-            pltpu.SemaphoreType.DMA((len(parts),)),
-        ],
         compiler_params=params(16),
         name="middle",
     )(deg, cotangent, weight, *parts)
@@ -347,26 +338,17 @@
     for m in (1, 2):
         own[m] = chip_flip(pulled, low_bit(m))
     other = {0: swap(pulled)}
-    half = width // 2
-    wkeep, wsend = pl.pallas_call(
-        functools.partial(weight_kernel, float(nodes) ** (-0.5)),
-        out_shape=(jax.ShapeDtypeStruct((half, hidden), F32),) * 2,
-        in_specs=[vmem] * 2 + [any_space],
-        out_specs=(vmem,) * 2,
-        compiler_params=params(16),
-        name="weight_part",
-    )(prop, gprime, other[0])
-
     wsum = wkeep + swap(wsend)
+    wsum = wsum + chip_flip(wsum, 0)
+    own[2] = after(own[2], wsum)
     for m in range(3, n_chip):
         own[m] = chip_flip(own[m & (m - 1)], low_bit(m))
-    for m in range(1, n_chip):
+    for m in range(1, n_chip - 1):
         other[m] = swap(own[m])
-    for t in range(chip_bits):
+    for t in range(1, chip_bits):
         wsum = wsum + chip_flip(wsum, t)
 
     early = [x for m in range(n_chip - 1) for x in (own[m], other[m])]
-    late = [own[n_chip - 1], other[n_chip - 1]]
     sofar = pl.pallas_call(
         functools.partial(partial_kernel, len(early)),
         out_shape=jax.ShapeDtypeStruct((width, col_nodes), F32),
@@ -379,10 +361,13 @@
             pltpu.SemaphoreType.DMA((len(early),)),
             pltpu.SemaphoreType.DMA((len(early),)),
         ],
-        compiler_params=params(52),
+        compiler_params=params((row_nodes * col_nodes * 2 >> 20) + 20),
+        cost_estimate=cost(row_nodes * col_nodes * width * 4, 32 << 20),
         name="backward_early",
     )(tile, *early)
 
+    own[n_chip - 1] = after(after(own[n_chip - 1], sofar), wsum)
+    late = [own[n_chip - 1], swap(own[n_chip - 1])]
     n_piece = max(1, row_bits)
     while col_nodes % (EDGE * n_piece):
         n_piece -= 1
@@ -402,7 +387,7 @@
             pltpu.SemaphoreType.DMA,
             pltpu.SemaphoreType.DMA,
         ],
-        compiler_params=params(52),
+        compiler_params=params(24),
         name="backward_late",
     )(deg, tile, sofar, wsum, *late)
 

time: 75.7 us -> 84.4 us (1.11)
  local copies, waits for them, and re-layouts: 0.96 us -> 4.65 us
  other arithmetic: 4.44 us -> 1.75 us
  waiting for transfers between devices: 29.8 us -> 32.4 us
  Pallas kernels: 17.1 us -> 19.4 us
  between operations: 1.52 us -> 3.47 us
  starting transfers between devices: 21.6 us -> 22.5 us
    pallas_call x1, Pallas kernels: 10.1 us -> 14.7 us  [body(): pl.pallas_call(functools.partial(forward_kernel, n_col, chunk, panel_dev,...]
    add x3, other arithmetic: 2.77 us -> 0.06 us  [body(): functools.reduce(jnp.add, terms[m])]
    unnamed x8 -> x12, local copies, waits for them, and re-layouts: 0.91 us -> 3.07 us
    slice x0 -> x3, local copies, waits for them, and re-layouts: none -> 1.54 us  [after(): return x + 0.0 * other[0, 0]]
    pallas_call x2 -> x1, Pallas kernels: 2.23 us -> 1.09 us  [body(): pl.pallas_call(functools.partial(middle_kernel, n_col, len(parts), float(...]
    ppermute x4, waiting for transfers between devices: 11.3 us -> 12.4 us  [row_flip(): return lax.ppermute(x, 'row', [(i, i ^ 1 << bit) for i in range(n_row)])]
  transfers between devices with their start and end apart: 22 -> 22, of which waited for: 13 -> 10; matrix products, arithmetic and copies ran while one was open for 5% -> 3% of each run, Pallas kernels for 4% -> 3%
where the time goes in v6:
time: 84.4 us; the launch traced here: 84.1 us
  waiting for transfers between devices  32.4 us (38%)
  starting transfers between devices  22.5 us (27%)
  Pallas kernels  19.4 us (23%)
  local copies, waits for them, and re-layouts  4.65 us (6%)
  between operations  3.47 us (4%)
  other arithmetic  1.75 us (2%)
    ppermute x8, waiting for transfers between devices, chip_flip(): return lax.ppermute(x, 'col', [(i, i ^ 2 << bit) for i in range(n_col)])  17.7 us
    pallas_call x1, Pallas kernels, body(): pl.pallas_call(functools.partial(forward_kernel, n_col, chunk, panel_dev,...  14.7 us
    ppermute x8, starting transfers between devices, chip_flip(): return lax.ppermute(x, 'col', [(i, i ^ 2 << bit) for i in range(n_col)])  14.4 us
    ppermute x4, waiting for transfers between devices, row_flip(): return lax.ppermute(x, 'row', [(i, i ^ 1 << bit) for i in range(n_row)])  12.4 us
    ppermute x4, starting transfers between devices, row_flip(): return lax.ppermute(x, 'row', [(i, i ^ 1 << bit) for i in range(n_row)])  6.23 us
    unnamed x12, local copies, waits for them, and re-layouts  3.07 us
    pallas_call x1, Pallas kernels, body(): pl.pallas_call(functools.partial(partial_kernel, len(early)), out_shape=j...  2.43 us
    ppermute x10, waiting for transfers between devices, swap(): return lax.ppermute(x, 'col', swap_pairs)  2.24 us
  transfers between devices with their start and end apart: 22, of which 10 were waited for; matrix products, arithmetic and copies ran while one was open for 3% of the time, Pallas kernels for 3%

profile of v6, /device:TPU:0, one launch (start us, length us, event | category | flops | bytes accessed | tf_op | source)
XLA Modules:
  0.0 84.1 jit_solution(12143177850301951034)
XLA Ops:
  1.3 0.7 copy-done
  2.0 0.9 %copy-done.3 = bf16[1024,128]{1,0:T(8,128)(2,1)S(1)} copy-done((bf16[1024,128]{1,0:T(8,128)(2,1)S(1)}, bf16[1024,128]{1,0:T(8,128)(2,1)}, u32[]{:S(2)}) %copy-start.3) | copy-done | bytes 262168
  3.0 0.7 copy-done.4
  3.7 0.7 copy-done.5
  4.4 14.7 %densify_forward.1 = (f32[256,128]{1,0:T(8,128)S(1)}, f32[256,128]{1,0:T(8,128)S(1)}, f32[256,128]{1,0:T(8,128)S(1)}, f32[256,128]{1,0:T(8,128)S(1)}, f32[256,12...) custom-call(s32[1,1,384]{2,1,0:T(1,128)S(1)} %copy-done.4, ...), custom_call_target="tpu_custom_call" | custom-call | flops 26843545600 | bytes 1048576 | tf_op jit(solution)/shard_map/densify_forward/pallas_call | solution.py:280
  19.1 0.5 collective-permute-start.2
  20.7 3.0 %collective-permute-start.3 = (f32[256,128]{1,0:T(8,128)S(1)}, f32[256,128]{1,0:T(8,128)S(1)}, u32[]{:S(2)}, u32[]{:S(2)}) collective-permute-start(f32[256,128]{1,0:T(8,128)S(1)} %add.56), channel_id=1, source_target_pairs={{0,2},{1,3},{2,0},{3,1},{4,6},{5,7},{6,4},{7,5},{8,10},{9,11},{10,... | collective-permute-start | bytes 393224 | tf_op jit(solution)/shard_map/ppermute | solution.py:309
  24.0 3.9 %collective-permute-done.3 = f32[256,128]{1,0:T(8,128)S(1)} collective-permute-done((f32[256,128]{1,0:T(8,128)S(1)}, f32[256,128]{1,0:T(8,128)S(1)}, u32[]{:S(2)}, u32[]{:S(2)}) %collective-permute-start.3) | collective-permute-done | bytes 131104 | tf_op jit(solution)/shard_map/ppermute | solution.py:309
  28.0 3.1 %collective-permute-start.4 = (f32[256,128]{1,0:T(8,128)S(1)}, f32[256,128]{1,0:T(8,128)S(1)}, u32[]{:S(2)}, u32[]{:S(2)}) collective-permute-start(f32[256,128]{1,0:T(8,128)S(1)} %add_add_fusion.1), channel_id=1, source_target_pairs={{0,4},{1,5},{2,6},{3,7},{4,0},{5,1},{6,2},{7,3},{8,12},{9,13},{10,... | collective-permute-start | bytes 393224 | tf_op jit(solution)/shard_map/ppermute | solution.py:309
  31.1 5.3 %collective-permute-done.4.refs_2_ = f32[256,128]{1,0:T(8,128)S(1)} collective-permute-done((f32[256,128]{1,0:T(8,128)S(1)}, f32[256,128]{1,0:T(8,128)S(1)}, u32[]{:S(2)}, u32[]{:S(2)}) %collective-permute-start.4) | collective-permute-done | bytes 131104 | tf_op jit(solution)/shard_map/ppermute | solution.py:309
  36.4 1.1 %middle.1 = (bf16[256,256]{1,0:T(8,128)(2,1)}, f32[128,256]{1,0:T(8,128)S(1)}, f32[64,256]{1,0:T(8,128)S(1)}, f32[64,256]{1,0:T(8,128)S(1)}) custom-call(s32[64,128]{1,0:T(8,128)S(1)} %bitcast.5, bf16[256,256]{1,0:T(8,128)(2,1)S(1)} %copy-done.1, bf16[128,256]{1,0:T(8,128)(2,1)S(1)} %copy-done.2, f32[256,128]{1,0:T(8,128)S(1)} %get-tuple-element.18.refs_0_, ...), custom_call_target="tpu_custom_call" | custom-call | tf_op jit(solution)/shard_map/middle/pallas_call | solution.py:323
  37.9 3.4 %collective-permute-start.10 = (f32[128,256]{1,0:T(8,128)S(1)}, f32[128,256]{1,0:T(8,128)S(1)}, u32[]{:S(2)}, u32[]{:S(2)}) collective-permute-start(f32[128,256]{1,0:T(8,128)S(1)} %get-tuple-element.28.refs_0_), channel_id=1, source_target_pairs={{0,4},{1,5},{2,6},{3,7},{4,0},{5,1},{6,2},{7,3},{8,12},{9,13},{10,... | collective-permute-start | bytes 393224 | tf_op jit(solution)/shard_map/ppermute | solution.py:309
  41.5 5.9 %collective-permute-done.12 = f32[64,256]{1,0:T(8,128)S(1)} collective-permute-done((f32[64,256]{1,0:T(8,128)S(1)}, f32[64,256]{1,0:T(8,128)S(1)}, u32[]{:S(2)}, u32[]{:S(2)}) %collective-permute-start.12) | collective-permute-done | bytes 65568 | tf_op jit(solution)/shard_map/ppermute | solution.py:309
  47.4 0.5 slice.28
  48.7 0.5 collective-permute-start.13
  49.2 2.4 %collective-permute-start.14 = (f32[64,256]{1,0:T(8,128)S(1)}, f32[64,256]{1,0:T(8,128)S(1)}, u32[]{:S(2)}, u32[]{:S(2)}) collective-permute-start(f32[64,256]{1,0:T(8,128)S(1)} %add.60), channel_id=1, source_target_pairs={{0,4},{1,5},{2,6},{3,7},{4,0},{5,1},{6,2},{7,3},{8,12},{9,13},{10,... | collective-permute-start | bytes 196616 | tf_op jit(solution)/shard_map/ppermute | solution.py:309
  51.6 1.7 %collective-permute-start.15 = (f32[128,256]{1,0:T(8,128)S(1)}, f32[128,256]{1,0:T(8,128)S(1)}, u32[]{:S(2)}, u32[]{:S(2)}) collective-permute-start(f32[128,256]{1,0:T(8,128)S(1)} %broadcast_add_fusion.refs_4_), channel_id=1, source_target_pairs={{0,2},{1,3},{2,0},{3,1},{4,6},{5,7},{6,4},{7,5},{8,10},{9,11},{10,... | collective-permute-start | bytes 393224 | tf_op jit(solution)/shard_map/ppermute | solution.py:309
  53.3 2.6 %collective-permute-done.14 = f32[64,256]{1,0:T(8,128)S(1)} collective-permute-done((f32[64,256]{1,0:T(8,128)S(1)}, f32[64,256]{1,0:T(8,128)S(1)}, u32[]{:S(2)}, u32[]{:S(2)}) %collective-permute-start.14) | collective-permute-done | bytes 65568 | tf_op jit(solution)/shard_map/ppermute | solution.py:309
  55.9 0.5 slice.30
  57.1 2.4 %backward_early.1.sofar_ref = f32[128,1024]{1,0:T(8,128)S(1)} custom-call(bf16[2048,1024]{1,0:T(8,128)(2,1)S(1)} %get-tuple-element.27.dense_ref, f32[128,256]{1,0:T(8,128)S(1)} %get-tuple-element.28.refs_0_, f32[128,256]{1,0:T(8,128)S(1)} %collective-permute-done.7.refs_1_, f32[128,256]{1,0:T(8,128)S(1)} %collective-permute-done.8.refs_2_, ...), custom_call_target="tpu_custom_call" | custom-call | flops 1073741824 | bytes 33554432 | tf_op jit(solution)/shard_map/backward_early/pallas_call | solution.py:352
  59.5 0.5 slice.29
  60.8 1.3 %collective-permute-done.16.refs_1_ = f32[128,256]{1,0:T(8,128)S(1)} collective-permute-done((f32[128,256]{1,0:T(8,128)S(1)}, f32[128,256]{1,0:T(8,128)S(1)}, u32[]{:S(2)}, u32[]{:S(2)}) %collective-permute-start.16) | collective-permute-done | bytes 131104 | tf_op jit(solution)/shard_map/ppermute | solution.py:306
  62.1 1.1 %backward_late.1 = (f32[576,128]{1,0:T(8,128)S(1)}, f32[576,128]{1,0:T(8,128)S(1)}) custom-call(s32[64,128]{1,0:T(8,128)S(1)} %bitcast.6, bf16[2048,1024]{1,0:T(8,128)(2,1)S(1)} %get-tuple-element.27.dense_ref, f32[128,1024]{1,0:T(8,128)S(1)} %backward_early.1.sofar_ref, f32[64,256]{1,0:T(8,128)S(1)} %add.63.wsum_ref, f32[128,256]{1,0:T(8,128)S(1)} %add_add_fusion.refs_0_, ...), custom_call_target="tpu_custom_call" | custom-call | tf_op jit(solution)/shard_map/backward_late/pallas_call | solution.py:376
  63.3 1.6 %collective-permute-start.19 = (f32[576,128]{1,0:T(8,128)S(1)}, f32[576,128]{1,0:T(8,128)S(1)}, u32[]{:S(2)}, u32[]{:S(2)}) collective-permute-start(f32[576,128]{1,0:T(8,128)S(1)} %get-tuple-element.32), channel_id=1, source_target_pairs={{0,16},{8,24},{16,0},{24,8},{1,17},{9,25},{17,1},{25,9},{2,18},{10... | collective-permute-start | bytes 884744 | tf_op jit(solution)/shard_map/ppermute | solution.py:312
  64.9 1.5 %collective-permute-start.17 = (f32[576,128]{1,0:T(8,128)S(1)}, f32[576,128]{1,0:T(8,128)S(1)}, u32[]{:S(2)}, u32[]{:S(2)}) collective-permute-start(f32[576,128]{1,0:T(8,128)S(1)} %get-tuple-element.31), channel_id=1, source_target_pairs={{0,8},{8,0},{16,24},{24,16},{1,9},{9,1},{17,25},{25,17},{2,10},{10... | collective-permute-start | bytes 884744 | tf_op jit(solution)/shard_map/ppermute | solution.py:312
  66.3 6.0 %collective-permute-done.19 = f32[576,128]{1,0:T(8,128)S(1)} collective-permute-done((f32[576,128]{1,0:T(8,128)S(1)}, f32[576,128]{1,0:T(8,128)S(1)}, u32[]{:S(2)}, u32[]{:S(2)}) %collective-permute-start.19) | collective-permute-done | bytes 294944 | tf_op jit(solution)/shard_map/ppermute | solution.py:312
  72.4 1.6 %collective-permute-start.20 = (f32[576,128]{1,0:T(8,128)S(1)}, f32[576,128]{1,0:T(8,128)S(1)}, u32[]{:S(2)}, u32[]{:S(2)}) collective-permute-start(f32[576,128]{1,0:T(8,128)S(1)} %add.70), channel_id=1, source_target_pairs={{0,8},{8,0},{16,24},{24,16},{1,9},{9,1},{17,25},{25,17},{2,10},{10... | collective-permute-start | bytes 884744 | tf_op jit(solution)/shard_map/ppermute | solution.py:312
  74.0 1.6 %collective-permute-start.18 = (f32[576,128]{1,0:T(8,128)S(1)}, f32[576,128]{1,0:T(8,128)S(1)}, u32[]{:S(2)}, u32[]{:S(2)}) collective-permute-start(f32[576,128]{1,0:T(8,128)S(1)} %add.68), channel_id=1, source_target_pairs={{0,16},{8,24},{16,0},{24,8},{1,17},{9,25},{17,1},{25,9},{2,18},{10... | collective-permute-start | bytes 884744 | tf_op jit(solution)/shard_map/ppermute | solution.py:312
  75.6 5.1 %collective-permute-done.20 = f32[576,128]{1,0:T(8,128)S(1)} collective-permute-done((f32[576,128]{1,0:T(8,128)S(1)}, f32[576,128]{1,0:T(8,128)S(1)}, u32[]{:S(2)}, u32[]{:S(2)}) %collective-permute-start.20) | collective-permute-done | bytes 294944 | tf_op jit(solution)/shard_map/ppermute | solution.py:312
  80.8 1.2 %collective-permute-done.18 = f32[576,128]{1,0:T(8,128)S(1)} collective-permute-done((f32[576,128]{1,0:T(8,128)S(1)}, f32[576,128]{1,0:T(8,128)S(1)}, u32[]{:S(2)}, u32[]{:S(2)}) %collective-permute-start.18) | collective-permute-done | bytes 294944 | tf_op jit(solution)/shard_map/ppermute | solution.py:312
  82.2 0.8 pad_maximum_fusion
  83.5 0.7 pad_maximum_fusion.1
  (51 shorter events, 2.9 us)
Async XLA Ops:
  1.3 0.8 copy-start
  2.0 0.9 %copy-start.3 = (bf16[1024,128]{1,0:T(8,128)(2,1)S(1)}, bf16[1024,128]{1,0:T(8,128)(2,1)}, u32[]{:S(2)}) copy-start(bf16[1024,128]{1,0:T(8,128)(2,1)} %feat_ref.1) | copy-start | bytes 786436
  3.0 0.7 copy-start.4
  3.7 0.7 copy-start.5
  4.3 32.0 %copy-start.1 = (bf16[256,256]{1,0:T(8,128)(2,1)S(1)}, bf16[256,256]{1,0:T(8,128)(2,1)}, u32[]{:S(2)}) copy-start(bf16[256,256]{1,0:T(8,128)(2,1)} %cot_ref.1) | copy-start | bytes 393220
  4.4 32.0 %copy-start.2 = (bf16[128,256]{1,0:T(8,128)(2,1)S(1)}, bf16[128,256]{1,0:T(8,128)(2,1)}, u32[]{:S(2)}) copy-start(bf16[128,256]{1,0:T(8,128)(2,1)} %weight_ref.1) | copy-start | bytes 196612
  19.1 1.5 %collective-permute-start.2 = (f32[256,128]{1,0:T(8,128)S(1)}, f32[256,128]{1,0:T(8,128)S(1)}, u32[]{:S(2)}, u32[]{:S(2)}) collective-permute-start(f32[256,128]{1,0:T(8,128)S(1)} %get-tuple-element.23), channel_id=1, source_target_pairs={{0,1},{1,0},{2,3},{3,2},{4,5},{5,4},{6,7},{7,6},{8,9},{9,8},{10,11... | collective-permute-start | bytes 393224 | tf_op jit(solution)/shard_map/ppermute | solution.py:306
  19.6 4.0 %collective-permute-start.5 = (f32[256,128]{1,0:T(8,128)S(1)}, f32[256,128]{1,0:T(8,128)S(1)}, u32[]{:S(2)}, u32[]{:S(2)}) collective-permute-start(f32[256,128]{1,0:T(8,128)S(1)} %get-tuple-element.25), channel_id=1, source_target_pairs={{0,1},{1,0},{2,3},{3,2},{4,5},{5,4},{6,7},{7,6},{8,9},{9,8},{10,11... | collective-permute-start | bytes 393224 | tf_op jit(solution)/shard_map/ppermute | solution.py:306
  19.7 4.3 %collective-permute-start.1 = (f32[256,128]{1,0:T(8,128)S(1)}, f32[256,128]{1,0:T(8,128)S(1)}, u32[]{:S(2)}, u32[]{:S(2)}) collective-permute-start(f32[256,128]{1,0:T(8,128)S(1)} %get-tuple-element.21), channel_id=1, source_target_pairs={{0,1},{1,0},{2,3},{3,2},{4,5},{5,4},{6,7},{7,6},{8,9},{9,8},{10,11... | collective-permute-start | bytes 393224 | tf_op jit(solution)/shard_map/ppermute | solution.py:306
  20.7 7.3 %collective-permute-start.3 = (f32[256,128]{1,0:T(8,128)S(1)}, f32[256,128]{1,0:T(8,128)S(1)}, u32[]{:S(2)}, u32[]{:S(2)}) collective-permute-start(f32[256,128]{1,0:T(8,128)S(1)} %add.56), channel_id=1, source_target_pairs={{0,2},{1,3},{2,0},{3,1},{4,6},{5,7},{6,4},{7,5},{8,10},{9,11},{10,... | collective-permute-start | bytes 393224 | tf_op jit(solution)/shard_map/ppermute | solution.py:309
  23.7 7.4 %collective-permute-start = (f32[256,128]{1,0:T(8,128)S(1)}, f32[256,128]{1,0:T(8,128)S(1)}, u32[]{:S(2)}, u32[]{:S(2)}) collective-permute-start(f32[256,128]{1,0:T(8,128)S(1)} %get-tuple-element.19), channel_id=1, source_target_pairs={{0,1},{1,0},{2,3},{3,2},{4,5},{5,4},{6,7},{7,6},{8,9},{9,8},{10,11... | collective-permute-start | bytes 393224 | tf_op jit(solution)/shard_map/ppermute | solution.py:306
  23.7 7.4 %collective-permute-start.6 = (f32[256,128]{1,0:T(8,128)S(1)}, f32[256,128]{1,0:T(8,128)S(1)}, u32[]{:S(2)}, u32[]{:S(2)}) collective-permute-start(f32[256,128]{1,0:T(8,128)S(1)} %add.58), channel_id=1, source_target_pairs={{0,2},{1,3},{2,0},{3,1},{4,6},{5,7},{6,4},{7,5},{8,10},{9,11},{10,... | collective-permute-start | bytes 393224 | tf_op jit(solution)/shard_map/ppermute | solution.py:309
  28.0 8.4 %collective-permute-start.4 = (f32[256,128]{1,0:T(8,128)S(1)}, f32[256,128]{1,0:T(8,128)S(1)}, u32[]{:S(2)}, u32[]{:S(2)}) collective-permute-start(f32[256,128]{1,0:T(8,128)S(1)} %add_add_fusion.1), channel_id=1, source_target_pairs={{0,4},{1,5},{2,6},{3,7},{4,0},{5,1},{6,2},{7,3},{8,12},{9,13},{10,... | collective-permute-start | bytes 393224 | tf_op jit(solution)/shard_map/ppermute | solution.py:309
  37.5 3.8 %collective-permute-start.11 = (f32[64,256]{1,0:T(8,128)S(1)}, f32[64,256]{1,0:T(8,128)S(1)}, u32[]{:S(2)}, u32[]{:S(2)}) collective-permute-start(f32[64,256]{1,0:T(8,128)S(1)} %get-tuple-element.30), channel_id=1, source_target_pairs={{0,1},{1,0},{2,3},{3,2},{4,5},{5,4},{6,7},{7,6},{8,9},{9,8},{10,11... | collective-permute-start | bytes 196616 | tf_op jit(solution)/shard_map/ppermute | solution.py:306
  37.5 11.1 %collective-permute-start.8 = (f32[128,256]{1,0:T(8,128)S(1)}, f32[128,256]{1,0:T(8,128)S(1)}, u32[]{:S(2)}, u32[]{:S(2)}) collective-permute-start(f32[128,256]{1,0:T(8,128)S(1)} %get-tuple-element.28.refs_0_), channel_id=1, source_target_pairs={{0,2},{1,3},{2,0},{3,1},{4,6},{5,7},{6,4},{7,5},{8,10},{9,11},{10,... | collective-permute-start | bytes 393224 | tf_op jit(solution)/shard_map/ppermute | solution.py:309
  37.9 10.7 %collective-permute-start.10 = (f32[128,256]{1,0:T(8,128)S(1)}, f32[128,256]{1,0:T(8,128)S(1)}, u32[]{:S(2)}, u32[]{:S(2)}) collective-permute-start(f32[128,256]{1,0:T(8,128)S(1)} %get-tuple-element.28.refs_0_), channel_id=1, source_target_pairs={{0,4},{1,5},{2,6},{3,7},{4,0},{5,1},{6,2},{7,3},{8,12},{9,13},{10,... | collective-permute-start | bytes 393224 | tf_op jit(solution)/shard_map/ppermute | solution.py:309
  41.3 6.0 %collective-permute-start.12 = (f32[64,256]{1,0:T(8,128)S(1)}, f32[64,256]{1,0:T(8,128)S(1)}, u32[]{:S(2)}, u32[]{:S(2)}) collective-permute-start(f32[64,256]{1,0:T(8,128)S(1)} %add.59), channel_id=1, source_target_pairs={{0,2},{1,3},{2,0},{3,1},{4,6},{5,7},{6,4},{7,5},{8,10},{9,11},{10,... | collective-permute-start | bytes 196616 | tf_op jit(solution)/shard_map/ppermute | solution.py:309
  41.4 15.6 %collective-permute-start.7 = (f32[128,256]{1,0:T(8,128)S(1)}, f32[128,256]{1,0:T(8,128)S(1)}, u32[]{:S(2)}, u32[]{:S(2)}) collective-permute-start(f32[128,256]{1,0:T(8,128)S(1)} %get-tuple-element.28.refs_0_), channel_id=1, source_target_pairs={{0,1},{1,0},{2,3},{3,2},{4,5},{5,4},{6,7},{7,6},{8,9},{9,8},{10,11... | collective-permute-start | bytes 393224 | tf_op jit(solution)/shard_map/ppermute | solution.py:306
  48.6 8.5 %collective-permute-start.9 = (f32[128,256]{1,0:T(8,128)S(1)}, f32[128,256]{1,0:T(8,128)S(1)}, u32[]{:S(2)}, u32[]{:S(2)}) collective-permute-start(f32[128,256]{1,0:T(8,128)S(1)} %collective-permute-done.8.refs_2_), channel_id=1, source_target_pairs={{0,1},{1,0},{2,3},{3,2},{4,5},{5,4},{6,7},{7,6},{8,9},{9,8},{10,11... | collective-permute-start | bytes 393224 | tf_op jit(solution)/shard_map/ppermute | solution.py:306
  48.7 8.4 %collective-permute-start.13 = (f32[128,256]{1,0:T(8,128)S(1)}, f32[128,256]{1,0:T(8,128)S(1)}, u32[]{:S(2)}, u32[]{:S(2)}) collective-permute-start(f32[128,256]{1,0:T(8,128)S(1)} %broadcast_add_fusion.refs_4_), channel_id=1, source_target_pairs={{0,1},{1,0},{2,3},{3,2},{4,5},{5,4},{6,7},{7,6},{8,9},{9,8},{10,11... | collective-permute-start | bytes 393224 | tf_op jit(solution)/shard_map/ppermute | solution.py:306
  49.2 6.6 %collective-permute-start.14 = (f32[64,256]{1,0:T(8,128)S(1)}, f32[64,256]{1,0:T(8,128)S(1)}, u32[]{:S(2)}, u32[]{:S(2)}) collective-permute-start(f32[64,256]{1,0:T(8,128)S(1)} %add.60), channel_id=1, source_target_pairs={{0,4},{1,5},{2,6},{3,7},{4,0},{5,1},{6,2},{7,3},{8,12},{9,13},{10,... | collective-permute-start | bytes 196616 | tf_op jit(solution)/shard_map/ppermute | solution.py:309
  51.6 9.1 %collective-permute-start.15 = (f32[128,256]{1,0:T(8,128)S(1)}, f32[128,256]{1,0:T(8,128)S(1)}, u32[]{:S(2)}, u32[]{:S(2)}) collective-permute-start(f32[128,256]{1,0:T(8,128)S(1)} %broadcast_add_fusion.refs_4_), channel_id=1, source_target_pairs={{0,2},{1,3},{2,0},{3,1},{4,6},{5,7},{6,4},{7,5},{8,10},{9,11},{10,... | collective-permute-start | bytes 393224 | tf_op jit(solution)/shard_map/ppermute | solution.py:309
  60.7 1.4 %collective-permute-start.16 = (f32[128,256]{1,0:T(8,128)S(1)}, f32[128,256]{1,0:T(8,128)S(1)}, u32[]{:S(2)}, u32[]{:S(2)}) collective-permute-start(f32[128,256]{1,0:T(8,128)S(1)} %add_add_fusion.refs_0_), channel_id=1, source_target_pairs={{0,1},{1,0},{2,3},{3,2},{4,5},{5,4},{6,7},{7,6},{8,9},{9,8},{10,11... | collective-permute-start | bytes 393224 | tf_op jit(solution)/shard_map/ppermute | solution.py:306
  63.3 9.1 %collective-permute-start.19 = (f32[576,128]{1,0:T(8,128)S(1)}, f32[576,128]{1,0:T(8,128)S(1)}, u32[]{:S(2)}, u32[]{:S(2)}) collective-permute-start(f32[576,128]{1,0:T(8,128)S(1)} %get-tuple-element.32), channel_id=1, source_target_pairs={{0,16},{8,24},{16,0},{24,8},{1,17},{9,25},{17,1},{25,9},{2,18},{10... | collective-permute-start | bytes 884744 | tf_op jit(solution)/shard_map/ppermute | solution.py:312
  64.9 9.1 %collective-permute-start.17 = (f32[576,128]{1,0:T(8,128)S(1)}, f32[576,128]{1,0:T(8,128)S(1)}, u32[]{:S(2)}, u32[]{:S(2)}) collective-permute-start(f32[576,128]{1,0:T(8,128)S(1)} %get-tuple-element.31), channel_id=1, source_target_pairs={{0,8},{8,0},{16,24},{24,16},{1,9},{9,1},{17,25},{25,17},{2,10},{10... | collective-permute-start | bytes 884744 | tf_op jit(solution)/shard_map/ppermute | solution.py:312
  72.4 8.3 %collective-permute-start.20 = (f32[576,128]{1,0:T(8,128)S(1)}, f32[576,128]{1,0:T(8,128)S(1)}, u32[]{:S(2)}, u32[]{:S(2)}) collective-permute-start(f32[576,128]{1,0:T(8,128)S(1)} %add.70), channel_id=1, source_target_pairs={{0,8},{8,0},{16,24},{24,16},{1,9},{9,1},{17,25},{25,17},{2,10},{10... | collective-permute-start | bytes 884744 | tf_op jit(solution)/shard_map/ppermute | solution.py:312
  74.0 8.0 %collective-permute-start.18 = (f32[576,128]{1,0:T(8,128)S(1)}, f32[576,128]{1,0:T(8,128)S(1)}, u32[]{:S(2)}, u32[]{:S(2)}) collective-permute-start(f32[576,128]{1,0:T(8,128)S(1)} %add.68), channel_id=1, source_target_pairs={{0,16},{8,24},{16,0},{24,8},{1,17},{9,25},{17,1},{25,9},{2,18},{10... | collective-permute-start | bytes 884744 | tf_op jit(solution)/shard_map/ppermute | solution.py:312
  82.1 1.3 %collective-permute-start.21 = (f32[64,256]{1,0:T(8,128)S(1)}, f32[64,256]{1,0:T(8,128)S(1)}, u32[]{:S(2)}, u32[]{:S(2)}) collective-permute-start(f32[64,256]{1,0:T(8,128)S(1)} %pad_maximum_fusion.2), channel_id=1, source_target_pairs={{0,1},{1,0},{2,3},{3,2},{4,5},{5,4},{6,7},{7,6},{8,9},{9,8},{10,11... | collective-permute-start | bytes 196616 | tf_op jit(solution)/shard_map/ppermute | solution.py:306

commit v7 on v6

--- a/solution.py
+++ b/solution.py
@@ -12,8 +12,7 @@
 EDGE = 128
 GROUP = 16
 QUARTERS = 4
-AHEAD = 2
-FWD = 46
+AHEAD = 3
 ACC_BYTES = 8 << 20
 GELU_C = 0.7978845608028654
 GELU_K = 0.044715
@@ -89,18 +88,13 @@
         pending = []
 
         def finish():
-            acc, p0, p1, same, a0, a1, b0, b1 = pending.pop(0)
-            b0, b1 = b0.astype(F32), b1.astype(F32)
-            acc[p0] = a0 + b0
-            acc[p1] = a1 + (b1 + same * b0)
-
-        for u in range(0, GROUP, 2):
-            s = first + u
-            p0, p1 = place(s), place(s + 1)
-            same = jnp.where(p0 == p1, 1.0, 0.0).astype(F32)
+            acc, p, sofar, block = pending.pop(0)
+            acc[p] = sofar + block.astype(F32)
+
+        for s in range(GROUP):
+            p = place(first + s)
             for q, acc in enumerate(accs):
-                at = slice(q * part, (q + 1) * part)
-                pending.append((acc, p0, p1, same, acc[p0], acc[p1], buf[s, at, :], buf[s + 1, at, :]))
+                pending.append((acc, p, acc[p], buf[first + s, q * part:(q + 1) * part, :]))
                 if len(pending) > AHEAD:
                     finish()
         while pending:
@@ -156,7 +150,7 @@
 
 def middle_kernel(n_col, n_in, scale, deg_ref, cot_ref, weight_ref, *refs):
     parts = refs[:n_in]
-    act_ref, pulled_ref, keep_ref, send_ref = refs[n_in:]
+    act_ref, pulled_ref, message_ref = refs[n_in:]
     node_dev = cot_ref.shape[0]
     dev_blocks = node_dev // EDGE
     base = (lax.axis_index("row") * n_col + lax.axis_index("col")) * dev_blocks
@@ -179,19 +173,16 @@
         jnp.concatenate([hi, lo], axis=0), weight, (((1,), (1,)), ((), ())),
         preferred_element_type=F32,
     )
-    pulled_ref[...] = jnp.transpose(inv * (pair[:node_dev] + pair[node_dev:]))
+    pulled = jnp.transpose(inv * (pair[:node_dev] + pair[node_dev:]))
+    pulled_ref[...] = pulled
+    message_ref[:EDGE] = pulled
     pair = across(jnp.concatenate([prop_hi, prop_lo], axis=1), hi)
-    part = scale * (pair[:EDGE] + (pair[EDGE:] + across(prop_hi, lo)))
-    half = keep_ref.shape[0]
-    low = lax.axis_index("col") % 2 == 0
-    keep_ref[...] = jnp.where(low, part[:half], part[half:])
-    send_ref[...] = jnp.where(low, part[half:], part[:half])
-
-
-def load_lhs(parts, stage, lhs, copies):
-    width = parts[0].shape[0]
-    node_dev = parts[0].shape[1]
-    for i in range(len(parts)):
+    message_ref[EDGE:] = scale * (pair[:EDGE] + (pair[EDGE:] + across(prop_hi, lo)))
+
+
+def load_lhs(stage, lhs, copies):
+    width, node_dev = stage.shape[1:]
+    for i in range(len(copies)):
         copies[i].wait()
         hi, lo = split(stage[i])
         lhs[:width, i * node_dev:(i + 1) * node_dev] = hi
@@ -199,13 +190,23 @@
 
 
 def partial_kernel(n_in, dense_ref, *refs):
-    parts, (out_ref, dense, stage, lhs, sems, dense_sems) = refs[:n_in], refs[n_in:]
-    width, node_dev = parts[0].shape
+    parts = refs[:n_in]
+    out_ref, wsum_ref, dense, stage, wstage, lhs, sems, wsems, dense_sems = refs[n_in:]
+    width, node_dev = stage.shape[1:]
     col_nodes = dense.shape[1]
+    half = wstage.shape[1]
+    mine = pl.ds(width + (lax.axis_index("col") % 2) * half, half)
     blocks = fetch(
         [(dense_ref.at[pl.ds(i * node_dev, node_dev)], dense.at[pl.ds(i * node_dev, node_dev)])
          for i in range(n_in)], dense_sems)
-    load_lhs(parts, stage, lhs, fetch([(r, stage.at[i]) for i, r in enumerate(parts)], sems))
+    copies = fetch([(r.at[pl.ds(0, width)], stage.at[i]) for i, r in enumerate(parts)], sems)
+    weights = fetch([(parts[i].at[mine], wstage.at[i]) for i in range(4)], wsems)
+    load_lhs(stage, lhs, copies)
+    for copy in weights:
+        copy.wait()
+    total = (wstage[0] + wstage[1]) + (wstage[2] + wstage[3])
+    for n in range(0, total.shape[1], EDGE):
+        wsum_ref[n // EDGE * half:(n // EDGE + 1) * half, :] = total[:, n:n + EDGE]
     for copy in blocks:
         copy.wait()
     step = 2 * EDGE if col_nodes % (2 * EDGE) == 0 else EDGE
@@ -214,7 +215,7 @@
         out_ref[:, n:n + step] = pair[:width] + pair[width:]
 
 
-def last_kernel(n_in, n_out, deg_ref, dense_ref, sofar_ref, wsum_ref, *refs):
+def last_kernel(n_in, n_out, deg_ref, dense_ref, sofar_ref, *refs):
     parts, outs = refs[:n_in], refs[n_in:n_in + n_out]
     dense, stage, lhs, sofar, sems, dense_sem, sofar_sem = refs[n_in + n_out:]
     width, node_dev = parts[0].shape
@@ -225,14 +226,9 @@
     before = pltpu.make_async_copy(sofar_ref, sofar, sofar_sem)
     block.start()
     size = col_nodes // n_out
-    lanes = wsum_ref.shape[1] // n_out
-    for i, out in enumerate(outs):
-        for n in range(0, lanes, EDGE):
-            at = size + wsum_ref.shape[0] * (n // EDGE)
-            out[at:at + wsum_ref.shape[0], :] = wsum_ref[:, i * lanes + n:i * lanes + n + EDGE]
     copies = fetch([(r, stage.at[i]) for i, r in enumerate(parts)], sems)
     before.start()
-    load_lhs(parts, stage, lhs, copies)
+    load_lhs(stage, lhs, copies)
     block.wait()
     before.wait()
     step = 2 * EDGE if col_nodes % (2 * EDGE) == 0 else EDGE
@@ -259,7 +255,7 @@
     col_blocks = col_nodes // EDGE
     dev_blocks = node_dev // EDGE
     assert n_chip >= 4
-    chunk = 32
+    chunk = 16
     panel_dev = n_col
     while panel_dev % 2 == 0 and panel_dev * node_dev * col_nodes * 4 > ACC_BYTES:
         panel_dev //= 2
@@ -272,7 +268,10 @@
         return pltpu.CompilerParams(vmem_limit_bytes=mib << 20)
 
     def after(x, other):
-        return x + 0.0 * other[0, 0]
+        corner = 0.0 * other[:8, :EDGE]
+        if x.shape == other.shape[:1] + x.shape[1:]:
+            return x + 0.0 * other[:, :x.shape[1]]
+        return (x.reshape(-1, 8, EDGE) + corner).reshape(x.shape)
 
     def cost(flops, read):
         return pl.CostEstimate(flops=flops, bytes_accessed=read, transcendentals=0)
@@ -294,8 +293,7 @@
             pltpu.SemaphoreType.DMA((panel_dev,)),
             pltpu.SemaphoreType.DMA((panel_dev,)),
         ],
-        compiler_params=params(FWD),
-        cost_estimate=cost(100 * row_nodes * col_nodes * width, 1 << 20),
+        compiler_params=params(54),
         name="densify_forward",
     )(block_rows, block_cols, live_slots, deg, features, blocks)
     keep, send = pieces[0::2], pieces[1::2]
@@ -319,64 +317,61 @@
         terms[m & (m - 1)].append(chip_flip(functools.reduce(jnp.add, terms[m]), low_bit(m)))
     parts = terms[0]
 
-    half = width // 2
-    out_act, pulled, wkeep, wsend = pl.pallas_call(
+    out_act, pulled, message = pl.pallas_call(
         functools.partial(middle_kernel, n_col, len(parts), float(nodes) ** (-0.5)),
         out_shape=(
             jax.ShapeDtypeStruct((node_dev, hidden), BF16),
             jax.ShapeDtypeStruct((width, node_dev), F32),
-            jax.ShapeDtypeStruct((half, hidden), F32),
-            jax.ShapeDtypeStruct((half, hidden), F32),
+            jax.ShapeDtypeStruct((2 * width, hidden), F32),
         ),
         in_specs=[vmem] * (3 + len(parts)),
-        out_specs=(vmem,) * 4,
+        out_specs=(vmem,) * 3,
         compiler_params=params(16),
         name="middle",
     )(deg, cotangent, weight, *parts)
 
-    own = {0: pulled}
-    for m in (1, 2):
-        own[m] = chip_flip(pulled, low_bit(m))
-    other = {0: swap(pulled)}
-    wsum = wkeep + swap(wsend)
-    wsum = wsum + chip_flip(wsum, 0)
-    own[2] = after(own[2], wsum)
+    last = n_chip - 1
+    own = {0: message, 1: chip_flip(message, 0), 2: chip_flip(pulled, 1)}
     for m in range(3, n_chip):
-        own[m] = chip_flip(own[m & (m - 1)], low_bit(m))
-    for m in range(1, n_chip - 1):
-        other[m] = swap(own[m])
-    for t in range(1, chip_bits):
-        wsum = wsum + chip_flip(wsum, t)
-
-    early = [x for m in range(n_chip - 1) for x in (own[m], other[m])]
-    sofar = pl.pallas_call(
+        own[m] = chip_flip(own[m & (m - 1)][:width], low_bit(m))
+    other = {m: swap(own[m]) for m in range(last)}
+
+    half = width // 2
+    early = [x for m in range(last) for x in (own[m], other[m])]
+    sofar, wsum = pl.pallas_call(
         functools.partial(partial_kernel, len(early)),
-        out_shape=jax.ShapeDtypeStruct((width, col_nodes), F32),
+        out_shape=(
+            jax.ShapeDtypeStruct((width, col_nodes), F32),
+            jax.ShapeDtypeStruct((half * hidden // EDGE, EDGE), F32),
+        ),
         in_specs=[any_space] * (1 + len(early)),
-        out_specs=vmem,
+        out_specs=(vmem,) * 2,
         scratch_shapes=[
             pltpu.VMEM((len(early) * node_dev, col_nodes), BF16),
             pltpu.VMEM((len(early), width, node_dev), F32),
+            pltpu.VMEM((4, half, hidden), F32),
             pltpu.VMEM((2 * width, len(early) * node_dev), BF16),
             pltpu.SemaphoreType.DMA((len(early),)),
+            pltpu.SemaphoreType.DMA((4,)),
             pltpu.SemaphoreType.DMA((len(early),)),
         ],
-        compiler_params=params((row_nodes * col_nodes * 2 >> 20) + 20),
+        compiler_params=params(52),
         cost_estimate=cost(row_nodes * col_nodes * width * 4, 32 << 20),
         name="backward_early",
     )(tile, *early)
 
-    own[n_chip - 1] = after(after(own[n_chip - 1], sofar), wsum)
-    late = [own[n_chip - 1], swap(own[n_chip - 1])]
+    own[last] = after(own[last], sofar)
+    late = [own[last], swap(own[last])]
+    for t in range(1, chip_bits):
+        wsum = wsum + chip_flip(wsum, t)
     n_piece = max(1, row_bits)
     while col_nodes % (EDGE * n_piece):
         n_piece -= 1
     size = col_nodes // n_piece
-    extra = half * hidden // n_piece // EDGE
     done = pl.pallas_call(
         functools.partial(last_kernel, len(late), n_piece),
-        out_shape=(jax.ShapeDtypeStruct((size + extra, width), F32),) * n_piece,
-        in_specs=[vmem, any_space, any_space, vmem] + [any_space] * len(late),
+        out_shape=(jax.ShapeDtypeStruct((size, width), F32),) * n_piece,
+        in_specs=[vmem, any_space, any_space] + [any_space] * len(late),
         out_specs=(vmem,) * n_piece,
         scratch_shapes=[
             pltpu.VMEM((len(late) * node_dev, col_nodes), BF16),
@@ -387,20 +382,26 @@
             pltpu.SemaphoreType.DMA,
             pltpu.SemaphoreType.DMA,
         ],
-        compiler_params=params(24),
+        compiler_params=params(52),
         name="backward_late",
-    )(deg, tile, sofar, wsum, *late)
-
+    )(deg, tile, sofar, *late)
+
+    done = list(done)
     for t in range(row_bits):
+        wsum = after(wsum, done[0])
+        wsum = wsum + row_flip(wsum, t)
         done = [x + row_flip(x, (i + t) % row_bits) for i, x in enumerate(done)]
-    feat_grad = jnp.concatenate([x[:size] for x in done], axis=0)
-    wsum = jnp.concatenate(
-        [x[size + i:size + i + half] for x in done for i in range(0, extra, half)], axis=1)
+        if t == 0:
+            done[-1] = after(done[-1], wsum)
+    wsum = after(wsum, done[0])
+    feat_grad = jnp.concatenate(done, axis=0)
 
     wother = swap(wsum)
     low = lax.axis_index("col") % 2 == 0
+    halves = (jnp.where(low, wsum, wother), jnp.where(low, wother, wsum))
     weight_grad = jnp.concatenate(
-        [jnp.where(low, wsum, wother), jnp.where(low, wother, wsum)], axis=0
+        [jnp.concatenate([x[i:i + half] for i in range(0, x.shape[0], half)], axis=1) for x in halves],
+        axis=0,
     )
     return out_act, feat_grad, weight_grad
 

time: 84.4 us -> 73.4 us (0.87)
  waiting for transfers between devices: 32.4 us -> 25.6 us
  local copies, waits for them, and re-layouts: 4.65 us -> 0.92 us
  Pallas kernels: 19.4 us -> 15.9 us
  other arithmetic: 1.75 us -> 4.47 us
  starting transfers between devices: 22.5 us -> 24.7 us
  between operations: 3.47 us -> 1.52 us
    pallas_call x1, Pallas kernels: 14.7 us -> 10 us  [body(): pl.pallas_call(functools.partial(forward_kernel, n_col, chunk, panel_dev,...]
    ppermute x4 -> x6, waiting for transfers between devices: 12.4 us -> 8.91 us  [row_flip(): return lax.ppermute(x, 'row', [(i, i ^ 1 << bit) for i in range(n_row)])]
    add x3, other arithmetic: 0.06 us -> 2.77 us  [body(): functools.reduce(jnp.add, terms[m])]
    unnamed x12 -> x8, local copies, waits for them, and re-layouts: 3.07 us -> 0.91 us
    ppermute x8 -> x7, waiting for transfers between devices: 17.7 us -> 15.6 us  [chip_flip(): return lax.ppermute(x, 'col', [(i, i ^ 2 << bit) for i in range(n_col)])]
    ppermute x4 -> x6, starting transfers between devices: 6.23 us -> 8.36 us  [row_flip(): return lax.ppermute(x, 'row', [(i, i ^ 1 << bit) for i in range(n_row)])]
    slice x7 -> x1, local copies, waits for them, and re-layouts: 1.59 us -> 0.01 us  [body(): x[i:i + half]]
    ppermute x10 -> x9, waiting for transfers between devices: 2.24 us -> 1.07 us  [swap(): return lax.ppermute(x, 'col', swap_pairs)]
  transfers between devices with their start and end apart: 22 -> 22, of which waited for: 10 -> 9; matrix products, arithmetic and copies ran while one was open for 3% -> 5% of each run, Pallas kernels for 3% -> 7%
where the time goes in v7:
time: 73.4 us; the launch traced here: 73.1 us
  waiting for transfers between devices  25.6 us (35%)
  starting transfers between devices  24.7 us (34%)
  Pallas kernels  15.9 us (22%)
  other arithmetic  4.47 us (6%)
  between operations  1.52 us (2%)
  local copies, waits for them, and re-layouts  0.92 us (1%)
    ppermute x7, waiting for transfers between devices, chip_flip(): return lax.ppermute(x, 'col', [(i, i ^ 2 << bit) for i in range(n_col)])  15.6 us
    ppermute x7, starting transfers between devices, chip_flip(): return lax.ppermute(x, 'col', [(i, i ^ 2 << bit) for i in range(n_col)])  14.7 us
    pallas_call x1, Pallas kernels, body(): pl.pallas_call(functools.partial(forward_kernel, n_col, chunk, panel_dev,...  10 us
    ppermute x6, waiting for transfers between devices, row_flip(): return lax.ppermute(x, 'row', [(i, i ^ 1 << bit) for i in range(n_row)])  8.91 us
    ppermute x6, starting transfers between devices, row_flip(): return lax.ppermute(x, 'row', [(i, i ^ 1 << bit) for i in range(n_row)])  8.36 us
    pallas_call x1, Pallas kernels, body(): pl.pallas_call(functools.partial(partial_kernel, len(early)), out_shape=(...  2.96 us
    add x3, other arithmetic, body(): functools.reduce(jnp.add, terms[m])  2.77 us
    pallas_call x1, Pallas kernels, body(): pl.pallas_call(functools.partial(last_kernel, len(late), n_piece), out_sh...  1.87 us
  transfers between devices with their start and end apart: 22, of which 9 were waited for; matrix products, arithmetic and copies ran while one was open for 5% of the time, Pallas kernels for 7%

profile of v7, /device:TPU:0, one launch (start us, length us, event | category | flops | bytes accessed | tf_op | source)
XLA Modules:
  0.0 73.1 jit_solution(5855619427518941177)
XLA Ops:
  1.3 10.0 %densify_forward.1 = (f32[256,128]{1,0:T(8,128)}, f32[256,128]{1,0:T(8,128)}, f32[256,128]{1,0:T(8,128)}, f32[256,128]{1,0:T(8,128)}, f32[256,128]{1,0:T(8,128)}...) custom-call(s32[1,1,384]{2,1,0:T(1,128)} %rows_ref.1, ...), custom_call_target="tpu_custom_call" | custom-call | tf_op jit(solution)/shard_map/densify_forward/pallas_call | solution.py:279
  11.4 0.5 collective-permute-start.2
  12.4 0.7 collective-permute-done.2
  13.1 0.9 %add.85 = f32[256,128]{1,0:T(8,128)S(1)} add(f32[256,128]{1,0:T(8,128)} %get-tuple-element.23, f32[256,128]{1,0:T(8,128)S(1)} %collective-permute-done.2) | non-fusion elementwise | flops 32768 | bytes 393216 | tf_op jit(solution)/shard_map/add | solution.py:317
  14.0 3.0 %collective-permute-start.3 = (f32[256,128]{1,0:T(8,128)S(1)}, f32[256,128]{1,0:T(8,128)S(1)}, u32[]{:S(2)}, u32[]{:S(2)}) collective-permute-start(f32[256,128]{1,0:T(8,128)S(1)} %add.85), channel_id=1, source_target_pairs={{0,2},{1,3},{2,0},{3,1},{4,6},{5,7},{6,4},{7,5},{8,10},{9,11},{10,... | collective-permute-start | bytes 393224 | tf_op jit(solution)/shard_map/ppermute | solution.py:307
  17.0 0.9 %add.87 = f32[256,128]{1,0:T(8,128)S(1)} add(f32[256,128]{1,0:T(8,128)} %get-tuple-element.25, f32[256,128]{1,0:T(8,128)S(1)} %collective-permute-done.5) | non-fusion elementwise | flops 32768 | bytes 393216 | tf_op jit(solution)/shard_map/add | solution.py:317
  18.3 2.6 %collective-permute-done.3 = f32[256,128]{1,0:T(8,128)S(1)} collective-permute-done((f32[256,128]{1,0:T(8,128)S(1)}, f32[256,128]{1,0:T(8,128)S(1)}, u32[]{:S(2)}, u32[]{:S(2)}) %collective-permute-start.3) | collective-permute-done | bytes 131104 | tf_op jit(solution)/shard_map/ppermute | solution.py:307
  20.9 0.9 %add_add_fusion = f32[256,128]{1,0:T(8,128)S(1)} fusion(f32[256,128]{1,0:T(8,128)S(1)} %collective-permute-done.3, f32[256,128]{1,0:T(8,128)} %get-tuple-element.21, f32[256,128]{1,0:T(8,128)S(1)} %collective-permute-done.1), kind=kLoop, calls=%fused_computation.4 | loop fusion | flops 65536 | bytes 524288 | tf_op jit(solution)/shard_map/add | solution.py:317
  21.8 2.8 %collective-permute-start.4 = (f32[256,128]{1,0:T(8,128)S(1)}, f32[256,128]{1,0:T(8,128)S(1)}, u32[]{:S(2)}, u32[]{:S(2)}) collective-permute-start(f32[256,128]{1,0:T(8,128)S(1)} %add_add_fusion), channel_id=1, source_target_pairs={{0,4},{1,5},{2,6},{3,7},{4,0},{5,1},{6,2},{7,3},{8,12},{9,13},{10,... | collective-permute-start | bytes 393224 | tf_op jit(solution)/shard_map/ppermute | solution.py:307
  24.6 6.0 %collective-permute-done.4.refs_2_ = f32[256,128]{1,0:T(8,128)S(1)} collective-permute-done((f32[256,128]{1,0:T(8,128)S(1)}, f32[256,128]{1,0:T(8,128)S(1)}, u32[]{:S(2)}, u32[]{:S(2)}) %collective-permute-start.4) | collective-permute-done | bytes 131104 | tf_op jit(solution)/shard_map/ppermute | solution.py:307
  30.6 0.9 %copy-done.2 = f32[256,128]{1,0:T(8,128)S(1)} copy-done((f32[256,128]{1,0:T(8,128)S(1)}, f32[256,128]{1,0:T(8,128)}, u32[]{:S(2)}) %copy-start.2) | copy-done | bytes 131096
  31.5 1.1 %middle.1 = (bf16[256,256]{1,0:T(8,128)(2,1)}, f32[128,256]{1,0:T(8,128)S(1)}, f32[256,256]{1,0:T(8,128)S(1)}) custom-call(s32[64,128]{1,0:T(8,128)S(1)} %bitcast.10, bf16[256,256]{1,0:T(8,128)(2,1)S(1)} %copy-done.1, bf16[128,256]{1,0:T(8,128)(2,1)S(1)} %copy-done.3, f32[256,128]{1,0:T(8,128)S(1)} %copy-done.2, ...), custom_call_target="tpu_custom_call" | custom-call | tf_op jit(solution)/shard_map/middle/pallas_call | solution.py:320
  32.6 0.5 collective-permute-start.8
  33.1 3.4 %collective-permute-start.10 = (f32[128,256]{1,0:T(8,128)S(1)}, f32[128,256]{1,0:T(8,128)S(1)}, u32[]{:S(2)}, u32[]{:S(2)}) collective-permute-start(f32[128,256]{1,0:T(8,128)S(1)} %get-tuple-element.30), channel_id=1, source_target_pairs={{0,4},{1,5},{2,6},{3,7},{4,0},{5,1},{6,2},{7,3},{8,12},{9,13},{10,... | collective-permute-start | bytes 393224 | tf_op jit(solution)/shard_map/ppermute | solution.py:307
  36.5 5.8 %collective-permute-done.8.refs_2_ = f32[256,256]{1,0:T(8,128)S(1)} collective-permute-done((f32[256,256]{1,0:T(8,128)S(1)}, f32[256,256]{1,0:T(8,128)S(1)}, u32[]{:S(2)}, u32[]{:S(2)}) %collective-permute-start.8) | collective-permute-done | bytes 262176 | tf_op jit(solution)/shard_map/ppermute | solution.py:307
  42.3 0.5 collective-permute-start.11
  42.8 2.9 %collective-permute-start.12 = (f32[128,256]{1,0:T(8,128)S(1)}, f32[128,256]{1,0:T(8,128)S(1)}, u32[]{:S(2)}, u32[]{:S(2)}) collective-permute-start(f32[128,256]{1,0:T(8,128)S(1)} %collective-permute-done.10.refs_4_), channel_id=1, source_target_pairs={{0,2},{1,3},{2,0},{3,1},{4,6},{5,7},{6,4},{7,5},{8,10},{9,11},{10,... | collective-permute-start | bytes 393224 | tf_op jit(solution)/shard_map/ppermute | solution.py:307
  45.7 3.0 %backward_early.1 = (f32[128,1024]{1,0:T(8,128)S(1)}, f32[128,128]{1,0:T(8,128)S(1)}) custom-call(bf16[2048,1024]{1,0:T(8,128)(2,1)} %get-tuple-element.28.dense_ref, f32[256,256]{1,0:T(8,128)S(1)} %get-tuple-element.29.refs_0_, f32[256,256]{1,0:T(8,128)S(1)} %collective-permute-done.7.refs_1_, f32[256,256]{1,0:T(8,128)S(1)} %collective-permute-done.8.refs_2_, ...), custom_call_target="tpu_custom_call" | custom-call | flops 1073741824 | bytes 33554432 | tf_op jit(solution)/shard_map/backward_early/pallas_call | solution.py:341
  48.6 1.2 %collective-permute-done.12 = f32[128,256]{1,0:T(8,128)S(1)} collective-permute-done((f32[128,256]{1,0:T(8,128)S(1)}, f32[128,256]{1,0:T(8,128)S(1)}, u32[]{:S(2)}, u32[]{:S(2)}) %collective-permute-start.12) | collective-permute-done | bytes 131104 | tf_op jit(solution)/shard_map/ppermute | solution.py:307
  49.9 1.8 %collective-permute-start.17 = (f32[128,128]{1,0:T(8,128)S(1)}, f32[128,128]{1,0:T(8,128)S(1)}, u32[]{:S(2)}, u32[]{:S(2)}) collective-permute-start(f32[128,128]{1,0:T(8,128)S(1)} %get-tuple-element.34), channel_id=1, source_target_pairs={{0,4},{1,5},{2,6},{3,7},{4,0},{5,1},{6,2},{7,3},{8,12},{9,13},{10,... | collective-permute-start | bytes 196616 | tf_op jit(solution)/shard_map/ppermute | solution.py:307
  51.7 1.9 %backward_late.1 = (f32[512,128]{1,0:T(8,128)S(1)}, f32[512,128]{1,0:T(8,128)S(1)}) custom-call(s32[64,128]{1,0:T(8,128)S(1)} %bitcast.11, bf16[2048,1024]{1,0:T(8,128)(2,1)} %get-tuple-element.28.dense_ref, f32[128,1024]{1,0:T(8,128)S(1)} %get-tuple-element.31.sofar_ref, f32[128,256]{1,0:T(8,128)S(1)} %multiply_add_fusion.refs_0_, ...), custom_call_target="tpu_custom_call" | custom-call | tf_op jit(solution)/shard_map/backward_late/pallas_call | solution.py:371
  53.6 1.6 %collective-permute-start.14 = (f32[512,128]{1,0:T(8,128)S(1)}, f32[512,128]{1,0:T(8,128)S(1)}, u32[]{:S(2)}, u32[]{:S(2)}) collective-permute-start(f32[512,128]{1,0:T(8,128)S(1)} %get-tuple-element.32), channel_id=1, source_target_pairs={{0,8},{8,0},{16,24},{24,16},{1,9},{9,1},{17,25},{25,17},{2,10},{10... | collective-permute-start | bytes 786440 | tf_op jit(solution)/shard_map/ppermute | solution.py:310
  55.2 1.5 %collective-permute-start.16 = (f32[512,128]{1,0:T(8,128)S(1)}, f32[512,128]{1,0:T(8,128)S(1)}, u32[]{:S(2)}, u32[]{:S(2)}) collective-permute-start(f32[512,128]{1,0:T(8,128)S(1)} %get-tuple-element.33), channel_id=1, source_target_pairs={{0,16},{8,24},{16,0},{24,8},{1,17},{9,25},{17,1},{25,9},{2,18},{10... | collective-permute-start | bytes 786440 | tf_op jit(solution)/shard_map/ppermute | solution.py:310
  56.7 1.6 %collective-permute-start.18 = (f32[128,128]{1,0:T(8,128)S(1)}, f32[128,128]{1,0:T(8,128)S(1)}, u32[]{:S(2)}, u32[]{:S(2)}) collective-permute-start(f32[128,128]{1,0:T(8,128)S(1)} %bitcast_add_fusion.3), channel_id=1, source_target_pairs={{0,8},{8,0},{16,24},{24,16},{1,9},{9,1},{17,25},{25,17},{2,10},{10... | collective-permute-start | bytes 196616 | tf_op jit(solution)/shard_map/ppermute | solution.py:310
  58.3 4.5 %collective-permute-done.14 = f32[512,128]{1,0:T(8,128)S(1)} collective-permute-done((f32[512,128]{1,0:T(8,128)S(1)}, f32[512,128]{1,0:T(8,128)S(1)}, u32[]{:S(2)}, u32[]{:S(2)}) %collective-permute-start.14) | collective-permute-done | bytes 262176 | tf_op jit(solution)/shard_map/ppermute | solution.py:310
  62.8 1.6 %collective-permute-start.15 = (f32[512,128]{1,0:T(8,128)S(1)}, f32[512,128]{1,0:T(8,128)S(1)}, u32[]{:S(2)}, u32[]{:S(2)}) collective-permute-start(f32[512,128]{1,0:T(8,128)S(1)} %add.89), channel_id=1, source_target_pairs={{0,16},{8,24},{16,0},{24,8},{1,17},{9,25},{17,1},{25,9},{2,18},{10... | collective-permute-start | bytes 786440 | tf_op jit(solution)/shard_map/ppermute | solution.py:310
  64.5 1.6 %collective-permute-start.19 = (f32[512,128]{1,0:T(8,128)S(1)}, f32[512,128]{1,0:T(8,128)S(1)}, u32[]{:S(2)}, u32[]{:S(2)}) collective-permute-start(f32[512,128]{1,0:T(8,128)S(1)} %bitcast_add_fusion), channel_id=1, source_target_pairs={{0,8},{8,0},{16,24},{24,16},{1,9},{9,1},{17,25},{25,17},{2,10},{10... | collective-permute-start | bytes 786440 | tf_op jit(solution)/shard_map/ppermute | solution.py:310
  66.0 0.6 collective-permute-start.20
  66.6 3.8 %collective-permute-done.15 = f32[512,128]{1,0:T(8,128)S(1)} collective-permute-done((f32[512,128]{1,0:T(8,128)S(1)}, f32[512,128]{1,0:T(8,128)S(1)}, u32[]{:S(2)}, u32[]{:S(2)}) %collective-permute-start.15) | collective-permute-done | bytes 262176 | tf_op jit(solution)/shard_map/ppermute | solution.py:310
  70.5 0.7 collective-permute-done.20
  71.2 0.8 %pad_maximum_fusion = f32[1024,128]{1,0:T(8,128)} fusion(f32[512,128]{1,0:T(8,128)S(1)} %add.100, f32[512,128]{1,0:T(8,128)S(1)} %add.90), kind=kLoop, calls=%fused_computation | loop fusion | flops 131072 | bytes 1048576 | tf_op jit(solution)/shard_map/concatenate | solution.py:397
  72.5 0.7 maximum_maximum_fusion
  (43 shorter events, 1.6 us)
Async XLA Ops:
  0.6 30.0 %copy-start = (s32[8192]{0:T(1024)S(1)}, s32[8192]{0:T(1024)}, u32[]{:S(2)}) copy-start(s32[8192]{0:T(1024)} %param.9) | copy-start | bytes 98308
  0.6 30.0 %copy-start.1 = (bf16[256,256]{1,0:T(8,128)(2,1)S(1)}, bf16[256,256]{1,0:T(8,128)(2,1)}, u32[]{:S(2)}) copy-start(bf16[256,256]{1,0:T(8,128)(2,1)} %cot_ref.1) | copy-start | bytes 393220
  0.7 29.9 %copy-start.3 = (bf16[128,256]{1,0:T(8,128)(2,1)S(1)}, bf16[128,256]{1,0:T(8,128)(2,1)}, u32[]{:S(2)}) copy-start(bf16[128,256]{1,0:T(8,128)(2,1)} %weight_ref.1) | copy-start | bytes 196612
  11.4 1.7 %collective-permute-start.2 = (f32[256,128]{1,0:T(8,128)}, f32[256,128]{1,0:T(8,128)S(1)}, u32[]{:S(2)}, u32[]{:S(2)}) collective-permute-start(f32[256,128]{1,0:T(8,128)} %get-tuple-element.24), channel_id=1, source_target_pairs={{0,1},{1,0},{2,3},{3,2},{4,5},{5,4},{6,7},{7,6},{8,9},{9,8},{10,11... | collective-permute-start | bytes 393224 | tf_op jit(solution)/shard_map/ppermute | solution.py:304
  11.9 5.1 %collective-permute-start.5 = (f32[256,128]{1,0:T(8,128)}, f32[256,128]{1,0:T(8,128)S(1)}, u32[]{:S(2)}, u32[]{:S(2)}) collective-permute-start(f32[256,128]{1,0:T(8,128)} %get-tuple-element.26), channel_id=1, source_target_pairs={{0,1},{1,0},{2,3},{3,2},{4,5},{5,4},{6,7},{7,6},{8,9},{9,8},{10,11... | collective-permute-start | bytes 393224 | tf_op jit(solution)/shard_map/ppermute | solution.py:304
  12.0 6.3 %collective-permute-start.1 = (f32[256,128]{1,0:T(8,128)}, f32[256,128]{1,0:T(8,128)S(1)}, u32[]{:S(2)}, u32[]{:S(2)}) collective-permute-start(f32[256,128]{1,0:T(8,128)} %get-tuple-element.22), channel_id=1, source_target_pairs={{0,1},{1,0},{2,3},{3,2},{4,5},{5,4},{6,7},{7,6},{8,9},{9,8},{10,11... | collective-permute-start | bytes 393224 | tf_op jit(solution)/shard_map/ppermute | solution.py:304
  14.0 6.9 %collective-permute-start.3 = (f32[256,128]{1,0:T(8,128)S(1)}, f32[256,128]{1,0:T(8,128)S(1)}, u32[]{:S(2)}, u32[]{:S(2)}) collective-permute-start(f32[256,128]{1,0:T(8,128)S(1)} %add.85), channel_id=1, source_target_pairs={{0,2},{1,3},{2,0},{3,1},{4,6},{5,7},{6,4},{7,5},{8,10},{9,11},{10,... | collective-permute-start | bytes 393224 | tf_op jit(solution)/shard_map/ppermute | solution.py:307
  17.0 7.6 %collective-permute-start = (f32[256,128]{1,0:T(8,128)}, f32[256,128]{1,0:T(8,128)S(1)}, u32[]{:S(2)}, u32[]{:S(2)}) collective-permute-start(f32[256,128]{1,0:T(8,128)} %get-tuple-element.20), channel_id=1, source_target_pairs={{0,1},{1,0},{2,3},{3,2},{4,5},{5,4},{6,7},{7,6},{8,9},{9,8},{10,11... | collective-permute-start | bytes 393224 | tf_op jit(solution)/shard_map/ppermute | solution.py:304
  18.0 6.6 %collective-permute-start.6 = (f32[256,128]{1,0:T(8,128)S(1)}, f32[256,128]{1,0:T(8,128)S(1)}, u32[]{:S(2)}, u32[]{:S(2)}) collective-permute-start(f32[256,128]{1,0:T(8,128)S(1)} %add.87), channel_id=1, source_target_pairs={{0,2},{1,3},{2,0},{3,1},{4,6},{5,7},{6,4},{7,5},{8,10},{9,11},{10,... | collective-permute-start | bytes 393224 | tf_op jit(solution)/shard_map/ppermute | solution.py:307
  21.8 8.8 %collective-permute-start.4 = (f32[256,128]{1,0:T(8,128)S(1)}, f32[256,128]{1,0:T(8,128)S(1)}, u32[]{:S(2)}, u32[]{:S(2)}) collective-permute-start(f32[256,128]{1,0:T(8,128)S(1)} %add_add_fusion), channel_id=1, source_target_pairs={{0,4},{1,5},{2,6},{3,7},{4,0},{5,1},{6,2},{7,3},{8,12},{9,13},{10,... | collective-permute-start | bytes 393224 | tf_op jit(solution)/shard_map/ppermute | solution.py:307
  30.6 0.9 %copy-start.2 = (f32[256,128]{1,0:T(8,128)S(1)}, f32[256,128]{1,0:T(8,128)}, u32[]{:S(2)}) copy-start(f32[256,128]{1,0:T(8,128)} %get-tuple-element.19.refs_0_) | copy-start | bytes 393220
  32.6 9.7 %collective-permute-start.8 = (f32[256,256]{1,0:T(8,128)S(1)}, f32[256,256]{1,0:T(8,128)S(1)}, u32[]{:S(2)}, u32[]{:S(2)}) collective-permute-start(f32[256,256]{1,0:T(8,128)S(1)} %get-tuple-element.29.refs_0_), channel_id=1, source_target_pairs={{0,2},{1,3},{2,0},{3,1},{4,6},{5,7},{6,4},{7,5},{8,10},{9,11},{10,... | collective-permute-start | bytes 786440 | tf_op jit(solution)/shard_map/ppermute | solution.py:307
  33.1 12.5 %collective-permute-start.7 = (f32[256,256]{1,0:T(8,128)S(1)}, f32[256,256]{1,0:T(8,128)S(1)}, u32[]{:S(2)}, u32[]{:S(2)}) collective-permute-start(f32[256,256]{1,0:T(8,128)S(1)} %get-tuple-element.29.refs_0_), channel_id=1, source_target_pairs={{0,1},{1,0},{2,3},{3,2},{4,5},{5,4},{6,7},{7,6},{8,9},{9,8},{10,11... | collective-permute-start | bytes 786440 | tf_op jit(solution)/shard_map/ppermute | solution.py:304
  33.1 9.1 %collective-permute-start.10 = (f32[128,256]{1,0:T(8,128)S(1)}, f32[128,256]{1,0:T(8,128)S(1)}, u32[]{:S(2)}, u32[]{:S(2)}) collective-permute-start(f32[128,256]{1,0:T(8,128)S(1)} %get-tuple-element.30), channel_id=1, source_target_pairs={{0,4},{1,5},{2,6},{3,7},{4,0},{5,1},{6,2},{7,3},{8,12},{9,13},{10,... | collective-permute-start | bytes 393224 | tf_op jit(solution)/shard_map/ppermute | solution.py:307
  42.3 3.4 %collective-permute-start.9 = (f32[256,256]{1,0:T(8,128)S(1)}, f32[256,256]{1,0:T(8,128)S(1)}, u32[]{:S(2)}, u32[]{:S(2)}) collective-permute-start(f32[256,256]{1,0:T(8,128)S(1)} %collective-permute-done.8.refs_2_), channel_id=1, source_target_pairs={{0,1},{1,0},{2,3},{3,2},{4,5},{5,4},{6,7},{7,6},{8,9},{9,8},{10,11... | collective-permute-start | bytes 786440 | tf_op jit(solution)/shard_map/ppermute | solution.py:304
  42.3 3.4 %collective-permute-start.11 = (f32[128,256]{1,0:T(8,128)S(1)}, f32[128,256]{1,0:T(8,128)S(1)}, u32[]{:S(2)}, u32[]{:S(2)}) collective-permute-start(f32[128,256]{1,0:T(8,128)S(1)} %collective-permute-done.10.refs_4_), channel_id=1, source_target_pairs={{0,1},{1,0},{2,3},{3,2},{4,5},{5,4},{6,7},{7,6},{8,9},{9,8},{10,11... | collective-permute-start | bytes 393224 | tf_op jit(solution)/shard_map/ppermute | solution.py:304
  42.8 7.0 %collective-permute-start.12 = (f32[128,256]{1,0:T(8,128)S(1)}, f32[128,256]{1,0:T(8,128)S(1)}, u32[]{:S(2)}, u32[]{:S(2)}) collective-permute-start(f32[128,256]{1,0:T(8,128)S(1)} %collective-permute-done.10.refs_4_), channel_id=1, source_target_pairs={{0,2},{1,3},{2,0},{3,1},{4,6},{5,7},{6,4},{7,5},{8,10},{9,11},{10,... | collective-permute-start | bytes 393224 | tf_op jit(solution)/shard_map/ppermute | solution.py:307
  49.8 1.9 %collective-permute-start.13 = (f32[128,256]{1,0:T(8,128)S(1)}, f32[128,256]{1,0:T(8,128)S(1)}, u32[]{:S(2)}, u32[]{:S(2)}) collective-permute-start(f32[128,256]{1,0:T(8,128)S(1)} %multiply_add_fusion.refs_0_), channel_id=1, source_target_pairs={{0,1},{1,0},{2,3},{3,2},{4,5},{5,4},{6,7},{7,6},{8,9},{9,8},{10,11... | collective-permute-start | bytes 393224 | tf_op jit(solution)/shard_map/ppermute | solution.py:304
  49.9 6.8 %collective-permute-start.17 = (f32[128,128]{1,0:T(8,128)S(1)}, f32[128,128]{1,0:T(8,128)S(1)}, u32[]{:S(2)}, u32[]{:S(2)}) collective-permute-start(f32[128,128]{1,0:T(8,128)S(1)} %get-tuple-element.34), channel_id=1, source_target_pairs={{0,4},{1,5},{2,6},{3,7},{4,0},{5,1},{6,2},{7,3},{8,12},{9,13},{10,... | collective-permute-start | bytes 196616 | tf_op jit(solution)/shard_map/ppermute | solution.py:307
  53.6 9.1 %collective-permute-start.14 = (f32[512,128]{1,0:T(8,128)S(1)}, f32[512,128]{1,0:T(8,128)S(1)}, u32[]{:S(2)}, u32[]{:S(2)}) collective-permute-start(f32[512,128]{1,0:T(8,128)S(1)} %get-tuple-element.32), channel_id=1, source_target_pairs={{0,8},{8,0},{16,24},{24,16},{1,9},{9,1},{17,25},{25,17},{2,10},{10... | collective-permute-start | bytes 786440 | tf_op jit(solution)/shard_map/ppermute | solution.py:310
  55.2 9.2 %collective-permute-start.16 = (f32[512,128]{1,0:T(8,128)S(1)}, f32[512,128]{1,0:T(8,128)S(1)}, u32[]{:S(2)}, u32[]{:S(2)}) collective-permute-start(f32[512,128]{1,0:T(8,128)S(1)} %get-tuple-element.33), channel_id=1, source_target_pairs={{0,16},{8,24},{16,0},{24,8},{1,17},{9,25},{17,1},{25,9},{2,18},{10... | collective-permute-start | bytes 786440 | tf_op jit(solution)/shard_map/ppermute | solution.py:310
  56.7 7.6 %collective-permute-start.18 = (f32[128,128]{1,0:T(8,128)S(1)}, f32[128,128]{1,0:T(8,128)S(1)}, u32[]{:S(2)}, u32[]{:S(2)}) collective-permute-start(f32[128,128]{1,0:T(8,128)S(1)} %bitcast_add_fusion.3), channel_id=1, source_target_pairs={{0,8},{8,0},{16,24},{24,16},{1,9},{9,1},{17,25},{25,17},{2,10},{10... | collective-permute-start | bytes 196616 | tf_op jit(solution)/shard_map/ppermute | solution.py:310
  62.8 7.6 %collective-permute-start.15 = (f32[512,128]{1,0:T(8,128)S(1)}, f32[512,128]{1,0:T(8,128)S(1)}, u32[]{:S(2)}, u32[]{:S(2)}) collective-permute-start(f32[512,128]{1,0:T(8,128)S(1)} %add.89), channel_id=1, source_target_pairs={{0,16},{8,24},{16,0},{24,8},{1,17},{9,25},{17,1},{25,9},{2,18},{10... | collective-permute-start | bytes 786440 | tf_op jit(solution)/shard_map/ppermute | solution.py:310
  64.5 6.7 %collective-permute-start.19 = (f32[512,128]{1,0:T(8,128)S(1)}, f32[512,128]{1,0:T(8,128)S(1)}, u32[]{:S(2)}, u32[]{:S(2)}) collective-permute-start(f32[512,128]{1,0:T(8,128)S(1)} %bitcast_add_fusion), channel_id=1, source_target_pairs={{0,8},{8,0},{16,24},{24,16},{1,9},{9,1},{17,25},{25,17},{2,10},{10... | collective-permute-start | bytes 786440 | tf_op jit(solution)/shard_map/ppermute | solution.py:310
  66.0 5.1 %collective-permute-start.20 = (f32[128,128]{1,0:T(8,128)S(1)}, f32[128,128]{1,0:T(8,128)S(1)}, u32[]{:S(2)}, u32[]{:S(2)}) collective-permute-start(f32[128,128]{1,0:T(8,128)S(1)} %get-tuple-element.35), channel_id=1, source_target_pairs={{0,16},{8,24},{16,0},{24,8},{1,17},{9,25},{17,1},{25,9},{2,18},{10... | collective-permute-start | bytes 196616 | tf_op jit(solution)/shard_map/ppermute | solution.py:310
  71.1 1.3 %collective-permute-start.21 = (f32[128,128]{1,0:T(8,128)S(1)}, f32[128,128]{1,0:T(8,128)S(1)}, u32[]{:S(2)}, u32[]{:S(2)}) collective-permute-start(f32[128,128]{1,0:T(8,128)S(1)} %bitcast_add_fusion.1), channel_id=1, source_target_pairs={{0,1},{1,0},{2,3},{3,2},{4,5},{5,4},{6,7},{7,6},{8,9},{9,8},{10,11... | collective-permute-start | bytes 196616 | tf_op jit(solution)/shard_map/ppermute | solution.py:304

commit v8 on v7

--- a/solution.py
+++ b/solution.py
@@ -50,7 +50,7 @@
     n_col, chunk, panel_dev, node_dev,
     rows_ref, cols_ref, live_ref, deg_ref, feat_ref, blocks_ref, *refs,
 ):
-    outs, dense_ref = refs[:n_col], refs[n_col]
+    outs, tile_ref = refs[:n_col], refs[n_col]
     accs, (both, buf, scaled, result, in_sems, dense_sems, out_sems) = refs[n_col + 1:-7], refs[-7:]
     part = EDGE // len(accs)
     slots = buf.shape[0]
@@ -68,10 +68,9 @@
         span = pl.ds(c * chunk, chunk)
         return pltpu.make_async_copy(blocks_ref.at[0, 0, span], buf.at[span], in_sems.at[c])
 
-    def dense_copy(panel, j):
-        there = pl.ds((panel * panel_dev + j) * node_dev, node_dev)
-        return pltpu.make_async_copy(
-            both.at[j, pl.ds(0, node_dev)], dense_ref.at[there], dense_sems.at[j])
+    def dense_copy(rel, j):
+        there = tile_ref.at[pl.ds(rel * node_dev, node_dev)]
+        return pltpu.make_async_copy(both.at[j, pl.ds(0, node_dev)], there, dense_sems.at[j])
 
     def result_copy(rel, j):
         return pltpu.make_async_copy(result.at[j], outs[rel], out_sems.at[j])
@@ -128,7 +127,7 @@
         for j in reversed(range(panel_dev)):
             rel = panel * panel_dev + j
             if panel:
-                dense_copy(panel - 1, j).wait()
+                dense_copy(rel - panel_dev, j).wait()
                 result_copy(rel - panel_dev, j).wait()
             for b in range(dev_blocks):
                 for cb in range(col_blocks):
@@ -138,14 +137,15 @@
                         at = b * EDGE + q * part
                         both[j, at:at + part, lanes] = hi
                         both[j, node_dev + at:node_dev + at + part, lanes] = lo
-            dense_copy(panel, j).start()
+            dense_copy(rel, j).start()
             pair = jnp.dot(both[j], scaled[...], preferred_element_type=F32)
             result[j] = pair[:node_dev] + pair[node_dev:]
             result_copy(rel, j).start()
 
     for j in range(panel_dev):
-        dense_copy(n_panels - 1, j).wait()
-        result_copy((n_panels - 1) * panel_dev + j, j).wait()
+        rel = (n_panels - 1) * panel_dev + j
+        dense_copy(rel, j).wait()
+        result_copy(rel, j).wait()
 
 
 def middle_kernel(n_col, n_in, scale, deg_ref, cot_ref, weight_ref, *refs):
@@ -189,7 +189,7 @@
         lhs[width:, i * node_dev:(i + 1) * node_dev] = lo
 
 
-def partial_kernel(n_in, dense_ref, *refs):
+def partial_kernel(n_in, tile_ref, *refs):
     parts = refs[:n_in]
     out_ref, wsum_ref, dense, stage, wstage, lhs, sems, wsems, dense_sems = refs[n_in:]
     width, node_dev = stage.shape[1:]
@@ -197,14 +197,14 @@
     half = wstage.shape[1]
     mine = pl.ds(width + (lax.axis_index("col") % 2) * half, half)
     blocks = fetch(
-        [(dense_ref.at[pl.ds(i * node_dev, node_dev)], dense.at[pl.ds(i * node_dev, node_dev)])
-         for i in range(n_in)], dense_sems)
+        [(tile_ref.at[span], dense.at[span]) for span in (
+            pl.ds(i * node_dev, node_dev) for i in range(n_in))], dense_sems)
     copies = fetch([(r.at[pl.ds(0, width)], stage.at[i]) for i, r in enumerate(parts)], sems)
-    weights = fetch([(parts[i].at[mine], wstage.at[i]) for i in range(4)], wsems)
+    weights = fetch([(parts[i].at[mine], wstage.at[i]) for i in range(2)], wsems)
     load_lhs(stage, lhs, copies)
     for copy in weights:
         copy.wait()
-    total = (wstage[0] + wstage[1]) + (wstage[2] + wstage[3])
+    total = wstage[0] + wstage[1]
     for n in range(0, total.shape[1], EDGE):
         wsum_ref[n // EDGE * half:(n // EDGE + 1) * half, :] = total[:, n:n + EDGE]
     for copy in blocks:
@@ -269,7 +269,7 @@
 
     def after(x, other):
         corner = 0.0 * other[:8, :EDGE]
-        if x.shape == other.shape[:1] + x.shape[1:]:
+        if x.shape[0] == other.shape[0] and x.shape[1] <= other.shape[1]:
             return x + 0.0 * other[:, :x.shape[1]]
         return (x.reshape(-1, 8, EDGE) + corner).reshape(x.shape)
 
@@ -312,10 +312,16 @@
     def low_bit(m):
         return (m & -m).bit_length() - 1
 
-    terms = {m: [keep[m], swap(send[m])] for m in range(n_chip - 1, -1, -1)}
-    for m in range(n_chip - 1, 0, -1):
-        terms[m & (m - 1)].append(chip_flip(functools.reduce(jnp.add, terms[m]), low_bit(m)))
-    parts = terms[0]
+    last = n_chip - 1
+    kept = {m: [keep[m], swap(send[m])] for m in range(last, -1, -1)}
+    parts = [functools.reduce(jnp.add, kept[0])]
+    kept[0] = []
+    for m in range(last, 0, -1):
+        unit = functools.reduce(jnp.add, kept[m])
+        if m == 2:
+            unit = after(unit, parts[0])
+        kept[m & (m - 1)].append(chip_flip(unit, low_bit(m)))
+    parts += kept[0]
 
     out_act, pulled, message = pl.pallas_call(
         functools.partial(middle_kernel, n_col, len(parts), float(nodes) ** (-0.5)),
@@ -330,10 +336,10 @@
         name="middle",
     )(deg, cotangent, weight, *parts)
 
-    last = n_chip - 1
-    own = {0: message, 1: chip_flip(message, 0), 2: chip_flip(pulled, 1)}
-    for m in range(3, n_chip):
-        own[m] = chip_flip(own[m & (m - 1)][:width], low_bit(m))
+    own = {0: pulled}
+    for m in range(1, n_chip):
+        own[m] = chip_flip(own[m & (m - 1)], low_bit(m))
+    own[0], own[1] = message, after(own[1], own[2])
     other = {m: swap(own[m]) for m in range(last)}
 
     half = width // 2
@@ -349,10 +355,10 @@
         scratch_shapes=[
             pltpu.VMEM((len(early) * node_dev, col_nodes), BF16),
             pltpu.VMEM((len(early), width, node_dev), F32),
-            pltpu.VMEM((4, half, hidden), F32),
+            pltpu.VMEM((2, half, hidden), F32),
             pltpu.VMEM((2 * width, len(early) * node_dev), BF16),
             pltpu.SemaphoreType.DMA((len(early),)),
-            pltpu.SemaphoreType.DMA((4,)),
+            pltpu.SemaphoreType.DMA((2,)),
             pltpu.SemaphoreType.DMA((len(early),)),
         ],
         compiler_params=params(52),
@@ -362,8 +368,7 @@
 
     own[last] = after(own[last], sofar)
     late = [own[last], swap(own[last])]
-    for t in range(1, chip_bits):
-        wsum = wsum + chip_flip(wsum, t)
+    wsum = wsum + chip_flip(wsum, 0)
     n_piece = max(1, row_bits)
     while col_nodes % (EDGE * n_piece):
         n_piece -= 1
@@ -389,6 +394,9 @@
     done = list(done)
     for t in range(row_bits):
         wsum = after(wsum, done[0])
+        if t == 0:
+            for bit in range(1, chip_bits):
+                wsum = wsum + chip_flip(wsum, bit)
         wsum = wsum + row_flip(wsum, t)
         done = [x + row_flip(x, (i + t) % row_bits) for i, x in enumerate(done)]
         if t == 0:

time: 73.4 us -> 71.7 us (0.977)
  starting transfers between devices: 24.7 us -> 21.9 us
  waiting for transfers between devices: 25.6 us -> 27.5 us
  local copies, waits for them, and re-layouts: 0.92 us -> 0.02 us
    ppermute x7 -> x8, waiting for transfers between devices: 15.6 us -> 18.6 us  [chip_flip(): return lax.ppermute(x, 'col', [(i, i ^ 2 << bit) for i in range(n_col)])]
    ppermute x7 -> x8, starting transfers between devices: 14.7 us -> 12.3 us  [chip_flip(): return lax.ppermute(x, 'col', [(i, i ^ 2 << bit) for i in range(n_col)])]
    ppermute x6, waiting for transfers between devices: 8.91 us -> 6.54 us  [row_flip(): return lax.ppermute(x, 'row', [(i, i ^ 1 << bit) for i in range(n_row)])]
    ppermute x9, waiting for transfers between devices: 1.07 us -> 2.39 us  [swap(): return lax.ppermute(x, 'col', swap_pairs)]
    add x1 -> x3, other arithmetic: 0.02 us -> 1.05 us  [after(): return x + 0.0 * other[:, :x.shape[1]]]
    add x3, other arithmetic: 2.77 us -> 1.86 us  [the longest x2 1.85 us: body(): unit = functools.reduce(jnp.add, kept[m])]
    unnamed x8 -> x6, local copies, waits for them, and re-layouts: 0.91 us -> 0.01 us
  transfers between devices with their start and end apart: 22 -> 23, of which waited for: 9 -> 14; matrix products, arithmetic and copies ran while one was open for 5% -> 5% of each run, Pallas kernels for 7% -> 7%
where the time goes in v8:
time: 71.7 us; the launch traced here: 71.5 us
  waiting for transfers between devices  27.5 us (38%)
  starting transfers between devices  21.9 us (31%)
  Pallas kernels  15.9 us (22%)
  other arithmetic  4.59 us (6%)
  between operations  1.5 us (2%)
    ppermute x8, waiting for transfers between devices, chip_flip(): return lax.ppermute(x, 'col', [(i, i ^ 2 << bit) for i in range(n_col)])  18.6 us
    ppermute x8, starting transfers between devices, chip_flip(): return lax.ppermute(x, 'col', [(i, i ^ 2 << bit) for i in range(n_col)])  12.3 us
    pallas_call x1, Pallas kernels, body(): pl.pallas_call(functools.partial(forward_kernel, n_col, chunk, panel_dev,...  10 us
    ppermute x6, starting transfers between devices, row_flip(): return lax.ppermute(x, 'row', [(i, i ^ 1 << bit) for i in range(n_row)])  7.8 us
    ppermute x6, waiting for transfers between devices, row_flip(): return lax.ppermute(x, 'row', [(i, i ^ 1 << bit) for i in range(n_row)])  6.54 us
    pallas_call x1, Pallas kernels, body(): pl.pallas_call(functools.partial(partial_kernel, len(early)), out_shape=(...  2.93 us
    ppermute x9, waiting for transfers between devices, swap(): return lax.ppermute(x, 'col', swap_pairs)  2.39 us
    pallas_call x1, Pallas kernels, body(): pl.pallas_call(functools.partial(last_kernel, len(late), n_piece), out_sh...  1.87 us
  transfers between devices with their start and end apart: 23, of which 14 were waited for; matrix products, arithmetic and copies ran while one was open for 5% of the time, Pallas kernels for 7%

profile of v8, /device:TPU:0, one launch (start us, length us, event | category | flops | bytes accessed | tf_op | source)
XLA Modules:
  0.0 71.5 jit_solution(6253675867967488983)
XLA Ops:
  1.3 10.0 %densify_forward.1 = (f32[256,128]{1,0:T(8,128)}, f32[256,128]{1,0:T(8,128)}, f32[256,128]{1,0:T(8,128)}, f32[256,128]{1,0:T(8,128)}, f32[256,128]{1,0:T(8,128)}...) custom-call(s32[1,1,384]{2,1,0:T(1,128)} %rows_ref.1, ...), custom_call_target="tpu_custom_call" | custom-call | tf_op jit(solution)/shard_map/densify_forward/pallas_call | solution.py:279
  12.5 0.6 collective-permute-done.2
  13.1 0.9 %add.98 = f32[256,128]{1,0:T(8,128)S(1)} add(f32[256,128]{1,0:T(8,128)} %get-tuple-element.23, f32[256,128]{1,0:T(8,128)S(1)} %collective-permute-done.2) | non-fusion elementwise | flops 32768 | bytes 393216 | tf_op jit(solution)/shard_map/add | solution.py:320
  14.0 3.0 %collective-permute-start.3 = (f32[256,128]{1,0:T(8,128)S(1)}, f32[256,128]{1,0:T(8,128)S(1)}, u32[]{:S(2)}, u32[]{:S(2)}) collective-permute-start(f32[256,128]{1,0:T(8,128)S(1)} %add.98), channel_id=1, source_target_pairs={{0,2},{1,3},{2,0},{3,1},{4,6},{5,7},{6,4},{7,5},{8,10},{9,11},{10,... | collective-permute-start | bytes 393224 | tf_op jit(solution)/shard_map/ppermute | solution.py:307
  17.0 0.9 %add.101 = f32[256,128]{1,0:T(8,128)S(1)} add(f32[256,128]{1,0:T(8,128)} %get-tuple-element.25, f32[256,128]{1,0:T(8,128)S(1)} %collective-permute-done.5) | non-fusion elementwise | flops 32768 | bytes 393216 | tf_op jit(solution)/shard_map/add | solution.py:320
  18.1 3.1 %collective-permute-done.3 = f32[256,128]{1,0:T(8,128)S(1)} collective-permute-done((f32[256,128]{1,0:T(8,128)S(1)}, f32[256,128]{1,0:T(8,128)S(1)}, u32[]{:S(2)}, u32[]{:S(2)}) %collective-permute-start.3) | collective-permute-done | bytes 131104 | tf_op jit(solution)/shard_map/ppermute | solution.py:307
  21.1 1.0 %multiply_add_fusion.2 = (f32[256,128]{1,0:T(8,128)S(1)}, f32[256,128]{1,0:T(8,128)S(1)}) fusion(f32[256,128]{1,0:T(8,128)S(1)} %collective-permute-done.3, f32[256,128]{1,0:T(8,128)} %get-tuple-element.21, f32[256,128]{1,0:T(8,128)S(1)} %collective-permute-done.1, f32[256,128]{1,0:T(8,128)} %get-tuple-element.19, f32[256,128]{1,0:T(8,128)S(1)} %collective-permute-done), kind=kLoop, calls=%fused_computation.5 | loop fusion | flops 163840 | bytes 917504 | tf_op jit(solution)/shard_map/add | solution.py:273
  22.1 3.0 %collective-permute-start.4 = (f32[256,128]{1,0:T(8,128)S(1)}, f32[256,128]{1,0:T(8,128)S(1)}, u32[]{:S(2)}, u32[]{:S(2)}) collective-permute-start(f32[256,128]{1,0:T(8,128)S(1)} %get-tuple-element.37), channel_id=1, source_target_pairs={{0,4},{1,5},{2,6},{3,7},{4,0},{5,1},{6,2},{7,3},{8,12},{9,13},{10,... | collective-permute-start | bytes 393224 | tf_op jit(solution)/shard_map/ppermute | solution.py:307
  25.1 5.5 %collective-permute-done.4.refs_1_ = f32[256,128]{1,0:T(8,128)S(1)} collective-permute-done((f32[256,128]{1,0:T(8,128)S(1)}, f32[256,128]{1,0:T(8,128)S(1)}, u32[]{:S(2)}, u32[]{:S(2)}) %collective-permute-start.4) | collective-permute-done | bytes 131104 | tf_op jit(solution)/shard_map/ppermute | solution.py:307
  30.7 1.1 %middle.1 = (bf16[256,256]{1,0:T(8,128)(2,1)}, f32[128,256]{1,0:T(8,128)S(1)}, f32[256,256]{1,0:T(8,128)S(1)}) custom-call(s32[64,128]{1,0:T(8,128)S(1)} %bitcast.10, bf16[256,256]{1,0:T(8,128)(2,1)S(1)} %copy-done.1, bf16[128,256]{1,0:T(8,128)(2,1)S(1)} %copy-done.2, f32[256,128]{1,0:T(8,128)S(1)} %get-tuple-element.38.refs_0_, ...), custom_call_target="tpu_custom_call" | custom-call | tf_op jit(solution)/shard_map/middle/pallas_call | solution.py:326
  32.3 3.4 %collective-permute-start.9 = (f32[128,256]{1,0:T(8,128)S(1)}, f32[128,256]{1,0:T(8,128)S(1)}, u32[]{:S(2)}, u32[]{:S(2)}) collective-permute-start(f32[128,256]{1,0:T(8,128)S(1)} %get-tuple-element.30), channel_id=1, source_target_pairs={{0,4},{1,5},{2,6},{3,7},{4,0},{5,1},{6,2},{7,3},{8,12},{9,13},{10,... | collective-permute-start | bytes 393224 | tf_op jit(solution)/shard_map/ppermute | solution.py:307
  35.7 3.2 %collective-permute-done.8 = f32[128,256]{1,0:T(8,128)S(1)} collective-permute-done((f32[128,256]{1,0:T(8,128)S(1)}, f32[128,256]{1,0:T(8,128)S(1)}, u32[]{:S(2)}, u32[]{:S(2)}) %collective-permute-start.8) | collective-permute-done | bytes 131104 | tf_op jit(solution)/shard_map/ppermute | solution.py:307
  38.9 2.2 %collective-permute-done.9.refs_4_ = f32[128,256]{1,0:T(8,128)S(1)} collective-permute-done((f32[128,256]{1,0:T(8,128)S(1)}, f32[128,256]{1,0:T(8,128)S(1)}, u32[]{:S(2)}, u32[]{:S(2)}) %collective-permute-start.9) | collective-permute-done | bytes 131104 | tf_op jit(solution)/shard_map/ppermute | solution.py:307
  42.0 0.6 collective-permute-done.10.refs_3_
  42.8 2.9 %backward_early.1 = (f32[128,1024]{1,0:T(8,128)S(1)}, f32[128,128]{1,0:T(8,128)S(1)}) custom-call(bf16[2048,1024]{1,0:T(8,128)(2,1)} %get-tuple-element.28.tile_ref.dense_ref, f32[256,256]{1,0:T(8,128)S(1)} %get-tuple-element.29.refs_0_, f32[256,256]{1,0:T(8,128)S(1)} %collective-permute-done.7.refs_1_, f32[128,256]{1,0:T(8,128)S(1)} %multiply_add_fusion.1.refs_2_, ...), custom_call_target="tpu_custom_call" | custom-call | flops 1073741824 | bytes 33554432 | tf_op jit(solution)/shard_map/backward_early/pallas_call | solution.py:347
  45.7 1.5 %collective-permute-done.12 = f32[128,256]{1,0:T(8,128)S(1)} collective-permute-done((f32[128,256]{1,0:T(8,128)S(1)}, f32[128,256]{1,0:T(8,128)S(1)}, u32[]{:S(2)}, u32[]{:S(2)}) %collective-permute-start.12) | collective-permute-done | bytes 131104 | tf_op jit(solution)/shard_map/ppermute | solution.py:307
  47.7 1.0 %collective-permute-done.13.refs_1_ = f32[128,256]{1,0:T(8,128)S(1)} collective-permute-done((f32[128,256]{1,0:T(8,128)S(1)}, f32[128,256]{1,0:T(8,128)S(1)}, u32[]{:S(2)}, u32[]{:S(2)}) %collective-permute-start.13) | collective-permute-done | bytes 131104 | tf_op jit(solution)/shard_map/ppermute | solution.py:304
  48.7 1.9 %backward_late.1 = (f32[512,128]{1,0:T(8,128)S(1)}, f32[512,128]{1,0:T(8,128)S(1)}) custom-call(s32[64,128]{1,0:T(8,128)S(1)} %bitcast.11, bf16[2048,1024]{1,0:T(8,128)(2,1)} %get-tuple-element.28.tile_ref.dense_ref, f32[128,1024]{1,0:T(8,128)S(1)} %get-tuple-element.31.sofar_ref, f32[128,256]{1,0:T(8,128)S(1)} %multiply_add_fusion.refs_0_, ...), custom_call_target="tpu_custom_call" | custom-call | tf_op jit(solution)/shard_map/backward_late/pallas_call | solution.py:376
  50.6 1.6 %collective-permute-start.14 = (f32[512,128]{1,0:T(8,128)S(1)}, f32[512,128]{1,0:T(8,128)S(1)}, u32[]{:S(2)}, u32[]{:S(2)}) collective-permute-start(f32[512,128]{1,0:T(8,128)S(1)} %get-tuple-element.32), channel_id=1, source_target_pairs={{0,8},{8,0},{16,24},{24,16},{1,9},{9,1},{17,25},{25,17},{2,10},{10... | collective-permute-start | bytes 786440 | tf_op jit(solution)/shard_map/ppermute | solution.py:310
  52.1 1.7 %collective-permute-start.18 = (f32[128,128]{1,0:T(8,128)S(1)}, f32[128,128]{1,0:T(8,128)S(1)}, u32[]{:S(2)}, u32[]{:S(2)}) collective-permute-start(f32[128,128]{1,0:T(8,128)S(1)} %bitcast_add_fusion.3), channel_id=1, source_target_pairs={{0,4},{1,5},{2,6},{3,7},{4,0},{5,1},{6,2},{7,3},{8,12},{9,13},{10,... | collective-permute-start | bytes 196616 | tf_op jit(solution)/shard_map/ppermute | solution.py:307
  53.9 1.5 %collective-permute-start.16 = (f32[512,128]{1,0:T(8,128)S(1)}, f32[512,128]{1,0:T(8,128)S(1)}, u32[]{:S(2)}, u32[]{:S(2)}) collective-permute-start(f32[512,128]{1,0:T(8,128)S(1)} %get-tuple-element.33), channel_id=1, source_target_pairs={{0,16},{8,24},{16,0},{24,8},{1,17},{9,25},{17,1},{25,9},{2,18},{10... | collective-permute-start | bytes 786440 | tf_op jit(solution)/shard_map/ppermute | solution.py:310
  55.4 3.0 %collective-permute-done.18 = f32[128,128]{1,0:T(8,128)S(1)} collective-permute-done((f32[128,128]{1,0:T(8,128)S(1)}, f32[128,128]{1,0:T(8,128)S(1)}, u32[]{:S(2)}, u32[]{:S(2)}) %collective-permute-start.18) | collective-permute-done | bytes 65568 | tf_op jit(solution)/shard_map/ppermute | solution.py:307
  58.4 0.8 %collective-permute-start.19 = (f32[128,128]{1,0:T(8,128)S(1)}, f32[128,128]{1,0:T(8,128)S(1)}, u32[]{:S(2)}, u32[]{:S(2)}) collective-permute-start(f32[128,128]{1,0:T(8,128)S(1)} %add.111), channel_id=1, source_target_pairs={{0,8},{8,0},{16,24},{24,16},{1,9},{9,1},{17,25},{25,17},{2,10},{10... | collective-permute-start | bytes 196616 | tf_op jit(solution)/shard_map/ppermute | solution.py:310
  59.2 1.6 %collective-permute-start.15 = (f32[512,128]{1,0:T(8,128)S(1)}, f32[512,128]{1,0:T(8,128)S(1)}, u32[]{:S(2)}, u32[]{:S(2)}) collective-permute-start(f32[512,128]{1,0:T(8,128)S(1)} %add.104), channel_id=1, source_target_pairs={{0,16},{8,24},{16,0},{24,8},{1,17},{9,25},{17,1},{25,9},{2,18},{10... | collective-permute-start | bytes 786440 | tf_op jit(solution)/shard_map/ppermute | solution.py:310
  60.8 1.9 %collective-permute-done.19 = f32[128,128]{1,0:T(8,128)S(1)} collective-permute-done((f32[128,128]{1,0:T(8,128)S(1)}, f32[128,128]{1,0:T(8,128)S(1)}, u32[]{:S(2)}, u32[]{:S(2)}) %collective-permute-start.19) | collective-permute-done | bytes 65568 | tf_op jit(solution)/shard_map/ppermute | solution.py:310
  62.8 0.8 %collective-permute-start.20 = (f32[512,128]{1,0:T(8,128)S(1)}, f32[512,128]{1,0:T(8,128)S(1)}, u32[]{:S(2)}, u32[]{:S(2)}) collective-permute-start(f32[512,128]{1,0:T(8,128)S(1)} %bitcast_add_fusion), channel_id=1, source_target_pairs={{0,8},{8,0},{16,24},{24,16},{1,9},{9,1},{17,25},{25,17},{2,10},{10... | collective-permute-start | bytes 786440 | tf_op jit(solution)/shard_map/ppermute | solution.py:310
  63.6 1.5 %collective-permute-start.21 = (f32[128,128]{1,0:T(8,128)S(1)}, f32[128,128]{1,0:T(8,128)S(1)}, u32[]{:S(2)}, u32[]{:S(2)}) collective-permute-start(f32[128,128]{1,0:T(8,128)S(1)} %get-tuple-element.35), channel_id=1, source_target_pairs={{0,16},{8,24},{16,0},{24,8},{1,17},{9,25},{17,1},{25,9},{2,18},{10... | collective-permute-start | bytes 196616 | tf_op jit(solution)/shard_map/ppermute | solution.py:310
  65.1 2.9 %collective-permute-done.15 = f32[512,128]{1,0:T(8,128)S(1)} collective-permute-done((f32[512,128]{1,0:T(8,128)S(1)}, f32[512,128]{1,0:T(8,128)S(1)}, u32[]{:S(2)}, u32[]{:S(2)}) %collective-permute-start.15) | collective-permute-done | bytes 262176 | tf_op jit(solution)/shard_map/ppermute | solution.py:310
  68.0 0.7 collective-permute-done.21
  68.8 1.1 %collective-permute-done.20 = f32[512,128]{1,0:T(8,128)S(1)} collective-permute-done((f32[512,128]{1,0:T(8,128)S(1)}, f32[512,128]{1,0:T(8,128)S(1)}, u32[]{:S(2)}, u32[]{:S(2)}) %collective-permute-start.20) | collective-permute-done | bytes 262176 | tf_op jit(solution)/shard_map/ppermute | solution.py:310
  70.0 0.8 %pad_maximum_fusion = f32[1024,128]{1,0:T(8,128)} fusion(f32[512,128]{1,0:T(8,128)S(1)} %add.116, f32[512,128]{1,0:T(8,128)S(1)} %add.105), kind=kLoop, calls=%fused_computation | loop fusion | flops 131072 | bytes 1048576 | tf_op jit(solution)/shard_map/concatenate | solution.py:405
  70.8 0.7 maximum_maximum_fusion
  (45 shorter events, 3.5 us)
Async XLA Ops:
  0.6 30.0 %copy-start = (s32[8192]{0:T(1024)S(1)}, s32[8192]{0:T(1024)}, u32[]{:S(2)}) copy-start(s32[8192]{0:T(1024)} %param.9) | copy-start | bytes 98308
  0.6 30.0 %copy-start.1 = (bf16[256,256]{1,0:T(8,128)(2,1)S(1)}, bf16[256,256]{1,0:T(8,128)(2,1)}, u32[]{:S(2)}) copy-start(bf16[256,256]{1,0:T(8,128)(2,1)} %cot_ref.1) | copy-start | bytes 393220
  0.7 30.0 %copy-start.2 = (bf16[128,256]{1,0:T(8,128)(2,1)S(1)}, bf16[128,256]{1,0:T(8,128)(2,1)}, u32[]{:S(2)}) copy-start(bf16[128,256]{1,0:T(8,128)(2,1)} %weight_ref.1) | copy-start | bytes 196612
  11.4 1.7 %collective-permute-start.2 = (f32[256,128]{1,0:T(8,128)}, f32[256,128]{1,0:T(8,128)S(1)}, u32[]{:S(2)}, u32[]{:S(2)}) collective-permute-start(f32[256,128]{1,0:T(8,128)} %get-tuple-element.24), channel_id=1, source_target_pairs={{0,1},{1,0},{2,3},{3,2},{4,5},{5,4},{6,7},{7,6},{8,9},{9,8},{10,11... | collective-permute-start | bytes 393224 | tf_op jit(solution)/shard_map/ppermute | solution.py:304
  11.9 6.1 %collective-permute-start.1 = (f32[256,128]{1,0:T(8,128)}, f32[256,128]{1,0:T(8,128)S(1)}, u32[]{:S(2)}, u32[]{:S(2)}) collective-permute-start(f32[256,128]{1,0:T(8,128)} %get-tuple-element.22), channel_id=1, source_target_pairs={{0,1},{1,0},{2,3},{3,2},{4,5},{5,4},{6,7},{7,6},{8,9},{9,8},{10,11... | collective-permute-start | bytes 393224 | tf_op jit(solution)/shard_map/ppermute | solution.py:304
  12.0 5.0 %collective-permute-start.5 = (f32[256,128]{1,0:T(8,128)}, f32[256,128]{1,0:T(8,128)S(1)}, u32[]{:S(2)}, u32[]{:S(2)}) collective-permute-start(f32[256,128]{1,0:T(8,128)} %get-tuple-element.26), channel_id=1, source_target_pairs={{0,1},{1,0},{2,3},{3,2},{4,5},{5,4},{6,7},{7,6},{8,9},{9,8},{10,11... | collective-permute-start | bytes 393224 | tf_op jit(solution)/shard_map/ppermute | solution.py:304
  12.4 5.6 %collective-permute-start = (f32[256,128]{1,0:T(8,128)}, f32[256,128]{1,0:T(8,128)S(1)}, u32[]{:S(2)}, u32[]{:S(2)}) collective-permute-start(f32[256,128]{1,0:T(8,128)} %get-tuple-element.20), channel_id=1, source_target_pairs={{0,1},{1,0},{2,3},{3,2},{4,5},{5,4},{6,7},{7,6},{8,9},{9,8},{10,11... | collective-permute-start | bytes 393224 | tf_op jit(solution)/shard_map/ppermute | solution.py:304
  14.0 7.1 %collective-permute-start.3 = (f32[256,128]{1,0:T(8,128)S(1)}, f32[256,128]{1,0:T(8,128)S(1)}, u32[]{:S(2)}, u32[]{:S(2)}) collective-permute-start(f32[256,128]{1,0:T(8,128)S(1)} %add.98), channel_id=1, source_target_pairs={{0,2},{1,3},{2,0},{3,1},{4,6},{5,7},{6,4},{7,5},{8,10},{9,11},{10,... | collective-permute-start | bytes 393224 | tf_op jit(solution)/shard_map/ppermute | solution.py:307
  18.0 7.2 %collective-permute-start.6 = (f32[256,128]{1,0:T(8,128)S(1)}, f32[256,128]{1,0:T(8,128)S(1)}, u32[]{:S(2)}, u32[]{:S(2)}) collective-permute-start(f32[256,128]{1,0:T(8,128)S(1)} %add.101), channel_id=1, source_target_pairs={{0,2},{1,3},{2,0},{3,1},{4,6},{5,7},{6,4},{7,5},{8,10},{9,11},{10,... | collective-permute-start | bytes 393224 | tf_op jit(solution)/shard_map/ppermute | solution.py:307
  22.1 8.5 %collective-permute-start.4 = (f32[256,128]{1,0:T(8,128)S(1)}, f32[256,128]{1,0:T(8,128)S(1)}, u32[]{:S(2)}, u32[]{:S(2)}) collective-permute-start(f32[256,128]{1,0:T(8,128)S(1)} %get-tuple-element.37), channel_id=1, source_target_pairs={{0,4},{1,5},{2,6},{3,7},{4,0},{5,1},{6,2},{7,3},{8,12},{9,13},{10,... | collective-permute-start | bytes 393224 | tf_op jit(solution)/shard_map/ppermute | solution.py:307
  31.8 7.1 %collective-permute-start.8 = (f32[128,256]{1,0:T(8,128)S(1)}, f32[128,256]{1,0:T(8,128)S(1)}, u32[]{:S(2)}, u32[]{:S(2)}) collective-permute-start(f32[128,256]{1,0:T(8,128)S(1)} %get-tuple-element.30), channel_id=1, source_target_pairs={{0,2},{1,3},{2,0},{3,1},{4,6},{5,7},{6,4},{7,5},{8,10},{9,11},{10,... | collective-permute-start | bytes 393224 | tf_op jit(solution)/shard_map/ppermute | solution.py:307
  32.3 8.9 %collective-permute-start.9 = (f32[128,256]{1,0:T(8,128)S(1)}, f32[128,256]{1,0:T(8,128)S(1)}, u32[]{:S(2)}, u32[]{:S(2)}) collective-permute-start(f32[128,256]{1,0:T(8,128)S(1)} %get-tuple-element.30), channel_id=1, source_target_pairs={{0,4},{1,5},{2,6},{3,7},{4,0},{5,1},{6,2},{7,3},{8,12},{9,13},{10,... | collective-permute-start | bytes 393224 | tf_op jit(solution)/shard_map/ppermute | solution.py:307
  35.7 6.3 %collective-permute-start.7 = (f32[256,256]{1,0:T(8,128)S(1)}, f32[256,256]{1,0:T(8,128)S(1)}, u32[]{:S(2)}, u32[]{:S(2)}) collective-permute-start(f32[256,256]{1,0:T(8,128)S(1)} %get-tuple-element.29.refs_0_), channel_id=1, source_target_pairs={{0,1},{1,0},{2,3},{3,2},{4,5},{5,4},{6,7},{7,6},{8,9},{9,8},{10,11... | collective-permute-start | bytes 786440 | tf_op jit(solution)/shard_map/ppermute | solution.py:304
  41.2 1.4 %collective-permute-start.10 = (f32[128,256]{1,0:T(8,128)S(1)}, f32[128,256]{1,0:T(8,128)S(1)}, u32[]{:S(2)}, u32[]{:S(2)}) collective-permute-start(f32[128,256]{1,0:T(8,128)S(1)} %multiply_add_fusion.1.refs_2_), channel_id=1, source_target_pairs={{0,1},{1,0},{2,3},{3,2},{4,5},{5,4},{6,7},{7,6},{8,9},{9,8},{10,11... | collective-permute-start | bytes 393224 | tf_op jit(solution)/shard_map/ppermute | solution.py:304
  41.3 1.5 %collective-permute-start.11 = (f32[128,256]{1,0:T(8,128)S(1)}, f32[128,256]{1,0:T(8,128)S(1)}, u32[]{:S(2)}, u32[]{:S(2)}) collective-permute-start(f32[128,256]{1,0:T(8,128)S(1)} %collective-permute-done.9.refs_4_), channel_id=1, source_target_pairs={{0,1},{1,0},{2,3},{3,2},{4,5},{5,4},{6,7},{7,6},{8,9},{9,8},{10,11... | collective-permute-start | bytes 393224 | tf_op jit(solution)/shard_map/ppermute | solution.py:304
  41.8 5.5 %collective-permute-start.12 = (f32[128,256]{1,0:T(8,128)S(1)}, f32[128,256]{1,0:T(8,128)S(1)}, u32[]{:S(2)}, u32[]{:S(2)}) collective-permute-start(f32[128,256]{1,0:T(8,128)S(1)} %collective-permute-done.9.refs_4_), channel_id=1, source_target_pairs={{0,2},{1,3},{2,0},{3,1},{4,6},{5,7},{6,4},{7,5},{8,10},{9,11},{10,... | collective-permute-start | bytes 393224 | tf_op jit(solution)/shard_map/ppermute | solution.py:307
  47.3 1.4 %collective-permute-start.13 = (f32[128,256]{1,0:T(8,128)S(1)}, f32[128,256]{1,0:T(8,128)S(1)}, u32[]{:S(2)}, u32[]{:S(2)}) collective-permute-start(f32[128,256]{1,0:T(8,128)S(1)} %multiply_add_fusion.refs_0_), channel_id=1, source_target_pairs={{0,1},{1,0},{2,3},{3,2},{4,5},{5,4},{6,7},{7,6},{8,9},{9,8},{10,11... | collective-permute-start | bytes 393224 | tf_op jit(solution)/shard_map/ppermute | solution.py:304
  47.3 4.8 %collective-permute-start.17 = (f32[128,128]{1,0:T(8,128)S(1)}, f32[128,128]{1,0:T(8,128)S(1)}, u32[]{:S(2)}, u32[]{:S(2)}) collective-permute-start(f32[128,128]{1,0:T(8,128)S(1)} %get-tuple-element.34), channel_id=1, source_target_pairs={{0,2},{1,3},{2,0},{3,1},{4,6},{5,7},{6,4},{7,5},{8,10},{9,11},{10,... | collective-permute-start | bytes 196616 | tf_op jit(solution)/shard_map/ppermute | solution.py:307
  50.6 8.6 %collective-permute-start.14 = (f32[512,128]{1,0:T(8,128)S(1)}, f32[512,128]{1,0:T(8,128)S(1)}, u32[]{:S(2)}, u32[]{:S(2)}) collective-permute-start(f32[512,128]{1,0:T(8,128)S(1)} %get-tuple-element.32), channel_id=1, source_target_pairs={{0,8},{8,0},{16,24},{24,16},{1,9},{9,1},{17,25},{25,17},{2,10},{10... | collective-permute-start | bytes 786440 | tf_op jit(solution)/shard_map/ppermute | solution.py:310
  52.1 6.2 %collective-permute-start.18 = (f32[128,128]{1,0:T(8,128)S(1)}, f32[128,128]{1,0:T(8,128)S(1)}, u32[]{:S(2)}, u32[]{:S(2)}) collective-permute-start(f32[128,128]{1,0:T(8,128)S(1)} %bitcast_add_fusion.3), channel_id=1, source_target_pairs={{0,4},{1,5},{2,6},{3,7},{4,0},{5,1},{6,2},{7,3},{8,12},{9,13},{10,... | collective-permute-start | bytes 196616 | tf_op jit(solution)/shard_map/ppermute | solution.py:307
  53.9 8.9 %collective-permute-start.16 = (f32[512,128]{1,0:T(8,128)S(1)}, f32[512,128]{1,0:T(8,128)S(1)}, u32[]{:S(2)}, u32[]{:S(2)}) collective-permute-start(f32[512,128]{1,0:T(8,128)S(1)} %get-tuple-element.33), channel_id=1, source_target_pairs={{0,16},{8,24},{16,0},{24,8},{1,17},{9,25},{17,1},{25,9},{2,18},{10... | collective-permute-start | bytes 786440 | tf_op jit(solution)/shard_map/ppermute | solution.py:310
  58.4 4.3 %collective-permute-start.19 = (f32[128,128]{1,0:T(8,128)S(1)}, f32[128,128]{1,0:T(8,128)S(1)}, u32[]{:S(2)}, u32[]{:S(2)}) collective-permute-start(f32[128,128]{1,0:T(8,128)S(1)} %add.111), channel_id=1, source_target_pairs={{0,8},{8,0},{16,24},{24,16},{1,9},{9,1},{17,25},{25,17},{2,10},{10... | collective-permute-start | bytes 196616 | tf_op jit(solution)/shard_map/ppermute | solution.py:310
  59.2 8.7 %collective-permute-start.15 = (f32[512,128]{1,0:T(8,128)S(1)}, f32[512,128]{1,0:T(8,128)S(1)}, u32[]{:S(2)}, u32[]{:S(2)}) collective-permute-start(f32[512,128]{1,0:T(8,128)S(1)} %add.104), channel_id=1, source_target_pairs={{0,16},{8,24},{16,0},{24,8},{1,17},{9,25},{17,1},{25,9},{2,18},{10... | collective-permute-start | bytes 786440 | tf_op jit(solution)/shard_map/ppermute | solution.py:310
  62.8 7.1 %collective-permute-start.20 = (f32[512,128]{1,0:T(8,128)S(1)}, f32[512,128]{1,0:T(8,128)S(1)}, u32[]{:S(2)}, u32[]{:S(2)}) collective-permute-start(f32[512,128]{1,0:T(8,128)S(1)} %bitcast_add_fusion), channel_id=1, source_target_pairs={{0,8},{8,0},{16,24},{24,16},{1,9},{9,1},{17,25},{25,17},{2,10},{10... | collective-permute-start | bytes 786440 | tf_op jit(solution)/shard_map/ppermute | solution.py:310
  63.6 5.1 %collective-permute-start.21 = (f32[128,128]{1,0:T(8,128)S(1)}, f32[128,128]{1,0:T(8,128)S(1)}, u32[]{:S(2)}, u32[]{:S(2)}) collective-permute-start(f32[128,128]{1,0:T(8,128)S(1)} %get-tuple-element.35), channel_id=1, source_target_pairs={{0,16},{8,24},{16,0},{24,8},{1,17},{9,25},{17,1},{25,9},{2,18},{10... | collective-permute-start | bytes 196616 | tf_op jit(solution)/shard_map/ppermute | solution.py:310
  68.7 2.1 %collective-permute-start.22 = (f32[128,128]{1,0:T(8,128)S(1)}, f32[128,128]{1,0:T(8,128)S(1)}, u32[]{:S(2)}, u32[]{:S(2)}) collective-permute-start(f32[128,128]{1,0:T(8,128)S(1)} %bitcast_add_fusion.1), channel_id=1, source_target_pairs={{0,1},{1,0},{2,3},{3,2},{4,5},{5,4},{6,7},{7,6},{8,9},{9,8},{10,11... | collective-permute-start | bytes 196616 | tf_op jit(solution)/shard_map/ppermute | solution.py:304

commit v9 on v8

--- a/solution.py
+++ b/solution.py
@@ -13,6 +13,7 @@
 GROUP = 16
 QUARTERS = 4
 AHEAD = 3
+BWD = 50
 ACC_BYTES = 8 << 20
 GELU_C = 0.7978845608028654
 GELU_K = 0.044715
@@ -150,7 +151,7 @@
 
 def middle_kernel(n_col, n_in, scale, deg_ref, cot_ref, weight_ref, *refs):
     parts = refs[:n_in]
-    act_ref, pulled_ref, message_ref = refs[n_in:]
+    act_ref, pulled_ref, keep_ref, send_ref = refs[n_in:]
     node_dev = cot_ref.shape[0]
     dev_blocks = node_dev // EDGE
     base = (lax.axis_index("row") * n_col + lax.axis_index("col")) * dev_blocks
@@ -173,11 +174,16 @@
         jnp.concatenate([hi, lo], axis=0), weight, (((1,), (1,)), ((), ())),
         preferred_element_type=F32,
     )
-    pulled = jnp.transpose(inv * (pair[:node_dev] + pair[node_dev:]))
-    pulled_ref[...] = pulled
-    message_ref[:EDGE] = pulled
+    pulled_ref[...] = jnp.transpose(inv * (pair[:node_dev] + pair[node_dev:]))
     pair = across(jnp.concatenate([prop_hi, prop_lo], axis=1), hi)
-    message_ref[EDGE:] = scale * (pair[:EDGE] + (pair[EDGE:] + across(prop_hi, lo)))
+    part = scale * (pair[:EDGE] + (pair[EDGE:] + across(prop_hi, lo)))
+    half = EDGE // 2
+    low = lax.axis_index("col") % 2 == 0
+    for n in range(0, part.shape[1], EDGE):
+        upper, lower = part[:half, n:n + EDGE], part[half:, n:n + EDGE]
+        rows = pl.ds(n // EDGE * half, half)
+        keep_ref[rows, :] = jnp.where(low, upper, lower)
+        send_ref[rows, :] = jnp.where(low, lower, upper)
 
 
 def load_lhs(stage, lhs, copies):
@@ -191,28 +197,24 @@
 
 def partial_kernel(n_in, tile_ref, *refs):
     parts = refs[:n_in]
-    out_ref, wsum_ref, dense, stage, wstage, lhs, sems, wsems, dense_sems = refs[n_in:]
+    out_ref, rest_ref, dense, stage, lhs, sems, dense_sems, rest_sem = refs[n_in:]
     width, node_dev = stage.shape[1:]
     col_nodes = dense.shape[1]
-    half = wstage.shape[1]
-    mine = pl.ds(width + (lax.axis_index("col") % 2) * half, half)
     blocks = fetch(
         [(tile_ref.at[span], dense.at[span]) for span in (
             pl.ds(i * node_dev, node_dev) for i in range(n_in))], dense_sems)
-    copies = fetch([(r.at[pl.ds(0, width)], stage.at[i]) for i, r in enumerate(parts)], sems)
-    weights = fetch([(parts[i].at[mine], wstage.at[i]) for i in range(2)], wsems)
+    copies = fetch([(r, stage.at[i]) for i, r in enumerate(parts)], sems)
+    rest = pltpu.make_async_copy(
+        tile_ref.at[pl.ds(n_in * node_dev, rest_ref.shape[0])], rest_ref, rest_sem)
+    rest.start()
     load_lhs(stage, lhs, copies)
-    for copy in weights:
-        copy.wait()
-    total = wstage[0] + wstage[1]
-    for n in range(0, total.shape[1], EDGE):
-        wsum_ref[n // EDGE * half:(n // EDGE + 1) * half, :] = total[:, n:n + EDGE]
     for copy in blocks:
         copy.wait()
     step = 2 * EDGE if col_nodes % (2 * EDGE) == 0 else EDGE
     for n in range(0, col_nodes, step):
         pair = jnp.dot(lhs[...], dense[:, n:n + step], preferred_element_type=F32)
         out_ref[:, n:n + step] = pair[:width] + pair[width:]
+    rest.wait()
 
 
 def last_kernel(n_in, n_out, deg_ref, dense_ref, sofar_ref, *refs):
@@ -220,9 +222,7 @@
     dense, stage, lhs, sofar, sems, dense_sem, sofar_sem = refs[n_in + n_out:]
     width, node_dev = parts[0].shape
     col_nodes = dense.shape[1]
-    rows = n_in * node_dev
-    block = pltpu.make_async_copy(
-        dense_ref.at[pl.ds(dense_ref.shape[0] - rows, rows)], dense, dense_sem)
+    block = pltpu.make_async_copy(dense_ref, dense, dense_sem)
     before = pltpu.make_async_copy(sofar_ref, sofar, sofar_sem)
     block.start()
     size = col_nodes // n_out
@@ -273,6 +273,9 @@
             return x + 0.0 * other[:, :x.shape[1]]
         return (x.reshape(-1, 8, EDGE) + corner).reshape(x.shape)
 
+    def ahead(x):
+        return lax.optimization_barrier(x)
+
     def cost(flops, read):
         return pl.CostEstimate(flops=flops, bytes_accessed=read, transcendentals=0)
 
@@ -315,23 +318,30 @@
     last = n_chip - 1
     kept = {m: [keep[m], swap(send[m])] for m in range(last, -1, -1)}
     parts = [functools.reduce(jnp.add, kept[0])]
-    kept[0] = []
+    arrived = {m: [] for m in range(n_chip)}
     for m in range(last, 0, -1):
-        unit = functools.reduce(jnp.add, kept[m])
-        if m == 2:
-            unit = after(unit, parts[0])
-        kept[m & (m - 1)].append(chip_flip(unit, low_bit(m)))
+        if m == last:
+            unit = ahead(after(kept[m][0], kept[m][0])) + kept[m][1]
+        else:
+            unit = functools.reduce(jnp.add, kept[m])
+            if m == 2:
+                unit = ahead(after(unit, parts[0]))
+            unit = functools.reduce(jnp.add, [unit] + arrived[m])
+        arrived[m & (m - 1)].append(chip_flip(unit, low_bit(m)))
+    kept[0] = arrived[0]
     parts += kept[0]
 
-    out_act, pulled, message = pl.pallas_call(
+    half = width // 2
+    out_act, pulled, wkeep, wsend = pl.pallas_call(
         functools.partial(middle_kernel, n_col, len(parts), float(nodes) ** (-0.5)),
         out_shape=(
             jax.ShapeDtypeStruct((node_dev, hidden), BF16),
             jax.ShapeDtypeStruct((width, node_dev), F32),
-            jax.ShapeDtypeStruct((2 * width, hidden), F32),
+            jax.ShapeDtypeStruct((half * hidden // EDGE, EDGE), F32),
+            jax.ShapeDtypeStruct((half * hidden // EDGE, EDGE), F32),
         ),
         in_specs=[vmem] * (3 + len(parts)),
-        out_specs=(vmem,) * 3,
+        out_specs=(vmem,) * 4,
         compiler_params=params(16),
         name="middle",
     )(deg, cotangent, weight, *parts)
@@ -339,36 +349,38 @@
     own = {0: pulled}
     for m in range(1, n_chip):
         own[m] = chip_flip(own[m & (m - 1)], low_bit(m))
-    own[0], own[1] = message, after(own[1], own[2])
+    own[1] = after(own[1], own[2])
     other = {m: swap(own[m]) for m in range(last)}
 
-    half = width // 2
+    wsum = wkeep + swap(wsend)
+    wsum = wsum + chip_flip(wsum, 0)
     early = [x for m in range(last) for x in (own[m], other[m])]
-    sofar, wsum = pl.pallas_call(
+    late_rows = 2 * node_dev
+    sofar, rest = pl.pallas_call(
         functools.partial(partial_kernel, len(early)),
         out_shape=(
             jax.ShapeDtypeStruct((width, col_nodes), F32),
-            jax.ShapeDtypeStruct((half * hidden // EDGE, EDGE), F32),
+            jax.ShapeDtypeStruct((late_rows, col_nodes), BF16),
         ),
         in_specs=[any_space] * (1 + len(early)),
-        out_specs=(vmem,) * 2,
+        out_specs=(vmem, any_space),
         scratch_shapes=[
             pltpu.VMEM((len(early) * node_dev, col_nodes), BF16),
             pltpu.VMEM((len(early), width, node_dev), F32),
-            pltpu.VMEM((2, half, hidden), F32),
             pltpu.VMEM((2 * width, len(early) * node_dev), BF16),
             pltpu.SemaphoreType.DMA((len(early),)),
-            pltpu.SemaphoreType.DMA((2,)),
             pltpu.SemaphoreType.DMA((len(early),)),
+            pltpu.SemaphoreType.DMA,
         ],
-        compiler_params=params(52),
+        compiler_params=params(BWD),
         cost_estimate=cost(row_nodes * col_nodes * width * 4, 32 << 20),
         name="backward_early",
     )(tile, *early)
 
-    own[last] = after(own[last], sofar)
+    own[last] = after(after(own[last], sofar), wsum)
     late = [own[last], swap(own[last])]
-    wsum = wsum + chip_flip(wsum, 0)
+    for bit in range(1, chip_bits):
+        wsum = wsum + chip_flip(wsum, bit)
     n_piece = max(1, row_bits)
     while col_nodes % (EDGE * n_piece):
         n_piece -= 1
@@ -387,16 +399,13 @@
             pltpu.SemaphoreType.DMA,
             pltpu.SemaphoreType.DMA,
         ],
-        compiler_params=params(52),
+        compiler_params=params(BWD),
         name="backward_late",
-    )(deg, tile, sofar, *late)
+    )(deg, rest, sofar, *late)
 
     done = list(done)
     for t in range(row_bits):
         wsum = after(wsum, done[0])
-        if t == 0:
-            for bit in range(1, chip_bits):
-                wsum = wsum + chip_flip(wsum, bit)
         wsum = wsum + row_flip(wsum, t)
         done = [x + row_flip(x, (i + t) % row_bits) for i, x in enumerate(done)]
         if t == 0:

time: 71.7 us -> 70 us (0.976)
  waiting for transfers between devices: 27.5 us -> 26 us
    ppermute x8, waiting for transfers between devices: 18.6 us -> 16.8 us  [chip_flip(): return lax.ppermute(x, 'col', [(i, i ^ 2 << bit) for i in range(n_col)])]
    ppermute x6, waiting for transfers between devices: 6.54 us -> 8.14 us  [row_flip(): return lax.ppermute(x, 'row', [(i, i ^ 1 << bit) for i in range(n_row)])]
    ppermute x9 -> x10, waiting for transfers between devices: 2.39 us -> 1.11 us  [swap(): return lax.ppermute(x, 'col', swap_pairs)]
    add x2 -> x1, other arithmetic: 1.85 us -> 0.93 us  [body(): unit = functools.reduce(jnp.add, kept[m])]
    add x3, other arithmetic: 1.05 us -> 1.95 us  [after(): return x + 0.0 * other[:, :x.shape[1]]]
    pallas_call x1, Pallas kernels: 1.87 us -> 1.12 us  [body(): pl.pallas_call(functools.partial(last_kernel, len(late), n_piece), out_sh...]
    ppermute x9 -> x10, starting transfers between devices: 1.84 us -> 1.91 us  [swap(): return lax.ppermute(x, 'col', swap_pairs)]
  transfers between devices with their start and end apart: 23 -> 24, of which waited for: 14 -> 14; matrix products, arithmetic and copies ran while one was open for 5% -> 6% of each run, Pallas kernels for 7% -> 6%
where the time goes in v9:
time: 70 us; the launch traced here: 69.8 us
  waiting for transfers between devices  26 us (37%)
  starting transfers between devices  22.3 us (32%)
  Pallas kernels  15.2 us (22%)
  other arithmetic  4.64 us (7%)
  between operations  1.57 us (2%)
    ppermute x8, waiting for transfers between devices, chip_flip(): return lax.ppermute(x, 'col', [(i, i ^ 2 << bit) for i in range(n_col)])  16.8 us
    ppermute x8, starting transfers between devices, chip_flip(): return lax.ppermute(x, 'col', [(i, i ^ 2 << bit) for i in range(n_col)])  12 us
    pallas_call x1, Pallas kernels, body(): pl.pallas_call(functools.partial(forward_kernel, n_col, chunk, panel_dev,...  10 us
    ppermute x6, starting transfers between devices, row_flip(): return lax.ppermute(x, 'row', [(i, i ^ 1 << bit) for i in range(n_row)])  8.35 us
    ppermute x6, waiting for transfers between devices, row_flip(): return lax.ppermute(x, 'row', [(i, i ^ 1 << bit) for i in range(n_row)])  8.14 us
    pallas_call x1, Pallas kernels, body(): pl.pallas_call(functools.partial(partial_kernel, len(early)), out_shape=(...  2.93 us
    add x3, other arithmetic, after(): return x + 0.0 * other[:, :x.shape[1]]  1.95 us
    ppermute x10, starting transfers between devices, swap(): return lax.ppermute(x, 'col', swap_pairs)  1.91 us
  transfers between devices with their start and end apart: 24, of which 14 were waited for; matrix products, arithmetic and copies ran while one was open for 6% of the time, Pallas kernels for 6%

profile of v9, /device:TPU:0, one launch (start us, length us, event | category | flops | bytes accessed | tf_op | source)
XLA Modules:
  0.0 69.8 jit_solution(6698575446209343876)
XLA Ops:
  1.3 10.0 %densify_forward.1 = (f32[256,128]{1,0:T(8,128)}, f32[256,128]{1,0:T(8,128)}, f32[256,128]{1,0:T(8,128)}, f32[256,128]{1,0:T(8,128)}, f32[256,128]{1,0:T(8,128)}...) custom-call(s32[1,1,384]{2,1,0:T(1,128)} %rows_ref.1, ...), custom_call_target="tpu_custom_call" | custom-call | tf_op jit(solution)/shard_map/densify_forward/pallas_call | solution.py:282
  11.4 0.5 collective-permute-start.1
  12.5 0.9 %multiply_add_fusion = f32[256,128]{1,0:T(8,128)S(1)} fusion(f32[256,128]{1,0:T(8,128)} %get-tuple-element.24), kind=kLoop, calls=%fused_computation.2 | loop fusion | flops 65536 | bytes 262144 | tf_op jit(solution)/shard_map/add | solution.py:273
  13.7 3.0 %collective-permute-start.3 = (f32[256,128]{1,0:T(8,128)S(1)}, f32[256,128]{1,0:T(8,128)S(1)}, u32[]{:S(2)}, u32[]{:S(2)}) collective-permute-start(f32[256,128]{1,0:T(8,128)S(1)} %add.117), channel_id=1, source_target_pairs={{0,2},{1,3},{2,0},{3,1},{4,6},{5,7},{6,4},{7,5},{8,10},{9,11},{10,... | collective-permute-start | bytes 393224 | tf_op jit(solution)/shard_map/ppermute | solution.py:310
  16.6 1.0 %multiply_add_fusion.2 = (f32[256,128]{1,0:T(8,128)S(1)}, f32[256,128]{1,0:T(8,128)S(1)}) fusion(f32[256,128]{1,0:T(8,128)} %get-tuple-element.22, f32[256,128]{1,0:T(8,128)S(1)} %collective-permute-done.1, f32[256,128]{1,0:T(8,128)} %get-tuple-element.20, f32[256,128]{1,0:T(8,128)S(1)} %collective-permute-done), kind=kLoop, calls=%fused_computation.6 | loop fusion | flops 131072 | bytes 786432 | tf_op jit(solution)/shard_map/add | solution.py:273
  17.7 0.9 %add.119 = f32[256,128]{1,0:T(8,128)S(1)} add(f32[256,128]{1,0:T(8,128)} %get-tuple-element.26, f32[256,128]{1,0:T(8,128)S(1)} %collective-permute-done.5) | non-fusion elementwise | flops 32768 | bytes 393216 | tf_op jit(solution)/shard_map/add | solution.py:326
  18.7 1.8 %collective-permute-done.3 = f32[256,128]{1,0:T(8,128)S(1)} collective-permute-done((f32[256,128]{1,0:T(8,128)S(1)}, f32[256,128]{1,0:T(8,128)S(1)}, u32[]{:S(2)}, u32[]{:S(2)}) %collective-permute-start.3) | collective-permute-done | bytes 131104 | tf_op jit(solution)/shard_map/ppermute | solution.py:310
  20.5 2.8 %collective-permute-start.4 = (f32[256,128]{1,0:T(8,128)S(1)}, f32[256,128]{1,0:T(8,128)S(1)}, u32[]{:S(2)}, u32[]{:S(2)}) collective-permute-start(f32[256,128]{1,0:T(8,128)S(1)} %add.118), channel_id=1, source_target_pairs={{0,4},{1,5},{2,6},{3,7},{4,0},{5,1},{6,2},{7,3},{8,12},{9,13},{10,... | collective-permute-start | bytes 393224 | tf_op jit(solution)/shard_map/ppermute | solution.py:310
  23.3 2.0 %collective-permute-done.6.refs_2_ = f32[256,128]{1,0:T(8,128)S(1)} collective-permute-done((f32[256,128]{1,0:T(8,128)S(1)}, f32[256,128]{1,0:T(8,128)S(1)}, u32[]{:S(2)}, u32[]{:S(2)}) %collective-permute-start.6) | collective-permute-done | bytes 131104 | tf_op jit(solution)/shard_map/ppermute | solution.py:310
  25.3 4.1 %collective-permute-done.4.refs_1_ = f32[256,128]{1,0:T(8,128)S(1)} collective-permute-done((f32[256,128]{1,0:T(8,128)S(1)}, f32[256,128]{1,0:T(8,128)S(1)}, u32[]{:S(2)}, u32[]{:S(2)}) %collective-permute-start.4) | collective-permute-done | bytes 131104 | tf_op jit(solution)/shard_map/ppermute | solution.py:310
  29.4 1.1 %middle.1 = (bf16[256,256]{1,0:T(8,128)(2,1)}, f32[128,256]{1,0:T(8,128)S(1)}, f32[128,128]{1,0:T(8,128)S(1)}, f32[128,128]{1,0:T(8,128)S(1)}) custom-call(s32[64,128]{1,0:T(8,128)S(1)} %bitcast.10, bf16[256,256]{1,0:T(8,128)(2,1)S(1)} %copy-done.1, bf16[128,256]{1,0:T(8,128)(2,1)S(1)} %copy-done.2, f32[256,128]{1,0:T(8,128)S(1)} %get-tuple-element.40.refs_0_, ...), custom_call_target="tpu_custom_call" | custom-call | tf_op jit(solution)/shard_map/middle/pallas_call | solution.py:335
  30.5 0.5 collective-permute-start.8
  31.0 3.4 %collective-permute-start.9 = (f32[128,256]{1,0:T(8,128)S(1)}, f32[128,256]{1,0:T(8,128)S(1)}, u32[]{:S(2)}, u32[]{:S(2)}) collective-permute-start(f32[128,256]{1,0:T(8,128)S(1)} %get-tuple-element.30.refs_0_), channel_id=1, source_target_pairs={{0,4},{1,5},{2,6},{3,7},{4,0},{5,1},{6,2},{7,3},{8,12},{9,13},{10,... | collective-permute-start | bytes 393224 | tf_op jit(solution)/shard_map/ppermute | solution.py:310
  34.5 5.9 %collective-permute-done.14 = f32[128,128]{1,0:T(8,128)S(1)} collective-permute-done((f32[128,128]{1,0:T(8,128)S(1)}, f32[128,128]{1,0:T(8,128)S(1)}, u32[]{:S(2)}, u32[]{:S(2)}) %collective-permute-start.14) | collective-permute-done | bytes 65568 | tf_op jit(solution)/shard_map/ppermute | solution.py:310
  40.4 0.7 collective-permute-done.9.refs_4_
  41.2 0.5 collective-permute-start.11
  42.7 2.9 %backward_early.1 = (f32[128,1024]{1,0:T(8,128)S(1)}, bf16[512,1024]{1,0:T(8,128)(2,1)S(1)}) custom-call(bf16[2048,1024]{1,0:T(8,128)(2,1)} %get-tuple-element.29.tile_ref, f32[128,256]{1,0:T(8,128)S(1)} %get-tuple-element.30.refs_0_, f32[128,256]{1,0:T(8,128)S(1)} %collective-permute-done.7.refs_1_, f32[128,256]{1,0:T(8,128)S(1)} %multiply_add_fusion.1.refs_2_, ...), custom_call_target="tpu_custom_call" | custom-call | flops 1073741824 | bytes 33554432 | tf_op jit(solution)/shard_map/backward_early/pallas_call | solution.py:359
  45.7 1.5 %collective-permute-done.12 = f32[128,256]{1,0:T(8,128)S(1)} collective-permute-done((f32[128,256]{1,0:T(8,128)S(1)}, f32[128,256]{1,0:T(8,128)S(1)}, u32[]{:S(2)}, u32[]{:S(2)}) %collective-permute-start.12) | collective-permute-done | bytes 131104 | tf_op jit(solution)/shard_map/ppermute | solution.py:310
  47.3 1.8 %collective-permute-start.19 = (f32[128,128]{1,0:T(8,128)S(1)}, f32[128,128]{1,0:T(8,128)S(1)}, u32[]{:S(2)}, u32[]{:S(2)}) collective-permute-start(f32[128,128]{1,0:T(8,128)S(1)} %add.123), channel_id=1, source_target_pairs={{0,4},{1,5},{2,6},{3,7},{4,0},{5,1},{6,2},{7,3},{8,12},{9,13},{10,... | collective-permute-start | bytes 196616 | tf_op jit(solution)/shard_map/ppermute | solution.py:310
  49.1 1.1 %backward_late.1 = (f32[512,128]{1,0:T(8,128)S(1)}, f32[512,128]{1,0:T(8,128)S(1)}) custom-call(s32[64,128]{1,0:T(8,128)S(1)} %bitcast.11, bf16[512,1024]{1,0:T(8,128)(2,1)S(1)} %get-tuple-element.31.dense_ref, f32[128,1024]{1,0:T(8,128)S(1)} %get-tuple-element.32.sofar_ref, f32[128,256]{1,0:T(8,128)S(1)} %add_add_fusion.refs_0_, ...), custom_call_target="tpu_custom_call" | custom-call | tf_op jit(solution)/shard_map/backward_late/pallas_call | solution.py:388
  50.2 1.6 %collective-permute-start.16 = (f32[512,128]{1,0:T(8,128)S(1)}, f32[512,128]{1,0:T(8,128)S(1)}, u32[]{:S(2)}, u32[]{:S(2)}) collective-permute-start(f32[512,128]{1,0:T(8,128)S(1)} %get-tuple-element.35), channel_id=1, source_target_pairs={{0,8},{8,0},{16,24},{24,16},{1,9},{9,1},{17,25},{25,17},{2,10},{10... | collective-permute-start | bytes 786440 | tf_op jit(solution)/shard_map/ppermute | solution.py:313
  51.8 1.5 %collective-permute-start.18 = (f32[512,128]{1,0:T(8,128)S(1)}, f32[512,128]{1,0:T(8,128)S(1)}, u32[]{:S(2)}, u32[]{:S(2)}) collective-permute-start(f32[512,128]{1,0:T(8,128)S(1)} %get-tuple-element.36), channel_id=1, source_target_pairs={{0,16},{8,24},{16,0},{24,8},{1,17},{9,25},{17,1},{25,9},{2,18},{10... | collective-permute-start | bytes 786440 | tf_op jit(solution)/shard_map/ppermute | solution.py:313
  53.3 0.8 %collective-permute-done.19 = f32[128,128]{1,0:T(8,128)S(1)} collective-permute-done((f32[128,128]{1,0:T(8,128)S(1)}, f32[128,128]{1,0:T(8,128)S(1)}, u32[]{:S(2)}, u32[]{:S(2)}) %collective-permute-start.19) | collective-permute-done | bytes 65568 | tf_op jit(solution)/shard_map/ppermute | solution.py:310
  54.1 1.6 %collective-permute-start.20 = (f32[128,128]{1,0:T(8,128)S(1)}, f32[128,128]{1,0:T(8,128)S(1)}, u32[]{:S(2)}, u32[]{:S(2)}) collective-permute-start(f32[128,128]{1,0:T(8,128)S(1)} %bitcast_add_fusion.3), channel_id=1, source_target_pairs={{0,8},{8,0},{16,24},{24,16},{1,9},{9,1},{17,25},{25,17},{2,10},{10... | collective-permute-start | bytes 196616 | tf_op jit(solution)/shard_map/ppermute | solution.py:313
  55.7 3.7 %collective-permute-done.16 = f32[512,128]{1,0:T(8,128)S(1)} collective-permute-done((f32[512,128]{1,0:T(8,128)S(1)}, f32[512,128]{1,0:T(8,128)S(1)}, u32[]{:S(2)}, u32[]{:S(2)}) %collective-permute-start.16) | collective-permute-done | bytes 262176 | tf_op jit(solution)/shard_map/ppermute | solution.py:313
  59.4 1.6 %collective-permute-start.17 = (f32[512,128]{1,0:T(8,128)S(1)}, f32[512,128]{1,0:T(8,128)S(1)}, u32[]{:S(2)}, u32[]{:S(2)}) collective-permute-start(f32[512,128]{1,0:T(8,128)S(1)} %add.127), channel_id=1, source_target_pairs={{0,16},{8,24},{16,0},{24,8},{1,17},{9,25},{17,1},{25,9},{2,18},{10... | collective-permute-start | bytes 786440 | tf_op jit(solution)/shard_map/ppermute | solution.py:313
  61.1 1.6 %collective-permute-start.21 = (f32[512,128]{1,0:T(8,128)S(1)}, f32[512,128]{1,0:T(8,128)S(1)}, u32[]{:S(2)}, u32[]{:S(2)}) collective-permute-start(f32[512,128]{1,0:T(8,128)S(1)} %bitcast_add_fusion), channel_id=1, source_target_pairs={{0,8},{8,0},{16,24},{24,16},{1,9},{9,1},{17,25},{25,17},{2,10},{10... | collective-permute-start | bytes 786440 | tf_op jit(solution)/shard_map/ppermute | solution.py:313
  62.6 0.6 collective-permute-start.22
  63.2 3.8 %collective-permute-done.17 = f32[512,128]{1,0:T(8,128)S(1)} collective-permute-done((f32[512,128]{1,0:T(8,128)S(1)}, f32[512,128]{1,0:T(8,128)S(1)}, u32[]{:S(2)}, u32[]{:S(2)}) %collective-permute-start.17) | collective-permute-done | bytes 262176 | tf_op jit(solution)/shard_map/ppermute | solution.py:313
  67.1 0.7 collective-permute-done.22
  67.9 0.8 %pad_maximum_fusion = f32[1024,128]{1,0:T(8,128)} fusion(f32[512,128]{1,0:T(8,128)S(1)} %add.138, f32[512,128]{1,0:T(8,128)S(1)} %add.128), kind=kLoop, calls=%fused_computation | loop fusion | flops 131072 | bytes 1048576 | tf_op jit(solution)/shard_map/concatenate | solution.py:414
  69.1 0.7 maximum_maximum_fusion
  (53 shorter events, 3.0 us)
Async XLA Ops:
  0.6 28.8 %copy-start = (s32[8192]{0:T(1024)S(1)}, s32[8192]{0:T(1024)}, u32[]{:S(2)}) copy-start(s32[8192]{0:T(1024)} %param.9) | copy-start | bytes 98308
  0.6 28.8 %copy-start.1 = (bf16[256,256]{1,0:T(8,128)(2,1)S(1)}, bf16[256,256]{1,0:T(8,128)(2,1)}, u32[]{:S(2)}) copy-start(bf16[256,256]{1,0:T(8,128)(2,1)} %cot_ref.1) | copy-start | bytes 393220
  0.7 28.8 %copy-start.2 = (bf16[128,256]{1,0:T(8,128)(2,1)S(1)}, bf16[128,256]{1,0:T(8,128)(2,1)}, u32[]{:S(2)}) copy-start(bf16[128,256]{1,0:T(8,128)(2,1)} %weight_ref.1) | copy-start | bytes 196612
  11.4 5.3 %collective-permute-start.1 = (f32[256,128]{1,0:T(8,128)}, f32[256,128]{1,0:T(8,128)S(1)}, u32[]{:S(2)}, u32[]{:S(2)}) collective-permute-start(f32[256,128]{1,0:T(8,128)} %get-tuple-element.23), channel_id=1, source_target_pairs={{0,1},{1,0},{2,3},{3,2},{4,5},{5,4},{6,7},{7,6},{8,9},{9,8},{10,11... | collective-permute-start | bytes 393224 | tf_op jit(solution)/shard_map/ppermute | solution.py:307
  11.9 4.7 %collective-permute-start = (f32[256,128]{1,0:T(8,128)}, f32[256,128]{1,0:T(8,128)S(1)}, u32[]{:S(2)}, u32[]{:S(2)}) collective-permute-start(f32[256,128]{1,0:T(8,128)} %get-tuple-element.21), channel_id=1, source_target_pairs={{0,1},{1,0},{2,3},{3,2},{4,5},{5,4},{6,7},{7,6},{8,9},{9,8},{10,11... | collective-permute-start | bytes 393224 | tf_op jit(solution)/shard_map/ppermute | solution.py:307
  12.0 1.7 %collective-permute-start.2 = (f32[256,128]{1,0:T(8,128)}, f32[256,128]{1,0:T(8,128)S(1)}, u32[]{:S(2)}, u32[]{:S(2)}) collective-permute-start(f32[256,128]{1,0:T(8,128)} %get-tuple-element.25), channel_id=1, source_target_pairs={{0,1},{1,0},{2,3},{3,2},{4,5},{5,4},{6,7},{7,6},{8,9},{9,8},{10,11... | collective-permute-start | bytes 393224 | tf_op jit(solution)/shard_map/ppermute | solution.py:307
  12.4 5.2 %collective-permute-start.5 = (f32[256,128]{1,0:T(8,128)}, f32[256,128]{1,0:T(8,128)S(1)}, u32[]{:S(2)}, u32[]{:S(2)}) collective-permute-start(f32[256,128]{1,0:T(8,128)} %get-tuple-element.27), channel_id=1, source_target_pairs={{0,1},{1,0},{2,3},{3,2},{4,5},{5,4},{6,7},{7,6},{8,9},{9,8},{10,11... | collective-permute-start | bytes 393224 | tf_op jit(solution)/shard_map/ppermute | solution.py:307
  13.7 6.8 %collective-permute-start.3 = (f32[256,128]{1,0:T(8,128)S(1)}, f32[256,128]{1,0:T(8,128)S(1)}, u32[]{:S(2)}, u32[]{:S(2)}) collective-permute-start(f32[256,128]{1,0:T(8,128)S(1)} %add.117), channel_id=1, source_target_pairs={{0,2},{1,3},{2,0},{3,1},{4,6},{5,7},{6,4},{7,5},{8,10},{9,11},{10,... | collective-permute-start | bytes 393224 | tf_op jit(solution)/shard_map/ppermute | solution.py:310
  18.6 6.7 %collective-permute-start.6 = (f32[256,128]{1,0:T(8,128)S(1)}, f32[256,128]{1,0:T(8,128)S(1)}, u32[]{:S(2)}, u32[]{:S(2)}) collective-permute-start(f32[256,128]{1,0:T(8,128)S(1)} %add.119), channel_id=1, source_target_pairs={{0,2},{1,3},{2,0},{3,1},{4,6},{5,7},{6,4},{7,5},{8,10},{9,11},{10,... | collective-permute-start | bytes 393224 | tf_op jit(solution)/shard_map/ppermute | solution.py:310
  20.5 8.9 %collective-permute-start.4 = (f32[256,128]{1,0:T(8,128)S(1)}, f32[256,128]{1,0:T(8,128)S(1)}, u32[]{:S(2)}, u32[]{:S(2)}) collective-permute-start(f32[256,128]{1,0:T(8,128)S(1)} %add.118), channel_id=1, source_target_pairs={{0,4},{1,5},{2,6},{3,7},{4,0},{5,1},{6,2},{7,3},{8,12},{9,13},{10,... | collective-permute-start | bytes 393224 | tf_op jit(solution)/shard_map/ppermute | solution.py:310
  30.5 3.9 %collective-permute-start.13 = (f32[128,128]{1,0:T(8,128)S(1)}, f32[128,128]{1,0:T(8,128)S(1)}, u32[]{:S(2)}, u32[]{:S(2)}) collective-permute-start(f32[128,128]{1,0:T(8,128)S(1)} %get-tuple-element.34), channel_id=1, source_target_pairs={{0,1},{1,0},{2,3},{3,2},{4,5},{5,4},{6,7},{7,6},{8,9},{9,8},{10,11... | collective-permute-start | bytes 196616 | tf_op jit(solution)/shard_map/ppermute | solution.py:307
  30.5 9.9 %collective-permute-start.8 = (f32[128,256]{1,0:T(8,128)S(1)}, f32[128,256]{1,0:T(8,128)S(1)}, u32[]{:S(2)}, u32[]{:S(2)}) collective-permute-start(f32[128,256]{1,0:T(8,128)S(1)} %get-tuple-element.30.refs_0_), channel_id=1, source_target_pairs={{0,2},{1,3},{2,0},{3,1},{4,6},{5,7},{6,4},{7,5},{8,10},{9,11},{10,... | collective-permute-start | bytes 393224 | tf_op jit(solution)/shard_map/ppermute | solution.py:310
  31.0 10.1 %collective-permute-start.9 = (f32[128,256]{1,0:T(8,128)S(1)}, f32[128,256]{1,0:T(8,128)S(1)}, u32[]{:S(2)}, u32[]{:S(2)}) collective-permute-start(f32[128,256]{1,0:T(8,128)S(1)} %get-tuple-element.30.refs_0_), channel_id=1, source_target_pairs={{0,4},{1,5},{2,6},{3,7},{4,0},{5,1},{6,2},{7,3},{8,12},{9,13},{10,... | collective-permute-start | bytes 393224 | tf_op jit(solution)/shard_map/ppermute | solution.py:310
  34.4 6.0 %collective-permute-start.14 = (f32[128,128]{1,0:T(8,128)S(1)}, f32[128,128]{1,0:T(8,128)S(1)}, u32[]{:S(2)}, u32[]{:S(2)}) collective-permute-start(f32[128,128]{1,0:T(8,128)S(1)} %add.122), channel_id=1, source_target_pairs={{0,2},{1,3},{2,0},{3,1},{4,6},{5,7},{6,4},{7,5},{8,10},{9,11},{10,... | collective-permute-start | bytes 196616 | tf_op jit(solution)/shard_map/ppermute | solution.py:310
  34.5 7.8 %collective-permute-start.7 = (f32[128,256]{1,0:T(8,128)S(1)}, f32[128,256]{1,0:T(8,128)S(1)}, u32[]{:S(2)}, u32[]{:S(2)}) collective-permute-start(f32[128,256]{1,0:T(8,128)S(1)} %get-tuple-element.30.refs_0_), channel_id=1, source_target_pairs={{0,1},{1,0},{2,3},{3,2},{4,5},{5,4},{6,7},{7,6},{8,9},{9,8},{10,11... | collective-permute-start | bytes 393224 | tf_op jit(solution)/shard_map/ppermute | solution.py:307
  41.1 1.4 %collective-permute-start.10 = (f32[128,256]{1,0:T(8,128)S(1)}, f32[128,256]{1,0:T(8,128)S(1)}, u32[]{:S(2)}, u32[]{:S(2)}) collective-permute-start(f32[128,256]{1,0:T(8,128)S(1)} %multiply_add_fusion.1.refs_2_), channel_id=1, source_target_pairs={{0,1},{1,0},{2,3},{3,2},{4,5},{5,4},{6,7},{7,6},{8,9},{9,8},{10,11... | collective-permute-start | bytes 393224 | tf_op jit(solution)/shard_map/ppermute | solution.py:307
  41.2 1.5 %collective-permute-start.11 = (f32[128,256]{1,0:T(8,128)S(1)}, f32[128,256]{1,0:T(8,128)S(1)}, u32[]{:S(2)}, u32[]{:S(2)}) collective-permute-start(f32[128,256]{1,0:T(8,128)S(1)} %collective-permute-done.9.refs_4_), channel_id=1, source_target_pairs={{0,1},{1,0},{2,3},{3,2},{4,5},{5,4},{6,7},{7,6},{8,9},{9,8},{10,11... | collective-permute-start | bytes 393224 | tf_op jit(solution)/shard_map/ppermute | solution.py:307
  41.7 5.5 %collective-permute-start.12 = (f32[128,256]{1,0:T(8,128)S(1)}, f32[128,256]{1,0:T(8,128)S(1)}, u32[]{:S(2)}, u32[]{:S(2)}) collective-permute-start(f32[128,256]{1,0:T(8,128)S(1)} %collective-permute-done.9.refs_4_), channel_id=1, source_target_pairs={{0,2},{1,3},{2,0},{3,1},{4,6},{5,7},{6,4},{7,5},{8,10},{9,11},{10,... | collective-permute-start | bytes 393224 | tf_op jit(solution)/shard_map/ppermute | solution.py:310
  47.2 1.9 %collective-permute-start.15 = (f32[128,256]{1,0:T(8,128)S(1)}, f32[128,256]{1,0:T(8,128)S(1)}, u32[]{:S(2)}, u32[]{:S(2)}) collective-permute-start(f32[128,256]{1,0:T(8,128)S(1)} %add_add_fusion.refs_0_), channel_id=1, source_target_pairs={{0,1},{1,0},{2,3},{3,2},{4,5},{5,4},{6,7},{7,6},{8,9},{9,8},{10,11... | collective-permute-start | bytes 393224 | tf_op jit(solution)/shard_map/ppermute | solution.py:307
  47.3 6.8 %collective-permute-start.19 = (f32[128,128]{1,0:T(8,128)S(1)}, f32[128,128]{1,0:T(8,128)S(1)}, u32[]{:S(2)}, u32[]{:S(2)}) collective-permute-start(f32[128,128]{1,0:T(8,128)S(1)} %add.123), channel_id=1, source_target_pairs={{0,4},{1,5},{2,6},{3,7},{4,0},{5,1},{6,2},{7,3},{8,12},{9,13},{10,... | collective-permute-start | bytes 196616 | tf_op jit(solution)/shard_map/ppermute | solution.py:310
  50.2 9.1 %collective-permute-start.16 = (f32[512,128]{1,0:T(8,128)S(1)}, f32[512,128]{1,0:T(8,128)S(1)}, u32[]{:S(2)}, u32[]{:S(2)}) collective-permute-start(f32[512,128]{1,0:T(8,128)S(1)} %get-tuple-element.35), channel_id=1, source_target_pairs={{0,8},{8,0},{16,24},{24,16},{1,9},{9,1},{17,25},{25,17},{2,10},{10... | collective-permute-start | bytes 786440 | tf_op jit(solution)/shard_map/ppermute | solution.py:313
  51.8 9.2 %collective-permute-start.18 = (f32[512,128]{1,0:T(8,128)S(1)}, f32[512,128]{1,0:T(8,128)S(1)}, u32[]{:S(2)}, u32[]{:S(2)}) collective-permute-start(f32[512,128]{1,0:T(8,128)S(1)} %get-tuple-element.36), channel_id=1, source_target_pairs={{0,16},{8,24},{16,0},{24,8},{1,17},{9,25},{17,1},{25,9},{2,18},{10... | collective-permute-start | bytes 786440 | tf_op jit(solution)/shard_map/ppermute | solution.py:313
  54.1 6.9 %collective-permute-start.20 = (f32[128,128]{1,0:T(8,128)S(1)}, f32[128,128]{1,0:T(8,128)S(1)}, u32[]{:S(2)}, u32[]{:S(2)}) collective-permute-start(f32[128,128]{1,0:T(8,128)S(1)} %bitcast_add_fusion.3), channel_id=1, source_target_pairs={{0,8},{8,0},{16,24},{24,16},{1,9},{9,1},{17,25},{25,17},{2,10},{10... | collective-permute-start | bytes 196616 | tf_op jit(solution)/shard_map/ppermute | solution.py:313
  59.4 7.6 %collective-permute-start.17 = (f32[512,128]{1,0:T(8,128)S(1)}, f32[512,128]{1,0:T(8,128)S(1)}, u32[]{:S(2)}, u32[]{:S(2)}) collective-permute-start(f32[512,128]{1,0:T(8,128)S(1)} %add.127), channel_id=1, source_target_pairs={{0,16},{8,24},{16,0},{24,8},{1,17},{9,25},{17,1},{25,9},{2,18},{10... | collective-permute-start | bytes 786440 | tf_op jit(solution)/shard_map/ppermute | solution.py:313
  61.1 6.7 %collective-permute-start.21 = (f32[512,128]{1,0:T(8,128)S(1)}, f32[512,128]{1,0:T(8,128)S(1)}, u32[]{:S(2)}, u32[]{:S(2)}) collective-permute-start(f32[512,128]{1,0:T(8,128)S(1)} %bitcast_add_fusion), channel_id=1, source_target_pairs={{0,8},{8,0},{16,24},{24,16},{1,9},{9,1},{17,25},{25,17},{2,10},{10... | collective-permute-start | bytes 786440 | tf_op jit(solution)/shard_map/ppermute | solution.py:313
  62.6 5.1 %collective-permute-start.22 = (f32[128,128]{1,0:T(8,128)S(1)}, f32[128,128]{1,0:T(8,128)S(1)}, u32[]{:S(2)}, u32[]{:S(2)}) collective-permute-start(f32[128,128]{1,0:T(8,128)S(1)} %get-tuple-element.37), channel_id=1, source_target_pairs={{0,16},{8,24},{16,0},{24,8},{1,17},{9,25},{17,1},{25,9},{2,18},{10... | collective-permute-start | bytes 196616 | tf_op jit(solution)/shard_map/ppermute | solution.py:313
  67.7 1.3 %collective-permute-start.23 = (f32[128,128]{1,0:T(8,128)S(1)}, f32[128,128]{1,0:T(8,128)S(1)}, u32[]{:S(2)}, u32[]{:S(2)}) collective-permute-start(f32[128,128]{1,0:T(8,128)S(1)} %bitcast_add_fusion.1), channel_id=1, source_target_pairs={{0,1},{1,0},{2,3},{3,2},{4,5},{5,4},{6,7},{7,6},{8,9},{9,8},{10,11... | collective-permute-start | bytes 196616 | tf_op jit(solution)/shard_map/ppermute | solution.py:307

commit v10 on v9

--- a/solution.py
+++ b/solution.py
@@ -349,11 +349,10 @@
     own = {0: pulled}
     for m in range(1, n_chip):
         own[m] = chip_flip(own[m & (m - 1)], low_bit(m))
-    own[1] = after(own[1], own[2])
     other = {m: swap(own[m]) for m in range(last)}
 
-    wsum = wkeep + swap(wsend)
-    wsum = wsum + chip_flip(wsum, 0)
+    wsum = after(wkeep + swap(wsend), other[2])
+    moved = chip_flip(wsum, 0)
     early = [x for m in range(last) for x in (own[m], other[m])]
     late_rows = 2 * node_dev
     sofar, rest = pl.pallas_call(
@@ -377,6 +376,7 @@
         name="backward_early",
     )(tile, *early)
 
+    wsum = after(wsum, sofar) + moved
     own[last] = after(after(own[last], sofar), wsum)
     late = [own[last], swap(own[last])]
     for bit in range(1, chip_bits):
@@ -405,7 +405,7 @@
 
     done = list(done)
     for t in range(row_bits):
-        wsum = after(wsum, done[0])
+        wsum = after(wsum, done[-1 if t == 0 else 0])
         wsum = wsum + row_flip(wsum, t)
         done = [x + row_flip(x, (i + t) % row_bits) for i, x in enumerate(done)]
         if t == 0:

time: 70 us -> 70 us (level)
    ppermute x8, waiting for transfers between devices: 16.8 us -> 15.4 us  [chip_flip(): return lax.ppermute(x, 'col', [(i, i ^ 2 << bit) for i in range(n_col)])]
    ppermute x6, waiting for transfers between devices: 8.14 us -> 9.12 us  [row_flip(): return lax.ppermute(x, 'row', [(i, i ^ 1 << bit) for i in range(n_row)])]
    ppermute x8, starting transfers between devices: 12 us -> 11.3 us  [chip_flip(): return lax.ppermute(x, 'col', [(i, i ^ 2 << bit) for i in range(n_col)])]
  transfers between devices with their start and end apart: 24 -> 24, of which waited for: 14 -> 13; matrix products, arithmetic and copies ran while one was open for 6% -> 6% of each run, Pallas kernels for 6% -> 6%
where the time goes in v10:
time: 70 us; the launch traced here: 69.8 us
  waiting for transfers between devices  26.3 us (38%)
  starting transfers between devices  22 us (31%)
  Pallas kernels  15.2 us (22%)
  other arithmetic  4.62 us (7%)
  between operations  1.53 us (2%)
    ppermute x8, waiting for transfers between devices, chip_flip(): return lax.ppermute(x, 'col', [(i, i ^ 2 << bit) for i in range(n_col)])  15.4 us
    ppermute x8, starting transfers between devices, chip_flip(): return lax.ppermute(x, 'col', [(i, i ^ 2 << bit) for i in range(n_col)])  11.3 us
    pallas_call x1, Pallas kernels, body(): pl.pallas_call(functools.partial(forward_kernel, n_col, chunk, panel_dev,...  10 us
    ppermute x6, waiting for transfers between devices, row_flip(): return lax.ppermute(x, 'row', [(i, i ^ 1 << bit) for i in range(n_row)])  9.12 us
    ppermute x6, starting transfers between devices, row_flip(): return lax.ppermute(x, 'row', [(i, i ^ 1 << bit) for i in range(n_row)])  8.43 us
    pallas_call x1, Pallas kernels, body(): pl.pallas_call(functools.partial(partial_kernel, len(early)), out_shape=(...  2.93 us
    ppermute x10, starting transfers between devices, swap(): return lax.ppermute(x, 'col', swap_pairs)  2.29 us
    add x3, other arithmetic, after(): return x + 0.0 * other[:, :x.shape[1]]  1.94 us
  transfers between devices with their start and end apart: 24, of which 13 were waited for; matrix products, arithmetic and copies ran while one was open for 6% of the time, Pallas kernels for 6%

profile of v10, /device:TPU:0, one launch (start us, length us, event | category | flops | bytes accessed | tf_op | source)
XLA Modules:
  0.0 69.8 jit_solution(12966061240267303746)
XLA Ops:
  1.3 10.0 %densify_forward.1 = (f32[256,128]{1,0:T(8,128)}, f32[256,128]{1,0:T(8,128)}, f32[256,128]{1,0:T(8,128)}, f32[256,128]{1,0:T(8,128)}, f32[256,128]{1,0:T(8,128)}...) custom-call(s32[1,1,384]{2,1,0:T(1,128)} %rows_ref.1, ...), custom_call_target="tpu_custom_call" | custom-call | tf_op jit(solution)/shard_map/densify_forward/pallas_call | solution.py:282
  11.4 0.5 collective-permute-start
  12.5 0.9 %multiply_add_fusion = f32[256,128]{1,0:T(8,128)S(1)} fusion(f32[256,128]{1,0:T(8,128)} %get-tuple-element.24), kind=kLoop, calls=%fused_computation.2 | loop fusion | flops 65536 | bytes 262144 | tf_op jit(solution)/shard_map/add | solution.py:273
  13.7 3.0 %collective-permute-start.3 = (f32[256,128]{1,0:T(8,128)S(1)}, f32[256,128]{1,0:T(8,128)S(1)}, u32[]{:S(2)}, u32[]{:S(2)}) collective-permute-start(f32[256,128]{1,0:T(8,128)S(1)} %add.120), channel_id=1, source_target_pairs={{0,2},{1,3},{2,0},{3,1},{4,6},{5,7},{6,4},{7,5},{8,10},{9,11},{10,... | collective-permute-start | bytes 393224 | tf_op jit(solution)/shard_map/ppermute | solution.py:310
  16.6 1.0 %multiply_add_fusion.1 = (f32[256,128]{1,0:T(8,128)S(1)}, f32[256,128]{1,0:T(8,128)S(1)}) fusion(f32[256,128]{1,0:T(8,128)} %get-tuple-element.22, f32[256,128]{1,0:T(8,128)S(1)} %collective-permute-done.1, f32[256,128]{1,0:T(8,128)} %get-tuple-element.20, f32[256,128]{1,0:T(8,128)S(1)} %collective-permute-done), kind=kLoop, calls=%fused_computation.5 | loop fusion | flops 131072 | bytes 786432 | tf_op jit(solution)/shard_map/add | solution.py:273
  17.7 0.9 %add.122 = f32[256,128]{1,0:T(8,128)S(1)} add(f32[256,128]{1,0:T(8,128)} %get-tuple-element.26, f32[256,128]{1,0:T(8,128)S(1)} %collective-permute-done.5) | non-fusion elementwise | flops 32768 | bytes 393216 | tf_op jit(solution)/shard_map/add | solution.py:326
  18.7 1.8 %collective-permute-done.3 = f32[256,128]{1,0:T(8,128)S(1)} collective-permute-done((f32[256,128]{1,0:T(8,128)S(1)}, f32[256,128]{1,0:T(8,128)S(1)}, u32[]{:S(2)}, u32[]{:S(2)}) %collective-permute-start.3) | collective-permute-done | bytes 131104 | tf_op jit(solution)/shard_map/ppermute | solution.py:310
  20.5 2.8 %collective-permute-start.4 = (f32[256,128]{1,0:T(8,128)S(1)}, f32[256,128]{1,0:T(8,128)S(1)}, u32[]{:S(2)}, u32[]{:S(2)}) collective-permute-start(f32[256,128]{1,0:T(8,128)S(1)} %add.121), channel_id=1, source_target_pairs={{0,4},{1,5},{2,6},{3,7},{4,0},{5,1},{6,2},{7,3},{8,12},{9,13},{10,... | collective-permute-start | bytes 393224 | tf_op jit(solution)/shard_map/ppermute | solution.py:310
  23.3 2.0 %collective-permute-done.6.refs_2_ = f32[256,128]{1,0:T(8,128)S(1)} collective-permute-done((f32[256,128]{1,0:T(8,128)S(1)}, f32[256,128]{1,0:T(8,128)S(1)}, u32[]{:S(2)}, u32[]{:S(2)}) %collective-permute-start.6) | collective-permute-done | bytes 131104 | tf_op jit(solution)/shard_map/ppermute | solution.py:310
  25.3 4.1 %collective-permute-done.4.refs_1_ = f32[256,128]{1,0:T(8,128)S(1)} collective-permute-done((f32[256,128]{1,0:T(8,128)S(1)}, f32[256,128]{1,0:T(8,128)S(1)}, u32[]{:S(2)}, u32[]{:S(2)}) %collective-permute-start.4) | collective-permute-done | bytes 131104 | tf_op jit(solution)/shard_map/ppermute | solution.py:310
  29.4 1.1 %middle.1 = (bf16[256,256]{1,0:T(8,128)(2,1)}, f32[128,256]{1,0:T(8,128)S(1)}, f32[128,128]{1,0:T(8,128)S(1)}, f32[128,128]{1,0:T(8,128)S(1)}) custom-call(s32[64,128]{1,0:T(8,128)S(1)} %bitcast.10, bf16[256,256]{1,0:T(8,128)(2,1)S(1)} %copy-done.1, bf16[128,256]{1,0:T(8,128)(2,1)S(1)} %copy-done.2, f32[256,128]{1,0:T(8,128)S(1)} %get-tuple-element.40.refs_0_, ...), custom_call_target="tpu_custom_call" | custom-call | tf_op jit(solution)/shard_map/middle/pallas_call | solution.py:335
  30.5 3.9 %collective-permute-start.8 = (f32[128,256]{1,0:T(8,128)S(1)}, f32[128,256]{1,0:T(8,128)S(1)}, u32[]{:S(2)}, u32[]{:S(2)}) collective-permute-start(f32[128,256]{1,0:T(8,128)S(1)} %get-tuple-element.30.refs_0_), channel_id=1, source_target_pairs={{0,2},{1,3},{2,0},{3,1},{4,6},{5,7},{6,4},{7,5},{8,10},{9,11},{10,... | collective-permute-start | bytes 393224 | tf_op jit(solution)/shard_map/ppermute | solution.py:310
  34.4 4.5 %collective-permute-done.10.refs_4_ = f32[128,256]{1,0:T(8,128)S(1)} collective-permute-done((f32[128,256]{1,0:T(8,128)S(1)}, f32[128,256]{1,0:T(8,128)S(1)}, u32[]{:S(2)}, u32[]{:S(2)}) %collective-permute-start.10) | collective-permute-done | bytes 131104 | tf_op jit(solution)/shard_map/ppermute | solution.py:310
  38.9 0.5 collective-permute-start.13
  40.4 1.4 %collective-permute-start.14 = (f32[128,128]{1,0:T(8,128)S(1)}, f32[128,128]{1,0:T(8,128)S(1)}, u32[]{:S(2)}, u32[]{:S(2)}) collective-permute-start(f32[128,128]{1,0:T(8,128)S(1)} %fusion), channel_id=1, source_target_pairs={{0,2},{1,3},{2,0},{3,1},{4,6},{5,7},{6,4},{7,5},{8,10},{9,11},{10,... | collective-permute-start | bytes 196616 | tf_op jit(solution)/shard_map/ppermute | solution.py:310
  41.8 2.9 %backward_early.1 = (f32[128,1024]{1,0:T(8,128)S(1)}, bf16[512,1024]{1,0:T(8,128)(2,1)S(1)}) custom-call(bf16[2048,1024]{1,0:T(8,128)(2,1)} %get-tuple-element.29.tile_ref, f32[128,256]{1,0:T(8,128)S(1)} %get-tuple-element.30.refs_0_, f32[128,256]{1,0:T(8,128)S(1)} %collective-permute-done.7.refs_1_, f32[128,256]{1,0:T(8,128)S(1)} %collective-permute-done.8.refs_2_, ...), custom_call_target="tpu_custom_call" | custom-call | flops 1073741824 | bytes 33554432 | tf_op jit(solution)/shard_map/backward_early/pallas_call | solution.py:358
  44.7 2.0 %collective-permute-done.14 = f32[128,128]{1,0:T(8,128)S(1)} collective-permute-done((f32[128,128]{1,0:T(8,128)S(1)}, f32[128,128]{1,0:T(8,128)S(1)}, u32[]{:S(2)}, u32[]{:S(2)}) %collective-permute-start.14) | collective-permute-done | bytes 65568 | tf_op jit(solution)/shard_map/ppermute | solution.py:310
  47.1 1.1 %collective-permute-done.15.refs_1_ = f32[128,256]{1,0:T(8,128)S(1)} collective-permute-done((f32[128,256]{1,0:T(8,128)S(1)}, f32[128,256]{1,0:T(8,128)S(1)}, u32[]{:S(2)}, u32[]{:S(2)}) %collective-permute-start.15) | collective-permute-done | bytes 131104 | tf_op jit(solution)/shard_map/ppermute | solution.py:307
  48.3 1.1 %backward_late.1 = (f32[512,128]{1,0:T(8,128)S(1)}, f32[512,128]{1,0:T(8,128)S(1)}) custom-call(s32[64,128]{1,0:T(8,128)S(1)} %bitcast.11, bf16[512,1024]{1,0:T(8,128)(2,1)S(1)} %get-tuple-element.31.dense_ref, f32[128,1024]{1,0:T(8,128)S(1)} %get-tuple-element.32.sofar_ref, f32[128,256]{1,0:T(8,128)S(1)} %add_add_fusion.refs_0_, ...), custom_call_target="tpu_custom_call" | custom-call | tf_op jit(solution)/shard_map/backward_late/pallas_call | solution.py:388
  49.4 1.6 %collective-permute-start.16 = (f32[512,128]{1,0:T(8,128)S(1)}, f32[512,128]{1,0:T(8,128)S(1)}, u32[]{:S(2)}, u32[]{:S(2)}) collective-permute-start(f32[512,128]{1,0:T(8,128)S(1)} %get-tuple-element.35), channel_id=1, source_target_pairs={{0,8},{8,0},{16,24},{24,16},{1,9},{9,1},{17,25},{25,17},{2,10},{10... | collective-permute-start | bytes 786440 | tf_op jit(solution)/shard_map/ppermute | solution.py:313
  51.0 1.5 %collective-permute-start.18 = (f32[512,128]{1,0:T(8,128)S(1)}, f32[512,128]{1,0:T(8,128)S(1)}, u32[]{:S(2)}, u32[]{:S(2)}) collective-permute-start(f32[512,128]{1,0:T(8,128)S(1)} %get-tuple-element.36), channel_id=1, source_target_pairs={{0,16},{8,24},{16,0},{24,8},{1,17},{9,25},{17,1},{25,9},{2,18},{10... | collective-permute-start | bytes 786440 | tf_op jit(solution)/shard_map/ppermute | solution.py:313
  52.5 1.0 %collective-permute-done.19 = f32[128,128]{1,0:T(8,128)S(1)} collective-permute-done((f32[128,128]{1,0:T(8,128)S(1)}, f32[128,128]{1,0:T(8,128)S(1)}, u32[]{:S(2)}, u32[]{:S(2)}) %collective-permute-start.19) | collective-permute-done | bytes 65568 | tf_op jit(solution)/shard_map/ppermute | solution.py:310
  53.5 1.6 %collective-permute-start.20 = (f32[128,128]{1,0:T(8,128)S(1)}, f32[128,128]{1,0:T(8,128)S(1)}, u32[]{:S(2)}, u32[]{:S(2)}) collective-permute-start(f32[128,128]{1,0:T(8,128)S(1)} %bitcast_add_fusion.3), channel_id=1, source_target_pairs={{0,8},{8,0},{16,24},{24,16},{1,9},{9,1},{17,25},{25,17},{2,10},{10... | collective-permute-start | bytes 196616 | tf_op jit(solution)/shard_map/ppermute | solution.py:313
  55.0 3.5 %collective-permute-done.16 = f32[512,128]{1,0:T(8,128)S(1)} collective-permute-done((f32[512,128]{1,0:T(8,128)S(1)}, f32[512,128]{1,0:T(8,128)S(1)}, u32[]{:S(2)}, u32[]{:S(2)}) %collective-permute-start.16) | collective-permute-done | bytes 262176 | tf_op jit(solution)/shard_map/ppermute | solution.py:313
  58.6 1.6 %collective-permute-start.17 = (f32[512,128]{1,0:T(8,128)S(1)}, f32[512,128]{1,0:T(8,128)S(1)}, u32[]{:S(2)}, u32[]{:S(2)}) collective-permute-start(f32[512,128]{1,0:T(8,128)S(1)} %add.131), channel_id=1, source_target_pairs={{0,16},{8,24},{16,0},{24,8},{1,17},{9,25},{17,1},{25,9},{2,18},{10... | collective-permute-start | bytes 786440 | tf_op jit(solution)/shard_map/ppermute | solution.py:313
  60.2 0.7 collective-permute-start.22
  60.9 1.6 %collective-permute-start.21 = (f32[512,128]{1,0:T(8,128)S(1)}, f32[512,128]{1,0:T(8,128)S(1)}, u32[]{:S(2)}, u32[]{:S(2)}) collective-permute-start(f32[512,128]{1,0:T(8,128)S(1)} %bitcast_add_fusion), channel_id=1, source_target_pairs={{0,8},{8,0},{16,24},{24,16},{1,9},{9,1},{17,25},{25,17},{2,10},{10... | collective-permute-start | bytes 786440 | tf_op jit(solution)/shard_map/ppermute | solution.py:313
  62.4 3.7 %collective-permute-done.17 = f32[512,128]{1,0:T(8,128)S(1)} collective-permute-done((f32[512,128]{1,0:T(8,128)S(1)}, f32[512,128]{1,0:T(8,128)S(1)}, u32[]{:S(2)}, u32[]{:S(2)}) %collective-permute-start.17) | collective-permute-done | bytes 262176 | tf_op jit(solution)/shard_map/ppermute | solution.py:313
  66.2 0.7 collective-permute-done.22
  67.0 1.2 %collective-permute-done.21 = f32[512,128]{1,0:T(8,128)S(1)} collective-permute-done((f32[512,128]{1,0:T(8,128)S(1)}, f32[512,128]{1,0:T(8,128)S(1)}, u32[]{:S(2)}, u32[]{:S(2)}) %collective-permute-start.21) | collective-permute-done | bytes 262176 | tf_op jit(solution)/shard_map/ppermute | solution.py:313
  68.2 0.8 %pad_maximum_fusion = f32[1024,128]{1,0:T(8,128)} fusion(f32[512,128]{1,0:T(8,128)S(1)} %add.142, f32[512,128]{1,0:T(8,128)S(1)} %add.132), kind=kLoop, calls=%fused_computation | loop fusion | flops 131072 | bytes 1048576 | tf_op jit(solution)/shard_map/concatenate | solution.py:414
  69.1 0.7 maximum_maximum_fusion
  (52 shorter events, 2.6 us)
Async XLA Ops:
  0.6 28.8 %copy-start = (s32[8192]{0:T(1024)S(1)}, s32[8192]{0:T(1024)}, u32[]{:S(2)}) copy-start(s32[8192]{0:T(1024)} %param.9) | copy-start | bytes 98308
  0.6 28.8 %copy-start.2 = (bf16[128,256]{1,0:T(8,128)(2,1)S(1)}, bf16[128,256]{1,0:T(8,128)(2,1)}, u32[]{:S(2)}) copy-start(bf16[128,256]{1,0:T(8,128)(2,1)} %weight_ref.1) | copy-start | bytes 196612
  0.7 28.8 %copy-start.1 = (bf16[256,256]{1,0:T(8,128)(2,1)S(1)}, bf16[256,256]{1,0:T(8,128)(2,1)}, u32[]{:S(2)}) copy-start(bf16[256,256]{1,0:T(8,128)(2,1)} %cot_ref.1) | copy-start | bytes 393220
  11.4 5.3 %collective-permute-start = (f32[256,128]{1,0:T(8,128)}, f32[256,128]{1,0:T(8,128)S(1)}, u32[]{:S(2)}, u32[]{:S(2)}) collective-permute-start(f32[256,128]{1,0:T(8,128)} %get-tuple-element.21), channel_id=1, source_target_pairs={{0,1},{1,0},{2,3},{3,2},{4,5},{5,4},{6,7},{7,6},{8,9},{9,8},{10,11... | collective-permute-start | bytes 393224 | tf_op jit(solution)/shard_map/ppermute | solution.py:307
  11.9 4.7 %collective-permute-start.1 = (f32[256,128]{1,0:T(8,128)}, f32[256,128]{1,0:T(8,128)S(1)}, u32[]{:S(2)}, u32[]{:S(2)}) collective-permute-start(f32[256,128]{1,0:T(8,128)} %get-tuple-element.23), channel_id=1, source_target_pairs={{0,1},{1,0},{2,3},{3,2},{4,5},{5,4},{6,7},{7,6},{8,9},{9,8},{10,11... | collective-permute-start | bytes 393224 | tf_op jit(solution)/shard_map/ppermute | solution.py:307
  12.0 1.7 %collective-permute-start.2 = (f32[256,128]{1,0:T(8,128)}, f32[256,128]{1,0:T(8,128)S(1)}, u32[]{:S(2)}, u32[]{:S(2)}) collective-permute-start(f32[256,128]{1,0:T(8,128)} %get-tuple-element.25), channel_id=1, source_target_pairs={{0,1},{1,0},{2,3},{3,2},{4,5},{5,4},{6,7},{7,6},{8,9},{9,8},{10,11... | collective-permute-start | bytes 393224 | tf_op jit(solution)/shard_map/ppermute | solution.py:307
  12.4 5.2 %collective-permute-start.5 = (f32[256,128]{1,0:T(8,128)}, f32[256,128]{1,0:T(8,128)S(1)}, u32[]{:S(2)}, u32[]{:S(2)}) collective-permute-start(f32[256,128]{1,0:T(8,128)} %get-tuple-element.27), channel_id=1, source_target_pairs={{0,1},{1,0},{2,3},{3,2},{4,5},{5,4},{6,7},{7,6},{8,9},{9,8},{10,11... | collective-permute-start | bytes 393224 | tf_op jit(solution)/shard_map/ppermute | solution.py:307
  13.7 6.8 %collective-permute-start.3 = (f32[256,128]{1,0:T(8,128)S(1)}, f32[256,128]{1,0:T(8,128)S(1)}, u32[]{:S(2)}, u32[]{:S(2)}) collective-permute-start(f32[256,128]{1,0:T(8,128)S(1)} %add.120), channel_id=1, source_target_pairs={{0,2},{1,3},{2,0},{3,1},{4,6},{5,7},{6,4},{7,5},{8,10},{9,11},{10,... | collective-permute-start | bytes 393224 | tf_op jit(solution)/shard_map/ppermute | solution.py:310
  18.6 6.7 %collective-permute-start.6 = (f32[256,128]{1,0:T(8,128)S(1)}, f32[256,128]{1,0:T(8,128)S(1)}, u32[]{:S(2)}, u32[]{:S(2)}) collective-permute-start(f32[256,128]{1,0:T(8,128)S(1)} %add.122), channel_id=1, source_target_pairs={{0,2},{1,3},{2,0},{3,1},{4,6},{5,7},{6,4},{7,5},{8,10},{9,11},{10,... | collective-permute-start | bytes 393224 | tf_op jit(solution)/shard_map/ppermute | solution.py:310
  20.5 8.9 %collective-permute-start.4 = (f32[256,128]{1,0:T(8,128)S(1)}, f32[256,128]{1,0:T(8,128)S(1)}, u32[]{:S(2)}, u32[]{:S(2)}) collective-permute-start(f32[256,128]{1,0:T(8,128)S(1)} %add.121), channel_id=1, source_target_pairs={{0,4},{1,5},{2,6},{3,7},{4,0},{5,1},{6,2},{7,3},{8,12},{9,13},{10,... | collective-permute-start | bytes 393224 | tf_op jit(solution)/shard_map/ppermute | solution.py:310
  30.5 8.4 %collective-permute-start.10 = (f32[128,256]{1,0:T(8,128)S(1)}, f32[128,256]{1,0:T(8,128)S(1)}, u32[]{:S(2)}, u32[]{:S(2)}) collective-permute-start(f32[128,256]{1,0:T(8,128)S(1)} %get-tuple-element.30.refs_0_), channel_id=1, source_target_pairs={{0,4},{1,5},{2,6},{3,7},{4,0},{5,1},{6,2},{7,3},{8,12},{9,13},{10,... | collective-permute-start | bytes 393224 | tf_op jit(solution)/shard_map/ppermute | solution.py:310
  30.5 8.9 %collective-permute-start.8 = (f32[128,256]{1,0:T(8,128)S(1)}, f32[128,256]{1,0:T(8,128)S(1)}, u32[]{:S(2)}, u32[]{:S(2)}) collective-permute-start(f32[128,256]{1,0:T(8,128)S(1)} %get-tuple-element.30.refs_0_), channel_id=1, source_target_pairs={{0,2},{1,3},{2,0},{3,1},{4,6},{5,7},{6,4},{7,5},{8,10},{9,11},{10,... | collective-permute-start | bytes 393224 | tf_op jit(solution)/shard_map/ppermute | solution.py:310
  38.9 1.4 %collective-permute-start.11 = (f32[128,256]{1,0:T(8,128)S(1)}, f32[128,256]{1,0:T(8,128)S(1)}, u32[]{:S(2)}, u32[]{:S(2)}) collective-permute-start(f32[128,256]{1,0:T(8,128)S(1)} %collective-permute-done.10.refs_4_), channel_id=1, source_target_pairs={{0,1},{1,0},{2,3},{3,2},{4,5},{5,4},{6,7},{7,6},{8,9},{9,8},{10,11... | collective-permute-start | bytes 393224 | tf_op jit(solution)/shard_map/ppermute | solution.py:307
  38.9 1.4 %collective-permute-start.13 = (f32[128,128]{1,0:T(8,128)S(1)}, f32[128,128]{1,0:T(8,128)S(1)}, u32[]{:S(2)}, u32[]{:S(2)}) collective-permute-start(f32[128,128]{1,0:T(8,128)S(1)} %get-tuple-element.34), channel_id=1, source_target_pairs={{0,1},{1,0},{2,3},{3,2},{4,5},{5,4},{6,7},{7,6},{8,9},{9,8},{10,11... | collective-permute-start | bytes 196616 | tf_op jit(solution)/shard_map/ppermute | solution.py:307
  39.4 2.4 %collective-permute-start.7 = (f32[128,256]{1,0:T(8,128)S(1)}, f32[128,256]{1,0:T(8,128)S(1)}, u32[]{:S(2)}, u32[]{:S(2)}) collective-permute-start(f32[128,256]{1,0:T(8,128)S(1)} %get-tuple-element.30.refs_0_), channel_id=1, source_target_pairs={{0,1},{1,0},{2,3},{3,2},{4,5},{5,4},{6,7},{7,6},{8,9},{9,8},{10,11... | collective-permute-start | bytes 393224 | tf_op jit(solution)/shard_map/ppermute | solution.py:307
  39.4 7.4 %collective-permute-start.12 = (f32[128,256]{1,0:T(8,128)S(1)}, f32[128,256]{1,0:T(8,128)S(1)}, u32[]{:S(2)}, u32[]{:S(2)}) collective-permute-start(f32[128,256]{1,0:T(8,128)S(1)} %collective-permute-done.10.refs_4_), channel_id=1, source_target_pairs={{0,2},{1,3},{2,0},{3,1},{4,6},{5,7},{6,4},{7,5},{8,10},{9,11},{10,... | collective-permute-start | bytes 393224 | tf_op jit(solution)/shard_map/ppermute | solution.py:310
  39.4 2.3 %collective-permute-start.9 = (f32[128,256]{1,0:T(8,128)S(1)}, f32[128,256]{1,0:T(8,128)S(1)}, u32[]{:S(2)}, u32[]{:S(2)}) collective-permute-start(f32[128,256]{1,0:T(8,128)S(1)} %collective-permute-done.8.refs_2_), channel_id=1, source_target_pairs={{0,1},{1,0},{2,3},{3,2},{4,5},{5,4},{6,7},{7,6},{8,9},{9,8},{10,11... | collective-permute-start | bytes 393224 | tf_op jit(solution)/shard_map/ppermute | solution.py:307
  40.4 6.4 %collective-permute-start.14 = (f32[128,128]{1,0:T(8,128)S(1)}, f32[128,128]{1,0:T(8,128)S(1)}, u32[]{:S(2)}, u32[]{:S(2)}) collective-permute-start(f32[128,128]{1,0:T(8,128)S(1)} %fusion), channel_id=1, source_target_pairs={{0,2},{1,3},{2,0},{3,1},{4,6},{5,7},{6,4},{7,5},{8,10},{9,11},{10,... | collective-permute-start | bytes 196616 | tf_op jit(solution)/shard_map/ppermute | solution.py:310
  46.9 1.4 %collective-permute-start.15 = (f32[128,256]{1,0:T(8,128)S(1)}, f32[128,256]{1,0:T(8,128)S(1)}, u32[]{:S(2)}, u32[]{:S(2)}) collective-permute-start(f32[128,256]{1,0:T(8,128)S(1)} %add_add_fusion.refs_0_), channel_id=1, source_target_pairs={{0,1},{1,0},{2,3},{3,2},{4,5},{5,4},{6,7},{7,6},{8,9},{9,8},{10,11... | collective-permute-start | bytes 393224 | tf_op jit(solution)/shard_map/ppermute | solution.py:307
  47.0 6.5 %collective-permute-start.19 = (f32[128,128]{1,0:T(8,128)S(1)}, f32[128,128]{1,0:T(8,128)S(1)}, u32[]{:S(2)}, u32[]{:S(2)}) collective-permute-start(f32[128,128]{1,0:T(8,128)S(1)} %add_add_fusion.1), channel_id=1, source_target_pairs={{0,4},{1,5},{2,6},{3,7},{4,0},{5,1},{6,2},{7,3},{8,12},{9,13},{10,... | collective-permute-start | bytes 196616 | tf_op jit(solution)/shard_map/ppermute | solution.py:310
  49.4 9.1 %collective-permute-start.16 = (f32[512,128]{1,0:T(8,128)S(1)}, f32[512,128]{1,0:T(8,128)S(1)}, u32[]{:S(2)}, u32[]{:S(2)}) collective-permute-start(f32[512,128]{1,0:T(8,128)S(1)} %get-tuple-element.35), channel_id=1, source_target_pairs={{0,8},{8,0},{16,24},{24,16},{1,9},{9,1},{17,25},{25,17},{2,10},{10... | collective-permute-start | bytes 786440 | tf_op jit(solution)/shard_map/ppermute | solution.py:313
  51.0 9.9 %collective-permute-start.18 = (f32[512,128]{1,0:T(8,128)S(1)}, f32[512,128]{1,0:T(8,128)S(1)}, u32[]{:S(2)}, u32[]{:S(2)}) collective-permute-start(f32[512,128]{1,0:T(8,128)S(1)} %get-tuple-element.36), channel_id=1, source_target_pairs={{0,16},{8,24},{16,0},{24,8},{1,17},{9,25},{17,1},{25,9},{2,18},{10... | collective-permute-start | bytes 786440 | tf_op jit(solution)/shard_map/ppermute | solution.py:313
  53.5 6.7 %collective-permute-start.20 = (f32[128,128]{1,0:T(8,128)S(1)}, f32[128,128]{1,0:T(8,128)S(1)}, u32[]{:S(2)}, u32[]{:S(2)}) collective-permute-start(f32[128,128]{1,0:T(8,128)S(1)} %bitcast_add_fusion.3), channel_id=1, source_target_pairs={{0,8},{8,0},{16,24},{24,16},{1,9},{9,1},{17,25},{25,17},{2,10},{10... | collective-permute-start | bytes 196616 | tf_op jit(solution)/shard_map/ppermute | solution.py:313
  58.6 7.6 %collective-permute-start.17 = (f32[512,128]{1,0:T(8,128)S(1)}, f32[512,128]{1,0:T(8,128)S(1)}, u32[]{:S(2)}, u32[]{:S(2)}) collective-permute-start(f32[512,128]{1,0:T(8,128)S(1)} %add.131), channel_id=1, source_target_pairs={{0,16},{8,24},{16,0},{24,8},{1,17},{9,25},{17,1},{25,9},{2,18},{10... | collective-permute-start | bytes 786440 | tf_op jit(solution)/shard_map/ppermute | solution.py:313
  60.2 6.7 %collective-permute-start.22 = (f32[128,128]{1,0:T(8,128)S(1)}, f32[128,128]{1,0:T(8,128)S(1)}, u32[]{:S(2)}, u32[]{:S(2)}) collective-permute-start(f32[128,128]{1,0:T(8,128)S(1)} %get-tuple-element.37), channel_id=1, source_target_pairs={{0,16},{8,24},{16,0},{24,8},{1,17},{9,25},{17,1},{25,9},{2,18},{10... | collective-permute-start | bytes 196616 | tf_op jit(solution)/shard_map/ppermute | solution.py:313
  60.9 7.3 %collective-permute-start.21 = (f32[512,128]{1,0:T(8,128)S(1)}, f32[512,128]{1,0:T(8,128)S(1)}, u32[]{:S(2)}, u32[]{:S(2)}) collective-permute-start(f32[512,128]{1,0:T(8,128)S(1)} %bitcast_add_fusion), channel_id=1, source_target_pairs={{0,8},{8,0},{16,24},{24,16},{1,9},{9,1},{17,25},{25,17},{2,10},{10... | collective-permute-start | bytes 786440 | tf_op jit(solution)/shard_map/ppermute | solution.py:313
  66.9 2.2 %collective-permute-start.23 = (f32[128,128]{1,0:T(8,128)S(1)}, f32[128,128]{1,0:T(8,128)S(1)}, u32[]{:S(2)}, u32[]{:S(2)}) collective-permute-start(f32[128,128]{1,0:T(8,128)S(1)} %bitcast_add_fusion.1), channel_id=1, source_target_pairs={{0,1},{1,0},{2,3},{3,2},{4,5},{5,4},{6,7},{7,6},{8,9},{9,8},{10,11... | collective-permute-start | bytes 196616 | tf_op jit(solution)/shard_map/ppermute | solution.py:307

commit v11 on v10

--- a/solution.py
+++ b/solution.py
@@ -49,10 +49,12 @@
 
 def forward_kernel(
     n_col, chunk, panel_dev, node_dev,
-    rows_ref, cols_ref, live_ref, deg_ref, feat_ref, blocks_ref, *refs,
+    rows_hbm, cols_hbm, live_ref, deg_hbm, feat_hbm, blocks_ref, *refs,
 ):
     outs, tile_ref = refs[:n_col], refs[n_col]
-    accs, (both, buf, scaled, result, in_sems, dense_sems, out_sems) = refs[n_col + 1:-7], refs[-7:]
+    accs, refs = refs[n_col + 1:-12], refs[-12:]
+    both, buf, scaled, result, rows_ref, cols_ref, deg_ref, feat_ref = refs[:8]
+    in_sems, dense_sems, out_sems, small_sems = refs[8:]
     part = EDGE // len(accs)
     slots = buf.shape[0]
     col_nodes, width = feat_ref.shape
@@ -76,8 +78,14 @@
     def result_copy(rel, j):
         return pltpu.make_async_copy(result.at[j], outs[rel], out_sems.at[j])
 
-    for c in range(n_chunks):
+    block_copy(0).start()
+    small = fetch(
+        [(rows_hbm, rows_ref), (cols_hbm, cols_ref), (deg_hbm, deg_ref), (feat_hbm, feat_ref)],
+        small_sems)
+    for c in range(1, n_chunks):
         block_copy(c).start()
+    for copy in small:
+        copy.wait()
 
     for k in range(col_blocks):
         inv = inv_column(deg_ref, me * col_blocks + k)
@@ -283,7 +291,7 @@
         functools.partial(forward_kernel, n_col, chunk, panel_dev, node_dev),
         out_shape=[jax.ShapeDtypeStruct((node_dev, width), F32)] * n_col
         + [jax.ShapeDtypeStruct((row_nodes, col_nodes), BF16)],
-        in_specs=[smem, smem, smem, vmem, vmem, any_space],
+        in_specs=[any_space, any_space, smem, any_space, any_space, any_space],
         out_specs=[any_space] * (n_col + 1),
         scratch_shapes=[
             pltpu.VMEM((positions + 1, EDGE // QUARTERS, EDGE), F32) for _ in range(QUARTERS)
@@ -292,9 +300,14 @@
             pltpu.VMEM((slots, EDGE, EDGE), BF16),
             pltpu.VMEM((col_nodes, width), BF16),
             pltpu.VMEM((panel_dev, node_dev, width), F32),
+            pltpu.SMEM(block_rows.shape, jnp.int32),
+            pltpu.SMEM(block_cols.shape, jnp.int32),
+            pltpu.VMEM(deg.shape, jnp.int32),
+            pltpu.VMEM(features.shape, BF16),
             pltpu.SemaphoreType.DMA((slots // chunk,)),
             pltpu.SemaphoreType.DMA((panel_dev,)),
             pltpu.SemaphoreType.DMA((panel_dev,)),
+            pltpu.SemaphoreType.DMA((4,)),
         ],
         compiler_params=params(54),
         name="densify_forward",
@@ -377,7 +390,7 @@
     )(tile, *early)
 
     wsum = after(wsum, sofar) + moved
-    own[last] = after(after(own[last], sofar), wsum)
+    own[last] = after(own[last], sofar)
     late = [own[last], swap(own[last])]
     for bit in range(1, chip_bits):
         wsum = wsum + chip_flip(wsum, bit)
@@ -406,7 +419,7 @@
     done = list(done)
     for t in range(row_bits):
         wsum = after(wsum, done[-1 if t == 0 else 0])
-        wsum = wsum + row_flip(wsum, t)
+        wsum = wsum + row_flip(wsum, (t + 1) % row_bits)
         done = [x + row_flip(x, (i + t) % row_bits) for i, x in enumerate(done)]
         if t == 0:
             done[-1] = after(done[-1], wsum)

time: 70 us -> 72.6 us (1.037)
  Pallas kernels: 15.2 us -> 17.7 us
    pallas_call x1, Pallas kernels: 10 us -> 12.6 us  [body(): pl.pallas_call(functools.partial(forward_kernel, n_col, chunk, panel_dev,...]
    ppermute x10, waiting for transfers between devices: 1.8 us -> 0.87 us  [swap(): return lax.ppermute(x, 'col', swap_pairs)]
    ppermute x6, waiting for transfers between devices: 9.12 us -> 9.88 us  [row_flip(): return lax.ppermute(x, 'row', [(i, i ^ 1 << bit) for i in range(n_row)])]
    add x3 -> x4, other arithmetic: 1.94 us -> 1.96 us  [after(): return x + 0.0 * other[:, :x.shape[1]]]
  transfers between devices with their start and end apart: 24 -> 24, of which waited for: 13 -> 15; matrix products, arithmetic and copies ran while one was open for 6% -> 5% of each run, Pallas kernels for 6% -> 6%
where the time goes in v11:
time: 72.6 us; the launch traced here: 72.5 us
  waiting for transfers between devices  26.4 us (36%)
  starting transfers between devices  22.2 us (31%)
  Pallas kernels  17.7 us (24%)
  other arithmetic  4.64 us (6%)
  between operations  1.5 us (2%)
    ppermute x8, waiting for transfers between devices, chip_flip(): return lax.ppermute(x, 'col', [(i, i ^ 2 << bit) for i in range(n_col)])  15.6 us
    pallas_call x1, Pallas kernels, body(): pl.pallas_call(functools.partial(forward_kernel, n_col, chunk, panel_dev,...  12.6 us
    ppermute x8, starting transfers between devices, chip_flip(): return lax.ppermute(x, 'col', [(i, i ^ 2 << bit) for i in range(n_col)])  11.1 us
    ppermute x6, waiting for transfers between devices, row_flip(): return lax.ppermute(x, 'row', [(i, i ^ 1 << bit) for i in range(n_row)])  9.88 us
    ppermute x6, starting transfers between devices, row_flip(): return lax.ppermute(x, 'row', [(i, i ^ 1 << bit) for i in range(n_row)])  8.45 us
    pallas_call x1, Pallas kernels, body(): pl.pallas_call(functools.partial(partial_kernel, len(early)), out_shape=(...  2.93 us
    ppermute x10, starting transfers between devices, swap(): return lax.ppermute(x, 'col', swap_pairs)  2.59 us
    add x4, other arithmetic, after(): return x + 0.0 * other[:, :x.shape[1]]  1.96 us
  transfers between devices with their start and end apart: 24, of which 15 were waited for; matrix products, arithmetic and copies ran while one was open for 5% of the time, Pallas kernels for 6%

profile of v11, /device:TPU:0, one launch (start us, length us, event | category | flops | bytes accessed | tf_op | source)
XLA Modules:
  0.0 72.5 jit_solution(7734194158500657018)
XLA Ops:
  1.3 12.6 %densify_forward.1 = (f32[256,128]{1,0:T(8,128)}, f32[256,128]{1,0:T(8,128)}, f32[256,128]{1,0:T(8,128)}, f32[256,128]{1,0:T(8,128)}, f32[256,128]{1,0:T(8,128)}...) custom-call(s32[1,1,384]{2,1,0:T(1,128)} %rows_hbm.1, ...), custom_call_target="tpu_custom_call" | custom-call | tf_op jit(solution)/shard_map/densify_forward/pallas_call | solution.py:290
  14.0 0.8 %collective-permute-start = (f32[256,128]{1,0:T(8,128)}, f32[256,128]{1,0:T(8,128)S(1)}, u32[]{:S(2)}, u32[]{:S(2)}) collective-permute-start(f32[256,128]{1,0:T(8,128)} %get-tuple-element.21), channel_id=1, source_target_pairs={{0,1},{1,0},{2,3},{3,2},{4,5},{5,4},{6,7},{7,6},{8,9},{9,8},{10,11... | collective-permute-start | bytes 393224 | tf_op jit(solution)/shard_map/ppermute | solution.py:320
  15.4 0.9 %multiply_add_fusion = f32[256,128]{1,0:T(8,128)S(1)} fusion(f32[256,128]{1,0:T(8,128)} %get-tuple-element.24), kind=kLoop, calls=%fused_computation.2 | loop fusion | flops 65536 | bytes 262144 | tf_op jit(solution)/shard_map/add | solution.py:281
  16.6 2.8 %collective-permute-start.3 = (f32[256,128]{1,0:T(8,128)S(1)}, f32[256,128]{1,0:T(8,128)S(1)}, u32[]{:S(2)}, u32[]{:S(2)}) collective-permute-start(f32[256,128]{1,0:T(8,128)S(1)} %add.109), channel_id=1, source_target_pairs={{0,2},{1,3},{2,0},{3,1},{4,6},{5,7},{6,4},{7,5},{8,10},{9,11},{10,... | collective-permute-start | bytes 393224 | tf_op jit(solution)/shard_map/ppermute | solution.py:323
  19.3 1.0 %multiply_add_fusion.2 = (f32[256,128]{1,0:T(8,128)S(1)}, f32[256,128]{1,0:T(8,128)S(1)}) fusion(f32[256,128]{1,0:T(8,128)} %get-tuple-element.22, f32[256,128]{1,0:T(8,128)S(1)} %collective-permute-done.1, f32[256,128]{1,0:T(8,128)} %get-tuple-element.20, f32[256,128]{1,0:T(8,128)S(1)} %collective-permute-done), kind=kLoop, calls=%fused_computation.5 | loop fusion | flops 131072 | bytes 786432 | tf_op jit(solution)/shard_map/add | solution.py:281
  20.4 0.9 %add.111 = f32[256,128]{1,0:T(8,128)S(1)} add(f32[256,128]{1,0:T(8,128)} %get-tuple-element.26, f32[256,128]{1,0:T(8,128)S(1)} %collective-permute-done.5) | non-fusion elementwise | flops 32768 | bytes 393216 | tf_op jit(solution)/shard_map/add | solution.py:339
  21.4 1.8 %collective-permute-done.3 = f32[256,128]{1,0:T(8,128)S(1)} collective-permute-done((f32[256,128]{1,0:T(8,128)S(1)}, f32[256,128]{1,0:T(8,128)S(1)}, u32[]{:S(2)}, u32[]{:S(2)}) %collective-permute-start.3) | collective-permute-done | bytes 131104 | tf_op jit(solution)/shard_map/ppermute | solution.py:323
  23.2 2.8 %collective-permute-start.4 = (f32[256,128]{1,0:T(8,128)S(1)}, f32[256,128]{1,0:T(8,128)S(1)}, u32[]{:S(2)}, u32[]{:S(2)}) collective-permute-start(f32[256,128]{1,0:T(8,128)S(1)} %add.110), channel_id=1, source_target_pairs={{0,4},{1,5},{2,6},{3,7},{4,0},{5,1},{6,2},{7,3},{8,12},{9,13},{10,... | collective-permute-start | bytes 393224 | tf_op jit(solution)/shard_map/ppermute | solution.py:323
  26.0 2.1 %collective-permute-done.6.refs_2_ = f32[256,128]{1,0:T(8,128)S(1)} collective-permute-done((f32[256,128]{1,0:T(8,128)S(1)}, f32[256,128]{1,0:T(8,128)S(1)}, u32[]{:S(2)}, u32[]{:S(2)}) %collective-permute-start.6) | collective-permute-done | bytes 131104 | tf_op jit(solution)/shard_map/ppermute | solution.py:323
  28.1 4.0 %collective-permute-done.4.refs_1_ = f32[256,128]{1,0:T(8,128)S(1)} collective-permute-done((f32[256,128]{1,0:T(8,128)S(1)}, f32[256,128]{1,0:T(8,128)S(1)}, u32[]{:S(2)}, u32[]{:S(2)}) %collective-permute-start.4) | collective-permute-done | bytes 131104 | tf_op jit(solution)/shard_map/ppermute | solution.py:323
  32.1 1.1 %middle.1 = (bf16[256,256]{1,0:T(8,128)(2,1)}, f32[128,256]{1,0:T(8,128)S(1)}, f32[128,128]{1,0:T(8,128)S(1)}, f32[128,128]{1,0:T(8,128)S(1)}) custom-call(s32[64,128]{1,0:T(8,128)S(1)} %bitcast.10, bf16[256,256]{1,0:T(8,128)(2,1)S(1)} %copy-done.1, bf16[128,256]{1,0:T(8,128)(2,1)S(1)} %copy-done.2, f32[256,128]{1,0:T(8,128)S(1)} %get-tuple-element.40.refs_0_, ...), custom_call_target="tpu_custom_call" | custom-call | tf_op jit(solution)/shard_map/middle/pallas_call | solution.py:348
  33.2 3.9 %collective-permute-start.8 = (f32[128,256]{1,0:T(8,128)S(1)}, f32[128,256]{1,0:T(8,128)S(1)}, u32[]{:S(2)}, u32[]{:S(2)}) collective-permute-start(f32[128,256]{1,0:T(8,128)S(1)} %get-tuple-element.30.refs_0_), channel_id=1, source_target_pairs={{0,2},{1,3},{2,0},{3,1},{4,6},{5,7},{6,4},{7,5},{8,10},{9,11},{10,... | collective-permute-start | bytes 393224 | tf_op jit(solution)/shard_map/ppermute | solution.py:323
  37.1 4.5 %collective-permute-done.10.refs_4_ = f32[128,256]{1,0:T(8,128)S(1)} collective-permute-done((f32[128,256]{1,0:T(8,128)S(1)}, f32[128,256]{1,0:T(8,128)S(1)}, u32[]{:S(2)}, u32[]{:S(2)}) %collective-permute-start.10) | collective-permute-done | bytes 131104 | tf_op jit(solution)/shard_map/ppermute | solution.py:323
  41.6 0.5 collective-permute-start.17
  42.1 0.5 collective-permute-start.9
  43.1 1.4 %collective-permute-start.18 = (f32[128,128]{1,0:T(8,128)S(1)}, f32[128,128]{1,0:T(8,128)S(1)}, u32[]{:S(2)}, u32[]{:S(2)}) collective-permute-start(f32[128,128]{1,0:T(8,128)S(1)} %fusion), channel_id=1, source_target_pairs={{0,2},{1,3},{2,0},{3,1},{4,6},{5,7},{6,4},{7,5},{8,10},{9,11},{10,... | collective-permute-start | bytes 196616 | tf_op jit(solution)/shard_map/ppermute | solution.py:323
  44.5 2.9 %backward_early.1 = (f32[128,1024]{1,0:T(8,128)S(1)}, bf16[512,1024]{1,0:T(8,128)(2,1)S(1)}) custom-call(bf16[2048,1024]{1,0:T(8,128)(2,1)} %get-tuple-element.29.tile_ref, f32[128,256]{1,0:T(8,128)S(1)} %get-tuple-element.30.refs_0_, f32[128,256]{1,0:T(8,128)S(1)} %collective-permute-done.7.refs_1_, f32[128,256]{1,0:T(8,128)S(1)} %collective-permute-done.8.refs_2_, ...), custom_call_target="tpu_custom_call" | custom-call | flops 1073741824 | bytes 33554432 | tf_op jit(solution)/shard_map/backward_early/pallas_call | solution.py:371
  47.4 1.0 %collective-permute-done.12 = f32[128,256]{1,0:T(8,128)S(1)} collective-permute-done((f32[128,256]{1,0:T(8,128)S(1)}, f32[128,256]{1,0:T(8,128)S(1)}, u32[]{:S(2)}, u32[]{:S(2)}) %collective-permute-start.12) | collective-permute-done | bytes 131104 | tf_op jit(solution)/shard_map/ppermute | solution.py:323
  48.5 0.9 %collective-permute-done.18 = f32[128,128]{1,0:T(8,128)S(1)} collective-permute-done((f32[128,128]{1,0:T(8,128)S(1)}, f32[128,128]{1,0:T(8,128)S(1)}, u32[]{:S(2)}, u32[]{:S(2)}) %collective-permute-start.18) | collective-permute-done | bytes 65568 | tf_op jit(solution)/shard_map/ppermute | solution.py:323
  49.8 1.1 %backward_late.1 = (f32[512,128]{1,0:T(8,128)S(1)}, f32[512,128]{1,0:T(8,128)S(1)}) custom-call(s32[64,128]{1,0:T(8,128)S(1)} %bitcast.11, bf16[512,1024]{1,0:T(8,128)(2,1)S(1)} %get-tuple-element.31.dense_ref, f32[128,1024]{1,0:T(8,128)S(1)} %get-tuple-element.32.sofar_ref, f32[128,256]{1,0:T(8,128)S(1)} %multiply_add_fusion.1.refs_0_, ...), custom_call_target="tpu_custom_call" | custom-call | tf_op jit(solution)/shard_map/backward_late/pallas_call | solution.py:401
  51.0 1.7 %collective-permute-start.14 = (f32[512,128]{1,0:T(8,128)S(1)}, f32[512,128]{1,0:T(8,128)S(1)}, u32[]{:S(2)}, u32[]{:S(2)}) collective-permute-start(f32[512,128]{1,0:T(8,128)S(1)} %get-tuple-element.33), channel_id=1, source_target_pairs={{0,8},{8,0},{16,24},{24,16},{1,9},{9,1},{17,25},{25,17},{2,10},{10... | collective-permute-start | bytes 786440 | tf_op jit(solution)/shard_map/ppermute | solution.py:326
  52.7 1.5 %collective-permute-start.16 = (f32[512,128]{1,0:T(8,128)S(1)}, f32[512,128]{1,0:T(8,128)S(1)}, u32[]{:S(2)}, u32[]{:S(2)}) collective-permute-start(f32[512,128]{1,0:T(8,128)S(1)} %get-tuple-element.34), channel_id=1, source_target_pairs={{0,16},{8,24},{16,0},{24,8},{1,17},{9,25},{17,1},{25,9},{2,18},{10... | collective-permute-start | bytes 786440 | tf_op jit(solution)/shard_map/ppermute | solution.py:326
  54.2 1.3 %collective-permute-done.19 = f32[128,128]{1,0:T(8,128)S(1)} collective-permute-done((f32[128,128]{1,0:T(8,128)S(1)}, f32[128,128]{1,0:T(8,128)S(1)}, u32[]{:S(2)}, u32[]{:S(2)}) %collective-permute-start.19) | collective-permute-done | bytes 65568 | tf_op jit(solution)/shard_map/ppermute | solution.py:323
  55.5 1.6 %collective-permute-start.20 = (f32[128,128]{1,0:T(8,128)S(1)}, f32[128,128]{1,0:T(8,128)S(1)}, u32[]{:S(2)}, u32[]{:S(2)}) collective-permute-start(f32[128,128]{1,0:T(8,128)S(1)} %bitcast_add_fusion.3), channel_id=1, source_target_pairs={{0,16},{8,24},{16,0},{24,8},{1,17},{9,25},{17,1},{25,9},{2,18},{10... | collective-permute-start | bytes 196616 | tf_op jit(solution)/shard_map/ppermute | solution.py:326
  57.0 2.4 %collective-permute-done.14 = f32[512,128]{1,0:T(8,128)S(1)} collective-permute-done((f32[512,128]{1,0:T(8,128)S(1)}, f32[512,128]{1,0:T(8,128)S(1)}, u32[]{:S(2)}, u32[]{:S(2)}) %collective-permute-start.14) | collective-permute-done | bytes 262176 | tf_op jit(solution)/shard_map/ppermute | solution.py:326
  59.4 1.6 %collective-permute-start.15 = (f32[512,128]{1,0:T(8,128)S(1)}, f32[512,128]{1,0:T(8,128)S(1)}, u32[]{:S(2)}, u32[]{:S(2)}) collective-permute-start(f32[512,128]{1,0:T(8,128)S(1)} %add.113), channel_id=1, source_target_pairs={{0,16},{8,24},{16,0},{24,8},{1,17},{9,25},{17,1},{25,9},{2,18},{10... | collective-permute-start | bytes 786440 | tf_op jit(solution)/shard_map/ppermute | solution.py:326
  61.0 1.9 %collective-permute-done.20 = f32[128,128]{1,0:T(8,128)S(1)} collective-permute-done((f32[128,128]{1,0:T(8,128)S(1)}, f32[128,128]{1,0:T(8,128)S(1)}, u32[]{:S(2)}, u32[]{:S(2)}) %collective-permute-start.20) | collective-permute-done | bytes 65568 | tf_op jit(solution)/shard_map/ppermute | solution.py:326
  63.1 2.1 %collective-permute-start.21 = (f32[512,128]{1,0:T(8,128)S(1)}, f32[512,128]{1,0:T(8,128)S(1)}, u32[]{:S(2)}, u32[]{:S(2)}) collective-permute-start(f32[512,128]{1,0:T(8,128)S(1)} %bitcast_add_fusion), channel_id=1, source_target_pairs={{0,8},{8,0},{16,24},{24,16},{1,9},{9,1},{17,25},{25,17},{2,10},{10... | collective-permute-start | bytes 786440 | tf_op jit(solution)/shard_map/ppermute | solution.py:326
  65.1 2.7 %collective-permute-done.15 = f32[512,128]{1,0:T(8,128)S(1)} collective-permute-done((f32[512,128]{1,0:T(8,128)S(1)}, f32[512,128]{1,0:T(8,128)S(1)}, u32[]{:S(2)}, u32[]{:S(2)}) %collective-permute-start.15) | collective-permute-done | bytes 262176 | tf_op jit(solution)/shard_map/ppermute | solution.py:326
  68.1 2.8 %collective-permute-done.21 = f32[512,128]{1,0:T(8,128)S(1)} collective-permute-done((f32[512,128]{1,0:T(8,128)S(1)}, f32[512,128]{1,0:T(8,128)S(1)}, u32[]{:S(2)}, u32[]{:S(2)}) %collective-permute-start.21) | collective-permute-done | bytes 262176 | tf_op jit(solution)/shard_map/ppermute | solution.py:326
  70.9 0.8 %pad_maximum_fusion = f32[1024,128]{1,0:T(8,128)} fusion(f32[512,128]{1,0:T(8,128)S(1)} %add.128, f32[512,128]{1,0:T(8,128)S(1)} %add.114), kind=kLoop, calls=%fused_computation | loop fusion | flops 131072 | bytes 1048576 | tf_op jit(solution)/shard_map/concatenate | solution.py:427
  71.8 0.7 maximum_maximum_fusion
  (49 shorter events, 2.4 us)
Async XLA Ops:
  0.6 31.5 %copy-start = (s32[8192]{0:T(1024)S(1)}, s32[8192]{0:T(1024)}, u32[]{:S(2)}) copy-start(s32[8192]{0:T(1024)} %param.9) | copy-start | bytes 98308
  0.6 31.5 %copy-start.2 = (bf16[128,256]{1,0:T(8,128)(2,1)S(1)}, bf16[128,256]{1,0:T(8,128)(2,1)}, u32[]{:S(2)}) copy-start(bf16[128,256]{1,0:T(8,128)(2,1)} %weight_ref.1) | copy-start | bytes 196612
  0.7 31.5 %copy-start.1 = (bf16[256,256]{1,0:T(8,128)(2,1)S(1)}, bf16[256,256]{1,0:T(8,128)(2,1)}, u32[]{:S(2)}) copy-start(bf16[256,256]{1,0:T(8,128)(2,1)} %cot_ref.1) | copy-start | bytes 393220
  14.0 5.4 %collective-permute-start = (f32[256,128]{1,0:T(8,128)}, f32[256,128]{1,0:T(8,128)S(1)}, u32[]{:S(2)}, u32[]{:S(2)}) collective-permute-start(f32[256,128]{1,0:T(8,128)} %get-tuple-element.21), channel_id=1, source_target_pairs={{0,1},{1,0},{2,3},{3,2},{4,5},{5,4},{6,7},{7,6},{8,9},{9,8},{10,11... | collective-permute-start | bytes 393224 | tf_op jit(solution)/shard_map/ppermute | solution.py:320
  14.8 4.6 %collective-permute-start.1 = (f32[256,128]{1,0:T(8,128)}, f32[256,128]{1,0:T(8,128)S(1)}, u32[]{:S(2)}, u32[]{:S(2)}) collective-permute-start(f32[256,128]{1,0:T(8,128)} %get-tuple-element.23), channel_id=1, source_target_pairs={{0,1},{1,0},{2,3},{3,2},{4,5},{5,4},{6,7},{7,6},{8,9},{9,8},{10,11... | collective-permute-start | bytes 393224 | tf_op jit(solution)/shard_map/ppermute | solution.py:320
  14.9 1.7 %collective-permute-start.2 = (f32[256,128]{1,0:T(8,128)}, f32[256,128]{1,0:T(8,128)S(1)}, u32[]{:S(2)}, u32[]{:S(2)}) collective-permute-start(f32[256,128]{1,0:T(8,128)} %get-tuple-element.25), channel_id=1, source_target_pairs={{0,1},{1,0},{2,3},{3,2},{4,5},{5,4},{6,7},{7,6},{8,9},{9,8},{10,11... | collective-permute-start | bytes 393224 | tf_op jit(solution)/shard_map/ppermute | solution.py:320
  15.3 5.1 %collective-permute-start.5 = (f32[256,128]{1,0:T(8,128)}, f32[256,128]{1,0:T(8,128)S(1)}, u32[]{:S(2)}, u32[]{:S(2)}) collective-permute-start(f32[256,128]{1,0:T(8,128)} %get-tuple-element.27), channel_id=1, source_target_pairs={{0,1},{1,0},{2,3},{3,2},{4,5},{5,4},{6,7},{7,6},{8,9},{9,8},{10,11... | collective-permute-start | bytes 393224 | tf_op jit(solution)/shard_map/ppermute | solution.py:320
  16.6 6.6 %collective-permute-start.3 = (f32[256,128]{1,0:T(8,128)S(1)}, f32[256,128]{1,0:T(8,128)S(1)}, u32[]{:S(2)}, u32[]{:S(2)}) collective-permute-start(f32[256,128]{1,0:T(8,128)S(1)} %add.109), channel_id=1, source_target_pairs={{0,2},{1,3},{2,0},{3,1},{4,6},{5,7},{6,4},{7,5},{8,10},{9,11},{10,... | collective-permute-start | bytes 393224 | tf_op jit(solution)/shard_map/ppermute | solution.py:323
  21.3 6.8 %collective-permute-start.6 = (f32[256,128]{1,0:T(8,128)S(1)}, f32[256,128]{1,0:T(8,128)S(1)}, u32[]{:S(2)}, u32[]{:S(2)}) collective-permute-start(f32[256,128]{1,0:T(8,128)S(1)} %add.111), channel_id=1, source_target_pairs={{0,2},{1,3},{2,0},{3,1},{4,6},{5,7},{6,4},{7,5},{8,10},{9,11},{10,... | collective-permute-start | bytes 393224 | tf_op jit(solution)/shard_map/ppermute | solution.py:323
  23.2 8.9 %collective-permute-start.4 = (f32[256,128]{1,0:T(8,128)S(1)}, f32[256,128]{1,0:T(8,128)S(1)}, u32[]{:S(2)}, u32[]{:S(2)}) collective-permute-start(f32[256,128]{1,0:T(8,128)S(1)} %add.110), channel_id=1, source_target_pairs={{0,4},{1,5},{2,6},{3,7},{4,0},{5,1},{6,2},{7,3},{8,12},{9,13},{10,... | collective-permute-start | bytes 393224 | tf_op jit(solution)/shard_map/ppermute | solution.py:323
  33.2 8.4 %collective-permute-start.10 = (f32[128,256]{1,0:T(8,128)S(1)}, f32[128,256]{1,0:T(8,128)S(1)}, u32[]{:S(2)}, u32[]{:S(2)}) collective-permute-start(f32[128,256]{1,0:T(8,128)S(1)} %get-tuple-element.30.refs_0_), channel_id=1, source_target_pairs={{0,4},{1,5},{2,6},{3,7},{4,0},{5,1},{6,2},{7,3},{8,12},{9,13},{10,... | collective-permute-start | bytes 393224 | tf_op jit(solution)/shard_map/ppermute | solution.py:323
  33.2 8.9 %collective-permute-start.8 = (f32[128,256]{1,0:T(8,128)S(1)}, f32[128,256]{1,0:T(8,128)S(1)}, u32[]{:S(2)}, u32[]{:S(2)}) collective-permute-start(f32[128,256]{1,0:T(8,128)S(1)} %get-tuple-element.30.refs_0_), channel_id=1, source_target_pairs={{0,2},{1,3},{2,0},{3,1},{4,6},{5,7},{6,4},{7,5},{8,10},{9,11},{10,... | collective-permute-start | bytes 393224 | tf_op jit(solution)/shard_map/ppermute | solution.py:323
  41.6 1.4 %collective-permute-start.11 = (f32[128,256]{1,0:T(8,128)S(1)}, f32[128,256]{1,0:T(8,128)S(1)}, u32[]{:S(2)}, u32[]{:S(2)}) collective-permute-start(f32[128,256]{1,0:T(8,128)S(1)} %collective-permute-done.10.refs_4_), channel_id=1, source_target_pairs={{0,1},{1,0},{2,3},{3,2},{4,5},{5,4},{6,7},{7,6},{8,9},{9,8},{10,11... | collective-permute-start | bytes 393224 | tf_op jit(solution)/shard_map/ppermute | solution.py:320
  41.6 1.4 %collective-permute-start.17 = (f32[128,128]{1,0:T(8,128)S(1)}, f32[128,128]{1,0:T(8,128)S(1)}, u32[]{:S(2)}, u32[]{:S(2)}) collective-permute-start(f32[128,128]{1,0:T(8,128)S(1)} %get-tuple-element.36), channel_id=1, source_target_pairs={{0,1},{1,0},{2,3},{3,2},{4,5},{5,4},{6,7},{7,6},{8,9},{9,8},{10,11... | collective-permute-start | bytes 196616 | tf_op jit(solution)/shard_map/ppermute | solution.py:320
  42.1 2.4 %collective-permute-start.7 = (f32[128,256]{1,0:T(8,128)S(1)}, f32[128,256]{1,0:T(8,128)S(1)}, u32[]{:S(2)}, u32[]{:S(2)}) collective-permute-start(f32[128,256]{1,0:T(8,128)S(1)} %get-tuple-element.30.refs_0_), channel_id=1, source_target_pairs={{0,1},{1,0},{2,3},{3,2},{4,5},{5,4},{6,7},{7,6},{8,9},{9,8},{10,11... | collective-permute-start | bytes 393224 | tf_op jit(solution)/shard_map/ppermute | solution.py:320
  42.1 6.3 %collective-permute-start.12 = (f32[128,256]{1,0:T(8,128)S(1)}, f32[128,256]{1,0:T(8,128)S(1)}, u32[]{:S(2)}, u32[]{:S(2)}) collective-permute-start(f32[128,256]{1,0:T(8,128)S(1)} %collective-permute-done.10.refs_4_), channel_id=1, source_target_pairs={{0,2},{1,3},{2,0},{3,1},{4,6},{5,7},{6,4},{7,5},{8,10},{9,11},{10,... | collective-permute-start | bytes 393224 | tf_op jit(solution)/shard_map/ppermute | solution.py:323
  42.1 2.3 %collective-permute-start.9 = (f32[128,256]{1,0:T(8,128)S(1)}, f32[128,256]{1,0:T(8,128)S(1)}, u32[]{:S(2)}, u32[]{:S(2)}) collective-permute-start(f32[128,256]{1,0:T(8,128)S(1)} %collective-permute-done.8.refs_2_), channel_id=1, source_target_pairs={{0,1},{1,0},{2,3},{3,2},{4,5},{5,4},{6,7},{7,6},{8,9},{9,8},{10,11... | collective-permute-start | bytes 393224 | tf_op jit(solution)/shard_map/ppermute | solution.py:320
  43.1 6.4 %collective-permute-start.18 = (f32[128,128]{1,0:T(8,128)S(1)}, f32[128,128]{1,0:T(8,128)S(1)}, u32[]{:S(2)}, u32[]{:S(2)}) collective-permute-start(f32[128,128]{1,0:T(8,128)S(1)} %fusion), channel_id=1, source_target_pairs={{0,2},{1,3},{2,0},{3,1},{4,6},{5,7},{6,4},{7,5},{8,10},{9,11},{10,... | collective-permute-start | bytes 196616 | tf_op jit(solution)/shard_map/ppermute | solution.py:323
  48.4 1.4 %collective-permute-start.13 = (f32[128,256]{1,0:T(8,128)S(1)}, f32[128,256]{1,0:T(8,128)S(1)}, u32[]{:S(2)}, u32[]{:S(2)}) collective-permute-start(f32[128,256]{1,0:T(8,128)S(1)} %multiply_add_fusion.1.refs_0_), channel_id=1, source_target_pairs={{0,1},{1,0},{2,3},{3,2},{4,5},{5,4},{6,7},{7,6},{8,9},{9,8},{10,11... | collective-permute-start | bytes 393224 | tf_op jit(solution)/shard_map/ppermute | solution.py:320
  49.4 6.0 %collective-permute-start.19 = (f32[128,128]{1,0:T(8,128)S(1)}, f32[128,128]{1,0:T(8,128)S(1)}, u32[]{:S(2)}, u32[]{:S(2)}) collective-permute-start(f32[128,128]{1,0:T(8,128)S(1)} %add_add_fusion), channel_id=1, source_target_pairs={{0,4},{1,5},{2,6},{3,7},{4,0},{5,1},{6,2},{7,3},{8,12},{9,13},{10,... | collective-permute-start | bytes 196616 | tf_op jit(solution)/shard_map/ppermute | solution.py:323
  51.0 8.4 %collective-permute-start.14 = (f32[512,128]{1,0:T(8,128)S(1)}, f32[512,128]{1,0:T(8,128)S(1)}, u32[]{:S(2)}, u32[]{:S(2)}) collective-permute-start(f32[512,128]{1,0:T(8,128)S(1)} %get-tuple-element.33), channel_id=1, source_target_pairs={{0,8},{8,0},{16,24},{24,16},{1,9},{9,1},{17,25},{25,17},{2,10},{10... | collective-permute-start | bytes 786440 | tf_op jit(solution)/shard_map/ppermute | solution.py:326
  52.7 10.3 %collective-permute-start.16 = (f32[512,128]{1,0:T(8,128)S(1)}, f32[512,128]{1,0:T(8,128)S(1)}, u32[]{:S(2)}, u32[]{:S(2)}) collective-permute-start(f32[512,128]{1,0:T(8,128)S(1)} %get-tuple-element.34), channel_id=1, source_target_pairs={{0,16},{8,24},{16,0},{24,8},{1,17},{9,25},{17,1},{25,9},{2,18},{10... | collective-permute-start | bytes 786440 | tf_op jit(solution)/shard_map/ppermute | solution.py:326
  55.5 7.4 %collective-permute-start.20 = (f32[128,128]{1,0:T(8,128)S(1)}, f32[128,128]{1,0:T(8,128)S(1)}, u32[]{:S(2)}, u32[]{:S(2)}) collective-permute-start(f32[128,128]{1,0:T(8,128)S(1)} %bitcast_add_fusion.3), channel_id=1, source_target_pairs={{0,16},{8,24},{16,0},{24,8},{1,17},{9,25},{17,1},{25,9},{2,18},{10... | collective-permute-start | bytes 196616 | tf_op jit(solution)/shard_map/ppermute | solution.py:326
  59.4 8.4 %collective-permute-start.15 = (f32[512,128]{1,0:T(8,128)S(1)}, f32[512,128]{1,0:T(8,128)S(1)}, u32[]{:S(2)}, u32[]{:S(2)}) collective-permute-start(f32[512,128]{1,0:T(8,128)S(1)} %add.113), channel_id=1, source_target_pairs={{0,16},{8,24},{16,0},{24,8},{1,17},{9,25},{17,1},{25,9},{2,18},{10... | collective-permute-start | bytes 786440 | tf_op jit(solution)/shard_map/ppermute | solution.py:326
  62.9 5.1 %collective-permute-start.22 = (f32[128,128]{1,0:T(8,128)S(1)}, f32[128,128]{1,0:T(8,128)S(1)}, u32[]{:S(2)}, u32[]{:S(2)}) collective-permute-start(f32[128,128]{1,0:T(8,128)S(1)} %get-tuple-element.37), channel_id=1, source_target_pairs={{0,8},{8,0},{16,24},{24,16},{1,9},{9,1},{17,25},{25,17},{2,10},{10... | collective-permute-start | bytes 196616 | tf_op jit(solution)/shard_map/ppermute | solution.py:326
  63.1 7.8 %collective-permute-start.21 = (f32[512,128]{1,0:T(8,128)S(1)}, f32[512,128]{1,0:T(8,128)S(1)}, u32[]{:S(2)}, u32[]{:S(2)}) collective-permute-start(f32[512,128]{1,0:T(8,128)S(1)} %bitcast_add_fusion), channel_id=1, source_target_pairs={{0,8},{8,0},{16,24},{24,16},{1,9},{9,1},{17,25},{25,17},{2,10},{10... | collective-permute-start | bytes 786440 | tf_op jit(solution)/shard_map/ppermute | solution.py:326
  68.0 3.7 %collective-permute-start.23 = (f32[128,128]{1,0:T(8,128)S(1)}, f32[128,128]{1,0:T(8,128)S(1)}, u32[]{:S(2)}, u32[]{:S(2)}) collective-permute-start(f32[128,128]{1,0:T(8,128)S(1)} %bitcast_add_fusion.1), channel_id=1, source_target_pairs={{0,1},{1,0},{2,3},{3,2},{4,5},{5,4},{6,7},{7,6},{8,9},{9,8},{10,11... | collective-permute-start | bytes 196616 | tf_op jit(solution)/shard_map/ppermute | solution.py:320

commit v12 on v11

--- a/solution.py
+++ b/solution.py
@@ -78,15 +78,21 @@
     def result_copy(rel, j):
         return pltpu.make_async_copy(result.at[j], outs[rel], out_sems.at[j])
 
-    block_copy(0).start()
     small = fetch(
         [(rows_hbm, rows_ref), (cols_hbm, cols_ref), (deg_hbm, deg_ref), (feat_hbm, feat_ref)],
         small_sems)
-    for c in range(1, n_chunks):
+    for c in range(n_chunks):
         block_copy(c).start()
+
+    def clear():
+        @pl.loop(0, positions // 4)
+        def _(p):
+            for acc in accs:
+                acc[pl.ds(p * 4, 4)] = jnp.zeros((4, part, EDGE), F32)
+
+    clear()
     for copy in small:
         copy.wait()
-
     for k in range(col_blocks):
         inv = inv_column(deg_ref, me * col_blocks + k)
         span = pl.ds(k * EDGE, EDGE)
@@ -111,10 +117,8 @@
     for panel in range(n_panels):
         base = panel * panel_blocks
 
-        @pl.loop(0, positions)
-        def _(p):
-            for acc in accs:
-                acc[p] = jnp.zeros((part, EDGE), F32)
+        if panel:
+            clear()
 
         def place(s):
             dev, inner = halve(rows_ref[0, 0, s], dev_blocks)
@@ -362,10 +366,11 @@
     own = {0: pulled}
     for m in range(1, n_chip):
         own[m] = chip_flip(own[m & (m - 1)], low_bit(m))
+    own[1] = after(own[1], own[2])
     other = {m: swap(own[m]) for m in range(last)}
 
-    wsum = after(wkeep + swap(wsend), other[2])
-    moved = chip_flip(wsum, 0)
+    wsum = wkeep + swap(wsend)
+    wsum = wsum + chip_flip(wsum, 0)
     early = [x for m in range(last) for x in (own[m], other[m])]
     late_rows = 2 * node_dev
     sofar, rest = pl.pallas_call(
@@ -389,8 +394,7 @@
         name="backward_early",
     )(tile, *early)
 
-    wsum = after(wsum, sofar) + moved
-    own[last] = after(own[last], sofar)
+    own[last] = after(after(own[last], sofar), wsum)
     late = [own[last], swap(own[last])]
     for bit in range(1, chip_bits):
         wsum = wsum + chip_flip(wsum, bit)
@@ -418,8 +422,8 @@
 
     done = list(done)
     for t in range(row_bits):
-        wsum = after(wsum, done[-1 if t == 0 else 0])
-        wsum = wsum + row_flip(wsum, (t + 1) % row_bits)
+        wsum = after(wsum, done[0])
+        wsum = wsum + row_flip(wsum, t)
         done = [x + row_flip(x, (i + t) % row_bits) for i, x in enumerate(done)]
         if t == 0:
             done[-1] = after(done[-1], wsum)

time: 72.6 us -> 71.8 us (0.989)
  Pallas kernels: 17.7 us -> 16.9 us
    ppermute x6, waiting for transfers between devices: 9.88 us -> 7.91 us  [row_flip(): return lax.ppermute(x, 'row', [(i, i ^ 1 << bit) for i in range(n_row)])]
    ppermute x8, waiting for transfers between devices: 15.6 us -> 16.9 us  [chip_flip(): return lax.ppermute(x, 'col', [(i, i ^ 2 << bit) for i in range(n_col)])]
    pallas_call x1, Pallas kernels: 12.6 us -> 11.7 us  [body(): pl.pallas_call(functools.partial(forward_kernel, n_col, chunk, panel_dev,...]
    add x4 -> x3, other arithmetic: 1.96 us -> 1.95 us  [after(): return x + 0.0 * other[:, :x.shape[1]]]
  transfers between devices with their start and end apart: 24 -> 24, of which waited for: 15 -> 15; matrix products, arithmetic and copies ran while one was open for 5% -> 6% of each run, Pallas kernels for 6% -> 6%
where the time goes in v12:
time: 71.8 us; the launch traced here: 71.5 us
  waiting for transfers between devices  25.8 us (36%)
  starting transfers between devices  22.6 us (31%)
  Pallas kernels  16.9 us (24%)
  other arithmetic  4.64 us (6%)
  between operations  1.56 us (2%)
    ppermute x8, waiting for transfers between devices, chip_flip(): return lax.ppermute(x, 'col', [(i, i ^ 2 << bit) for i in range(n_col)])  16.9 us
    pallas_call x1, Pallas kernels, body(): pl.pallas_call(functools.partial(forward_kernel, n_col, chunk, panel_dev,...  11.7 us
    ppermute x8, starting transfers between devices, chip_flip(): return lax.ppermute(x, 'col', [(i, i ^ 2 << bit) for i in range(n_col)])  11.7 us
    ppermute x6, starting transfers between devices, row_flip(): return lax.ppermute(x, 'row', [(i, i ^ 1 << bit) for i in range(n_row)])  8.75 us
    ppermute x6, waiting for transfers between devices, row_flip(): return lax.ppermute(x, 'row', [(i, i ^ 1 << bit) for i in range(n_row)])  7.91 us
    pallas_call x1, Pallas kernels, body(): pl.pallas_call(functools.partial(partial_kernel, len(early)), out_shape=(...  2.92 us
    ppermute x10, starting transfers between devices, swap(): return lax.ppermute(x, 'col', swap_pairs)  2.12 us
    add x3, other arithmetic, after(): return x + 0.0 * other[:, :x.shape[1]]  1.95 us
  transfers between devices with their start and end apart: 24, of which 15 were waited for; matrix products, arithmetic and copies ran while one was open for 6% of the time, Pallas kernels for 6%

profile of v12, /device:TPU:0, one launch (start us, length us, event | category | flops | bytes accessed | tf_op | source)
XLA Modules:
  0.0 71.5 jit_solution(11647522283296680578)
XLA Ops:
  1.3 11.7 %densify_forward.1 = (f32[256,128]{1,0:T(8,128)}, f32[256,128]{1,0:T(8,128)}, f32[256,128]{1,0:T(8,128)}, f32[256,128]{1,0:T(8,128)}, f32[256,128]{1,0:T(8,128)}...) custom-call(s32[1,1,384]{2,1,0:T(1,128)} %rows_hbm.1, ...), custom_call_target="tpu_custom_call" | custom-call | tf_op jit(solution)/shard_map/densify_forward/pallas_call | solution.py:294
  13.1 0.7 %collective-permute-start.1 = (f32[256,128]{1,0:T(8,128)}, f32[256,128]{1,0:T(8,128)S(1)}, u32[]{:S(2)}, u32[]{:S(2)}) collective-permute-start(f32[256,128]{1,0:T(8,128)} %get-tuple-element.23), channel_id=1, source_target_pairs={{0,1},{1,0},{2,3},{3,2},{4,5},{5,4},{6,7},{7,6},{8,9},{9,8},{10,11... | collective-permute-start | bytes 393224 | tf_op jit(solution)/shard_map/ppermute | solution.py:324
  14.4 0.9 %multiply_add_fusion = f32[256,128]{1,0:T(8,128)S(1)} fusion(f32[256,128]{1,0:T(8,128)} %get-tuple-element.24), kind=kLoop, calls=%fused_computation.2 | loop fusion | flops 65536 | bytes 262144 | tf_op jit(solution)/shard_map/add | solution.py:285
  15.6 3.0 %collective-permute-start.3 = (f32[256,128]{1,0:T(8,128)S(1)}, f32[256,128]{1,0:T(8,128)S(1)}, u32[]{:S(2)}, u32[]{:S(2)}) collective-permute-start(f32[256,128]{1,0:T(8,128)S(1)} %add.117), channel_id=1, source_target_pairs={{0,2},{1,3},{2,0},{3,1},{4,6},{5,7},{6,4},{7,5},{8,10},{9,11},{10,... | collective-permute-start | bytes 393224 | tf_op jit(solution)/shard_map/ppermute | solution.py:327
  18.7 1.0 %multiply_add_fusion.2 = (f32[256,128]{1,0:T(8,128)S(1)}, f32[256,128]{1,0:T(8,128)S(1)}) fusion(f32[256,128]{1,0:T(8,128)} %get-tuple-element.22, f32[256,128]{1,0:T(8,128)S(1)} %collective-permute-done.1, f32[256,128]{1,0:T(8,128)} %get-tuple-element.20, f32[256,128]{1,0:T(8,128)S(1)} %collective-permute-done), kind=kLoop, calls=%fused_computation.6 | loop fusion | flops 131072 | bytes 786432 | tf_op jit(solution)/shard_map/add | solution.py:285
  19.7 0.9 %add.119 = f32[256,128]{1,0:T(8,128)S(1)} add(f32[256,128]{1,0:T(8,128)} %get-tuple-element.26, f32[256,128]{1,0:T(8,128)S(1)} %collective-permute-done.5) | non-fusion elementwise | flops 32768 | bytes 393216 | tf_op jit(solution)/shard_map/add | solution.py:343
  20.7 1.8 %collective-permute-done.3 = f32[256,128]{1,0:T(8,128)S(1)} collective-permute-done((f32[256,128]{1,0:T(8,128)S(1)}, f32[256,128]{1,0:T(8,128)S(1)}, u32[]{:S(2)}, u32[]{:S(2)}) %collective-permute-start.3) | collective-permute-done | bytes 131104 | tf_op jit(solution)/shard_map/ppermute | solution.py:327
  22.5 2.6 %collective-permute-start.4 = (f32[256,128]{1,0:T(8,128)S(1)}, f32[256,128]{1,0:T(8,128)S(1)}, u32[]{:S(2)}, u32[]{:S(2)}) collective-permute-start(f32[256,128]{1,0:T(8,128)S(1)} %add.118), channel_id=1, source_target_pairs={{0,4},{1,5},{2,6},{3,7},{4,0},{5,1},{6,2},{7,3},{8,12},{9,13},{10,... | collective-permute-start | bytes 393224 | tf_op jit(solution)/shard_map/ppermute | solution.py:327
  25.1 2.1 %collective-permute-done.6.refs_2_ = f32[256,128]{1,0:T(8,128)S(1)} collective-permute-done((f32[256,128]{1,0:T(8,128)S(1)}, f32[256,128]{1,0:T(8,128)S(1)}, u32[]{:S(2)}, u32[]{:S(2)}) %collective-permute-start.6) | collective-permute-done | bytes 131104 | tf_op jit(solution)/shard_map/ppermute | solution.py:327
  27.2 4.2 %collective-permute-done.4.refs_1_ = f32[256,128]{1,0:T(8,128)S(1)} collective-permute-done((f32[256,128]{1,0:T(8,128)S(1)}, f32[256,128]{1,0:T(8,128)S(1)}, u32[]{:S(2)}, u32[]{:S(2)}) %collective-permute-start.4) | collective-permute-done | bytes 131104 | tf_op jit(solution)/shard_map/ppermute | solution.py:327
  31.4 1.1 %middle.1 = (bf16[256,256]{1,0:T(8,128)(2,1)}, f32[128,256]{1,0:T(8,128)S(1)}, f32[128,128]{1,0:T(8,128)S(1)}, f32[128,128]{1,0:T(8,128)S(1)}) custom-call(s32[64,128]{1,0:T(8,128)S(1)} %bitcast.10, bf16[256,256]{1,0:T(8,128)(2,1)S(1)} %copy-done.1, bf16[128,256]{1,0:T(8,128)(2,1)S(1)} %copy-done.2, f32[256,128]{1,0:T(8,128)S(1)} %get-tuple-element.40.refs_0_, ...), custom_call_target="tpu_custom_call" | custom-call | tf_op jit(solution)/shard_map/middle/pallas_call | solution.py:352
  32.8 3.4 %collective-permute-start.9 = (f32[128,256]{1,0:T(8,128)S(1)}, f32[128,256]{1,0:T(8,128)S(1)}, u32[]{:S(2)}, u32[]{:S(2)}) collective-permute-start(f32[128,256]{1,0:T(8,128)S(1)} %get-tuple-element.30.refs_0_), channel_id=1, source_target_pairs={{0,4},{1,5},{2,6},{3,7},{4,0},{5,1},{6,2},{7,3},{8,12},{9,13},{10,... | collective-permute-start | bytes 393224 | tf_op jit(solution)/shard_map/ppermute | solution.py:327
  36.3 6.1 %collective-permute-done.14 = f32[128,128]{1,0:T(8,128)S(1)} collective-permute-done((f32[128,128]{1,0:T(8,128)S(1)}, f32[128,128]{1,0:T(8,128)S(1)}, u32[]{:S(2)}, u32[]{:S(2)}) %collective-permute-start.14) | collective-permute-done | bytes 65568 | tf_op jit(solution)/shard_map/ppermute | solution.py:327
  42.4 0.5 collective-permute-done.9.refs_4_
  43.0 0.5 collective-permute-start.11
  43.5 0.5 collective-permute-start.12
  44.5 2.9 %backward_early.1 = (f32[128,1024]{1,0:T(8,128)S(1)}, bf16[512,1024]{1,0:T(8,128)(2,1)S(1)}) custom-call(bf16[2048,1024]{1,0:T(8,128)(2,1)} %get-tuple-element.29.tile_ref, f32[128,256]{1,0:T(8,128)S(1)} %get-tuple-element.30.refs_0_, f32[128,256]{1,0:T(8,128)S(1)} %collective-permute-done.7.refs_1_, f32[128,256]{1,0:T(8,128)S(1)} %multiply_add_fusion.1.refs_2_, ...), custom_call_target="tpu_custom_call" | custom-call | flops 1073741824 | bytes 33554432 | tf_op jit(solution)/shard_map/backward_early/pallas_call | solution.py:376
  47.5 1.5 %collective-permute-done.12 = f32[128,256]{1,0:T(8,128)S(1)} collective-permute-done((f32[128,256]{1,0:T(8,128)S(1)}, f32[128,256]{1,0:T(8,128)S(1)}, u32[]{:S(2)}, u32[]{:S(2)}) %collective-permute-start.12) | collective-permute-done | bytes 131104 | tf_op jit(solution)/shard_map/ppermute | solution.py:327
  49.1 1.8 %collective-permute-start.19 = (f32[128,128]{1,0:T(8,128)S(1)}, f32[128,128]{1,0:T(8,128)S(1)}, u32[]{:S(2)}, u32[]{:S(2)}) collective-permute-start(f32[128,128]{1,0:T(8,128)S(1)} %add.123), channel_id=1, source_target_pairs={{0,4},{1,5},{2,6},{3,7},{4,0},{5,1},{6,2},{7,3},{8,12},{9,13},{10,... | collective-permute-start | bytes 196616 | tf_op jit(solution)/shard_map/ppermute | solution.py:327
  50.9 1.1 %backward_late.1 = (f32[512,128]{1,0:T(8,128)S(1)}, f32[512,128]{1,0:T(8,128)S(1)}) custom-call(s32[64,128]{1,0:T(8,128)S(1)} %bitcast.11, bf16[512,1024]{1,0:T(8,128)(2,1)S(1)} %get-tuple-element.31.dense_ref, f32[128,1024]{1,0:T(8,128)S(1)} %get-tuple-element.32.sofar_ref, f32[128,256]{1,0:T(8,128)S(1)} %add_add_fusion.refs_0_, ...), custom_call_target="tpu_custom_call" | custom-call | tf_op jit(solution)/shard_map/backward_late/pallas_call | solution.py:405
  52.0 1.7 %collective-permute-start.16 = (f32[512,128]{1,0:T(8,128)S(1)}, f32[512,128]{1,0:T(8,128)S(1)}, u32[]{:S(2)}, u32[]{:S(2)}) collective-permute-start(f32[512,128]{1,0:T(8,128)S(1)} %get-tuple-element.35), channel_id=1, source_target_pairs={{0,8},{8,0},{16,24},{24,16},{1,9},{9,1},{17,25},{25,17},{2,10},{10... | collective-permute-start | bytes 786440 | tf_op jit(solution)/shard_map/ppermute | solution.py:330
  53.8 1.4 %collective-permute-start.18 = (f32[512,128]{1,0:T(8,128)S(1)}, f32[512,128]{1,0:T(8,128)S(1)}, u32[]{:S(2)}, u32[]{:S(2)}) collective-permute-start(f32[512,128]{1,0:T(8,128)S(1)} %get-tuple-element.36), channel_id=1, source_target_pairs={{0,16},{8,24},{16,0},{24,8},{1,17},{9,25},{17,1},{25,9},{2,18},{10... | collective-permute-start | bytes 786440 | tf_op jit(solution)/shard_map/ppermute | solution.py:330
  55.2 0.7 collective-permute-done.19
  55.9 1.8 %collective-permute-start.20 = (f32[128,128]{1,0:T(8,128)S(1)}, f32[128,128]{1,0:T(8,128)S(1)}, u32[]{:S(2)}, u32[]{:S(2)}) collective-permute-start(f32[128,128]{1,0:T(8,128)S(1)} %bitcast_add_fusion.3), channel_id=1, source_target_pairs={{0,8},{8,0},{16,24},{24,16},{1,9},{9,1},{17,25},{25,17},{2,10},{10... | collective-permute-start | bytes 196616 | tf_op jit(solution)/shard_map/ppermute | solution.py:330
  57.7 3.5 %collective-permute-done.16 = f32[512,128]{1,0:T(8,128)S(1)} collective-permute-done((f32[512,128]{1,0:T(8,128)S(1)}, f32[512,128]{1,0:T(8,128)S(1)}, u32[]{:S(2)}, u32[]{:S(2)}) %collective-permute-start.16) | collective-permute-done | bytes 262176 | tf_op jit(solution)/shard_map/ppermute | solution.py:330
  61.2 1.8 %collective-permute-start.17 = (f32[512,128]{1,0:T(8,128)S(1)}, f32[512,128]{1,0:T(8,128)S(1)}, u32[]{:S(2)}, u32[]{:S(2)}) collective-permute-start(f32[512,128]{1,0:T(8,128)S(1)} %add.127), channel_id=1, source_target_pairs={{0,16},{8,24},{16,0},{24,8},{1,17},{9,25},{17,1},{25,9},{2,18},{10... | collective-permute-start | bytes 786440 | tf_op jit(solution)/shard_map/ppermute | solution.py:330
  63.1 1.4 %collective-permute-start.21 = (f32[512,128]{1,0:T(8,128)S(1)}, f32[512,128]{1,0:T(8,128)S(1)}, u32[]{:S(2)}, u32[]{:S(2)}) collective-permute-start(f32[512,128]{1,0:T(8,128)S(1)} %bitcast_add_fusion), channel_id=1, source_target_pairs={{0,8},{8,0},{16,24},{24,16},{1,9},{9,1},{17,25},{25,17},{2,10},{10... | collective-permute-start | bytes 786440 | tf_op jit(solution)/shard_map/ppermute | solution.py:330
  64.5 0.6 collective-permute-start.22
  65.1 3.7 %collective-permute-done.17 = f32[512,128]{1,0:T(8,128)S(1)} collective-permute-done((f32[512,128]{1,0:T(8,128)S(1)}, f32[512,128]{1,0:T(8,128)S(1)}, u32[]{:S(2)}, u32[]{:S(2)}) %collective-permute-start.17) | collective-permute-done | bytes 262176 | tf_op jit(solution)/shard_map/ppermute | solution.py:330
  68.9 0.7 collective-permute-done.22
  69.7 0.8 %pad_maximum_fusion = f32[1024,128]{1,0:T(8,128)} fusion(f32[512,128]{1,0:T(8,128)S(1)} %add.138, f32[512,128]{1,0:T(8,128)S(1)} %add.128), kind=kLoop, calls=%fused_computation | loop fusion | flops 131072 | bytes 1048576 | tf_op jit(solution)/shard_map/concatenate | solution.py:431
  70.9 0.7 maximum_maximum_fusion
  (53 shorter events, 2.8 us)
Async XLA Ops:
  0.6 30.8 %copy-start = (s32[8192]{0:T(1024)S(1)}, s32[8192]{0:T(1024)}, u32[]{:S(2)}) copy-start(s32[8192]{0:T(1024)} %param.9) | copy-start | bytes 98308
  0.6 30.8 %copy-start.1 = (bf16[256,256]{1,0:T(8,128)(2,1)S(1)}, bf16[256,256]{1,0:T(8,128)(2,1)}, u32[]{:S(2)}) copy-start(bf16[256,256]{1,0:T(8,128)(2,1)} %cot_ref.1) | copy-start | bytes 393220
  0.7 30.8 %copy-start.2 = (bf16[128,256]{1,0:T(8,128)(2,1)S(1)}, bf16[128,256]{1,0:T(8,128)(2,1)}, u32[]{:S(2)}) copy-start(bf16[128,256]{1,0:T(8,128)(2,1)} %weight_ref.1) | copy-start | bytes 196612
  13.1 5.6 %collective-permute-start.1 = (f32[256,128]{1,0:T(8,128)}, f32[256,128]{1,0:T(8,128)S(1)}, u32[]{:S(2)}, u32[]{:S(2)}) collective-permute-start(f32[256,128]{1,0:T(8,128)} %get-tuple-element.23), channel_id=1, source_target_pairs={{0,1},{1,0},{2,3},{3,2},{4,5},{5,4},{6,7},{7,6},{8,9},{9,8},{10,11... | collective-permute-start | bytes 393224 | tf_op jit(solution)/shard_map/ppermute | solution.py:324
  13.8 4.8 %collective-permute-start = (f32[256,128]{1,0:T(8,128)}, f32[256,128]{1,0:T(8,128)S(1)}, u32[]{:S(2)}, u32[]{:S(2)}) collective-permute-start(f32[256,128]{1,0:T(8,128)} %get-tuple-element.21), channel_id=1, source_target_pairs={{0,1},{1,0},{2,3},{3,2},{4,5},{5,4},{6,7},{7,6},{8,9},{9,8},{10,11... | collective-permute-start | bytes 393224 | tf_op jit(solution)/shard_map/ppermute | solution.py:324
  13.9 1.7 %collective-permute-start.2 = (f32[256,128]{1,0:T(8,128)}, f32[256,128]{1,0:T(8,128)S(1)}, u32[]{:S(2)}, u32[]{:S(2)}) collective-permute-start(f32[256,128]{1,0:T(8,128)} %get-tuple-element.25), channel_id=1, source_target_pairs={{0,1},{1,0},{2,3},{3,2},{4,5},{5,4},{6,7},{7,6},{8,9},{9,8},{10,11... | collective-permute-start | bytes 393224 | tf_op jit(solution)/shard_map/ppermute | solution.py:324
  14.3 5.3 %collective-permute-start.5 = (f32[256,128]{1,0:T(8,128)}, f32[256,128]{1,0:T(8,128)S(1)}, u32[]{:S(2)}, u32[]{:S(2)}) collective-permute-start(f32[256,128]{1,0:T(8,128)} %get-tuple-element.27), channel_id=1, source_target_pairs={{0,1},{1,0},{2,3},{3,2},{4,5},{5,4},{6,7},{7,6},{8,9},{9,8},{10,11... | collective-permute-start | bytes 393224 | tf_op jit(solution)/shard_map/ppermute | solution.py:324
  15.6 6.9 %collective-permute-start.3 = (f32[256,128]{1,0:T(8,128)S(1)}, f32[256,128]{1,0:T(8,128)S(1)}, u32[]{:S(2)}, u32[]{:S(2)}) collective-permute-start(f32[256,128]{1,0:T(8,128)S(1)} %add.117), channel_id=1, source_target_pairs={{0,2},{1,3},{2,0},{3,1},{4,6},{5,7},{6,4},{7,5},{8,10},{9,11},{10,... | collective-permute-start | bytes 393224 | tf_op jit(solution)/shard_map/ppermute | solution.py:327
  20.6 6.6 %collective-permute-start.6 = (f32[256,128]{1,0:T(8,128)S(1)}, f32[256,128]{1,0:T(8,128)S(1)}, u32[]{:S(2)}, u32[]{:S(2)}) collective-permute-start(f32[256,128]{1,0:T(8,128)S(1)} %add.119), channel_id=1, source_target_pairs={{0,2},{1,3},{2,0},{3,1},{4,6},{5,7},{6,4},{7,5},{8,10},{9,11},{10,... | collective-permute-start | bytes 393224 | tf_op jit(solution)/shard_map/ppermute | solution.py:327
  22.5 8.9 %collective-permute-start.4 = (f32[256,128]{1,0:T(8,128)S(1)}, f32[256,128]{1,0:T(8,128)S(1)}, u32[]{:S(2)}, u32[]{:S(2)}) collective-permute-start(f32[256,128]{1,0:T(8,128)S(1)} %add.118), channel_id=1, source_target_pairs={{0,4},{1,5},{2,6},{3,7},{4,0},{5,1},{6,2},{7,3},{8,12},{9,13},{10,... | collective-permute-start | bytes 393224 | tf_op jit(solution)/shard_map/ppermute | solution.py:327
  32.5 3.7 %collective-permute-start.13 = (f32[128,128]{1,0:T(8,128)S(1)}, f32[128,128]{1,0:T(8,128)S(1)}, u32[]{:S(2)}, u32[]{:S(2)}) collective-permute-start(f32[128,128]{1,0:T(8,128)S(1)} %get-tuple-element.34), channel_id=1, source_target_pairs={{0,1},{1,0},{2,3},{3,2},{4,5},{5,4},{6,7},{7,6},{8,9},{9,8},{10,11... | collective-permute-start | bytes 196616 | tf_op jit(solution)/shard_map/ppermute | solution.py:324
  32.5 9.9 %collective-permute-start.8 = (f32[128,256]{1,0:T(8,128)S(1)}, f32[128,256]{1,0:T(8,128)S(1)}, u32[]{:S(2)}, u32[]{:S(2)}) collective-permute-start(f32[128,256]{1,0:T(8,128)S(1)} %get-tuple-element.30.refs_0_), channel_id=1, source_target_pairs={{0,2},{1,3},{2,0},{3,1},{4,6},{5,7},{6,4},{7,5},{8,10},{9,11},{10,... | collective-permute-start | bytes 393224 | tf_op jit(solution)/shard_map/ppermute | solution.py:327
  32.8 10.1 %collective-permute-start.9 = (f32[128,256]{1,0:T(8,128)S(1)}, f32[128,256]{1,0:T(8,128)S(1)}, u32[]{:S(2)}, u32[]{:S(2)}) collective-permute-start(f32[128,256]{1,0:T(8,128)S(1)} %get-tuple-element.30.refs_0_), channel_id=1, source_target_pairs={{0,4},{1,5},{2,6},{3,7},{4,0},{5,1},{6,2},{7,3},{8,12},{9,13},{10,... | collective-permute-start | bytes 393224 | tf_op jit(solution)/shard_map/ppermute | solution.py:327
  36.2 6.2 %collective-permute-start.14 = (f32[128,128]{1,0:T(8,128)S(1)}, f32[128,128]{1,0:T(8,128)S(1)}, u32[]{:S(2)}, u32[]{:S(2)}) collective-permute-start(f32[128,128]{1,0:T(8,128)S(1)} %add.122), channel_id=1, source_target_pairs={{0,2},{1,3},{2,0},{3,1},{4,6},{5,7},{6,4},{7,5},{8,10},{9,11},{10,... | collective-permute-start | bytes 196616 | tf_op jit(solution)/shard_map/ppermute | solution.py:327
  36.3 7.8 %collective-permute-start.7 = (f32[128,256]{1,0:T(8,128)S(1)}, f32[128,256]{1,0:T(8,128)S(1)}, u32[]{:S(2)}, u32[]{:S(2)}) collective-permute-start(f32[128,256]{1,0:T(8,128)S(1)} %get-tuple-element.30.refs_0_), channel_id=1, source_target_pairs={{0,1},{1,0},{2,3},{3,2},{4,5},{5,4},{6,7},{7,6},{8,9},{9,8},{10,11... | collective-permute-start | bytes 393224 | tf_op jit(solution)/shard_map/ppermute | solution.py:324
  42.9 1.4 %collective-permute-start.10 = (f32[128,256]{1,0:T(8,128)S(1)}, f32[128,256]{1,0:T(8,128)S(1)}, u32[]{:S(2)}, u32[]{:S(2)}) collective-permute-start(f32[128,256]{1,0:T(8,128)S(1)} %multiply_add_fusion.1.refs_2_), channel_id=1, source_target_pairs={{0,1},{1,0},{2,3},{3,2},{4,5},{5,4},{6,7},{7,6},{8,9},{9,8},{10,11... | collective-permute-start | bytes 393224 | tf_op jit(solution)/shard_map/ppermute | solution.py:324
  43.0 1.5 %collective-permute-start.11 = (f32[128,256]{1,0:T(8,128)S(1)}, f32[128,256]{1,0:T(8,128)S(1)}, u32[]{:S(2)}, u32[]{:S(2)}) collective-permute-start(f32[128,256]{1,0:T(8,128)S(1)} %collective-permute-done.9.refs_4_), channel_id=1, source_target_pairs={{0,1},{1,0},{2,3},{3,2},{4,5},{5,4},{6,7},{7,6},{8,9},{9,8},{10,11... | collective-permute-start | bytes 393224 | tf_op jit(solution)/shard_map/ppermute | solution.py:324
  43.5 5.5 %collective-permute-start.12 = (f32[128,256]{1,0:T(8,128)S(1)}, f32[128,256]{1,0:T(8,128)S(1)}, u32[]{:S(2)}, u32[]{:S(2)}) collective-permute-start(f32[128,256]{1,0:T(8,128)S(1)} %collective-permute-done.9.refs_4_), channel_id=1, source_target_pairs={{0,2},{1,3},{2,0},{3,1},{4,6},{5,7},{6,4},{7,5},{8,10},{9,11},{10,... | collective-permute-start | bytes 393224 | tf_op jit(solution)/shard_map/ppermute | solution.py:327
  49.0 1.9 %collective-permute-start.15 = (f32[128,256]{1,0:T(8,128)S(1)}, f32[128,256]{1,0:T(8,128)S(1)}, u32[]{:S(2)}, u32[]{:S(2)}) collective-permute-start(f32[128,256]{1,0:T(8,128)S(1)} %add_add_fusion.refs_0_), channel_id=1, source_target_pairs={{0,1},{1,0},{2,3},{3,2},{4,5},{5,4},{6,7},{7,6},{8,9},{9,8},{10,11... | collective-permute-start | bytes 393224 | tf_op jit(solution)/shard_map/ppermute | solution.py:324
  49.1 6.8 %collective-permute-start.19 = (f32[128,128]{1,0:T(8,128)S(1)}, f32[128,128]{1,0:T(8,128)S(1)}, u32[]{:S(2)}, u32[]{:S(2)}) collective-permute-start(f32[128,128]{1,0:T(8,128)S(1)} %add.123), channel_id=1, source_target_pairs={{0,4},{1,5},{2,6},{3,7},{4,0},{5,1},{6,2},{7,3},{8,12},{9,13},{10,... | collective-permute-start | bytes 196616 | tf_op jit(solution)/shard_map/ppermute | solution.py:327
  52.0 9.1 %collective-permute-start.16 = (f32[512,128]{1,0:T(8,128)S(1)}, f32[512,128]{1,0:T(8,128)S(1)}, u32[]{:S(2)}, u32[]{:S(2)}) collective-permute-start(f32[512,128]{1,0:T(8,128)S(1)} %get-tuple-element.35), channel_id=1, source_target_pairs={{0,8},{8,0},{16,24},{24,16},{1,9},{9,1},{17,25},{25,17},{2,10},{10... | collective-permute-start | bytes 786440 | tf_op jit(solution)/shard_map/ppermute | solution.py:330
  53.8 9.2 %collective-permute-start.18 = (f32[512,128]{1,0:T(8,128)S(1)}, f32[512,128]{1,0:T(8,128)S(1)}, u32[]{:S(2)}, u32[]{:S(2)}) collective-permute-start(f32[512,128]{1,0:T(8,128)S(1)} %get-tuple-element.36), channel_id=1, source_target_pairs={{0,16},{8,24},{16,0},{24,8},{1,17},{9,25},{17,1},{25,9},{2,18},{10... | collective-permute-start | bytes 786440 | tf_op jit(solution)/shard_map/ppermute | solution.py:330
  55.9 7.1 %collective-permute-start.20 = (f32[128,128]{1,0:T(8,128)S(1)}, f32[128,128]{1,0:T(8,128)S(1)}, u32[]{:S(2)}, u32[]{:S(2)}) collective-permute-start(f32[128,128]{1,0:T(8,128)S(1)} %bitcast_add_fusion.3), channel_id=1, source_target_pairs={{0,8},{8,0},{16,24},{24,16},{1,9},{9,1},{17,25},{25,17},{2,10},{10... | collective-permute-start | bytes 196616 | tf_op jit(solution)/shard_map/ppermute | solution.py:330
  61.2 7.6 %collective-permute-start.17 = (f32[512,128]{1,0:T(8,128)S(1)}, f32[512,128]{1,0:T(8,128)S(1)}, u32[]{:S(2)}, u32[]{:S(2)}) collective-permute-start(f32[512,128]{1,0:T(8,128)S(1)} %add.127), channel_id=1, source_target_pairs={{0,16},{8,24},{16,0},{24,8},{1,17},{9,25},{17,1},{25,9},{2,18},{10... | collective-permute-start | bytes 786440 | tf_op jit(solution)/shard_map/ppermute | solution.py:330
  63.1 6.6 %collective-permute-start.21 = (f32[512,128]{1,0:T(8,128)S(1)}, f32[512,128]{1,0:T(8,128)S(1)}, u32[]{:S(2)}, u32[]{:S(2)}) collective-permute-start(f32[512,128]{1,0:T(8,128)S(1)} %bitcast_add_fusion), channel_id=1, source_target_pairs={{0,8},{8,0},{16,24},{24,16},{1,9},{9,1},{17,25},{25,17},{2,10},{10... | collective-permute-start | bytes 786440 | tf_op jit(solution)/shard_map/ppermute | solution.py:330
  64.5 5.0 %collective-permute-start.22 = (f32[128,128]{1,0:T(8,128)S(1)}, f32[128,128]{1,0:T(8,128)S(1)}, u32[]{:S(2)}, u32[]{:S(2)}) collective-permute-start(f32[128,128]{1,0:T(8,128)S(1)} %get-tuple-element.37), channel_id=1, source_target_pairs={{0,16},{8,24},{16,0},{24,8},{1,17},{9,25},{17,1},{25,9},{2,18},{10... | collective-permute-start | bytes 196616 | tf_op jit(solution)/shard_map/ppermute | solution.py:330
  69.5 1.3 %collective-permute-start.23 = (f32[128,128]{1,0:T(8,128)S(1)}, f32[128,128]{1,0:T(8,128)S(1)}, u32[]{:S(2)}, u32[]{:S(2)}) collective-permute-start(f32[128,128]{1,0:T(8,128)S(1)} %bitcast_add_fusion.1), channel_id=1, source_target_pairs={{0,1},{1,0},{2,3},{3,2},{4,5},{5,4},{6,7},{7,6},{8,9},{9,8},{10,11... | collective-permute-start | bytes 196616 | tf_op jit(solution)/shard_map/ppermute | solution.py:324

commit v13 on v9

--- a/solution.py
+++ b/solution.py
@@ -13,6 +13,7 @@
 GROUP = 16
 QUARTERS = 4
 AHEAD = 3
+DEPTH = 2
 BWD = 50
 ACC_BYTES = 8 << 20
 GELU_C = 0.7978845608028654
@@ -47,16 +48,87 @@
     return lax.div(value, size), lax.rem(value, size)
 
 
-def forward_kernel(
+def product_kernel(
+    n_col, chunk, rows_ref, cols_ref, live_ref, deg_ref, feat_ref, blocks_ref, *refs,
+):
+    outs, (acc, buf, scaled, in_sems, out_sems) = refs[:n_col], refs[n_col:]
+    slots = buf.shape[0]
+    col_blocks = feat_ref.shape[0] // EDGE
+    dev_blocks = outs[0].shape[0]
+    row_blocks = n_col * dev_blocks
+    part = EDGE // QUARTERS
+    n_chunks = slots // chunk
+    me = lax.axis_index("col")
+    live = live_ref[0, 0]
+
+    def block_copy(c):
+        span = pl.ds(c * chunk, chunk)
+        return pltpu.make_async_copy(blocks_ref.at[0, 0, span], buf.at[span], in_sems.at[c])
+
+    for c in range(n_chunks):
+        block_copy(c).start()
+    for k in range(col_blocks):
+        inv = inv_column(deg_ref, me * col_blocks + k)
+        span = pl.ds(k * EDGE, EDGE)
+        scaled[span, :] = (inv * feat_ref[span, :].astype(F32)).astype(BF16)
+
+    @pl.loop(0, row_blocks)
+    def _(p):
+        acc[p] = jnp.zeros((EDGE, EDGE), F32)
+
+    def product(s):
+        dev, inner = halve(rows_ref[0, 0, s], dev_blocks)
+        p = jnp.where(s < live, (dev ^ me) * dev_blocks + inner, row_blocks)
+        at = pl.multiple_of(cols_ref[0, 0, s] * EDGE, EDGE)
+        return p, jnp.dot(buf[s], scaled[pl.ds(at, EDGE), :], preferred_element_type=F32)
+
+    def add_slots(first):
+        products, pending = [], []
+
+        def finish():
+            p, rows, sofar, value = pending.pop(0)
+            acc[p, rows, :] = sofar + value
+
+        for s in range(GROUP + DEPTH):
+            if s < GROUP:
+                products.append(product(first + s))
+            if s >= DEPTH:
+                p, value = products.pop(0)
+                for q in range(QUARTERS):
+                    rows = slice(q * part, (q + 1) * part)
+                    pending.append((p, rows, acc[p, rows, :], value[rows]))
+                    if len(pending) > AHEAD:
+                        finish()
+        while pending:
+            finish()
+
+    @pl.loop(0, n_chunks)
+    def _(c):
+        block_copy(c).wait()
+
+        @pl.loop(0, chunk // GROUP)
+        def _(g):
+            add_slots(c * chunk + g * GROUP)
+
+    copies = [
+        pltpu.make_async_copy(acc.at[pl.ds(j * dev_blocks, dev_blocks)], outs[j], out_sems.at[j])
+        for j in range(n_col)
+    ]
+    for copy in copies:
+        copy.start()
+    for copy in copies:
+        copy.wait()
+
+
+def densify_kernel(
     n_col, chunk, panel_dev, node_dev,
-    rows_ref, cols_ref, live_ref, deg_ref, feat_ref, blocks_ref, *refs,
+    rows_ref, cols_ref, live_ref, blocks_ref, tile_ref, mark_ref, *refs,
 ):
-    outs, tile_ref = refs[:n_col], refs[n_col]
-    accs, (both, buf, scaled, result, in_sems, dense_sems, out_sems) = refs[n_col + 1:-7], refs[-7:]
+    mark_ref[...] = jnp.zeros(mark_ref.shape, F32)
+    accs, (both, buf, in_sems, dense_sems) = refs[:-4], refs[-4:]
     part = EDGE // len(accs)
     slots = buf.shape[0]
-    col_nodes, width = feat_ref.shape
-    col_blocks = col_nodes // EDGE
+    col_blocks = tile_ref.shape[1] // EDGE
     dev_blocks = node_dev // EDGE
     panel_blocks = panel_dev * dev_blocks
     positions = panel_blocks * col_blocks
@@ -71,18 +143,10 @@
 
     def dense_copy(rel, j):
         there = tile_ref.at[pl.ds(rel * node_dev, node_dev)]
-        return pltpu.make_async_copy(both.at[j, pl.ds(0, node_dev)], there, dense_sems.at[j])
-
-    def result_copy(rel, j):
-        return pltpu.make_async_copy(result.at[j], outs[rel], out_sems.at[j])
+        return pltpu.make_async_copy(both.at[j], there, dense_sems.at[j])
 
     for c in range(n_chunks):
         block_copy(c).start()
-
-    for k in range(col_blocks):
-        inv = inv_column(deg_ref, me * col_blocks + k)
-        span = pl.ds(k * EDGE, EDGE)
-        scaled[span, :] = (inv * feat_ref[span, :].astype(F32)).astype(BF16)
 
     def add_slots(first, place):
         pending = []
@@ -129,29 +193,23 @@
             rel = panel * panel_dev + j
             if panel:
                 dense_copy(rel - panel_dev, j).wait()
-                result_copy(rel - panel_dev, j).wait()
             for b in range(dev_blocks):
                 for cb in range(col_blocks):
                     lanes = slice(cb * EDGE, (cb + 1) * EDGE)
                     for q, acc in enumerate(accs):
-                        hi, lo = split(acc[(j * dev_blocks + b) * col_blocks + cb])
                         at = b * EDGE + q * part
-                        both[j, at:at + part, lanes] = hi
-                        both[j, node_dev + at:node_dev + at + part, lanes] = lo
+                        total = acc[(j * dev_blocks + b) * col_blocks + cb]
+                        both[j, at:at + part, lanes] = total.astype(BF16)
             dense_copy(rel, j).start()
-            pair = jnp.dot(both[j], scaled[...], preferred_element_type=F32)
-            result[j] = pair[:node_dev] + pair[node_dev:]
-            result_copy(rel, j).start()
 
     for j in range(panel_dev):
         rel = (n_panels - 1) * panel_dev + j
         dense_copy(rel, j).wait()
-        result_copy(rel, j).wait()
 
 
 def middle_kernel(n_col, n_in, scale, deg_ref, cot_ref, weight_ref, *refs):
     parts = refs[:n_in]
-    act_ref, pulled_ref, keep_ref, send_ref = refs[n_in:]
+    act_ref, pulled_ref, keep_ref, send_ref = refs[n_in + 1:]
     node_dev = cot_ref.shape[0]
     dev_blocks = node_dev // EDGE
     base = (lax.axis_index("row") * n_col + lax.axis_index("col")) * dev_blocks
@@ -279,27 +337,44 @@
     def cost(flops, read):
         return pl.CostEstimate(flops=flops, bytes_accessed=read, transcendentals=0)
 
-    *pieces, tile = pl.pallas_call(
-        functools.partial(forward_kernel, n_col, chunk, panel_dev, node_dev),
-        out_shape=[jax.ShapeDtypeStruct((node_dev, width), F32)] * n_col
-        + [jax.ShapeDtypeStruct((row_nodes, col_nodes), BF16)],
+    pieces = pl.pallas_call(
+        functools.partial(product_kernel, n_col, chunk),
+        out_shape=[jax.ShapeDtypeStruct((dev_blocks, EDGE, width), F32)] * n_col,
         in_specs=[smem, smem, smem, vmem, vmem, any_space],
-        out_specs=[any_space] * (n_col + 1),
+        out_specs=[any_space] * n_col,
+        scratch_shapes=[
+            pltpu.VMEM((n_col * dev_blocks + 1, EDGE, width), F32),
+            pltpu.VMEM((slots, EDGE, EDGE), BF16),
+            pltpu.VMEM((col_nodes, width), BF16),
+            pltpu.SemaphoreType.DMA((slots // chunk,)),
+            pltpu.SemaphoreType.DMA((n_col,)),
+        ],
+        compiler_params=params(54),
+        name="product",
+    )(block_rows, block_cols, live_slots, deg, features, blocks)
+    pieces = [x.reshape(node_dev, width) for x in pieces]
+    keep, send = pieces[0::2], pieces[1::2]
+
+    tile, mark = pl.pallas_call(
+        functools.partial(densify_kernel, n_col, chunk, panel_dev, node_dev),
+        out_shape=(
+            jax.ShapeDtypeStruct((row_nodes, col_nodes), BF16),
+            jax.ShapeDtypeStruct((8, EDGE), F32),
+        ),
+        in_specs=[smem, smem, smem, any_space],
+        out_specs=(any_space, vmem),
         scratch_shapes=[
             pltpu.VMEM((positions + 1, EDGE // QUARTERS, EDGE), F32) for _ in range(QUARTERS)
         ] + [
-            pltpu.VMEM((panel_dev, 2 * node_dev, col_nodes), BF16),
+            pltpu.VMEM((panel_dev, node_dev, col_nodes), BF16),
             pltpu.VMEM((slots, EDGE, EDGE), BF16),
-            pltpu.VMEM((col_nodes, width), BF16),
-            pltpu.VMEM((panel_dev, node_dev, width), F32),
             pltpu.SemaphoreType.DMA((slots // chunk,)),
             pltpu.SemaphoreType.DMA((panel_dev,)),
-            pltpu.SemaphoreType.DMA((panel_dev,)),
         ],
-        compiler_params=params(54),
-        name="densify_forward",
-    )(block_rows, block_cols, live_slots, deg, features, blocks)
-    keep, send = pieces[0::2], pieces[1::2]
+        compiler_params=params(52),
+        cost_estimate=cost(0, 40 << 20),
+        name="densify",
+    )(block_rows, block_cols, live_slots, blocks)
 
     swap_pairs = [(i, i ^ 1) for i in range(n_col)]
 
@@ -321,11 +396,11 @@
     arrived = {m: [] for m in range(n_chip)}
     for m in range(last, 0, -1):
         if m == last:
-            unit = ahead(after(kept[m][0], kept[m][0])) + kept[m][1]
+            unit = first = ahead(after(kept[m][0], kept[m][0])) + kept[m][1]
         else:
             unit = functools.reduce(jnp.add, kept[m])
             if m == 2:
-                unit = ahead(after(unit, parts[0]))
+                unit = ahead(after(after(unit, parts[0]), first))
             unit = functools.reduce(jnp.add, [unit] + arrived[m])
         arrived[m & (m - 1)].append(chip_flip(unit, low_bit(m)))
     kept[0] = arrived[0]
@@ -340,11 +415,11 @@
             jax.ShapeDtypeStruct((half * hidden // EDGE, EDGE), F32),
             jax.ShapeDtypeStruct((half * hidden // EDGE, EDGE), F32),
         ),
-        in_specs=[vmem] * (3 + len(parts)),
+        in_specs=[vmem] * (3 + len(parts)) + [any_space],
         out_specs=(vmem,) * 4,
         compiler_params=params(16),
         name="middle",
-    )(deg, cotangent, weight, *parts)
+    )(deg, cotangent, weight, *parts, mark)
 
     own = {0: pulled}
     for m in range(1, n_chip):

time: 70 us -> 77 us (1.10)
  Pallas kernels: 15.2 us -> 25 us
  waiting for transfers between devices: 26 us -> 23.1 us
    pallas_call x1 -> x2, Pallas kernels: 10 us -> 19.8 us  [the longest x1 12.2 us: body(): pl.pallas_call(functools.partial(product_kernel, n_col, chunk), out_shape...]
    ppermute x8, waiting for transfers between devices: 16.8 us -> 14.1 us  [chip_flip(): return lax.ppermute(x, 'col', [(i, i ^ 2 << bit) for i in range(n_col)])]
  transfers between devices with their start and end apart: 24 -> 24, of which waited for: 14 -> 12; matrix products, arithmetic and copies ran while one was open for 6% -> 5% of each run, Pallas kernels for 6% -> 15%
where the time goes in v13:
time: 77 us; the launch traced here: 76.6 us
  Pallas kernels  25 us (32%)
  waiting for transfers between devices  23.1 us (30%)
  starting transfers between devices  22.2 us (29%)
  other arithmetic  4.61 us (6%)
  between operations  1.6 us (2%)
    ppermute x8, waiting for transfers between devices, chip_flip(): return lax.ppermute(x, 'col', [(i, i ^ 2 << bit) for i in range(n_col)])  14.1 us
    pallas_call x1, Pallas kernels, body(): pl.pallas_call(functools.partial(product_kernel, n_col, chunk), out_shape...  12.2 us
    ppermute x8, starting transfers between devices, chip_flip(): return lax.ppermute(x, 'col', [(i, i ^ 2 << bit) for i in range(n_col)])  11.9 us
    ppermute x6, starting transfers between devices, row_flip(): return lax.ppermute(x, 'row', [(i, i ^ 1 << bit) for i in range(n_row)])  8.26 us
    ppermute x6, waiting for transfers between devices, row_flip(): return lax.ppermute(x, 'row', [(i, i ^ 1 << bit) for i in range(n_row)])  7.66 us
    pallas_call x1, Pallas kernels, body(): pl.pallas_call(functools.partial(densify_kernel, n_col, chunk, panel_dev,...  7.63 us
    pallas_call x1, Pallas kernels, body(): pl.pallas_call(functools.partial(partial_kernel, len(early)), out_shape=(...  2.93 us
    ppermute x10, starting transfers between devices, swap(): return lax.ppermute(x, 'col', swap_pairs)  2.06 us
  transfers between devices with their start and end apart: 24, of which 12 were waited for; matrix products, arithmetic and copies ran while one was open for 5% of the time, Pallas kernels for 15%

profile of v13, /device:TPU:0, one launch (start us, length us, event | category | flops | bytes accessed | tf_op | source)
XLA Modules:
  0.0 76.6 jit_solution(13457006017662160737)
XLA Ops:
  1.3 12.2 %product.1 = (f32[2,128,128]{2,1,0:T(8,128)}, f32[2,128,128]{2,1,0:T(8,128)}, f32[2,128,128]{2,1,0:T(8,128)}, f32[2,128,128]{2,1,0:T(8,128)}, f32[2,128,128]{2,1...) custom-call(s32[1,1,384]{2,1,0:T(1,128)} %rows_ref.3, s32[1,1,384]{2,1,0:T(1,128)} %cols_ref.3, ...), custom_call_target="tpu_custom_call" | custom-call | tf_op jit(solution)/shard_map/product/pallas_call | solution.py:340
  13.6 0.8 collective-permute-start.1
  14.9 0.9 %multiply_add_fusion = f32[256,128]{1,0:T(8,128)S(1)} fusion(f32[2,128,128]{2,1,0:T(8,128)} %get-tuple-element.25), kind=kLoop, calls=%fused_computation.2 | loop fusion | flops 65536 | bytes 262144 | tf_op jit(solution)/shard_map/add | solution.py:331
  16.1 1.0 %fusion.1 = (f32[256,128]{1,0:T(8,128)S(1)}, f32[256,128]{1,0:T(8,128)S(1)}, f32[256,128]{1,0:T(8,128)S(1)}) fusion(f32[256,128]{1,0:T(8,128)S(1)} %collective-permute-done.1, f32[2,128,128]{2,1,0:T(8,128)} %get-tuple-element.23, f32[256,128]{1,0:T(8,128)S(1)} %multiply_add_fusion, f32[256,128]{1,0:T(8,128)S(1)} %collective-permute-done.2, ...), kind=kLoop, calls=%fused_computation.7 | loop fusion | flops 229376 | bytes 1179648 | tf_op jit(solution)/shard_map/add | solution.py:331
  17.1 4.4 %collective-permute-start.3 = (f32[256,128]{1,0:T(8,128)S(1)}, f32[256,128]{1,0:T(8,128)S(1)}, u32[]{:S(2)}, u32[]{:S(2)}) collective-permute-start(f32[256,128]{1,0:T(8,128)S(1)} %get-tuple-element.42), channel_id=1, source_target_pairs={{0,2},{1,3},{2,0},{3,1},{4,6},{5,7},{6,4},{7,5},{8,10},{9,11},{10,... | collective-permute-start | bytes 393224 | tf_op jit(solution)/shard_map/ppermute | solution.py:385
  21.5 0.9 %bitcast_add_fusion.1 = f32[256,128]{1,0:T(8,128)S(1)} fusion(f32[256,128]{1,0:T(8,128)S(1)} %collective-permute-done.5, f32[2,128,128]{2,1,0:T(8,128)} %get-tuple-element.27), kind=kLoop, calls=%fused_computation.4 | loop fusion | flops 32768 | bytes 393216 | tf_op jit(solution)/shard_map/add | solution.py:401
  22.5 3.2 %collective-permute-done.3 = f32[256,128]{1,0:T(8,128)S(1)} collective-permute-done((f32[256,128]{1,0:T(8,128)S(1)}, f32[256,128]{1,0:T(8,128)S(1)}, u32[]{:S(2)}, u32[]{:S(2)}) %collective-permute-start.3) | collective-permute-done | bytes 131104 | tf_op jit(solution)/shard_map/ppermute | solution.py:385
  25.7 3.0 %collective-permute-start.4 = (f32[256,128]{1,0:T(8,128)S(1)}, f32[256,128]{1,0:T(8,128)S(1)}, u32[]{:S(2)}, u32[]{:S(2)}) collective-permute-start(f32[256,128]{1,0:T(8,128)S(1)} %add.122), channel_id=1, source_target_pairs={{0,4},{1,5},{2,6},{3,7},{4,0},{5,1},{6,2},{7,3},{8,12},{9,13},{10,... | collective-permute-start | bytes 393224 | tf_op jit(solution)/shard_map/ppermute | solution.py:385
  28.8 7.6 %densify.1 = (bf16[2048,1024]{1,0:T(8,128)(2,1)}, f32[8,128]{1,0:T(8,128)S(1)}) custom-call(s32[1,1,384]{2,1,0:T(1,128)S(1)} %copy-done.3, s32[1,1,384]{2,1,0:T(1,128)S(1)} %copy-done.4, s32[1,1]{1,0:T(1,128)S(6)} %copy.11.live_ref, bf16[1,1,384,128,128]{4,3,2,1,0:T(8,128)(2,1)} %blocks_ref.3), custom_call_target="tpu_custom_call" | custom-call | bytes 41943040 | tf_op jit(solution)/shard_map/densify/pallas_call | solution.py:358
  36.4 1.1 %middle.1 = (bf16[256,256]{1,0:T(8,128)(2,1)}, f32[128,256]{1,0:T(8,128)S(1)}, f32[128,128]{1,0:T(8,128)S(1)}, f32[128,128]{1,0:T(8,128)S(1)}) custom-call(s32[64,128]{1,0:T(8,128)S(1)} %bitcast.27, bf16[256,256]{1,0:T(8,128)(2,1)S(1)} %copy-done.1, bf16[128,256]{1,0:T(8,128)(2,1)S(1)} %copy-done.2, f32[256,128]{1,0:T(8,128)S(1)} %get-tuple-element.43.refs_0_, ...), custom_call_target="tpu_custom_call" | custom-call | tf_op jit(solution)/shard_map/middle/pallas_call | solution.py:410
  37.5 1.6 %collective-permute-start.8 = (f32[128,256]{1,0:T(8,128)S(1)}, f32[128,256]{1,0:T(8,128)S(1)}, u32[]{:S(2)}, u32[]{:S(2)}) collective-permute-start(f32[128,256]{1,0:T(8,128)S(1)} %get-tuple-element.32.refs_0_), channel_id=1, source_target_pairs={{0,2},{1,3},{2,0},{3,1},{4,6},{5,7},{6,4},{7,5},{8,10},{9,11},{10,... | collective-permute-start | bytes 393224 | tf_op jit(solution)/shard_map/ppermute | solution.py:385
  39.6 0.8 %collective-permute-start.14 = (f32[128,128]{1,0:T(8,128)S(1)}, f32[128,128]{1,0:T(8,128)S(1)}, u32[]{:S(2)}, u32[]{:S(2)}) collective-permute-start(f32[128,128]{1,0:T(8,128)S(1)} %add.126), channel_id=1, source_target_pairs={{0,2},{1,3},{2,0},{3,1},{4,6},{5,7},{6,4},{7,5},{8,10},{9,11},{10,... | collective-permute-start | bytes 196616 | tf_op jit(solution)/shard_map/ppermute | solution.py:385
  40.4 6.3 %collective-permute-done.14 = f32[128,128]{1,0:T(8,128)S(1)} collective-permute-done((f32[128,128]{1,0:T(8,128)S(1)}, f32[128,128]{1,0:T(8,128)S(1)}, u32[]{:S(2)}, u32[]{:S(2)}) %collective-permute-start.14) | collective-permute-done | bytes 65568 | tf_op jit(solution)/shard_map/ppermute | solution.py:385
  46.8 1.7 %collective-permute-done.9.refs_4_ = f32[128,256]{1,0:T(8,128)S(1)} collective-permute-done((f32[128,256]{1,0:T(8,128)S(1)}, f32[128,256]{1,0:T(8,128)S(1)}, u32[]{:S(2)}, u32[]{:S(2)}) %collective-permute-start.9) | collective-permute-done | bytes 131104 | tf_op jit(solution)/shard_map/ppermute | solution.py:385
  49.0 0.8 %collective-permute-start.12 = (f32[128,256]{1,0:T(8,128)S(1)}, f32[128,256]{1,0:T(8,128)S(1)}, u32[]{:S(2)}, u32[]{:S(2)}) collective-permute-start(f32[128,256]{1,0:T(8,128)S(1)} %collective-permute-done.9.refs_4_), channel_id=1, source_target_pairs={{0,2},{1,3},{2,0},{3,1},{4,6},{5,7},{6,4},{7,5},{8,10},{9,11},{10,... | collective-permute-start | bytes 393224 | tf_op jit(solution)/shard_map/ppermute | solution.py:385
  50.1 2.9 %backward_early.1 = (f32[128,1024]{1,0:T(8,128)S(1)}, bf16[512,1024]{1,0:T(8,128)(2,1)S(1)}) custom-call(bf16[2048,1024]{1,0:T(8,128)(2,1)} %get-tuple-element.31.tile_ref, f32[128,256]{1,0:T(8,128)S(1)} %get-tuple-element.32.refs_0_, f32[128,256]{1,0:T(8,128)S(1)} %collective-permute-done.7.refs_1_, f32[128,256]{1,0:T(8,128)S(1)} %multiply_add_fusion.1.refs_2_, ...), custom_call_target="tpu_custom_call" | custom-call | flops 1073741824 | bytes 33554432 | tf_op jit(solution)/shard_map/backward_early/pallas_call | solution.py:434
  53.0 1.5 %collective-permute-done.12 = f32[128,256]{1,0:T(8,128)S(1)} collective-permute-done((f32[128,256]{1,0:T(8,128)S(1)}, f32[128,256]{1,0:T(8,128)S(1)}, u32[]{:S(2)}, u32[]{:S(2)}) %collective-permute-start.12) | collective-permute-done | bytes 131104 | tf_op jit(solution)/shard_map/ppermute | solution.py:385
  54.6 0.7 collective-permute-start.19
  55.4 0.6 collective-permute-done.15.refs_1_
  56.0 1.1 %backward_late.1 = (f32[512,128]{1,0:T(8,128)S(1)}, f32[512,128]{1,0:T(8,128)S(1)}) custom-call(s32[64,128]{1,0:T(8,128)S(1)} %bitcast.28, bf16[512,1024]{1,0:T(8,128)(2,1)S(1)} %get-tuple-element.33.dense_ref, f32[128,1024]{1,0:T(8,128)S(1)} %get-tuple-element.34.sofar_ref, f32[128,256]{1,0:T(8,128)S(1)} %add_add_fusion.refs_0_, ...), custom_call_target="tpu_custom_call" | custom-call | tf_op jit(solution)/shard_map/backward_late/pallas_call | solution.py:463
  57.1 1.6 %collective-permute-start.16 = (f32[512,128]{1,0:T(8,128)S(1)}, f32[512,128]{1,0:T(8,128)S(1)}, u32[]{:S(2)}, u32[]{:S(2)}) collective-permute-start(f32[512,128]{1,0:T(8,128)S(1)} %get-tuple-element.37), channel_id=1, source_target_pairs={{0,8},{8,0},{16,24},{24,16},{1,9},{9,1},{17,25},{25,17},{2,10},{10... | collective-permute-start | bytes 786440 | tf_op jit(solution)/shard_map/ppermute | solution.py:388
  58.7 1.3 %collective-permute-start.18 = (f32[512,128]{1,0:T(8,128)S(1)}, f32[512,128]{1,0:T(8,128)S(1)}, u32[]{:S(2)}, u32[]{:S(2)}) collective-permute-start(f32[512,128]{1,0:T(8,128)S(1)} %get-tuple-element.38), channel_id=1, source_target_pairs={{0,16},{8,24},{16,0},{24,8},{1,17},{9,25},{17,1},{25,9},{2,18},{10... | collective-permute-start | bytes 786440 | tf_op jit(solution)/shard_map/ppermute | solution.py:388
  60.1 1.4 %collective-permute-done.19 = f32[128,128]{1,0:T(8,128)S(1)} collective-permute-done((f32[128,128]{1,0:T(8,128)S(1)}, f32[128,128]{1,0:T(8,128)S(1)}, u32[]{:S(2)}, u32[]{:S(2)}) %collective-permute-start.19) | collective-permute-done | bytes 65568 | tf_op jit(solution)/shard_map/ppermute | solution.py:385
  61.5 1.6 %collective-permute-start.20 = (f32[128,128]{1,0:T(8,128)S(1)}, f32[128,128]{1,0:T(8,128)S(1)}, u32[]{:S(2)}, u32[]{:S(2)}) collective-permute-start(f32[128,128]{1,0:T(8,128)S(1)} %bitcast_add_fusion.6), channel_id=1, source_target_pairs={{0,8},{8,0},{16,24},{24,16},{1,9},{9,1},{17,25},{25,17},{2,10},{10... | collective-permute-start | bytes 196616 | tf_op jit(solution)/shard_map/ppermute | solution.py:388
  63.1 3.2 %collective-permute-done.16 = f32[512,128]{1,0:T(8,128)S(1)} collective-permute-done((f32[512,128]{1,0:T(8,128)S(1)}, f32[512,128]{1,0:T(8,128)S(1)}, u32[]{:S(2)}, u32[]{:S(2)}) %collective-permute-start.16) | collective-permute-done | bytes 262176 | tf_op jit(solution)/shard_map/ppermute | solution.py:388
  66.3 1.7 %collective-permute-start.17 = (f32[512,128]{1,0:T(8,128)S(1)}, f32[512,128]{1,0:T(8,128)S(1)}, u32[]{:S(2)}, u32[]{:S(2)}) collective-permute-start(f32[512,128]{1,0:T(8,128)S(1)} %add.131), channel_id=1, source_target_pairs={{0,16},{8,24},{16,0},{24,8},{1,17},{9,25},{17,1},{25,9},{2,18},{10... | collective-permute-start | bytes 786440 | tf_op jit(solution)/shard_map/ppermute | solution.py:388
  68.1 1.3 %collective-permute-start.21 = (f32[512,128]{1,0:T(8,128)S(1)}, f32[512,128]{1,0:T(8,128)S(1)}, u32[]{:S(2)}, u32[]{:S(2)}) collective-permute-start(f32[512,128]{1,0:T(8,128)S(1)} %bitcast_add_fusion), channel_id=1, source_target_pairs={{0,8},{8,0},{16,24},{24,16},{1,9},{9,1},{17,25},{25,17},{2,10},{10... | collective-permute-start | bytes 786440 | tf_op jit(solution)/shard_map/ppermute | solution.py:388
  69.4 0.7 collective-permute-start.22
  70.1 3.8 %collective-permute-done.17 = f32[512,128]{1,0:T(8,128)S(1)} collective-permute-done((f32[512,128]{1,0:T(8,128)S(1)}, f32[512,128]{1,0:T(8,128)S(1)}, u32[]{:S(2)}, u32[]{:S(2)}) %collective-permute-start.17) | collective-permute-done | bytes 262176 | tf_op jit(solution)/shard_map/ppermute | solution.py:388
  73.9 0.7 collective-permute-done.22
  74.7 0.8 %pad_maximum_fusion = f32[1024,128]{1,0:T(8,128)} fusion(f32[512,128]{1,0:T(8,128)S(1)} %add.142, f32[512,128]{1,0:T(8,128)S(1)} %add.132), kind=kLoop, calls=%fused_computation | loop fusion | flops 131072 | bytes 1048576 | tf_op jit(solution)/shard_map/concatenate | solution.py:489
  75.9 0.7 maximum_maximum_fusion
  (57 shorter events, 3.0 us)
Async XLA Ops:
  0.6 28.1 %copy-start.3 = (s32[1,1,384]{2,1,0:T(1,128)S(1)}, s32[1,1,384]{2,1,0:T(1,128)}, u32[]{:S(2)}) copy-start(s32[1,1,384]{2,1,0:T(1,128)} %rows_ref.3) | copy-start | bytes 4612
  0.6 28.1 %copy-start.4 = (s32[1,1,384]{2,1,0:T(1,128)S(1)}, s32[1,1,384]{2,1,0:T(1,128)}, u32[]{:S(2)}) copy-start(s32[1,1,384]{2,1,0:T(1,128)} %cols_ref.3) | copy-start | bytes 4612
  1.3 35.1 %copy-start = (s32[8192]{0:T(1024)S(1)}, s32[8192]{0:T(1024)}, u32[]{:S(2)}) copy-start(s32[8192]{0:T(1024)} %param.9) | copy-start | bytes 98308
  1.3 35.1 %copy-start.1 = (bf16[256,256]{1,0:T(8,128)(2,1)S(1)}, bf16[256,256]{1,0:T(8,128)(2,1)}, u32[]{:S(2)}) copy-start(bf16[256,256]{1,0:T(8,128)(2,1)} %cot_ref.1) | copy-start | bytes 393220
  1.3 35.1 %copy-start.2 = (bf16[128,256]{1,0:T(8,128)(2,1)S(1)}, bf16[128,256]{1,0:T(8,128)(2,1)}, u32[]{:S(2)}) copy-start(bf16[128,256]{1,0:T(8,128)(2,1)} %weight_ref.1) | copy-start | bytes 196612
  13.6 2.3 %collective-permute-start.1 = (f32[256,128]{1,0:T(8,128)}, f32[256,128]{1,0:T(8,128)S(1)}, u32[]{:S(2)}, u32[]{:S(2)}) collective-permute-start(f32[256,128]{1,0:T(8,128)} %bitcast.32), channel_id=1, source_target_pairs={{0,1},{1,0},{2,3},{3,2},{4,5},{5,4},{6,7},{7,6},{8,9},{9,8},{10,11... | collective-permute-start | bytes 393224 | tf_op jit(solution)/shard_map/ppermute | solution.py:382
  14.3 1.6 %collective-permute-start.2 = (f32[256,128]{1,0:T(8,128)}, f32[256,128]{1,0:T(8,128)S(1)}, u32[]{:S(2)}, u32[]{:S(2)}) collective-permute-start(f32[256,128]{1,0:T(8,128)} %bitcast.31), channel_id=1, source_target_pairs={{0,1},{1,0},{2,3},{3,2},{4,5},{5,4},{6,7},{7,6},{8,9},{9,8},{10,11... | collective-permute-start | bytes 393224 | tf_op jit(solution)/shard_map/ppermute | solution.py:382
  14.4 1.7 %collective-permute-start = (f32[256,128]{1,0:T(8,128)}, f32[256,128]{1,0:T(8,128)S(1)}, u32[]{:S(2)}, u32[]{:S(2)}) collective-permute-start(f32[256,128]{1,0:T(8,128)} %bitcast.30), channel_id=1, source_target_pairs={{0,1},{1,0},{2,3},{3,2},{4,5},{5,4},{6,7},{7,6},{8,9},{9,8},{10,11... | collective-permute-start | bytes 393224 | tf_op jit(solution)/shard_map/ppermute | solution.py:382
  14.8 6.6 %collective-permute-start.5 = (f32[256,128]{1,0:T(8,128)}, f32[256,128]{1,0:T(8,128)S(1)}, u32[]{:S(2)}, u32[]{:S(2)}) collective-permute-start(f32[256,128]{1,0:T(8,128)} %bitcast.29), channel_id=1, source_target_pairs={{0,1},{1,0},{2,3},{3,2},{4,5},{5,4},{6,7},{7,6},{8,9},{9,8},{10,11... | collective-permute-start | bytes 393224 | tf_op jit(solution)/shard_map/ppermute | solution.py:382
  17.1 8.6 %collective-permute-start.3 = (f32[256,128]{1,0:T(8,128)S(1)}, f32[256,128]{1,0:T(8,128)S(1)}, u32[]{:S(2)}, u32[]{:S(2)}) collective-permute-start(f32[256,128]{1,0:T(8,128)S(1)} %get-tuple-element.42), channel_id=1, source_target_pairs={{0,2},{1,3},{2,0},{3,1},{4,6},{5,7},{6,4},{7,5},{8,10},{9,11},{10,... | collective-permute-start | bytes 393224 | tf_op jit(solution)/shard_map/ppermute | solution.py:385
  22.4 14.0 %collective-permute-start.6 = (f32[256,128]{1,0:T(8,128)S(1)}, f32[256,128]{1,0:T(8,128)S(1)}, u32[]{:S(2)}, u32[]{:S(2)}) collective-permute-start(f32[256,128]{1,0:T(8,128)S(1)} %bitcast_add_fusion.1), channel_id=1, source_target_pairs={{0,2},{1,3},{2,0},{3,1},{4,6},{5,7},{6,4},{7,5},{8,10},{9,11},{10,... | collective-permute-start | bytes 393224 | tf_op jit(solution)/shard_map/ppermute | solution.py:385
  25.7 10.7 %collective-permute-start.4 = (f32[256,128]{1,0:T(8,128)S(1)}, f32[256,128]{1,0:T(8,128)S(1)}, u32[]{:S(2)}, u32[]{:S(2)}) collective-permute-start(f32[256,128]{1,0:T(8,128)S(1)} %add.122), channel_id=1, source_target_pairs={{0,4},{1,5},{2,6},{3,7},{4,0},{5,1},{6,2},{7,3},{8,12},{9,13},{10,... | collective-permute-start | bytes 393224 | tf_op jit(solution)/shard_map/ppermute | solution.py:385
  37.5 2.1 %collective-permute-start.13 = (f32[128,128]{1,0:T(8,128)S(1)}, f32[128,128]{1,0:T(8,128)S(1)}, u32[]{:S(2)}, u32[]{:S(2)}) collective-permute-start(f32[128,128]{1,0:T(8,128)S(1)} %get-tuple-element.36), channel_id=1, source_target_pairs={{0,1},{1,0},{2,3},{3,2},{4,5},{5,4},{6,7},{7,6},{8,9},{9,8},{10,11... | collective-permute-start | bytes 196616 | tf_op jit(solution)/shard_map/ppermute | solution.py:382
  37.5 9.2 %collective-permute-start.8 = (f32[128,256]{1,0:T(8,128)S(1)}, f32[128,256]{1,0:T(8,128)S(1)}, u32[]{:S(2)}, u32[]{:S(2)}) collective-permute-start(f32[128,256]{1,0:T(8,128)S(1)} %get-tuple-element.32.refs_0_), channel_id=1, source_target_pairs={{0,2},{1,3},{2,0},{3,1},{4,6},{5,7},{6,4},{7,5},{8,10},{9,11},{10,... | collective-permute-start | bytes 393224 | tf_op jit(solution)/shard_map/ppermute | solution.py:385
  39.1 9.3 %collective-permute-start.9 = (f32[128,256]{1,0:T(8,128)S(1)}, f32[128,256]{1,0:T(8,128)S(1)}, u32[]{:S(2)}, u32[]{:S(2)}) collective-permute-start(f32[128,256]{1,0:T(8,128)S(1)} %get-tuple-element.32.refs_0_), channel_id=1, source_target_pairs={{0,4},{1,5},{2,6},{3,7},{4,0},{5,1},{6,2},{7,3},{8,12},{9,13},{10,... | collective-permute-start | bytes 393224 | tf_op jit(solution)/shard_map/ppermute | solution.py:385
  39.6 7.2 %collective-permute-start.14 = (f32[128,128]{1,0:T(8,128)S(1)}, f32[128,128]{1,0:T(8,128)S(1)}, u32[]{:S(2)}, u32[]{:S(2)}) collective-permute-start(f32[128,128]{1,0:T(8,128)S(1)} %add.126), channel_id=1, source_target_pairs={{0,2},{1,3},{2,0},{3,1},{4,6},{5,7},{6,4},{7,5},{8,10},{9,11},{10,... | collective-permute-start | bytes 196616 | tf_op jit(solution)/shard_map/ppermute | solution.py:385
  40.4 9.5 %collective-permute-start.7 = (f32[128,256]{1,0:T(8,128)S(1)}, f32[128,256]{1,0:T(8,128)S(1)}, u32[]{:S(2)}, u32[]{:S(2)}) collective-permute-start(f32[128,256]{1,0:T(8,128)S(1)} %get-tuple-element.32.refs_0_), channel_id=1, source_target_pairs={{0,1},{1,0},{2,3},{3,2},{4,5},{5,4},{6,7},{7,6},{8,9},{9,8},{10,11... | collective-permute-start | bytes 393224 | tf_op jit(solution)/shard_map/ppermute | solution.py:382
  48.5 1.5 %collective-permute-start.10 = (f32[128,256]{1,0:T(8,128)S(1)}, f32[128,256]{1,0:T(8,128)S(1)}, u32[]{:S(2)}, u32[]{:S(2)}) collective-permute-start(f32[128,256]{1,0:T(8,128)S(1)} %multiply_add_fusion.1.refs_2_), channel_id=1, source_target_pairs={{0,1},{1,0},{2,3},{3,2},{4,5},{5,4},{6,7},{7,6},{8,9},{9,8},{10,11... | collective-permute-start | bytes 393224 | tf_op jit(solution)/shard_map/ppermute | solution.py:382
  48.5 1.5 %collective-permute-start.11 = (f32[128,256]{1,0:T(8,128)S(1)}, f32[128,256]{1,0:T(8,128)S(1)}, u32[]{:S(2)}, u32[]{:S(2)}) collective-permute-start(f32[128,256]{1,0:T(8,128)S(1)} %collective-permute-done.9.refs_4_), channel_id=1, source_target_pairs={{0,1},{1,0},{2,3},{3,2},{4,5},{5,4},{6,7},{7,6},{8,9},{9,8},{10,11... | collective-permute-start | bytes 393224 | tf_op jit(solution)/shard_map/ppermute | solution.py:382
  49.0 5.5 %collective-permute-start.12 = (f32[128,256]{1,0:T(8,128)S(1)}, f32[128,256]{1,0:T(8,128)S(1)}, u32[]{:S(2)}, u32[]{:S(2)}) collective-permute-start(f32[128,256]{1,0:T(8,128)S(1)} %collective-permute-done.9.refs_4_), channel_id=1, source_target_pairs={{0,2},{1,3},{2,0},{3,1},{4,6},{5,7},{6,4},{7,5},{8,10},{9,11},{10,... | collective-permute-start | bytes 393224 | tf_op jit(solution)/shard_map/ppermute | solution.py:385
  54.6 1.4 %collective-permute-start.15 = (f32[128,256]{1,0:T(8,128)S(1)}, f32[128,256]{1,0:T(8,128)S(1)}, u32[]{:S(2)}, u32[]{:S(2)}) collective-permute-start(f32[128,256]{1,0:T(8,128)S(1)} %add_add_fusion.refs_0_), channel_id=1, source_target_pairs={{0,1},{1,0},{2,3},{3,2},{4,5},{5,4},{6,7},{7,6},{8,9},{9,8},{10,11... | collective-permute-start | bytes 393224 | tf_op jit(solution)/shard_map/ppermute | solution.py:382
  54.6 6.8 %collective-permute-start.19 = (f32[128,128]{1,0:T(8,128)S(1)}, f32[128,128]{1,0:T(8,128)S(1)}, u32[]{:S(2)}, u32[]{:S(2)}) collective-permute-start(f32[128,128]{1,0:T(8,128)S(1)} %add.127), channel_id=1, source_target_pairs={{0,4},{1,5},{2,6},{3,7},{4,0},{5,1},{6,2},{7,3},{8,12},{9,13},{10,... | collective-permute-start | bytes 196616 | tf_op jit(solution)/shard_map/ppermute | solution.py:385
  57.1 9.1 %collective-permute-start.16 = (f32[512,128]{1,0:T(8,128)S(1)}, f32[512,128]{1,0:T(8,128)S(1)}, u32[]{:S(2)}, u32[]{:S(2)}) collective-permute-start(f32[512,128]{1,0:T(8,128)S(1)} %get-tuple-element.37), channel_id=1, source_target_pairs={{0,8},{8,0},{16,24},{24,16},{1,9},{9,1},{17,25},{25,17},{2,10},{10... | collective-permute-start | bytes 786440 | tf_op jit(solution)/shard_map/ppermute | solution.py:388
  58.7 9.3 %collective-permute-start.18 = (f32[512,128]{1,0:T(8,128)S(1)}, f32[512,128]{1,0:T(8,128)S(1)}, u32[]{:S(2)}, u32[]{:S(2)}) collective-permute-start(f32[512,128]{1,0:T(8,128)S(1)} %get-tuple-element.38), channel_id=1, source_target_pairs={{0,16},{8,24},{16,0},{24,8},{1,17},{9,25},{17,1},{25,9},{2,18},{10... | collective-permute-start | bytes 786440 | tf_op jit(solution)/shard_map/ppermute | solution.py:388
  61.5 6.5 %collective-permute-start.20 = (f32[128,128]{1,0:T(8,128)S(1)}, f32[128,128]{1,0:T(8,128)S(1)}, u32[]{:S(2)}, u32[]{:S(2)}) collective-permute-start(f32[128,128]{1,0:T(8,128)S(1)} %bitcast_add_fusion.6), channel_id=1, source_target_pairs={{0,8},{8,0},{16,24},{24,16},{1,9},{9,1},{17,25},{25,17},{2,10},{10... | collective-permute-start | bytes 196616 | tf_op jit(solution)/shard_map/ppermute | solution.py:388
  66.3 7.6 %collective-permute-start.17 = (f32[512,128]{1,0:T(8,128)S(1)}, f32[512,128]{1,0:T(8,128)S(1)}, u32[]{:S(2)}, u32[]{:S(2)}) collective-permute-start(f32[512,128]{1,0:T(8,128)S(1)} %add.131), channel_id=1, source_target_pairs={{0,16},{8,24},{16,0},{24,8},{1,17},{9,25},{17,1},{25,9},{2,18},{10... | collective-permute-start | bytes 786440 | tf_op jit(solution)/shard_map/ppermute | solution.py:388
  68.1 6.6 %collective-permute-start.21 = (f32[512,128]{1,0:T(8,128)S(1)}, f32[512,128]{1,0:T(8,128)S(1)}, u32[]{:S(2)}, u32[]{:S(2)}) collective-permute-start(f32[512,128]{1,0:T(8,128)S(1)} %bitcast_add_fusion), channel_id=1, source_target_pairs={{0,8},{8,0},{16,24},{24,16},{1,9},{9,1},{17,25},{25,17},{2,10},{10... | collective-permute-start | bytes 786440 | tf_op jit(solution)/shard_map/ppermute | solution.py:388
  69.4 5.2 %collective-permute-start.22 = (f32[128,128]{1,0:T(8,128)S(1)}, f32[128,128]{1,0:T(8,128)S(1)}, u32[]{:S(2)}, u32[]{:S(2)}) collective-permute-start(f32[128,128]{1,0:T(8,128)S(1)} %get-tuple-element.39), channel_id=1, source_target_pairs={{0,16},{8,24},{16,0},{24,8},{1,17},{9,25},{17,1},{25,9},{2,18},{10... | collective-permute-start | bytes 196616 | tf_op jit(solution)/shard_map/ppermute | solution.py:388
  74.6 1.3 %collective-permute-start.23 = (f32[128,128]{1,0:T(8,128)S(1)}, f32[128,128]{1,0:T(8,128)S(1)}, u32[]{:S(2)}, u32[]{:S(2)}) collective-permute-start(f32[128,128]{1,0:T(8,128)S(1)} %bitcast_add_fusion.4), channel_id=1, source_target_pairs={{0,1},{1,0},{2,3},{3,2},{4,5},{5,4},{6,7},{7,6},{8,9},{9,8},{10,11... | collective-permute-start | bytes 196616 | tf_op jit(solution)/shard_map/ppermute | solution.py:382

commit v14 on v10

--- a/solution.py
+++ b/solution.py
@@ -103,10 +103,10 @@
     for panel in range(n_panels):
         base = panel * panel_blocks
 
-        @pl.loop(0, positions)
+        @pl.loop(0, positions // 4)
         def _(p):
             for acc in accs:
-                acc[p] = jnp.zeros((part, EDGE), F32)
+                acc[pl.ds(p * 4, 4)] = jnp.zeros((4, part, EDGE), F32)
 
         def place(s):
             dev, inner = halve(rows_ref[0, 0, s], dev_blocks)
@@ -377,7 +377,7 @@
     )(tile, *early)
 
     wsum = after(wsum, sofar) + moved
-    own[last] = after(after(own[last], sofar), wsum)
+    own[last] = after(own[last], sofar)
     late = [own[last], swap(own[last])]
     for bit in range(1, chip_bits):
         wsum = wsum + chip_flip(wsum, bit)
@@ -405,11 +405,12 @@
 
     done = list(done)
     for t in range(row_bits):
-        wsum = after(wsum, done[-1 if t == 0 else 0])
+        if t == 0:
+            wsum = after(wsum, done[-1])
+        else:
+            wsum = after(wsum, done[-1])
         wsum = wsum + row_flip(wsum, t)
         done = [x + row_flip(x, (i + t) % row_bits) for i, x in enumerate(done)]
-        if t == 0:
-            done[-1] = after(done[-1], wsum)
     wsum = after(wsum, done[0])
     feat_grad = jnp.concatenate(done, axis=0)
 

time: 70 us -> 68.9 us (0.984)
  waiting for transfers between devices: 26.3 us -> 25.4 us
    add x3 -> x4, other arithmetic: 1.94 us -> 1.96 us  [after(): return x + 0.0 * other[:, :x.shape[1]]]
  transfers between devices with their start and end apart: 24 -> 24, of which waited for: 13 -> 14; matrix products, arithmetic and copies ran while one was open for 6% -> 6% of each run, Pallas kernels for 6% -> 6%
where the time goes in v14:
time: 68.9 us; the launch traced here: 68.7 us
  waiting for transfers between devices  25.4 us (37%)
  starting transfers between devices  22 us (32%)
  Pallas kernels  15.2 us (22%)
  other arithmetic  4.63 us (7%)
  between operations  1.49 us (2%)
    ppermute x8, waiting for transfers between devices, chip_flip(): return lax.ppermute(x, 'col', [(i, i ^ 2 << bit) for i in range(n_col)])  15.7 us
    ppermute x8, starting transfers between devices, chip_flip(): return lax.ppermute(x, 'col', [(i, i ^ 2 << bit) for i in range(n_col)])  11.3 us
    pallas_call x1, Pallas kernels, body(): pl.pallas_call(functools.partial(forward_kernel, n_col, chunk, panel_dev,...  10 us
    ppermute x6, waiting for transfers between devices, row_flip(): return lax.ppermute(x, 'row', [(i, i ^ 1 << bit) for i in range(n_row)])  8.46 us
    ppermute x6, starting transfers between devices, row_flip(): return lax.ppermute(x, 'row', [(i, i ^ 1 << bit) for i in range(n_row)])  8.34 us
    pallas_call x1, Pallas kernels, body(): pl.pallas_call(functools.partial(partial_kernel, len(early)), out_shape=(...  2.93 us
    ppermute x10, starting transfers between devices, swap(): return lax.ppermute(x, 'col', swap_pairs)  2.29 us
    add x4, other arithmetic, after(): return x + 0.0 * other[:, :x.shape[1]]  1.96 us
  transfers between devices with their start and end apart: 24, of which 14 were waited for; matrix products, arithmetic and copies ran while one was open for 6% of the time, Pallas kernels for 6%

profile of v14, /device:TPU:0, one launch (start us, length us, event | category | flops | bytes accessed | tf_op | source)
XLA Modules:
  0.0 68.7 jit_solution(16423106888084365431)
XLA Ops:
  1.3 10.0 %densify_forward.1 = (f32[256,128]{1,0:T(8,128)}, f32[256,128]{1,0:T(8,128)}, f32[256,128]{1,0:T(8,128)}, f32[256,128]{1,0:T(8,128)}, f32[256,128]{1,0:T(8,128)}...) custom-call(s32[1,1,384]{2,1,0:T(1,128)} %rows_ref.1, ...), custom_call_target="tpu_custom_call" | custom-call | tf_op jit(solution)/shard_map/densify_forward/pallas_call | solution.py:282
  11.4 0.5 collective-permute-start
  12.5 0.9 %multiply_add_fusion = f32[256,128]{1,0:T(8,128)S(1)} fusion(f32[256,128]{1,0:T(8,128)} %get-tuple-element.24), kind=kLoop, calls=%fused_computation.1 | loop fusion | flops 65536 | bytes 262144 | tf_op jit(solution)/shard_map/add | solution.py:273
  13.7 3.0 %collective-permute-start.3 = (f32[256,128]{1,0:T(8,128)S(1)}, f32[256,128]{1,0:T(8,128)S(1)}, u32[]{:S(2)}, u32[]{:S(2)}) collective-permute-start(f32[256,128]{1,0:T(8,128)S(1)} %add.98), channel_id=1, source_target_pairs={{0,2},{1,3},{2,0},{3,1},{4,6},{5,7},{6,4},{7,5},{8,10},{9,11},{10,... | collective-permute-start | bytes 393224 | tf_op jit(solution)/shard_map/ppermute | solution.py:310
  16.6 1.0 %multiply_add_fusion.2 = (f32[256,128]{1,0:T(8,128)S(1)}, f32[256,128]{1,0:T(8,128)S(1)}) fusion(f32[256,128]{1,0:T(8,128)} %get-tuple-element.22, f32[256,128]{1,0:T(8,128)S(1)} %collective-permute-done.1, f32[256,128]{1,0:T(8,128)} %get-tuple-element.20, f32[256,128]{1,0:T(8,128)S(1)} %collective-permute-done), kind=kLoop, calls=%fused_computation.4 | loop fusion | flops 131072 | bytes 786432 | tf_op jit(solution)/shard_map/add | solution.py:273
  17.7 0.9 %add.100 = f32[256,128]{1,0:T(8,128)S(1)} add(f32[256,128]{1,0:T(8,128)} %get-tuple-element.26, f32[256,128]{1,0:T(8,128)S(1)} %collective-permute-done.5) | non-fusion elementwise | flops 32768 | bytes 393216 | tf_op jit(solution)/shard_map/add | solution.py:326
  18.7 1.8 %collective-permute-done.3 = f32[256,128]{1,0:T(8,128)S(1)} collective-permute-done((f32[256,128]{1,0:T(8,128)S(1)}, f32[256,128]{1,0:T(8,128)S(1)}, u32[]{:S(2)}, u32[]{:S(2)}) %collective-permute-start.3) | collective-permute-done | bytes 131104 | tf_op jit(solution)/shard_map/ppermute | solution.py:310
  20.5 2.8 %collective-permute-start.4 = (f32[256,128]{1,0:T(8,128)S(1)}, f32[256,128]{1,0:T(8,128)S(1)}, u32[]{:S(2)}, u32[]{:S(2)}) collective-permute-start(f32[256,128]{1,0:T(8,128)S(1)} %add.99), channel_id=1, source_target_pairs={{0,4},{1,5},{2,6},{3,7},{4,0},{5,1},{6,2},{7,3},{8,12},{9,13},{10,... | collective-permute-start | bytes 393224 | tf_op jit(solution)/shard_map/ppermute | solution.py:310
  23.3 2.0 %collective-permute-done.6.refs_2_ = f32[256,128]{1,0:T(8,128)S(1)} collective-permute-done((f32[256,128]{1,0:T(8,128)S(1)}, f32[256,128]{1,0:T(8,128)S(1)}, u32[]{:S(2)}, u32[]{:S(2)}) %collective-permute-start.6) | collective-permute-done | bytes 131104 | tf_op jit(solution)/shard_map/ppermute | solution.py:310
  25.3 4.1 %collective-permute-done.4.refs_1_ = f32[256,128]{1,0:T(8,128)S(1)} collective-permute-done((f32[256,128]{1,0:T(8,128)S(1)}, f32[256,128]{1,0:T(8,128)S(1)}, u32[]{:S(2)}, u32[]{:S(2)}) %collective-permute-start.4) | collective-permute-done | bytes 131104 | tf_op jit(solution)/shard_map/ppermute | solution.py:310
  29.4 1.1 %middle.1 = (bf16[256,256]{1,0:T(8,128)(2,1)}, f32[128,256]{1,0:T(8,128)S(1)}, f32[128,128]{1,0:T(8,128)S(1)}, f32[128,128]{1,0:T(8,128)S(1)}) custom-call(s32[64,128]{1,0:T(8,128)S(1)} %bitcast.8, bf16[256,256]{1,0:T(8,128)(2,1)S(1)} %copy-done.1, bf16[128,256]{1,0:T(8,128)(2,1)S(1)} %copy-done.2, f32[256,128]{1,0:T(8,128)S(1)} %get-tuple-element.38.refs_0_, ...), custom_call_target="tpu_custom_call" | custom-call | tf_op jit(solution)/shard_map/middle/pallas_call | solution.py:335
  30.5 3.8 %collective-permute-start.8 = (f32[128,256]{1,0:T(8,128)S(1)}, f32[128,256]{1,0:T(8,128)S(1)}, u32[]{:S(2)}, u32[]{:S(2)}) collective-permute-start(f32[128,256]{1,0:T(8,128)S(1)} %get-tuple-element.30.refs_0_), channel_id=1, source_target_pairs={{0,2},{1,3},{2,0},{3,1},{4,6},{5,7},{6,4},{7,5},{8,10},{9,11},{10,... | collective-permute-start | bytes 393224 | tf_op jit(solution)/shard_map/ppermute | solution.py:310
  34.4 4.5 %collective-permute-done.10.refs_4_ = f32[128,256]{1,0:T(8,128)S(1)} collective-permute-done((f32[128,256]{1,0:T(8,128)S(1)}, f32[128,256]{1,0:T(8,128)S(1)}, u32[]{:S(2)}, u32[]{:S(2)}) %collective-permute-start.10) | collective-permute-done | bytes 131104 | tf_op jit(solution)/shard_map/ppermute | solution.py:310
  38.9 0.5 collective-permute-start.18
  39.4 0.5 collective-permute-start.9
  40.3 1.4 %collective-permute-start.19 = (f32[128,128]{1,0:T(8,128)S(1)}, f32[128,128]{1,0:T(8,128)S(1)}, u32[]{:S(2)}, u32[]{:S(2)}) collective-permute-start(f32[128,128]{1,0:T(8,128)S(1)} %fusion), channel_id=1, source_target_pairs={{0,2},{1,3},{2,0},{3,1},{4,6},{5,7},{6,4},{7,5},{8,10},{9,11},{10,... | collective-permute-start | bytes 196616 | tf_op jit(solution)/shard_map/ppermute | solution.py:310
  41.8 2.9 %backward_early.1 = (f32[128,1024]{1,0:T(8,128)S(1)}, bf16[512,1024]{1,0:T(8,128)(2,1)S(1)}) custom-call(bf16[2048,1024]{1,0:T(8,128)(2,1)} %get-tuple-element.29.tile_ref, f32[128,256]{1,0:T(8,128)S(1)} %get-tuple-element.30.refs_0_, f32[128,256]{1,0:T(8,128)S(1)} %collective-permute-done.7.refs_1_, f32[128,256]{1,0:T(8,128)S(1)} %collective-permute-done.8.refs_2_, ...), custom_call_target="tpu_custom_call" | custom-call | flops 1073741824 | bytes 33554432 | tf_op jit(solution)/shard_map/backward_early/pallas_call | solution.py:358
  44.7 1.0 %collective-permute-done.12 = f32[128,256]{1,0:T(8,128)S(1)} collective-permute-done((f32[128,256]{1,0:T(8,128)S(1)}, f32[128,256]{1,0:T(8,128)S(1)}, u32[]{:S(2)}, u32[]{:S(2)}) %collective-permute-start.12) | collective-permute-done | bytes 131104 | tf_op jit(solution)/shard_map/ppermute | solution.py:310
  45.8 0.9 %collective-permute-done.19 = f32[128,128]{1,0:T(8,128)S(1)} collective-permute-done((f32[128,128]{1,0:T(8,128)S(1)}, f32[128,128]{1,0:T(8,128)S(1)}, u32[]{:S(2)}, u32[]{:S(2)}) %collective-permute-start.19) | collective-permute-done | bytes 65568 | tf_op jit(solution)/shard_map/ppermute | solution.py:310
  47.1 1.1 %backward_late.1 = (f32[512,128]{1,0:T(8,128)S(1)}, f32[512,128]{1,0:T(8,128)S(1)}) custom-call(s32[64,128]{1,0:T(8,128)S(1)} %bitcast.9, bf16[512,1024]{1,0:T(8,128)(2,1)S(1)} %get-tuple-element.31.dense_ref, f32[128,1024]{1,0:T(8,128)S(1)} %get-tuple-element.32.sofar_ref, f32[128,256]{1,0:T(8,128)S(1)} %multiply_add_fusion.1.refs_0_, ...), custom_call_target="tpu_custom_call" | custom-call | tf_op jit(solution)/shard_map/backward_late/pallas_call | solution.py:388
  48.3 1.6 %collective-permute-start.16 = (f32[512,128]{1,0:T(8,128)S(1)}, f32[512,128]{1,0:T(8,128)S(1)}, u32[]{:S(2)}, u32[]{:S(2)}) collective-permute-start(f32[512,128]{1,0:T(8,128)S(1)} %get-tuple-element.34), channel_id=1, source_target_pairs={{0,16},{8,24},{16,0},{24,8},{1,17},{9,25},{17,1},{25,9},{2,18},{10... | collective-permute-start | bytes 786440 | tf_op jit(solution)/shard_map/ppermute | solution.py:313
  49.8 1.5 %collective-permute-start.14 = (f32[512,128]{1,0:T(8,128)S(1)}, f32[512,128]{1,0:T(8,128)S(1)}, u32[]{:S(2)}, u32[]{:S(2)}) collective-permute-start(f32[512,128]{1,0:T(8,128)S(1)} %get-tuple-element.33), channel_id=1, source_target_pairs={{0,8},{8,0},{16,24},{24,16},{1,9},{9,1},{17,25},{25,17},{2,10},{10... | collective-permute-start | bytes 786440 | tf_op jit(solution)/shard_map/ppermute | solution.py:313
  51.3 1.4 %collective-permute-done.20 = f32[128,128]{1,0:T(8,128)S(1)} collective-permute-done((f32[128,128]{1,0:T(8,128)S(1)}, f32[128,128]{1,0:T(8,128)S(1)}, u32[]{:S(2)}, u32[]{:S(2)}) %collective-permute-start.20) | collective-permute-done | bytes 65568 | tf_op jit(solution)/shard_map/ppermute | solution.py:310
  52.8 1.6 %collective-permute-start.21 = (f32[128,128]{1,0:T(8,128)S(1)}, f32[128,128]{1,0:T(8,128)S(1)}, u32[]{:S(2)}, u32[]{:S(2)}) collective-permute-start(f32[128,128]{1,0:T(8,128)S(1)} %bitcast_add_fusion.2), channel_id=1, source_target_pairs={{0,8},{8,0},{16,24},{24,16},{1,9},{9,1},{17,25},{25,17},{2,10},{10... | collective-permute-start | bytes 196616 | tf_op jit(solution)/shard_map/ppermute | solution.py:313
  54.3 4.3 %collective-permute-done.14 = f32[512,128]{1,0:T(8,128)S(1)} collective-permute-done((f32[512,128]{1,0:T(8,128)S(1)}, f32[512,128]{1,0:T(8,128)S(1)}, u32[]{:S(2)}, u32[]{:S(2)}) %collective-permute-start.14) | collective-permute-done | bytes 262176 | tf_op jit(solution)/shard_map/ppermute | solution.py:313
  58.7 0.6 collective-permute-start.15
  59.3 1.6 %collective-permute-start.17 = (f32[512,128]{1,0:T(8,128)S(1)}, f32[512,128]{1,0:T(8,128)S(1)}, u32[]{:S(2)}, u32[]{:S(2)}) collective-permute-start(f32[512,128]{1,0:T(8,128)S(1)} %add.104), channel_id=1, source_target_pairs={{0,8},{8,0},{16,24},{24,16},{1,9},{9,1},{17,25},{25,17},{2,10},{10... | collective-permute-start | bytes 786440 | tf_op jit(solution)/shard_map/ppermute | solution.py:313
  60.9 1.6 %collective-permute-start.22 = (f32[128,128]{1,0:T(8,128)S(1)}, f32[128,128]{1,0:T(8,128)S(1)}, u32[]{:S(2)}, u32[]{:S(2)}) collective-permute-start(f32[128,128]{1,0:T(8,128)S(1)} %bitcast_add_fusion.1), channel_id=1, source_target_pairs={{0,16},{8,24},{16,0},{24,8},{1,17},{9,25},{17,1},{25,9},{2,18},{10... | collective-permute-start | bytes 196616 | tf_op jit(solution)/shard_map/ppermute | solution.py:313
  62.5 3.5 %collective-permute-done.15 = f32[512,128]{1,0:T(8,128)S(1)} collective-permute-done((f32[512,128]{1,0:T(8,128)S(1)}, f32[512,128]{1,0:T(8,128)S(1)}, u32[]{:S(2)}, u32[]{:S(2)}) %collective-permute-start.15) | collective-permute-done | bytes 262176 | tf_op jit(solution)/shard_map/ppermute | solution.py:313
  66.0 0.7 collective-permute-done.22
  66.8 0.8 %pad_maximum_fusion = f32[1024,128]{1,0:T(8,128)} fusion(f32[512,128]{1,0:T(8,128)S(1)} %add.105, f32[512,128]{1,0:T(8,128)S(1)} %add.103), kind=kLoop, calls=%fused_computation | loop fusion | flops 131072 | bytes 1048576 | tf_op jit(solution)/shard_map/concatenate | solution.py:415
  68.0 0.7 maximum_maximum_fusion
  (48 shorter events, 2.6 us)
Async XLA Ops:
  0.6 28.8 %copy-start = (s32[8192]{0:T(1024)S(1)}, s32[8192]{0:T(1024)}, u32[]{:S(2)}) copy-start(s32[8192]{0:T(1024)} %param.9) | copy-start | bytes 98308
  0.6 28.8 %copy-start.2 = (bf16[128,256]{1,0:T(8,128)(2,1)S(1)}, bf16[128,256]{1,0:T(8,128)(2,1)}, u32[]{:S(2)}) copy-start(bf16[128,256]{1,0:T(8,128)(2,1)} %weight_ref.1) | copy-start | bytes 196612
  0.7 28.8 %copy-start.1 = (bf16[256,256]{1,0:T(8,128)(2,1)S(1)}, bf16[256,256]{1,0:T(8,128)(2,1)}, u32[]{:S(2)}) copy-start(bf16[256,256]{1,0:T(8,128)(2,1)} %cot_ref.1) | copy-start | bytes 393220
  11.4 5.3 %collective-permute-start = (f32[256,128]{1,0:T(8,128)}, f32[256,128]{1,0:T(8,128)S(1)}, u32[]{:S(2)}, u32[]{:S(2)}) collective-permute-start(f32[256,128]{1,0:T(8,128)} %get-tuple-element.21), channel_id=1, source_target_pairs={{0,1},{1,0},{2,3},{3,2},{4,5},{5,4},{6,7},{7,6},{8,9},{9,8},{10,11... | collective-permute-start | bytes 393224 | tf_op jit(solution)/shard_map/ppermute | solution.py:307
  11.9 4.7 %collective-permute-start.1 = (f32[256,128]{1,0:T(8,128)}, f32[256,128]{1,0:T(8,128)S(1)}, u32[]{:S(2)}, u32[]{:S(2)}) collective-permute-start(f32[256,128]{1,0:T(8,128)} %get-tuple-element.23), channel_id=1, source_target_pairs={{0,1},{1,0},{2,3},{3,2},{4,5},{5,4},{6,7},{7,6},{8,9},{9,8},{10,11... | collective-permute-start | bytes 393224 | tf_op jit(solution)/shard_map/ppermute | solution.py:307
  12.0 1.7 %collective-permute-start.2 = (f32[256,128]{1,0:T(8,128)}, f32[256,128]{1,0:T(8,128)S(1)}, u32[]{:S(2)}, u32[]{:S(2)}) collective-permute-start(f32[256,128]{1,0:T(8,128)} %get-tuple-element.25), channel_id=1, source_target_pairs={{0,1},{1,0},{2,3},{3,2},{4,5},{5,4},{6,7},{7,6},{8,9},{9,8},{10,11... | collective-permute-start | bytes 393224 | tf_op jit(solution)/shard_map/ppermute | solution.py:307
  12.4 5.2 %collective-permute-start.5 = (f32[256,128]{1,0:T(8,128)}, f32[256,128]{1,0:T(8,128)S(1)}, u32[]{:S(2)}, u32[]{:S(2)}) collective-permute-start(f32[256,128]{1,0:T(8,128)} %get-tuple-element.27), channel_id=1, source_target_pairs={{0,1},{1,0},{2,3},{3,2},{4,5},{5,4},{6,7},{7,6},{8,9},{9,8},{10,11... | collective-permute-start | bytes 393224 | tf_op jit(solution)/shard_map/ppermute | solution.py:307
  13.7 6.8 %collective-permute-start.3 = (f32[256,128]{1,0:T(8,128)S(1)}, f32[256,128]{1,0:T(8,128)S(1)}, u32[]{:S(2)}, u32[]{:S(2)}) collective-permute-start(f32[256,128]{1,0:T(8,128)S(1)} %add.98), channel_id=1, source_target_pairs={{0,2},{1,3},{2,0},{3,1},{4,6},{5,7},{6,4},{7,5},{8,10},{9,11},{10,... | collective-permute-start | bytes 393224 | tf_op jit(solution)/shard_map/ppermute | solution.py:310
  18.6 6.7 %collective-permute-start.6 = (f32[256,128]{1,0:T(8,128)S(1)}, f32[256,128]{1,0:T(8,128)S(1)}, u32[]{:S(2)}, u32[]{:S(2)}) collective-permute-start(f32[256,128]{1,0:T(8,128)S(1)} %add.100), channel_id=1, source_target_pairs={{0,2},{1,3},{2,0},{3,1},{4,6},{5,7},{6,4},{7,5},{8,10},{9,11},{10,... | collective-permute-start | bytes 393224 | tf_op jit(solution)/shard_map/ppermute | solution.py:310
  20.5 8.9 %collective-permute-start.4 = (f32[256,128]{1,0:T(8,128)S(1)}, f32[256,128]{1,0:T(8,128)S(1)}, u32[]{:S(2)}, u32[]{:S(2)}) collective-permute-start(f32[256,128]{1,0:T(8,128)S(1)} %add.99), channel_id=1, source_target_pairs={{0,4},{1,5},{2,6},{3,7},{4,0},{5,1},{6,2},{7,3},{8,12},{9,13},{10,... | collective-permute-start | bytes 393224 | tf_op jit(solution)/shard_map/ppermute | solution.py:310
  30.5 8.4 %collective-permute-start.10 = (f32[128,256]{1,0:T(8,128)S(1)}, f32[128,256]{1,0:T(8,128)S(1)}, u32[]{:S(2)}, u32[]{:S(2)}) collective-permute-start(f32[128,256]{1,0:T(8,128)S(1)} %get-tuple-element.30.refs_0_), channel_id=1, source_target_pairs={{0,4},{1,5},{2,6},{3,7},{4,0},{5,1},{6,2},{7,3},{8,12},{9,13},{10,... | collective-permute-start | bytes 393224 | tf_op jit(solution)/shard_map/ppermute | solution.py:310
  30.5 8.9 %collective-permute-start.8 = (f32[128,256]{1,0:T(8,128)S(1)}, f32[128,256]{1,0:T(8,128)S(1)}, u32[]{:S(2)}, u32[]{:S(2)}) collective-permute-start(f32[128,256]{1,0:T(8,128)S(1)} %get-tuple-element.30.refs_0_), channel_id=1, source_target_pairs={{0,2},{1,3},{2,0},{3,1},{4,6},{5,7},{6,4},{7,5},{8,10},{9,11},{10,... | collective-permute-start | bytes 393224 | tf_op jit(solution)/shard_map/ppermute | solution.py:310
  38.9 1.4 %collective-permute-start.11 = (f32[128,256]{1,0:T(8,128)S(1)}, f32[128,256]{1,0:T(8,128)S(1)}, u32[]{:S(2)}, u32[]{:S(2)}) collective-permute-start(f32[128,256]{1,0:T(8,128)S(1)} %collective-permute-done.10.refs_4_), channel_id=1, source_target_pairs={{0,1},{1,0},{2,3},{3,2},{4,5},{5,4},{6,7},{7,6},{8,9},{9,8},{10,11... | collective-permute-start | bytes 393224 | tf_op jit(solution)/shard_map/ppermute | solution.py:307
  38.9 1.4 %collective-permute-start.18 = (f32[128,128]{1,0:T(8,128)S(1)}, f32[128,128]{1,0:T(8,128)S(1)}, u32[]{:S(2)}, u32[]{:S(2)}) collective-permute-start(f32[128,128]{1,0:T(8,128)S(1)} %get-tuple-element.36), channel_id=1, source_target_pairs={{0,1},{1,0},{2,3},{3,2},{4,5},{5,4},{6,7},{7,6},{8,9},{9,8},{10,11... | collective-permute-start | bytes 196616 | tf_op jit(solution)/shard_map/ppermute | solution.py:307
  39.4 2.4 %collective-permute-start.7 = (f32[128,256]{1,0:T(8,128)S(1)}, f32[128,256]{1,0:T(8,128)S(1)}, u32[]{:S(2)}, u32[]{:S(2)}) collective-permute-start(f32[128,256]{1,0:T(8,128)S(1)} %get-tuple-element.30.refs_0_), channel_id=1, source_target_pairs={{0,1},{1,0},{2,3},{3,2},{4,5},{5,4},{6,7},{7,6},{8,9},{9,8},{10,11... | collective-permute-start | bytes 393224 | tf_op jit(solution)/shard_map/ppermute | solution.py:307
  39.4 6.3 %collective-permute-start.12 = (f32[128,256]{1,0:T(8,128)S(1)}, f32[128,256]{1,0:T(8,128)S(1)}, u32[]{:S(2)}, u32[]{:S(2)}) collective-permute-start(f32[128,256]{1,0:T(8,128)S(1)} %collective-permute-done.10.refs_4_), channel_id=1, source_target_pairs={{0,2},{1,3},{2,0},{3,1},{4,6},{5,7},{6,4},{7,5},{8,10},{9,11},{10,... | collective-permute-start | bytes 393224 | tf_op jit(solution)/shard_map/ppermute | solution.py:310
  39.4 2.3 %collective-permute-start.9 = (f32[128,256]{1,0:T(8,128)S(1)}, f32[128,256]{1,0:T(8,128)S(1)}, u32[]{:S(2)}, u32[]{:S(2)}) collective-permute-start(f32[128,256]{1,0:T(8,128)S(1)} %collective-permute-done.8.refs_2_), channel_id=1, source_target_pairs={{0,1},{1,0},{2,3},{3,2},{4,5},{5,4},{6,7},{7,6},{8,9},{9,8},{10,11... | collective-permute-start | bytes 393224 | tf_op jit(solution)/shard_map/ppermute | solution.py:307
  40.3 6.4 %collective-permute-start.19 = (f32[128,128]{1,0:T(8,128)S(1)}, f32[128,128]{1,0:T(8,128)S(1)}, u32[]{:S(2)}, u32[]{:S(2)}) collective-permute-start(f32[128,128]{1,0:T(8,128)S(1)} %fusion), channel_id=1, source_target_pairs={{0,2},{1,3},{2,0},{3,1},{4,6},{5,7},{6,4},{7,5},{8,10},{9,11},{10,... | collective-permute-start | bytes 196616 | tf_op jit(solution)/shard_map/ppermute | solution.py:310
  45.7 1.4 %collective-permute-start.13 = (f32[128,256]{1,0:T(8,128)S(1)}, f32[128,256]{1,0:T(8,128)S(1)}, u32[]{:S(2)}, u32[]{:S(2)}) collective-permute-start(f32[128,256]{1,0:T(8,128)S(1)} %multiply_add_fusion.1.refs_0_), channel_id=1, source_target_pairs={{0,1},{1,0},{2,3},{3,2},{4,5},{5,4},{6,7},{7,6},{8,9},{9,8},{10,11... | collective-permute-start | bytes 393224 | tf_op jit(solution)/shard_map/ppermute | solution.py:307
  46.7 6.0 %collective-permute-start.20 = (f32[128,128]{1,0:T(8,128)S(1)}, f32[128,128]{1,0:T(8,128)S(1)}, u32[]{:S(2)}, u32[]{:S(2)}) collective-permute-start(f32[128,128]{1,0:T(8,128)S(1)} %add_add_fusion), channel_id=1, source_target_pairs={{0,4},{1,5},{2,6},{3,7},{4,0},{5,1},{6,2},{7,3},{8,12},{9,13},{10,... | collective-permute-start | bytes 196616 | tf_op jit(solution)/shard_map/ppermute | solution.py:310
  48.3 11.0 %collective-permute-start.16 = (f32[512,128]{1,0:T(8,128)S(1)}, f32[512,128]{1,0:T(8,128)S(1)}, u32[]{:S(2)}, u32[]{:S(2)}) collective-permute-start(f32[512,128]{1,0:T(8,128)S(1)} %get-tuple-element.34), channel_id=1, source_target_pairs={{0,16},{8,24},{16,0},{24,8},{1,17},{9,25},{17,1},{25,9},{2,18},{10... | collective-permute-start | bytes 786440 | tf_op jit(solution)/shard_map/ppermute | solution.py:313
  49.8 8.8 %collective-permute-start.14 = (f32[512,128]{1,0:T(8,128)S(1)}, f32[512,128]{1,0:T(8,128)S(1)}, u32[]{:S(2)}, u32[]{:S(2)}) collective-permute-start(f32[512,128]{1,0:T(8,128)S(1)} %get-tuple-element.33), channel_id=1, source_target_pairs={{0,8},{8,0},{16,24},{24,16},{1,9},{9,1},{17,25},{25,17},{2,10},{10... | collective-permute-start | bytes 786440 | tf_op jit(solution)/shard_map/ppermute | solution.py:313
  52.8 8.1 %collective-permute-start.21 = (f32[128,128]{1,0:T(8,128)S(1)}, f32[128,128]{1,0:T(8,128)S(1)}, u32[]{:S(2)}, u32[]{:S(2)}) collective-permute-start(f32[128,128]{1,0:T(8,128)S(1)} %bitcast_add_fusion.2), channel_id=1, source_target_pairs={{0,8},{8,0},{16,24},{24,16},{1,9},{9,1},{17,25},{25,17},{2,10},{10... | collective-permute-start | bytes 196616 | tf_op jit(solution)/shard_map/ppermute | solution.py:313
  58.7 7.3 %collective-permute-start.15 = (f32[512,128]{1,0:T(8,128)S(1)}, f32[512,128]{1,0:T(8,128)S(1)}, u32[]{:S(2)}, u32[]{:S(2)}) collective-permute-start(f32[512,128]{1,0:T(8,128)S(1)} %add.102), channel_id=1, source_target_pairs={{0,16},{8,24},{16,0},{24,8},{1,17},{9,25},{17,1},{25,9},{2,18},{10... | collective-permute-start | bytes 786440 | tf_op jit(solution)/shard_map/ppermute | solution.py:313
  59.3 7.5 %collective-permute-start.17 = (f32[512,128]{1,0:T(8,128)S(1)}, f32[512,128]{1,0:T(8,128)S(1)}, u32[]{:S(2)}, u32[]{:S(2)}) collective-permute-start(f32[512,128]{1,0:T(8,128)S(1)} %add.104), channel_id=1, source_target_pairs={{0,8},{8,0},{16,24},{24,16},{1,9},{9,1},{17,25},{25,17},{2,10},{10... | collective-permute-start | bytes 786440 | tf_op jit(solution)/shard_map/ppermute | solution.py:313
  60.9 5.8 %collective-permute-start.22 = (f32[128,128]{1,0:T(8,128)S(1)}, f32[128,128]{1,0:T(8,128)S(1)}, u32[]{:S(2)}, u32[]{:S(2)}) collective-permute-start(f32[128,128]{1,0:T(8,128)S(1)} %bitcast_add_fusion.1), channel_id=1, source_target_pairs={{0,16},{8,24},{16,0},{24,8},{1,17},{9,25},{17,1},{25,9},{2,18},{10... | collective-permute-start | bytes 196616 | tf_op jit(solution)/shard_map/ppermute | solution.py:313
  66.7 1.3 %collective-permute-start.23 = (f32[128,128]{1,0:T(8,128)S(1)}, f32[128,128]{1,0:T(8,128)S(1)}, u32[]{:S(2)}, u32[]{:S(2)}) collective-permute-start(f32[128,128]{1,0:T(8,128)S(1)} %bitcast_add_fusion), channel_id=1, source_target_pairs={{0,1},{1,0},{2,3},{3,2},{4,5},{5,4},{6,7},{7,6},{8,9},{9,8},{10,11... | collective-permute-start | bytes 196616 | tf_op jit(solution)/shard_map/ppermute | solution.py:307

commit v15 on v14

--- a/solution.py
+++ b/solution.py
@@ -405,9 +405,7 @@
 
     done = list(done)
     for t in range(row_bits):
-        if t == 0:
-            wsum = after(wsum, done[-1])
-        else:
+        if t:
             wsum = after(wsum, done[-1])
         wsum = wsum + row_flip(wsum, t)
         done = [x + row_flip(x, (i + t) % row_bits) for i, x in enumerate(done)]

time: 68.9 us -> 68.3 us (level)
  starting transfers between devices: 22 us -> 21.2 us
    ppermute x6, waiting for transfers between devices: 8.46 us -> 5.82 us  [row_flip(): return lax.ppermute(x, 'row', [(i, i ^ 1 << bit) for i in range(n_row)])]
    ppermute x8, waiting for transfers between devices: 15.7 us -> 17.9 us  [chip_flip(): return lax.ppermute(x, 'col', [(i, i ^ 2 << bit) for i in range(n_col)])]
    ppermute x6, starting transfers between devices: 8.34 us -> 6.98 us  [row_flip(): return lax.ppermute(x, 'row', [(i, i ^ 1 << bit) for i in range(n_row)])]
    ppermute x8, starting transfers between devices: 11.3 us -> 12.4 us  [chip_flip(): return lax.ppermute(x, 'col', [(i, i ^ 2 << bit) for i in range(n_col)])]
    ppermute x10, waiting for transfers between devices: 1.22 us -> 1.95 us  [swap(): return lax.ppermute(x, 'col', swap_pairs)]
  transfers between devices with their start and end apart: 24 -> 24, of which waited for: 14 -> 15; matrix products, arithmetic and copies ran while one was open for 6% -> 6% of each run, Pallas kernels for 6% -> 6%
where the time goes in v15:
time: 68.3 us; the launch traced here: 68.1 us
  waiting for transfers between devices  25.7 us (38%)
  starting transfers between devices  21.2 us (31%)
  Pallas kernels  15.2 us (22%)
  other arithmetic  4.6 us (7%)
  between operations  1.5 us (2%)
    ppermute x8, waiting for transfers between devices, chip_flip(): return lax.ppermute(x, 'col', [(i, i ^ 2 << bit) for i in range(n_col)])  17.9 us
    ppermute x8, starting transfers between devices, chip_flip(): return lax.ppermute(x, 'col', [(i, i ^ 2 << bit) for i in range(n_col)])  12.4 us
    pallas_call x1, Pallas kernels, body(): pl.pallas_call(functools.partial(forward_kernel, n_col, chunk, panel_dev,...  10 us
    ppermute x6, starting transfers between devices, row_flip(): return lax.ppermute(x, 'row', [(i, i ^ 1 << bit) for i in range(n_row)])  6.98 us
    ppermute x6, waiting for transfers between devices, row_flip(): return lax.ppermute(x, 'row', [(i, i ^ 1 << bit) for i in range(n_row)])  5.82 us
    pallas_call x1, Pallas kernels, body(): pl.pallas_call(functools.partial(partial_kernel, len(early)), out_shape=(...  2.92 us
    add x4, other arithmetic, after(): return x + 0.0 * other[:, :x.shape[1]]  1.96 us
    ppermute x10, waiting for transfers between devices, swap(): return lax.ppermute(x, 'col', swap_pairs)  1.95 us
  transfers between devices with their start and end apart: 24, of which 15 were waited for; matrix products, arithmetic and copies ran while one was open for 6% of the time, Pallas kernels for 6%

profile of v15, /device:TPU:0, one launch (start us, length us, event | category | flops | bytes accessed | tf_op | source)
XLA Modules:
  0.0 68.1 jit_solution(11074260009762592862)
XLA Ops:
  1.3 10.0 %densify_forward.1 = (f32[256,128]{1,0:T(8,128)}, f32[256,128]{1,0:T(8,128)}, f32[256,128]{1,0:T(8,128)}, f32[256,128]{1,0:T(8,128)}, f32[256,128]{1,0:T(8,128)}...) custom-call(s32[1,1,384]{2,1,0:T(1,128)} %rows_ref.1, ...), custom_call_target="tpu_custom_call" | custom-call | tf_op jit(solution)/shard_map/densify_forward/pallas_call | solution.py:282
  11.4 0.5 collective-permute-start
  12.0 0.4 collective-permute-start.2
  12.5 0.9 %multiply_add_fusion = f32[256,128]{1,0:T(8,128)S(1)} fusion(f32[256,128]{1,0:T(8,128)} %get-tuple-element.24), kind=kLoop, calls=%fused_computation.1 | loop fusion | flops 65536 | bytes 262144 | tf_op jit(solution)/shard_map/add | solution.py:273
  13.7 3.0 %collective-permute-start.3 = (f32[256,128]{1,0:T(8,128)S(1)}, f32[256,128]{1,0:T(8,128)S(1)}, u32[]{:S(2)}, u32[]{:S(2)}) collective-permute-start(f32[256,128]{1,0:T(8,128)S(1)} %add.87), channel_id=1, source_target_pairs={{0,2},{1,3},{2,0},{3,1},{4,6},{5,7},{6,4},{7,5},{8,10},{9,11},{10,... | collective-permute-start | bytes 393224 | tf_op jit(solution)/shard_map/ppermute | solution.py:310
  16.6 1.0 %multiply_add_fusion.2 = (f32[256,128]{1,0:T(8,128)S(1)}, f32[256,128]{1,0:T(8,128)S(1)}) fusion(f32[256,128]{1,0:T(8,128)} %get-tuple-element.22, f32[256,128]{1,0:T(8,128)S(1)} %collective-permute-done.1, f32[256,128]{1,0:T(8,128)} %get-tuple-element.20, f32[256,128]{1,0:T(8,128)S(1)} %collective-permute-done), kind=kLoop, calls=%fused_computation.4 | loop fusion | flops 131072 | bytes 786432 | tf_op jit(solution)/shard_map/add | solution.py:273
  17.7 0.9 %add.89 = f32[256,128]{1,0:T(8,128)S(1)} add(f32[256,128]{1,0:T(8,128)} %get-tuple-element.26, f32[256,128]{1,0:T(8,128)S(1)} %collective-permute-done.5) | non-fusion elementwise | flops 32768 | bytes 393216 | tf_op jit(solution)/shard_map/add | solution.py:326
  18.7 1.8 %collective-permute-done.3 = f32[256,128]{1,0:T(8,128)S(1)} collective-permute-done((f32[256,128]{1,0:T(8,128)S(1)}, f32[256,128]{1,0:T(8,128)S(1)}, u32[]{:S(2)}, u32[]{:S(2)}) %collective-permute-start.3) | collective-permute-done | bytes 131104 | tf_op jit(solution)/shard_map/ppermute | solution.py:310
  20.5 2.8 %collective-permute-start.4 = (f32[256,128]{1,0:T(8,128)S(1)}, f32[256,128]{1,0:T(8,128)S(1)}, u32[]{:S(2)}, u32[]{:S(2)}) collective-permute-start(f32[256,128]{1,0:T(8,128)S(1)} %add.88), channel_id=1, source_target_pairs={{0,4},{1,5},{2,6},{3,7},{4,0},{5,1},{6,2},{7,3},{8,12},{9,13},{10,... | collective-permute-start | bytes 393224 | tf_op jit(solution)/shard_map/ppermute | solution.py:310
  23.3 2.0 %collective-permute-done.6.refs_2_ = f32[256,128]{1,0:T(8,128)S(1)} collective-permute-done((f32[256,128]{1,0:T(8,128)S(1)}, f32[256,128]{1,0:T(8,128)S(1)}, u32[]{:S(2)}, u32[]{:S(2)}) %collective-permute-start.6) | collective-permute-done | bytes 131104 | tf_op jit(solution)/shard_map/ppermute | solution.py:310
  25.3 4.1 %collective-permute-done.4.refs_1_ = f32[256,128]{1,0:T(8,128)S(1)} collective-permute-done((f32[256,128]{1,0:T(8,128)S(1)}, f32[256,128]{1,0:T(8,128)S(1)}, u32[]{:S(2)}, u32[]{:S(2)}) %collective-permute-start.4) | collective-permute-done | bytes 131104 | tf_op jit(solution)/shard_map/ppermute | solution.py:310
  29.4 1.1 %middle.1 = (bf16[256,256]{1,0:T(8,128)(2,1)}, f32[128,256]{1,0:T(8,128)S(1)}, f32[128,128]{1,0:T(8,128)S(1)}, f32[128,128]{1,0:T(8,128)S(1)}) custom-call(s32[64,128]{1,0:T(8,128)S(1)} %bitcast.6, bf16[256,256]{1,0:T(8,128)(2,1)S(1)} %copy-done.1, bf16[128,256]{1,0:T(8,128)(2,1)S(1)} %copy-done.2, f32[256,128]{1,0:T(8,128)S(1)} %get-tuple-element.38.refs_0_, ...), custom_call_target="tpu_custom_call" | custom-call | tf_op jit(solution)/shard_map/middle/pallas_call | solution.py:335
  30.5 3.8 %collective-permute-start.8 = (f32[128,256]{1,0:T(8,128)S(1)}, f32[128,256]{1,0:T(8,128)S(1)}, u32[]{:S(2)}, u32[]{:S(2)}) collective-permute-start(f32[128,256]{1,0:T(8,128)S(1)} %get-tuple-element.30.refs_0_), channel_id=1, source_target_pairs={{0,2},{1,3},{2,0},{3,1},{4,6},{5,7},{6,4},{7,5},{8,10},{9,11},{10,... | collective-permute-start | bytes 393224 | tf_op jit(solution)/shard_map/ppermute | solution.py:310
  34.4 4.5 %collective-permute-done.10.refs_4_ = f32[128,256]{1,0:T(8,128)S(1)} collective-permute-done((f32[128,256]{1,0:T(8,128)S(1)}, f32[128,256]{1,0:T(8,128)S(1)}, u32[]{:S(2)}, u32[]{:S(2)}) %collective-permute-start.10) | collective-permute-done | bytes 131104 | tf_op jit(solution)/shard_map/ppermute | solution.py:310
  39.6 0.6 collective-permute-done.11.refs_5_
  40.4 2.9 %backward_early.1 = (f32[128,1024]{1,0:T(8,128)S(1)}, bf16[512,1024]{1,0:T(8,128)(2,1)S(1)}) custom-call(bf16[2048,1024]{1,0:T(8,128)(2,1)} %get-tuple-element.29.tile_ref, f32[128,256]{1,0:T(8,128)S(1)} %get-tuple-element.30.refs_0_, f32[128,256]{1,0:T(8,128)S(1)} %collective-permute-done.7.refs_1_, f32[128,256]{1,0:T(8,128)S(1)} %collective-permute-done.8.refs_2_, ...), custom_call_target="tpu_custom_call" | custom-call | flops 1073741824 | bytes 33554432 | tf_op jit(solution)/shard_map/backward_early/pallas_call | solution.py:358
  43.4 1.6 %collective-permute-done.12 = f32[128,256]{1,0:T(8,128)S(1)} collective-permute-done((f32[128,256]{1,0:T(8,128)S(1)}, f32[128,256]{1,0:T(8,128)S(1)}, u32[]{:S(2)}, u32[]{:S(2)}) %collective-permute-start.12) | collective-permute-done | bytes 131104 | tf_op jit(solution)/shard_map/ppermute | solution.py:310
  45.5 0.9 %collective-permute-done.13.refs_1_ = f32[128,256]{1,0:T(8,128)S(1)} collective-permute-done((f32[128,256]{1,0:T(8,128)S(1)}, f32[128,256]{1,0:T(8,128)S(1)}, u32[]{:S(2)}, u32[]{:S(2)}) %collective-permute-start.13) | collective-permute-done | bytes 131104 | tf_op jit(solution)/shard_map/ppermute | solution.py:307
  46.4 1.1 %backward_late.1 = (f32[512,128]{1,0:T(8,128)S(1)}, f32[512,128]{1,0:T(8,128)S(1)}) custom-call(s32[64,128]{1,0:T(8,128)S(1)} %bitcast.7, bf16[512,1024]{1,0:T(8,128)(2,1)S(1)} %get-tuple-element.31.dense_ref, f32[128,1024]{1,0:T(8,128)S(1)} %get-tuple-element.32.sofar_ref, f32[128,256]{1,0:T(8,128)S(1)} %multiply_add_fusion.1.refs_0_, ...), custom_call_target="tpu_custom_call" | custom-call | tf_op jit(solution)/shard_map/backward_late/pallas_call | solution.py:388
  47.5 1.6 %collective-permute-start.16 = (f32[512,128]{1,0:T(8,128)S(1)}, f32[512,128]{1,0:T(8,128)S(1)}, u32[]{:S(2)}, u32[]{:S(2)}) collective-permute-start(f32[512,128]{1,0:T(8,128)S(1)} %get-tuple-element.34), channel_id=1, source_target_pairs={{0,16},{8,24},{16,0},{24,8},{1,17},{9,25},{17,1},{25,9},{2,18},{10... | collective-permute-start | bytes 786440 | tf_op jit(solution)/shard_map/ppermute | solution.py:313
  49.1 1.5 %collective-permute-start.14 = (f32[512,128]{1,0:T(8,128)S(1)}, f32[512,128]{1,0:T(8,128)S(1)}, u32[]{:S(2)}, u32[]{:S(2)}) collective-permute-start(f32[512,128]{1,0:T(8,128)S(1)} %get-tuple-element.33), channel_id=1, source_target_pairs={{0,8},{8,0},{16,24},{24,16},{1,9},{9,1},{17,25},{25,17},{2,10},{10... | collective-permute-start | bytes 786440 | tf_op jit(solution)/shard_map/ppermute | solution.py:313
  50.6 2.3 %collective-permute-start.20 = (f32[128,128]{1,0:T(8,128)S(1)}, f32[128,128]{1,0:T(8,128)S(1)}, u32[]{:S(2)}, u32[]{:S(2)}) collective-permute-start(f32[128,128]{1,0:T(8,128)S(1)} %add_add_fusion), channel_id=1, source_target_pairs={{0,4},{1,5},{2,6},{3,7},{4,0},{5,1},{6,2},{7,3},{8,12},{9,13},{10,... | collective-permute-start | bytes 196616 | tf_op jit(solution)/shard_map/ppermute | solution.py:310
  52.9 3.7 %collective-permute-done.20 = f32[128,128]{1,0:T(8,128)S(1)} collective-permute-done((f32[128,128]{1,0:T(8,128)S(1)}, f32[128,128]{1,0:T(8,128)S(1)}, u32[]{:S(2)}, u32[]{:S(2)}) %collective-permute-start.20) | collective-permute-done | bytes 65568 | tf_op jit(solution)/shard_map/ppermute | solution.py:310
  56.6 0.7 %collective-permute-start.21 = (f32[128,128]{1,0:T(8,128)S(1)}, f32[128,128]{1,0:T(8,128)S(1)}, u32[]{:S(2)}, u32[]{:S(2)}) collective-permute-start(f32[128,128]{1,0:T(8,128)S(1)} %add.100), channel_id=1, source_target_pairs={{0,8},{8,0},{16,24},{24,16},{1,9},{9,1},{17,25},{25,17},{2,10},{10... | collective-permute-start | bytes 196616 | tf_op jit(solution)/shard_map/ppermute | solution.py:313
  57.3 1.6 %collective-permute-start.15 = (f32[512,128]{1,0:T(8,128)S(1)}, f32[512,128]{1,0:T(8,128)S(1)}, u32[]{:S(2)}, u32[]{:S(2)}) collective-permute-start(f32[512,128]{1,0:T(8,128)S(1)} %add.91), channel_id=1, source_target_pairs={{0,16},{8,24},{16,0},{24,8},{1,17},{9,25},{17,1},{25,9},{2,18},{10... | collective-permute-start | bytes 786440 | tf_op jit(solution)/shard_map/ppermute | solution.py:313
  59.0 0.6 collective-permute-start.17
  59.6 1.7 %collective-permute-done.21 = f32[128,128]{1,0:T(8,128)S(1)} collective-permute-done((f32[128,128]{1,0:T(8,128)S(1)}, f32[128,128]{1,0:T(8,128)S(1)}, u32[]{:S(2)}, u32[]{:S(2)}) %collective-permute-start.21) | collective-permute-done | bytes 65568 | tf_op jit(solution)/shard_map/ppermute | solution.py:313
  61.3 1.0 %collective-permute-start.22 = (f32[128,128]{1,0:T(8,128)S(1)}, f32[128,128]{1,0:T(8,128)S(1)}, u32[]{:S(2)}, u32[]{:S(2)}) collective-permute-start(f32[128,128]{1,0:T(8,128)S(1)} %bitcast_add_fusion.1), channel_id=1, source_target_pairs={{0,16},{8,24},{16,0},{24,8},{1,17},{9,25},{17,1},{25,9},{2,18},{10... | collective-permute-start | bytes 196616 | tf_op jit(solution)/shard_map/ppermute | solution.py:313
  62.3 3.1 %collective-permute-done.15 = f32[512,128]{1,0:T(8,128)S(1)} collective-permute-done((f32[512,128]{1,0:T(8,128)S(1)}, f32[512,128]{1,0:T(8,128)S(1)}, u32[]{:S(2)}, u32[]{:S(2)}) %collective-permute-start.15) | collective-permute-done | bytes 262176 | tf_op jit(solution)/shard_map/ppermute | solution.py:313
  65.4 0.7 collective-permute-done.22
  66.6 0.8 %pad_maximum_fusion = f32[1024,128]{1,0:T(8,128)} fusion(f32[512,128]{1,0:T(8,128)S(1)} %add.94, f32[512,128]{1,0:T(8,128)S(1)} %add.92), kind=kLoop, calls=%fused_computation | loop fusion | flops 131072 | bytes 1048576 | tf_op jit(solution)/shard_map/concatenate | solution.py:413
  67.5 0.7 maximum_maximum_fusion
  (47 shorter events, 2.6 us)
Async XLA Ops:
  0.6 28.8 %copy-start = (s32[8192]{0:T(1024)S(1)}, s32[8192]{0:T(1024)}, u32[]{:S(2)}) copy-start(s32[8192]{0:T(1024)} %param.9) | copy-start | bytes 98308
  0.6 28.8 %copy-start.2 = (bf16[128,256]{1,0:T(8,128)(2,1)S(1)}, bf16[128,256]{1,0:T(8,128)(2,1)}, u32[]{:S(2)}) copy-start(bf16[128,256]{1,0:T(8,128)(2,1)} %weight_ref.1) | copy-start | bytes 196612
  0.7 28.8 %copy-start.1 = (bf16[256,256]{1,0:T(8,128)(2,1)S(1)}, bf16[256,256]{1,0:T(8,128)(2,1)}, u32[]{:S(2)}) copy-start(bf16[256,256]{1,0:T(8,128)(2,1)} %cot_ref.1) | copy-start | bytes 393220
  11.4 5.3 %collective-permute-start = (f32[256,128]{1,0:T(8,128)}, f32[256,128]{1,0:T(8,128)S(1)}, u32[]{:S(2)}, u32[]{:S(2)}) collective-permute-start(f32[256,128]{1,0:T(8,128)} %get-tuple-element.21), channel_id=1, source_target_pairs={{0,1},{1,0},{2,3},{3,2},{4,5},{5,4},{6,7},{7,6},{8,9},{9,8},{10,11... | collective-permute-start | bytes 393224 | tf_op jit(solution)/shard_map/ppermute | solution.py:307
  11.9 4.7 %collective-permute-start.1 = (f32[256,128]{1,0:T(8,128)}, f32[256,128]{1,0:T(8,128)S(1)}, u32[]{:S(2)}, u32[]{:S(2)}) collective-permute-start(f32[256,128]{1,0:T(8,128)} %get-tuple-element.23), channel_id=1, source_target_pairs={{0,1},{1,0},{2,3},{3,2},{4,5},{5,4},{6,7},{7,6},{8,9},{9,8},{10,11... | collective-permute-start | bytes 393224 | tf_op jit(solution)/shard_map/ppermute | solution.py:307
  12.0 1.7 %collective-permute-start.2 = (f32[256,128]{1,0:T(8,128)}, f32[256,128]{1,0:T(8,128)S(1)}, u32[]{:S(2)}, u32[]{:S(2)}) collective-permute-start(f32[256,128]{1,0:T(8,128)} %get-tuple-element.25), channel_id=1, source_target_pairs={{0,1},{1,0},{2,3},{3,2},{4,5},{5,4},{6,7},{7,6},{8,9},{9,8},{10,11... | collective-permute-start | bytes 393224 | tf_op jit(solution)/shard_map/ppermute | solution.py:307
  12.4 5.2 %collective-permute-start.5 = (f32[256,128]{1,0:T(8,128)}, f32[256,128]{1,0:T(8,128)S(1)}, u32[]{:S(2)}, u32[]{:S(2)}) collective-permute-start(f32[256,128]{1,0:T(8,128)} %get-tuple-element.27), channel_id=1, source_target_pairs={{0,1},{1,0},{2,3},{3,2},{4,5},{5,4},{6,7},{7,6},{8,9},{9,8},{10,11... | collective-permute-start | bytes 393224 | tf_op jit(solution)/shard_map/ppermute | solution.py:307
  13.7 6.8 %collective-permute-start.3 = (f32[256,128]{1,0:T(8,128)S(1)}, f32[256,128]{1,0:T(8,128)S(1)}, u32[]{:S(2)}, u32[]{:S(2)}) collective-permute-start(f32[256,128]{1,0:T(8,128)S(1)} %add.87), channel_id=1, source_target_pairs={{0,2},{1,3},{2,0},{3,1},{4,6},{5,7},{6,4},{7,5},{8,10},{9,11},{10,... | collective-permute-start | bytes 393224 | tf_op jit(solution)/shard_map/ppermute | solution.py:310
  18.6 6.7 %collective-permute-start.6 = (f32[256,128]{1,0:T(8,128)S(1)}, f32[256,128]{1,0:T(8,128)S(1)}, u32[]{:S(2)}, u32[]{:S(2)}) collective-permute-start(f32[256,128]{1,0:T(8,128)S(1)} %add.89), channel_id=1, source_target_pairs={{0,2},{1,3},{2,0},{3,1},{4,6},{5,7},{6,4},{7,5},{8,10},{9,11},{10,... | collective-permute-start | bytes 393224 | tf_op jit(solution)/shard_map/ppermute | solution.py:310
  20.5 8.9 %collective-permute-start.4 = (f32[256,128]{1,0:T(8,128)S(1)}, f32[256,128]{1,0:T(8,128)S(1)}, u32[]{:S(2)}, u32[]{:S(2)}) collective-permute-start(f32[256,128]{1,0:T(8,128)S(1)} %add.88), channel_id=1, source_target_pairs={{0,4},{1,5},{2,6},{3,7},{4,0},{5,1},{6,2},{7,3},{8,12},{9,13},{10,... | collective-permute-start | bytes 393224 | tf_op jit(solution)/shard_map/ppermute | solution.py:310
  30.5 8.4 %collective-permute-start.10 = (f32[128,256]{1,0:T(8,128)S(1)}, f32[128,256]{1,0:T(8,128)S(1)}, u32[]{:S(2)}, u32[]{:S(2)}) collective-permute-start(f32[128,256]{1,0:T(8,128)S(1)} %get-tuple-element.30.refs_0_), channel_id=1, source_target_pairs={{0,4},{1,5},{2,6},{3,7},{4,0},{5,1},{6,2},{7,3},{8,12},{9,13},{10,... | collective-permute-start | bytes 393224 | tf_op jit(solution)/shard_map/ppermute | solution.py:310
  30.5 8.5 %collective-permute-start.8 = (f32[128,256]{1,0:T(8,128)S(1)}, f32[128,256]{1,0:T(8,128)S(1)}, u32[]{:S(2)}, u32[]{:S(2)}) collective-permute-start(f32[128,256]{1,0:T(8,128)S(1)} %get-tuple-element.30.refs_0_), channel_id=1, source_target_pairs={{0,2},{1,3},{2,0},{3,1},{4,6},{5,7},{6,4},{7,5},{8,10},{9,11},{10,... | collective-permute-start | bytes 393224 | tf_op jit(solution)/shard_map/ppermute | solution.py:310
  34.4 5.3 %collective-permute-start.7 = (f32[128,256]{1,0:T(8,128)S(1)}, f32[128,256]{1,0:T(8,128)S(1)}, u32[]{:S(2)}, u32[]{:S(2)}) collective-permute-start(f32[128,256]{1,0:T(8,128)S(1)} %get-tuple-element.30.refs_0_), channel_id=1, source_target_pairs={{0,1},{1,0},{2,3},{3,2},{4,5},{5,4},{6,7},{7,6},{8,9},{9,8},{10,11... | collective-permute-start | bytes 393224 | tf_op jit(solution)/shard_map/ppermute | solution.py:307
  38.9 1.3 %collective-permute-start.11 = (f32[128,256]{1,0:T(8,128)S(1)}, f32[128,256]{1,0:T(8,128)S(1)}, u32[]{:S(2)}, u32[]{:S(2)}) collective-permute-start(f32[128,256]{1,0:T(8,128)S(1)} %collective-permute-done.10.refs_4_), channel_id=1, source_target_pairs={{0,1},{1,0},{2,3},{3,2},{4,5},{5,4},{6,7},{7,6},{8,9},{9,8},{10,11... | collective-permute-start | bytes 393224 | tf_op jit(solution)/shard_map/ppermute | solution.py:307
  39.1 1.4 %collective-permute-start.9 = (f32[128,256]{1,0:T(8,128)S(1)}, f32[128,256]{1,0:T(8,128)S(1)}, u32[]{:S(2)}, u32[]{:S(2)}) collective-permute-start(f32[128,256]{1,0:T(8,128)S(1)} %collective-permute-done.8.refs_2_), channel_id=1, source_target_pairs={{0,1},{1,0},{2,3},{3,2},{4,5},{5,4},{6,7},{7,6},{8,9},{9,8},{10,11... | collective-permute-start | bytes 393224 | tf_op jit(solution)/shard_map/ppermute | solution.py:307
  39.4 5.6 %collective-permute-start.12 = (f32[128,256]{1,0:T(8,128)S(1)}, f32[128,256]{1,0:T(8,128)S(1)}, u32[]{:S(2)}, u32[]{:S(2)}) collective-permute-start(f32[128,256]{1,0:T(8,128)S(1)} %collective-permute-done.10.refs_4_), channel_id=1, source_target_pairs={{0,2},{1,3},{2,0},{3,1},{4,6},{5,7},{6,4},{7,5},{8,10},{9,11},{10,... | collective-permute-start | bytes 393224 | tf_op jit(solution)/shard_map/ppermute | solution.py:310
  39.4 5.7 %collective-permute-start.18 = (f32[128,128]{1,0:T(8,128)S(1)}, f32[128,128]{1,0:T(8,128)S(1)}, u32[]{:S(2)}, u32[]{:S(2)}) collective-permute-start(f32[128,128]{1,0:T(8,128)S(1)} %get-tuple-element.36), channel_id=1, source_target_pairs={{0,1},{1,0},{2,3},{3,2},{4,5},{5,4},{6,7},{7,6},{8,9},{9,8},{10,11... | collective-permute-start | bytes 196616 | tf_op jit(solution)/shard_map/ppermute | solution.py:307
  45.0 1.4 %collective-permute-start.13 = (f32[128,256]{1,0:T(8,128)S(1)}, f32[128,256]{1,0:T(8,128)S(1)}, u32[]{:S(2)}, u32[]{:S(2)}) collective-permute-start(f32[128,256]{1,0:T(8,128)S(1)} %multiply_add_fusion.1.refs_0_), channel_id=1, source_target_pairs={{0,1},{1,0},{2,3},{3,2},{4,5},{5,4},{6,7},{7,6},{8,9},{9,8},{10,11... | collective-permute-start | bytes 393224 | tf_op jit(solution)/shard_map/ppermute | solution.py:307
  45.1 5.5 %collective-permute-start.19 = (f32[128,128]{1,0:T(8,128)S(1)}, f32[128,128]{1,0:T(8,128)S(1)}, u32[]{:S(2)}, u32[]{:S(2)}) collective-permute-start(f32[128,128]{1,0:T(8,128)S(1)} %fusion), channel_id=1, source_target_pairs={{0,2},{1,3},{2,0},{3,1},{4,6},{5,7},{6,4},{7,5},{8,10},{9,11},{10,... | collective-permute-start | bytes 196616 | tf_op jit(solution)/shard_map/ppermute | solution.py:310
  47.5 11.4 %collective-permute-start.16 = (f32[512,128]{1,0:T(8,128)S(1)}, f32[512,128]{1,0:T(8,128)S(1)}, u32[]{:S(2)}, u32[]{:S(2)}) collective-permute-start(f32[512,128]{1,0:T(8,128)S(1)} %get-tuple-element.34), channel_id=1, source_target_pairs={{0,16},{8,24},{16,0},{24,8},{1,17},{9,25},{17,1},{25,9},{2,18},{10... | collective-permute-start | bytes 786440 | tf_op jit(solution)/shard_map/ppermute | solution.py:313
  49.1 8.2 %collective-permute-start.14 = (f32[512,128]{1,0:T(8,128)S(1)}, f32[512,128]{1,0:T(8,128)S(1)}, u32[]{:S(2)}, u32[]{:S(2)}) collective-permute-start(f32[512,128]{1,0:T(8,128)S(1)} %get-tuple-element.33), channel_id=1, source_target_pairs={{0,8},{8,0},{16,24},{24,16},{1,9},{9,1},{17,25},{25,17},{2,10},{10... | collective-permute-start | bytes 786440 | tf_op jit(solution)/shard_map/ppermute | solution.py:313
  50.6 6.0 %collective-permute-start.20 = (f32[128,128]{1,0:T(8,128)S(1)}, f32[128,128]{1,0:T(8,128)S(1)}, u32[]{:S(2)}, u32[]{:S(2)}) collective-permute-start(f32[128,128]{1,0:T(8,128)S(1)} %add_add_fusion), channel_id=1, source_target_pairs={{0,4},{1,5},{2,6},{3,7},{4,0},{5,1},{6,2},{7,3},{8,12},{9,13},{10,... | collective-permute-start | bytes 196616 | tf_op jit(solution)/shard_map/ppermute | solution.py:310
  56.6 4.7 %collective-permute-start.21 = (f32[128,128]{1,0:T(8,128)S(1)}, f32[128,128]{1,0:T(8,128)S(1)}, u32[]{:S(2)}, u32[]{:S(2)}) collective-permute-start(f32[128,128]{1,0:T(8,128)S(1)} %add.100), channel_id=1, source_target_pairs={{0,8},{8,0},{16,24},{24,16},{1,9},{9,1},{17,25},{25,17},{2,10},{10... | collective-permute-start | bytes 196616 | tf_op jit(solution)/shard_map/ppermute | solution.py:313
  57.3 8.0 %collective-permute-start.15 = (f32[512,128]{1,0:T(8,128)S(1)}, f32[512,128]{1,0:T(8,128)S(1)}, u32[]{:S(2)}, u32[]{:S(2)}) collective-permute-start(f32[512,128]{1,0:T(8,128)S(1)} %add.91), channel_id=1, source_target_pairs={{0,16},{8,24},{16,0},{24,8},{1,17},{9,25},{17,1},{25,9},{2,18},{10... | collective-permute-start | bytes 786440 | tf_op jit(solution)/shard_map/ppermute | solution.py:313
  59.0 7.6 %collective-permute-start.17 = (f32[512,128]{1,0:T(8,128)S(1)}, f32[512,128]{1,0:T(8,128)S(1)}, u32[]{:S(2)}, u32[]{:S(2)}) collective-permute-start(f32[512,128]{1,0:T(8,128)S(1)} %add.93), channel_id=1, source_target_pairs={{0,8},{8,0},{16,24},{24,16},{1,9},{9,1},{17,25},{25,17},{2,10},{10... | collective-permute-start | bytes 786440 | tf_op jit(solution)/shard_map/ppermute | solution.py:313
  61.3 4.8 %collective-permute-start.22 = (f32[128,128]{1,0:T(8,128)S(1)}, f32[128,128]{1,0:T(8,128)S(1)}, u32[]{:S(2)}, u32[]{:S(2)}) collective-permute-start(f32[128,128]{1,0:T(8,128)S(1)} %bitcast_add_fusion.1), channel_id=1, source_target_pairs={{0,16},{8,24},{16,0},{24,8},{1,17},{9,25},{17,1},{25,9},{2,18},{10... | collective-permute-start | bytes 196616 | tf_op jit(solution)/shard_map/ppermute | solution.py:313
  66.1 1.3 %collective-permute-start.23 = (f32[128,128]{1,0:T(8,128)S(1)}, f32[128,128]{1,0:T(8,128)S(1)}, u32[]{:S(2)}, u32[]{:S(2)}) collective-permute-start(f32[128,128]{1,0:T(8,128)S(1)} %bitcast_add_fusion), channel_id=1, source_target_pairs={{0,1},{1,0},{2,3},{3,2},{4,5},{5,4},{6,7},{7,6},{8,9},{9,8},{10,11... | collective-permute-start | bytes 196616 | tf_op jit(solution)/shard_map/ppermute | solution.py:307

commit v16 on v15

--- a/solution.py
+++ b/solution.py
@@ -218,8 +218,9 @@
 
 
 def last_kernel(n_in, n_out, deg_ref, dense_ref, sofar_ref, *refs):
-    parts, outs = refs[:n_in], refs[n_in:n_in + n_out]
-    dense, stage, lhs, sofar, sems, dense_sem, sofar_sem = refs[n_in + n_out:]
+    parts, outs = refs[:n_in], refs[n_in:n_in + 2 * n_out]
+    dense, stage, lhs, sofar, sems, dense_sem, sofar_sem = refs[n_in + 2 * n_out:]
+    row = lax.axis_index("row")
     width, node_dev = parts[0].shape
     col_nodes = dense.shape[1]
     block = pltpu.make_async_copy(dense_ref, dense, dense_sem)
@@ -238,8 +239,18 @@
         total = sofar[:, n:n + step] + (pair[:width] + pair[width:])
         for at in range(n, n + step, EDGE):
             inv = inv_column(deg_ref, first + at // EDGE)
-            out = outs[at // size]
-            out[at % size:at % size + EDGE, :] = inv * jnp.transpose(total[:, at - n:at - n + EDGE])
+            value = inv * jnp.transpose(total[:, at - n:at - n + EDGE])
+            piece, upper = at // size, at % size >= size // 2
+            bit = lax.shift_right_logical(row, piece) & 1
+            span = pl.ds(at % (size // 2), EDGE)
+
+            @pl.when(bit == int(upper))
+            def _():
+                outs[2 * piece][span, :] = value
+
+            @pl.when(bit != int(upper))
+            def _():
+                outs[2 * piece + 1][span, :] = value
 
 
 def body(n_row, n_col, features, degrees, block_rows, block_cols, live_slots, blocks, weight, cotangent):
@@ -381,15 +392,16 @@
     late = [own[last], swap(own[last])]
     for bit in range(1, chip_bits):
         wsum = wsum + chip_flip(wsum, bit)
-    n_piece = max(1, row_bits)
-    while col_nodes % (EDGE * n_piece):
+    assert row_bits >= 2
+    n_piece = row_bits
+    while col_nodes % (2 * EDGE * n_piece):
         n_piece -= 1
     size = col_nodes // n_piece
     done = pl.pallas_call(
         functools.partial(last_kernel, len(late), n_piece),
-        out_shape=(jax.ShapeDtypeStruct((size, width), F32),) * n_piece,
+        out_shape=(jax.ShapeDtypeStruct((size // 2, width), F32),) * (2 * n_piece),
         in_specs=[vmem, any_space, any_space] + [any_space] * len(late),
-        out_specs=(vmem,) * n_piece,
+        out_specs=(vmem,) * (2 * n_piece),
         scratch_shapes=[
             pltpu.VMEM((len(late) * node_dev, col_nodes), BF16),
             pltpu.VMEM((len(late), width, node_dev), F32),
@@ -403,14 +415,20 @@
         name="backward_late",
     )(deg, rest, sofar, *late)
 
-    done = list(done)
-    for t in range(row_bits):
-        if t:
-            wsum = after(wsum, done[-1])
+    wsum = after(wsum, done[0])
+    done = [done[2 * i] + row_flip(done[2 * i + 1], i) for i in range(n_piece)]
+    wsum = wsum + row_flip(wsum, 0)
+    for t in range(1, row_bits):
+        done = [x + row_flip(x, (i + t) % row_bits) for i, x in enumerate(done)]
+        wsum = after(wsum, done[0])
         wsum = wsum + row_flip(wsum, t)
-        done = [x + row_flip(x, (i + t) % row_bits) for i, x in enumerate(done)]
     wsum = after(wsum, done[0])
-    feat_grad = jnp.concatenate(done, axis=0)
+    halves = []
+    for i, x in enumerate(done):
+        low = lax.shift_right_logical(lax.axis_index("row"), i) & 1 == 0
+        far = row_flip(x, i)
+        halves += [jnp.where(low, x, far), jnp.where(low, far, x)]
+    feat_grad = jnp.concatenate(halves, axis=0)
 
     wother = swap(wsum)
     low = lax.axis_index("col") % 2 == 0

time: 68.3 us -> 71.3 us (1.044)
  Pallas kernels: 15.2 us -> 16.4 us
  starting transfers between devices: 21.2 us -> 22.4 us
    ppermute x6 -> x8, waiting for transfers between devices: 5.82 us -> 11 us  [row_flip(): return lax.ppermute(x, 'row', [(i, i ^ 1 << bit) for i in range(n_row)])]
    ppermute x8, waiting for transfers between devices: 17.9 us -> 14.3 us  [chip_flip(): return lax.ppermute(x, 'col', [(i, i ^ 2 << bit) for i in range(n_col)])]
    ppermute x6 -> x8, starting transfers between devices: 6.98 us -> 8.83 us  [row_flip(): return lax.ppermute(x, 'row', [(i, i ^ 1 << bit) for i in range(n_row)])]
    pallas_call x1, Pallas kernels: 1.12 us -> 2.38 us  [body(): pl.pallas_call(functools.partial(last_kernel, len(late), n_piece), out_sh...]
    ppermute x10, waiting for transfers between devices: 1.95 us -> 0.86 us  [swap(): return lax.ppermute(x, 'col', swap_pairs)]
    ppermute x8, starting transfers between devices: 12.4 us -> 11.3 us  [chip_flip(): return lax.ppermute(x, 'col', [(i, i ^ 2 << bit) for i in range(n_col)])]
  transfers between devices with their start and end apart: 24 -> 26, of which waited for: 15 -> 16; matrix products, arithmetic and copies ran while one was open for 6% -> 6% of each run, Pallas kernels for 6% -> 7%
where the time goes in v16:
time: 71.3 us; the launch traced here: 71.1 us
  waiting for transfers between devices  26.2 us (37%)
  starting transfers between devices  22.4 us (31%)
  Pallas kernels  16.4 us (23%)
  other arithmetic  4.6 us (6%)
  between operations  1.49 us (2%)
    ppermute x8, waiting for transfers between devices, chip_flip(): return lax.ppermute(x, 'col', [(i, i ^ 2 << bit) for i in range(n_col)])  14.3 us
    ppermute x8, starting transfers between devices, chip_flip(): return lax.ppermute(x, 'col', [(i, i ^ 2 << bit) for i in range(n_col)])  11.3 us
    ppermute x8, waiting for transfers between devices, row_flip(): return lax.ppermute(x, 'row', [(i, i ^ 1 << bit) for i in range(n_row)])  11 us
    pallas_call x1, Pallas kernels, body(): pl.pallas_call(functools.partial(forward_kernel, n_col, chunk, panel_dev,...  10 us
    ppermute x8, starting transfers between devices, row_flip(): return lax.ppermute(x, 'row', [(i, i ^ 1 << bit) for i in range(n_row)])  8.83 us
    pallas_call x1, Pallas kernels, body(): pl.pallas_call(functools.partial(partial_kernel, len(early)), out_shape=(...  2.93 us
    pallas_call x1, Pallas kernels, body(): pl.pallas_call(functools.partial(last_kernel, len(late), n_piece), out_sh...  2.38 us
    ppermute x10, starting transfers between devices, swap(): return lax.ppermute(x, 'col', swap_pairs)  2.29 us
  transfers between devices with their start and end apart: 26, of which 16 were waited for; matrix products, arithmetic and copies ran while one was open for 6% of the time, Pallas kernels for 7%

profile of v16, /device:TPU:0, one launch (start us, length us, event | category | flops | bytes accessed | tf_op | source)
XLA Modules:
  0.0 71.1 jit_solution(14439481024831126666)
XLA Ops:
  1.3 10.0 %densify_forward.1 = (f32[256,128]{1,0:T(8,128)}, f32[256,128]{1,0:T(8,128)}, f32[256,128]{1,0:T(8,128)}, f32[256,128]{1,0:T(8,128)}, f32[256,128]{1,0:T(8,128)}...) custom-call(s32[1,1,384]{2,1,0:T(1,128)} %rows_ref.1, ...), custom_call_target="tpu_custom_call" | custom-call | tf_op jit(solution)/shard_map/densify_forward/pallas_call | solution.py:293
  12.5 0.9 %multiply_add_fusion = f32[256,128]{1,0:T(8,128)S(1)} fusion(f32[256,128]{1,0:T(8,128)} %get-tuple-element.26), kind=kLoop, calls=%fused_computation.1 | loop fusion | flops 65536 | bytes 262144 | tf_op jit(solution)/shard_map/add | solution.py:284
  13.7 3.0 %collective-permute-start.3 = (f32[256,128]{1,0:T(8,128)S(1)}, f32[256,128]{1,0:T(8,128)S(1)}, u32[]{:S(2)}, u32[]{:S(2)}) collective-permute-start(f32[256,128]{1,0:T(8,128)S(1)} %add.94), channel_id=1, source_target_pairs={{0,2},{1,3},{2,0},{3,1},{4,6},{5,7},{6,4},{7,5},{8,10},{9,11},{10,... | collective-permute-start | bytes 393224 | tf_op jit(solution)/shard_map/ppermute | solution.py:321
  16.6 1.0 %multiply_add_fusion.2 = (f32[256,128]{1,0:T(8,128)S(1)}, f32[256,128]{1,0:T(8,128)S(1)}) fusion(f32[256,128]{1,0:T(8,128)} %get-tuple-element.24, f32[256,128]{1,0:T(8,128)S(1)} %collective-permute-done.1, f32[256,128]{1,0:T(8,128)} %get-tuple-element.22, f32[256,128]{1,0:T(8,128)S(1)} %collective-permute-done), kind=kLoop, calls=%fused_computation.4 | loop fusion | flops 131072 | bytes 786432 | tf_op jit(solution)/shard_map/add | solution.py:284
  17.7 0.9 %add.96 = f32[256,128]{1,0:T(8,128)S(1)} add(f32[256,128]{1,0:T(8,128)} %get-tuple-element.28, f32[256,128]{1,0:T(8,128)S(1)} %collective-permute-done.5) | non-fusion elementwise | flops 32768 | bytes 393216 | tf_op jit(solution)/shard_map/add | solution.py:337
  18.7 1.8 %collective-permute-done.3 = f32[256,128]{1,0:T(8,128)S(1)} collective-permute-done((f32[256,128]{1,0:T(8,128)S(1)}, f32[256,128]{1,0:T(8,128)S(1)}, u32[]{:S(2)}, u32[]{:S(2)}) %collective-permute-start.3) | collective-permute-done | bytes 131104 | tf_op jit(solution)/shard_map/ppermute | solution.py:321
  20.5 2.8 %collective-permute-start.4 = (f32[256,128]{1,0:T(8,128)S(1)}, f32[256,128]{1,0:T(8,128)S(1)}, u32[]{:S(2)}, u32[]{:S(2)}) collective-permute-start(f32[256,128]{1,0:T(8,128)S(1)} %add.95), channel_id=1, source_target_pairs={{0,4},{1,5},{2,6},{3,7},{4,0},{5,1},{6,2},{7,3},{8,12},{9,13},{10,... | collective-permute-start | bytes 393224 | tf_op jit(solution)/shard_map/ppermute | solution.py:321
  23.3 2.0 %collective-permute-done.6.refs_2_ = f32[256,128]{1,0:T(8,128)S(1)} collective-permute-done((f32[256,128]{1,0:T(8,128)S(1)}, f32[256,128]{1,0:T(8,128)S(1)}, u32[]{:S(2)}, u32[]{:S(2)}) %collective-permute-start.6) | collective-permute-done | bytes 131104 | tf_op jit(solution)/shard_map/ppermute | solution.py:321
  25.3 4.1 %collective-permute-done.4.refs_1_ = f32[256,128]{1,0:T(8,128)S(1)} collective-permute-done((f32[256,128]{1,0:T(8,128)S(1)}, f32[256,128]{1,0:T(8,128)S(1)}, u32[]{:S(2)}, u32[]{:S(2)}) %collective-permute-start.4) | collective-permute-done | bytes 131104 | tf_op jit(solution)/shard_map/ppermute | solution.py:321
  29.4 1.1 %middle.1 = (bf16[256,256]{1,0:T(8,128)(2,1)}, f32[128,256]{1,0:T(8,128)S(1)}, f32[128,128]{1,0:T(8,128)S(1)}, f32[128,128]{1,0:T(8,128)S(1)}) custom-call(s32[64,128]{1,0:T(8,128)S(1)} %bitcast.7, bf16[256,256]{1,0:T(8,128)(2,1)S(1)} %copy-done.1, bf16[128,256]{1,0:T(8,128)(2,1)S(1)} %copy-done.2, f32[256,128]{1,0:T(8,128)S(1)} %get-tuple-element.42.refs_0_, ...), custom_call_target="tpu_custom_call" | custom-call | tf_op jit(solution)/shard_map/middle/pallas_call | solution.py:346
  30.5 3.8 %collective-permute-start.8 = (f32[128,256]{1,0:T(8,128)S(1)}, f32[128,256]{1,0:T(8,128)S(1)}, u32[]{:S(2)}, u32[]{:S(2)}) collective-permute-start(f32[128,256]{1,0:T(8,128)S(1)} %get-tuple-element.32.refs_0_), channel_id=1, source_target_pairs={{0,2},{1,3},{2,0},{3,1},{4,6},{5,7},{6,4},{7,5},{8,10},{9,11},{10,... | collective-permute-start | bytes 393224 | tf_op jit(solution)/shard_map/ppermute | solution.py:321
  34.4 4.5 %collective-permute-done.10.refs_4_ = f32[128,256]{1,0:T(8,128)S(1)} collective-permute-done((f32[128,256]{1,0:T(8,128)S(1)}, f32[128,256]{1,0:T(8,128)S(1)}, u32[]{:S(2)}, u32[]{:S(2)}) %collective-permute-start.10) | collective-permute-done | bytes 131104 | tf_op jit(solution)/shard_map/ppermute | solution.py:321
  40.3 1.4 %collective-permute-start.21 = (f32[128,128]{1,0:T(8,128)S(1)}, f32[128,128]{1,0:T(8,128)S(1)}, u32[]{:S(2)}, u32[]{:S(2)}) collective-permute-start(f32[128,128]{1,0:T(8,128)S(1)} %fusion), channel_id=1, source_target_pairs={{0,2},{1,3},{2,0},{3,1},{4,6},{5,7},{6,4},{7,5},{8,10},{9,11},{10,... | collective-permute-start | bytes 196616 | tf_op jit(solution)/shard_map/ppermute | solution.py:321
  41.8 2.9 %backward_early.1 = (f32[128,1024]{1,0:T(8,128)S(1)}, bf16[512,1024]{1,0:T(8,128)(2,1)S(1)}) custom-call(bf16[2048,1024]{1,0:T(8,128)(2,1)} %get-tuple-element.31.tile_ref, f32[128,256]{1,0:T(8,128)S(1)} %get-tuple-element.32.refs_0_, f32[128,256]{1,0:T(8,128)S(1)} %collective-permute-done.7.refs_1_, f32[128,256]{1,0:T(8,128)S(1)} %collective-permute-done.8.refs_2_, ...), custom_call_target="tpu_custom_call" | custom-call | flops 1073741824 | bytes 33554432 | tf_op jit(solution)/shard_map/backward_early/pallas_call | solution.py:369
  44.7 1.0 %collective-permute-done.12 = f32[128,256]{1,0:T(8,128)S(1)} collective-permute-done((f32[128,256]{1,0:T(8,128)S(1)}, f32[128,256]{1,0:T(8,128)S(1)}, u32[]{:S(2)}, u32[]{:S(2)}) %collective-permute-start.12) | collective-permute-done | bytes 131104 | tf_op jit(solution)/shard_map/ppermute | solution.py:321
  45.8 0.9 %collective-permute-done.21 = f32[128,128]{1,0:T(8,128)S(1)} collective-permute-done((f32[128,128]{1,0:T(8,128)S(1)}, f32[128,128]{1,0:T(8,128)S(1)}, u32[]{:S(2)}, u32[]{:S(2)}) %collective-permute-start.21) | collective-permute-done | bytes 65568 | tf_op jit(solution)/shard_map/ppermute | solution.py:321
  47.1 2.4 %backward_late.1 = (f32[256,128]{1,0:T(8,128)S(1)}, f32[256,128]{1,0:T(8,128)S(1)}, f32[256,128]{1,0:T(8,128)S(1)}, f32[256,128]{1,0:T(8,128)S(1)}) custom-call(s32[64,128]{1,0:T(8,128)S(1)} %bitcast.8, bf16[512,1024]{1,0:T(8,128)(2,1)S(1)} %get-tuple-element.33.dense_ref, f32[128,1024]{1,0:T(8,128)S(1)} %get-tuple-element.34.sofar_ref, ...), custom_call_target="tpu_custom_call" | custom-call | tf_op jit(solution)/shard_map/backward_late/pallas_call | solution.py:400
  49.5 1.6 %collective-permute-start.14 = (f32[256,128]{1,0:T(8,128)S(1)}, f32[256,128]{1,0:T(8,128)S(1)}, u32[]{:S(2)}, u32[]{:S(2)}) collective-permute-start(f32[256,128]{1,0:T(8,128)S(1)} %get-tuple-element.36), channel_id=1, source_target_pairs={{0,8},{8,0},{16,24},{24,16},{1,9},{9,1},{17,25},{25,17},{2,10},{10... | collective-permute-start | bytes 393224 | tf_op jit(solution)/shard_map/ppermute | solution.py:324
  51.1 1.5 %collective-permute-start.17 = (f32[256,128]{1,0:T(8,128)S(1)}, f32[256,128]{1,0:T(8,128)S(1)}, u32[]{:S(2)}, u32[]{:S(2)}) collective-permute-start(f32[256,128]{1,0:T(8,128)S(1)} %get-tuple-element.38), channel_id=1, source_target_pairs={{0,16},{8,24},{16,0},{24,8},{1,17},{9,25},{17,1},{25,9},{2,18},{10... | collective-permute-start | bytes 393224 | tf_op jit(solution)/shard_map/ppermute | solution.py:324
  52.6 2.5 %collective-permute-done.14 = f32[256,128]{1,0:T(8,128)S(1)} collective-permute-done((f32[256,128]{1,0:T(8,128)S(1)}, f32[256,128]{1,0:T(8,128)S(1)}, u32[]{:S(2)}, u32[]{:S(2)}) %collective-permute-start.14) | collective-permute-done | bytes 131104 | tf_op jit(solution)/shard_map/ppermute | solution.py:324
  55.2 1.6 %collective-permute-start.15 = (f32[256,128]{1,0:T(8,128)S(1)}, f32[256,128]{1,0:T(8,128)S(1)}, u32[]{:S(2)}, u32[]{:S(2)}) collective-permute-start(f32[256,128]{1,0:T(8,128)S(1)} %add.98), channel_id=1, source_target_pairs={{0,16},{8,24},{16,0},{24,8},{1,17},{9,25},{17,1},{25,9},{2,18},{10... | collective-permute-start | bytes 393224 | tf_op jit(solution)/shard_map/ppermute | solution.py:324
  56.8 1.6 %collective-permute-start.23 = (f32[128,128]{1,0:T(8,128)S(1)}, f32[128,128]{1,0:T(8,128)S(1)}, u32[]{:S(2)}, u32[]{:S(2)}) collective-permute-start(f32[128,128]{1,0:T(8,128)S(1)} %bitcast_add_fusion.2), channel_id=1, source_target_pairs={{0,8},{8,0},{16,24},{24,16},{1,9},{9,1},{17,25},{25,17},{2,10},{10... | collective-permute-start | bytes 196616 | tf_op jit(solution)/shard_map/ppermute | solution.py:324
  58.3 0.6 collective-permute-start.18
  58.9 1.3 %collective-permute-done.15 = f32[256,128]{1,0:T(8,128)S(1)} collective-permute-done((f32[256,128]{1,0:T(8,128)S(1)}, f32[256,128]{1,0:T(8,128)S(1)}, u32[]{:S(2)}, u32[]{:S(2)}) %collective-permute-start.15) | collective-permute-done | bytes 131104 | tf_op jit(solution)/shard_map/ppermute | solution.py:324
  60.2 1.5 %collective-permute-done.23 = f32[128,128]{1,0:T(8,128)S(1)} collective-permute-done((f32[128,128]{1,0:T(8,128)S(1)}, f32[128,128]{1,0:T(8,128)S(1)}, u32[]{:S(2)}, u32[]{:S(2)}) %collective-permute-start.23) | collective-permute-done | bytes 65568 | tf_op jit(solution)/shard_map/ppermute | solution.py:324
  61.7 0.6 collective-permute-start.24
  62.3 1.0 %collective-permute-start.16 = (f32[256,128]{1,0:T(8,128)S(1)}, f32[256,128]{1,0:T(8,128)S(1)}, u32[]{:S(2)}, u32[]{:S(2)}) collective-permute-start(f32[256,128]{1,0:T(8,128)S(1)} %add.99), channel_id=1, source_target_pairs={{0,8},{8,0},{16,24},{24,16},{1,9},{9,1},{17,25},{25,17},{2,10},{10... | collective-permute-start | bytes 393224 | tf_op jit(solution)/shard_map/ppermute | solution.py:324
  63.3 1.2 %collective-permute-done.18 = f32[256,128]{1,0:T(8,128)S(1)} collective-permute-done((f32[256,128]{1,0:T(8,128)S(1)}, f32[256,128]{1,0:T(8,128)S(1)}, u32[]{:S(2)}, u32[]{:S(2)}) %collective-permute-start.18) | collective-permute-done | bytes 131104 | tf_op jit(solution)/shard_map/ppermute | solution.py:324
  65.0 1.7 %collective-permute-done.24 = f32[128,128]{1,0:T(8,128)S(1)} collective-permute-done((f32[128,128]{1,0:T(8,128)S(1)}, f32[128,128]{1,0:T(8,128)S(1)}, u32[]{:S(2)}, u32[]{:S(2)}) %collective-permute-start.24) | collective-permute-done | bytes 65568 | tf_op jit(solution)/shard_map/ppermute | solution.py:324
  67.3 2.3 %collective-permute-done.19 = f32[256,128]{1,0:T(8,128)S(1)} collective-permute-done((f32[256,128]{1,0:T(8,128)S(1)}, f32[256,128]{1,0:T(8,128)S(1)}, u32[]{:S(2)}, u32[]{:S(2)}) %collective-permute-start.19) | collective-permute-done | bytes 131104 | tf_op jit(solution)/shard_map/ppermute | solution.py:324
  69.6 0.8 %pad_maximum_fusion = f32[1024,128]{1,0:T(8,128)} fusion(f32[256,128]{1,0:T(8,128)S(1)} %get-tuple-element.46, f32[256,128]{1,0:T(8,128)S(1)} %get-tuple-element.45, f32[256,128]{1,0:T(8,128)S(1)} %get-tuple-element.44, f32[256,128]{1,0:T(8,128)S(1)} %get-tuple-element.43), kind=kLoop, calls=%fused_computation | loop fusion | flops 393216 | bytes 1048576 | tf_op jit(solution)/shard_map/concatenate | solution.py:431
  70.5 0.7 maximum_maximum_fusion
  (53 shorter events, 4.7 us)
Async XLA Ops:
  0.6 28.8 %copy-start = (s32[8192]{0:T(1024)S(1)}, s32[8192]{0:T(1024)}, u32[]{:S(2)}) copy-start(s32[8192]{0:T(1024)} %param.9) | copy-start | bytes 98308
  0.6 28.8 %copy-start.2 = (bf16[128,256]{1,0:T(8,128)(2,1)S(1)}, bf16[128,256]{1,0:T(8,128)(2,1)}, u32[]{:S(2)}) copy-start(bf16[128,256]{1,0:T(8,128)(2,1)} %weight_ref.1) | copy-start | bytes 196612
  0.7 28.8 %copy-start.1 = (bf16[256,256]{1,0:T(8,128)(2,1)S(1)}, bf16[256,256]{1,0:T(8,128)(2,1)}, u32[]{:S(2)}) copy-start(bf16[256,256]{1,0:T(8,128)(2,1)} %cot_ref.1) | copy-start | bytes 393220
  11.4 5.3 %collective-permute-start = (f32[256,128]{1,0:T(8,128)}, f32[256,128]{1,0:T(8,128)S(1)}, u32[]{:S(2)}, u32[]{:S(2)}) collective-permute-start(f32[256,128]{1,0:T(8,128)} %get-tuple-element.23), channel_id=1, source_target_pairs={{0,1},{1,0},{2,3},{3,2},{4,5},{5,4},{6,7},{7,6},{8,9},{9,8},{10,11... | collective-permute-start | bytes 393224 | tf_op jit(solution)/shard_map/ppermute | solution.py:318
  11.9 4.7 %collective-permute-start.1 = (f32[256,128]{1,0:T(8,128)}, f32[256,128]{1,0:T(8,128)S(1)}, u32[]{:S(2)}, u32[]{:S(2)}) collective-permute-start(f32[256,128]{1,0:T(8,128)} %get-tuple-element.25), channel_id=1, source_target_pairs={{0,1},{1,0},{2,3},{3,2},{4,5},{5,4},{6,7},{7,6},{8,9},{9,8},{10,11... | collective-permute-start | bytes 393224 | tf_op jit(solution)/shard_map/ppermute | solution.py:318
  12.0 1.7 %collective-permute-start.2 = (f32[256,128]{1,0:T(8,128)}, f32[256,128]{1,0:T(8,128)S(1)}, u32[]{:S(2)}, u32[]{:S(2)}) collective-permute-start(f32[256,128]{1,0:T(8,128)} %get-tuple-element.27), channel_id=1, source_target_pairs={{0,1},{1,0},{2,3},{3,2},{4,5},{5,4},{6,7},{7,6},{8,9},{9,8},{10,11... | collective-permute-start | bytes 393224 | tf_op jit(solution)/shard_map/ppermute | solution.py:318
  12.4 5.2 %collective-permute-start.5 = (f32[256,128]{1,0:T(8,128)}, f32[256,128]{1,0:T(8,128)S(1)}, u32[]{:S(2)}, u32[]{:S(2)}) collective-permute-start(f32[256,128]{1,0:T(8,128)} %get-tuple-element.29), channel_id=1, source_target_pairs={{0,1},{1,0},{2,3},{3,2},{4,5},{5,4},{6,7},{7,6},{8,9},{9,8},{10,11... | collective-permute-start | bytes 393224 | tf_op jit(solution)/shard_map/ppermute | solution.py:318
  13.7 6.8 %collective-permute-start.3 = (f32[256,128]{1,0:T(8,128)S(1)}, f32[256,128]{1,0:T(8,128)S(1)}, u32[]{:S(2)}, u32[]{:S(2)}) collective-permute-start(f32[256,128]{1,0:T(8,128)S(1)} %add.94), channel_id=1, source_target_pairs={{0,2},{1,3},{2,0},{3,1},{4,6},{5,7},{6,4},{7,5},{8,10},{9,11},{10,... | collective-permute-start | bytes 393224 | tf_op jit(solution)/shard_map/ppermute | solution.py:321
  18.6 6.7 %collective-permute-start.6 = (f32[256,128]{1,0:T(8,128)S(1)}, f32[256,128]{1,0:T(8,128)S(1)}, u32[]{:S(2)}, u32[]{:S(2)}) collective-permute-start(f32[256,128]{1,0:T(8,128)S(1)} %add.96), channel_id=1, source_target_pairs={{0,2},{1,3},{2,0},{3,1},{4,6},{5,7},{6,4},{7,5},{8,10},{9,11},{10,... | collective-permute-start | bytes 393224 | tf_op jit(solution)/shard_map/ppermute | solution.py:321
  20.5 8.9 %collective-permute-start.4 = (f32[256,128]{1,0:T(8,128)S(1)}, f32[256,128]{1,0:T(8,128)S(1)}, u32[]{:S(2)}, u32[]{:S(2)}) collective-permute-start(f32[256,128]{1,0:T(8,128)S(1)} %add.95), channel_id=1, source_target_pairs={{0,4},{1,5},{2,6},{3,7},{4,0},{5,1},{6,2},{7,3},{8,12},{9,13},{10,... | collective-permute-start | bytes 393224 | tf_op jit(solution)/shard_map/ppermute | solution.py:321
  30.5 8.4 %collective-permute-start.10 = (f32[128,256]{1,0:T(8,128)S(1)}, f32[128,256]{1,0:T(8,128)S(1)}, u32[]{:S(2)}, u32[]{:S(2)}) collective-permute-start(f32[128,256]{1,0:T(8,128)S(1)} %get-tuple-element.32.refs_0_), channel_id=1, source_target_pairs={{0,4},{1,5},{2,6},{3,7},{4,0},{5,1},{6,2},{7,3},{8,12},{9,13},{10,... | collective-permute-start | bytes 393224 | tf_op jit(solution)/shard_map/ppermute | solution.py:321
  30.5 8.9 %collective-permute-start.8 = (f32[128,256]{1,0:T(8,128)S(1)}, f32[128,256]{1,0:T(8,128)S(1)}, u32[]{:S(2)}, u32[]{:S(2)}) collective-permute-start(f32[128,256]{1,0:T(8,128)S(1)} %get-tuple-element.32.refs_0_), channel_id=1, source_target_pairs={{0,2},{1,3},{2,0},{3,1},{4,6},{5,7},{6,4},{7,5},{8,10},{9,11},{10,... | collective-permute-start | bytes 393224 | tf_op jit(solution)/shard_map/ppermute | solution.py:321
  38.9 1.4 %collective-permute-start.11 = (f32[128,256]{1,0:T(8,128)S(1)}, f32[128,256]{1,0:T(8,128)S(1)}, u32[]{:S(2)}, u32[]{:S(2)}) collective-permute-start(f32[128,256]{1,0:T(8,128)S(1)} %collective-permute-done.10.refs_4_), channel_id=1, source_target_pairs={{0,1},{1,0},{2,3},{3,2},{4,5},{5,4},{6,7},{7,6},{8,9},{9,8},{10,11... | collective-permute-start | bytes 393224 | tf_op jit(solution)/shard_map/ppermute | solution.py:318
  38.9 1.4 %collective-permute-start.20 = (f32[128,128]{1,0:T(8,128)S(1)}, f32[128,128]{1,0:T(8,128)S(1)}, u32[]{:S(2)}, u32[]{:S(2)}) collective-permute-start(f32[128,128]{1,0:T(8,128)S(1)} %get-tuple-element.40), channel_id=1, source_target_pairs={{0,1},{1,0},{2,3},{3,2},{4,5},{5,4},{6,7},{7,6},{8,9},{9,8},{10,11... | collective-permute-start | bytes 196616 | tf_op jit(solution)/shard_map/ppermute | solution.py:318
  39.4 2.4 %collective-permute-start.7 = (f32[128,256]{1,0:T(8,128)S(1)}, f32[128,256]{1,0:T(8,128)S(1)}, u32[]{:S(2)}, u32[]{:S(2)}) collective-permute-start(f32[128,256]{1,0:T(8,128)S(1)} %get-tuple-element.32.refs_0_), channel_id=1, source_target_pairs={{0,1},{1,0},{2,3},{3,2},{4,5},{5,4},{6,7},{7,6},{8,9},{9,8},{10,11... | collective-permute-start | bytes 393224 | tf_op jit(solution)/shard_map/ppermute | solution.py:318
  39.4 6.3 %collective-permute-start.12 = (f32[128,256]{1,0:T(8,128)S(1)}, f32[128,256]{1,0:T(8,128)S(1)}, u32[]{:S(2)}, u32[]{:S(2)}) collective-permute-start(f32[128,256]{1,0:T(8,128)S(1)} %collective-permute-done.10.refs_4_), channel_id=1, source_target_pairs={{0,2},{1,3},{2,0},{3,1},{4,6},{5,7},{6,4},{7,5},{8,10},{9,11},{10,... | collective-permute-start | bytes 393224 | tf_op jit(solution)/shard_map/ppermute | solution.py:321
  39.4 2.3 %collective-permute-start.9 = (f32[128,256]{1,0:T(8,128)S(1)}, f32[128,256]{1,0:T(8,128)S(1)}, u32[]{:S(2)}, u32[]{:S(2)}) collective-permute-start(f32[128,256]{1,0:T(8,128)S(1)} %collective-permute-done.8.refs_2_), channel_id=1, source_target_pairs={{0,1},{1,0},{2,3},{3,2},{4,5},{5,4},{6,7},{7,6},{8,9},{9,8},{10,11... | collective-permute-start | bytes 393224 | tf_op jit(solution)/shard_map/ppermute | solution.py:318
  40.3 6.4 %collective-permute-start.21 = (f32[128,128]{1,0:T(8,128)S(1)}, f32[128,128]{1,0:T(8,128)S(1)}, u32[]{:S(2)}, u32[]{:S(2)}) collective-permute-start(f32[128,128]{1,0:T(8,128)S(1)} %fusion), channel_id=1, source_target_pairs={{0,2},{1,3},{2,0},{3,1},{4,6},{5,7},{6,4},{7,5},{8,10},{9,11},{10,... | collective-permute-start | bytes 196616 | tf_op jit(solution)/shard_map/ppermute | solution.py:321
  45.7 1.4 %collective-permute-start.13 = (f32[128,256]{1,0:T(8,128)S(1)}, f32[128,256]{1,0:T(8,128)S(1)}, u32[]{:S(2)}, u32[]{:S(2)}) collective-permute-start(f32[128,256]{1,0:T(8,128)S(1)} %multiply_add_fusion.1.refs_0_), channel_id=1, source_target_pairs={{0,1},{1,0},{2,3},{3,2},{4,5},{5,4},{6,7},{7,6},{8,9},{9,8},{10,11... | collective-permute-start | bytes 393224 | tf_op jit(solution)/shard_map/ppermute | solution.py:318
  46.7 10.0 %collective-permute-start.22 = (f32[128,128]{1,0:T(8,128)S(1)}, f32[128,128]{1,0:T(8,128)S(1)}, u32[]{:S(2)}, u32[]{:S(2)}) collective-permute-start(f32[128,128]{1,0:T(8,128)S(1)} %add_add_fusion), channel_id=1, source_target_pairs={{0,4},{1,5},{2,6},{3,7},{4,0},{5,1},{6,2},{7,3},{8,12},{9,13},{10,... | collective-permute-start | bytes 196616 | tf_op jit(solution)/shard_map/ppermute | solution.py:321
  49.5 5.6 %collective-permute-start.14 = (f32[256,128]{1,0:T(8,128)S(1)}, f32[256,128]{1,0:T(8,128)S(1)}, u32[]{:S(2)}, u32[]{:S(2)}) collective-permute-start(f32[256,128]{1,0:T(8,128)S(1)} %get-tuple-element.36), channel_id=1, source_target_pairs={{0,8},{8,0},{16,24},{24,16},{1,9},{9,1},{17,25},{25,17},{2,10},{10... | collective-permute-start | bytes 393224 | tf_op jit(solution)/shard_map/ppermute | solution.py:324
  51.1 7.2 %collective-permute-start.17 = (f32[256,128]{1,0:T(8,128)S(1)}, f32[256,128]{1,0:T(8,128)S(1)}, u32[]{:S(2)}, u32[]{:S(2)}) collective-permute-start(f32[256,128]{1,0:T(8,128)S(1)} %get-tuple-element.38), channel_id=1, source_target_pairs={{0,16},{8,24},{16,0},{24,8},{1,17},{9,25},{17,1},{25,9},{2,18},{10... | collective-permute-start | bytes 393224 | tf_op jit(solution)/shard_map/ppermute | solution.py:324
  55.2 5.0 %collective-permute-start.15 = (f32[256,128]{1,0:T(8,128)S(1)}, f32[256,128]{1,0:T(8,128)S(1)}, u32[]{:S(2)}, u32[]{:S(2)}) collective-permute-start(f32[256,128]{1,0:T(8,128)S(1)} %add.98), channel_id=1, source_target_pairs={{0,16},{8,24},{16,0},{24,8},{1,17},{9,25},{17,1},{25,9},{2,18},{10... | collective-permute-start | bytes 393224 | tf_op jit(solution)/shard_map/ppermute | solution.py:324
  56.8 5.0 %collective-permute-start.23 = (f32[128,128]{1,0:T(8,128)S(1)}, f32[128,128]{1,0:T(8,128)S(1)}, u32[]{:S(2)}, u32[]{:S(2)}) collective-permute-start(f32[128,128]{1,0:T(8,128)S(1)} %bitcast_add_fusion.2), channel_id=1, source_target_pairs={{0,8},{8,0},{16,24},{24,16},{1,9},{9,1},{17,25},{25,17},{2,10},{10... | collective-permute-start | bytes 196616 | tf_op jit(solution)/shard_map/ppermute | solution.py:324
  58.3 6.2 %collective-permute-start.18 = (f32[256,128]{1,0:T(8,128)S(1)}, f32[256,128]{1,0:T(8,128)S(1)}, u32[]{:S(2)}, u32[]{:S(2)}) collective-permute-start(f32[256,128]{1,0:T(8,128)S(1)} %add.100), channel_id=1, source_target_pairs={{0,8},{8,0},{16,24},{24,16},{1,9},{9,1},{17,25},{25,17},{2,10},{10... | collective-permute-start | bytes 393224 | tf_op jit(solution)/shard_map/ppermute | solution.py:324
  61.7 4.9 %collective-permute-start.24 = (f32[128,128]{1,0:T(8,128)S(1)}, f32[128,128]{1,0:T(8,128)S(1)}, u32[]{:S(2)}, u32[]{:S(2)}) collective-permute-start(f32[128,128]{1,0:T(8,128)S(1)} %bitcast_add_fusion.1), channel_id=1, source_target_pairs={{0,16},{8,24},{16,0},{24,8},{1,17},{9,25},{17,1},{25,9},{2,18},{10... | collective-permute-start | bytes 196616 | tf_op jit(solution)/shard_map/ppermute | solution.py:324
  62.3 5.0 %collective-permute-start.16 = (f32[256,128]{1,0:T(8,128)S(1)}, f32[256,128]{1,0:T(8,128)S(1)}, u32[]{:S(2)}, u32[]{:S(2)}) collective-permute-start(f32[256,128]{1,0:T(8,128)S(1)} %add.99), channel_id=1, source_target_pairs={{0,8},{8,0},{16,24},{24,16},{1,9},{9,1},{17,25},{25,17},{2,10},{10... | collective-permute-start | bytes 393224 | tf_op jit(solution)/shard_map/ppermute | solution.py:324
  64.5 5.0 %collective-permute-start.19 = (f32[256,128]{1,0:T(8,128)S(1)}, f32[256,128]{1,0:T(8,128)S(1)}, u32[]{:S(2)}, u32[]{:S(2)}) collective-permute-start(f32[256,128]{1,0:T(8,128)S(1)} %add.101), channel_id=1, source_target_pairs={{0,16},{8,24},{16,0},{24,8},{1,17},{9,25},{17,1},{25,9},{2,18},{10... | collective-permute-start | bytes 393224 | tf_op jit(solution)/shard_map/ppermute | solution.py:324
  66.6 3.8 %collective-permute-start.25 = (f32[128,128]{1,0:T(8,128)S(1)}, f32[128,128]{1,0:T(8,128)S(1)}, u32[]{:S(2)}, u32[]{:S(2)}) collective-permute-start(f32[128,128]{1,0:T(8,128)S(1)} %bitcast_add_fusion), channel_id=1, source_target_pairs={{0,1},{1,0},{2,3},{3,2},{4,5},{5,4},{6,7},{7,6},{8,9},{9,8},{10,11... | collective-permute-start | bytes 196616 | tf_op jit(solution)/shard_map/ppermute | solution.py:318
